TPU v7x, 32 devices: a whole 2x2x4 slice. The times are simulated.
32 devices in a mesh: gal: 4 (over y, core), pix: 8 (over z, x).
Axes of the slice: x: 2, y: 2, z: 4, core: 2. Of those that a mesh axis runs over, the one named last changes fastest.
Arguments:
- observed: float32 [8192, 4096], P('pix', 'gal'), may hold values from -6 to 6
- sparse_init: float32 [8192, 4096], P('pix', 'gal'), may hold values from -4 to 4
- dual_init: float32 [8192, 4096], P('pix', 'gal'), may hold values from -4 to 4
- right_init: float32 [64, 4096], P(None, 'gal'), may hold values from -0.09375 to 0.09375
Outputs:
- sparse: float32 [8192, 4096], P('pix', 'gal')
- dual: float32 [8192, 4096], P('pix', 'gal')
- left: float32 [64, 8192], P(None, 'pix')
- right: float32 [64, 4096], P(None, 'gal')
All inputs are finite; a program needn't handle non-finite values.
Results may differ from a plain program's by a relative error of at most 0.0003.
Values sent between devices are 32-bit elements; how exact they have to be, the bound alone decides.
No kernel may reach another device: no remote copies, remote signals or barrier semaphores. Data moves between devices by JAX's collectives and lax.ppermute only.
A program may use at most 64 MiB of HBM per device.

v0:
```python
import jax
import jax.numpy as jnp
from jax import lax
from jax.sharding import PartitionSpec as P

ITERS = 2


MU = 1.25
TAU = 0.6 / 1.25
HIGH = lax.Precision.HIGHEST


def gram_of(panel):
    return lax.dot_general(panel, panel, (((1,), (1,)), ((), ())), precision=HIGH)


def orth_with(panel, gram):
    factor = jnp.linalg.cholesky(gram)
    return jax.scipy.linalg.solve_triangular(factor, panel, lower=True)


def shrink(values):
    return jnp.sign(values) * jnp.maximum(jnp.abs(values) - TAU, 0.0)


def per_device(observed, sparse_init, dual_init, right_init):
    sparse, dual, right = (sparse_init, dual_init, right_init)
    left = None
    for step in range(ITERS):
        target = observed - sparse + dual / MU
        partial_left = lax.dot_general(right, target, (((1,), (1,)), ((), ())), precision=HIGH)
        panel = lax.psum(partial_left, "gal")
        gram_left = lax.psum(gram_of(panel), "pix")
        left = orth_with(panel, gram_left)
        partial_wide = jnp.dot(left, target, precision=HIGH)
        wide = lax.psum(partial_wide, "pix")
        lowrank = lax.dot_general(left, wide, (((0,), (0,)), ((), ())), precision=HIGH)
        sparse = shrink(observed - lowrank + dual / MU)
        dual = dual + MU * (observed - lowrank - sparse)
        whole_wide = lax.all_gather(wide, "gal", axis=1, tiled=True)
        gram_right = gram_of(whole_wide)
        right = orth_with(wide, gram_right)
    return (sparse, dual, left, right)


def solution(mesh):
    return jax.shard_map(
        per_device,
        mesh=mesh,
        in_specs=(P("pix", "gal"), P("pix", "gal"), P("pix", "gal"), P(None, "gal")),
        out_specs=(P("pix", "gal"), P("pix", "gal"), P(None, "pix"), P(None, "gal")),
        check_vma=False,
    )
```

profile of v0, /device:TPU:0, one launch (start us, length us, event | category | flops | bytes accessed | tf_op | source)
XLA Modules:
  0.0 417.0 jit_solution(7218161778816642125)
XLA Ops:
  7.2 0.9 copy-done
  8.1 9.9 %convolution_bitcast_fusion = f32[64,1024]{1,0:T(8,128)} fusion(f32[64,1024]{1,0:T(8,128)S(1)} %copy-done, f32[1024,1024]{1,0:T(8,128)} %param.7, f32[1024,1024]{1,0:T(8,128)} %param.8, f32[1024,1024]{1,0:T(8,128)} %param.9), kind=kOutput, calls=%fused_computation.8 | convolution fusion | flops 808452096 | bytes 13107200 | tf_op jit(solution)/shard_map/dot_general | solution.py:32
  18.1 0.0 all-reduce.7.cloned.1.call-start
  18.1 34.8 %all-reduce.5.cloned.1.call-done = f32[64,1024]{1,0:T(8,128)} async-done(((f32[64,1024]{1,0:T(8,128)}), f32[64,1024]{1,0:T(8,128)}) %all-reduce.5.cloned.1.call-update) | async-done | bytes 262160 | tf_op jit(solution)/shard_map/psum | solution.py:33
  52.9 1.4 fusion.21
  54.3 37.1 %psum.43 = f32[64,64]{0,1:T(8,128)S(1)} all-reduce(f32[64,64]{0,1:T(8,128)S(1)} %fusion.21), channel_id=1, replica_groups=mesh['gal'=4,'pix'=8] {'pix'}, use_global_device_ids=true, to_apply=%region_1.0 | all-reduce | flops 4096 | bytes 32768 | tf_op jit(solution)/shard_map/psum | solution.py:34
  91.4 0.1 copy.9
  91.5 5.8 %cholesky.74 = f32[64,64]{1,0:T(8,128)S(1)} custom-call(f32[64,64]{1,0:T(8,128)S(1)} %fusion.15), custom_call_target="Cholesky" | custom-call | tf_op jit(solution)/shard_map/jit(cholesky)/cholesky | solution.py:19
  97.3 0.6 compare_reduce_fusion.3
  98.0 0.7 fusion
  98.6 4.9 %custom-call.8 = f32[1,64,64]{1,2,0:T(8,128)S(1)} custom-call(f32[1,64,64]{2,1,0:T(8,128)S(1)} %fusion), custom_call_target="InvertDiagBlocksLowerTriangular" | custom-call | tf_op jit(solution)/shard_map/jit(_solve_triangular)/triangular_solve | solution.py:20
  103.6 1.4 fusion.13
  104.9 8.4 %fusion.20 = f32[64,1024]{1,0:T(8,128)} fusion(f32[64,1024]{1,0:T(8,128)S(1)} %fusion.13, f32[1024,1024]{1,0:T(8,128)} %param.7, f32[1024,1024]{1,0:T(8,128)} %param.8, f32[1024,1024]{1,0:T(8,128)} %param.9), kind=kOutput, calls=%fused_computation.45 | convolution fusion | flops 808452096 | bytes 13107200 | tf_op jit(solution)/shard_map/dot_general | solution.py:36
  113.3 0.0 all-gather.3.cloned.1.call-start
  113.4 66.9 %all-reduce.7.cloned.1.call-done = f32[64,1024]{1,0:T(8,128)} async-done(((f32[64,1024]{1,0:T(8,128)}), f32[64,1024]{1,0:T(8,128)}) %all-reduce.7.cloned.1.call-update) | async-done | bytes 262160 | tf_op jit(solution)/shard_map/psum | solution.py:37
  180.3 0.2 all-reduce.9.cloned.1.call-start
  180.5 11.6 %subtract_add_fusion = (f32[1024,1024]{1,0:T(8,128)}, f32[1024,1024]{1,0:T(8,128)}) fusion(f32[1024,1024]{1,0:T(8,128)} %param.7, f32[1024,1024]{1,0:T(8,128)} %param.9, f32[64,1024]{1,0:T(8,128)S(1)} %fusion.13, f32[64,1024]{1,0:T(8,128)} %all-reduce.7.cloned.1.call-done), kind=kOutput, calls=%fused_computation.3 | convolution fusion | flops 819986432 | bytes 17301504 | tf_op jit(solution)/shard_map/dot_general | solution.py:38
  192.1 5.8 %all-gather.3.cloned.1.call-done = f32[64,4096]{1,0:T(8,128)} async-done(((f32[64,1024]{1,0:T(8,128)}), f32[64,4096]{1,0:T(8,128)}) %all-gather.3.cloned.1.call-update) | async-done | bytes 1048592 | tf_op jit(solution)/shard_map/all_gather | solution.py:41
  197.9 2.5 fusion.22
  200.4 0.1 copy.10
  200.5 5.8 %cholesky.85 = f32[64,64]{1,0:T(8,128)S(1)} custom-call(f32[64,64]{1,0:T(8,128)S(1)} %fusion.12), custom_call_target="Cholesky" | custom-call | tf_op jit(solution)/shard_map/jit(cholesky)/cholesky | solution.py:19
  206.4 0.6 compare_reduce_fusion.2
  207.0 0.7 fusion.1
  207.7 4.9 %custom-call.9 = f32[1,64,64]{1,2,0:T(8,128)S(1)} custom-call(f32[1,64,64]{2,1,0:T(8,128)S(1)} %fusion.1), custom_call_target="InvertDiagBlocksLowerTriangular" | custom-call | tf_op jit(solution)/shard_map/jit(_solve_triangular)/triangular_solve | solution.py:20
  212.6 0.4 fusion.10
  213.0 7.0 %fusion.23 = f32[64,1024]{1,0:T(8,128)} fusion(f32[64,1024]{1,0:T(8,128)S(1)} %fusion.10, f32[1024,1024]{1,0:T(8,128)} %get-tuple-element.8), kind=kOutput, calls=%fused_computation.48 | convolution fusion | flops 805306368 | bytes 4718592 | tf_op jit(solution)/shard_map/dot_general | solution.py:32
  220.0 0.0 all-reduce.11.cloned.1.call-start
  220.0 32.1 %all-reduce.9.cloned.1.call-done = f32[64,1024]{1,0:T(8,128)} async-done(((f32[64,1024]{1,0:T(8,128)}), f32[64,1024]{1,0:T(8,128)}) %all-reduce.9.cloned.1.call-update) | async-done | bytes 262160 | tf_op jit(solution)/shard_map/psum | solution.py:33
  252.1 1.4 fusion.24
  253.5 37.1 %psum.46 = f32[64,64]{0,1:T(8,128)S(1)} all-reduce(f32[64,64]{0,1:T(8,128)S(1)} %fusion.24), channel_id=1, replica_groups=mesh['gal'=4,'pix'=8] {'pix'}, use_global_device_ids=true, to_apply=%region_6.9 | all-reduce | flops 4096 | bytes 32768 | tf_op jit(solution)/shard_map/psum | solution.py:34
  290.6 0.1 copy.12
  290.7 5.8 %cholesky.96 = f32[64,64]{1,0:T(8,128)S(1)} custom-call(f32[64,64]{1,0:T(8,128)S(1)} %fusion.9), custom_call_target="Cholesky" | custom-call | tf_op jit(solution)/shard_map/jit(cholesky)/cholesky | solution.py:19
  296.6 0.6 compare_reduce_fusion.1
  297.3 0.7 fusion.2
  297.9 4.9 %custom-call.10 = f32[1,64,64]{1,2,0:T(8,128)S(1)} custom-call(f32[1,64,64]{2,1,0:T(8,128)S(1)} %fusion.2), custom_call_target="InvertDiagBlocksLowerTriangular" | custom-call | tf_op jit(solution)/shard_map/jit(_solve_triangular)/triangular_solve | solution.py:20
  302.8 1.4 fusion.7
  304.2 5.6 %fusion.25 = f32[64,1024]{1,0:T(8,128)} fusion(f32[64,1024]{1,0:T(8,128)S(1)} %fusion.7, f32[1024,1024]{1,0:T(8,128)} %get-tuple-element.8), kind=kOutput, calls=%fused_computation.50 | convolution fusion | flops 805306368 | bytes 4718592 | tf_op jit(solution)/shard_map/dot_general | solution.py:36
  309.9 0.0 all-gather.5.cloned.1.call-start
  309.9 66.9 %all-reduce.11.cloned.1.call-done = f32[64,1024]{1,0:T(8,128)} async-done(((f32[64,1024]{1,0:T(8,128)}), f32[64,1024]{1,0:T(8,128)}) %all-reduce.11.cloned.1.call-update) | async-done | bytes 262160 | tf_op jit(solution)/shard_map/psum | solution.py:37
  376.8 14.0 %multiply_add_fusion = (f32[1024,1024]{1,0:T(8,128)}, f32[1024,1024]{1,0:T(8,128)}) fusion(f32[1024,1024]{1,0:T(8,128)} %param.9, f32[1024,1024]{1,0:T(8,128)} %get-tuple-element.9, f32[1024,1024]{1,0:T(8,128)} %param.7, f32[64,1024]{1,0:T(8,128)S(1)} %fusion.7, f32[64,1024]{1,0:T(8,128)} %all-reduce.11.cloned.1.call-done), kind=kOutput, calls=%fused_computation | convolution fusion | flops 827326464 | bytes 21495808 | tf_op jit(solution)/shard_map/dot_general | solution.py:38
  390.8 3.4 all-gather.5.cloned.1.call-done
  394.3 2.5 fusion.26
  396.8 0.1 copy.13
  396.9 5.8 %cholesky.107 = f32[64,64]{1,0:T(8,128)S(1)} custom-call(f32[64,64]{1,0:T(8,128)S(1)} %fusion.6), custom_call_target="Cholesky" | custom-call | tf_op jit(solution)/shard_map/jit(cholesky)/cholesky | solution.py:19
  402.8 0.6 compare_reduce_fusion
  403.4 0.7 fusion.3
  404.1 4.9 %custom-call.11 = f32[1,64,64]{1,2,0:T(8,128)S(1)} custom-call(f32[1,64,64]{2,1,0:T(8,128)S(1)} %fusion.3), custom_call_target="InvertDiagBlocksLowerTriangular" | custom-call | tf_op jit(solution)/shard_map/jit(_solve_triangular)/triangular_solve | solution.py:20
  409.0 1.1 fusion.4
  (22 shorter events, 0.3 us)
Async XLA Ops:
  7.2 1.0 copy-start
  7.2 45.7 %all-reduce.5.cloned.1.call-start = ((), (), s32[]{:S(2)}) async-start(), calls=%async_computation | async-start | bytes 524288 | tf_op jit(solution)/shard_map/psum | solution.py:33
  18.1 162.2 %all-reduce.7.cloned.1.call-start = ((), (), s32[]{:S(2)}) async-start(), calls=%async_computation.1 | async-start | bytes 524288 | tf_op jit(solution)/shard_map/psum | solution.py:37
  113.3 84.5 %all-gather.3.cloned.1.call-start = ((), (), s32[]{:S(2)}) async-start(), calls=%async_computation.2 | async-start | bytes 1310720 | tf_op jit(solution)/shard_map/all_gather | solution.py:41
  180.3 32.3 %copy-start.2 = (f32[64,1024]{1,0:T(8,128)S(1)}, f32[64,1024]{1,0:T(8,128)}, u32[]{:S(2)}) copy-start(f32[64,1024]{1,0:T(8,128)} %all-reduce.7.cloned.1.call-done) | copy-start | bytes 786436
  180.3 71.8 %all-reduce.9.cloned.1.call-start = ((), (), s32[]{:S(2)}) async-start(), calls=%async_computation.3 | async-start | bytes 524288 | tf_op jit(solution)/shard_map/psum | solution.py:33
  220.0 156.8 %all-reduce.11.cloned.1.call-start = ((), (), s32[]{:S(2)}) async-start(), calls=%async_computation.4 | async-start | bytes 524288 | tf_op jit(solution)/shard_map/psum | solution.py:37
  304.2 86.6 %copy-start.1 = (f32[64,1024]{1,0:T(8,128)}, f32[64,1024]{1,0:T(8,128)S(1)}, u32[]{:S(2)}) copy-start(f32[64,1024]{1,0:T(8,128)S(1)} %fusion.7) | copy-start | bytes 786436
  309.9 84.4 %all-gather.5.cloned.1.call-start = ((), (), s32[]{:S(2)}) async-start(), calls=%async_computation.5 | async-start | bytes 1310720 | tf_op jit(solution)/shard_map/all_gather | solution.py:41
  376.8 32.2 %copy-start.3 = (f32[64,1024]{1,0:T(8,128)S(1)}, f32[64,1024]{1,0:T(8,128)}, u32[]{:S(2)}) copy-start(f32[64,1024]{1,0:T(8,128)} %all-reduce.11.cloned.1.call-done) | copy-start | bytes 786436
Sparse Core Ops, SparseCore 0:
  18.2 34.6 all-reduce.4
  113.4 66.7 all-reduce.6
  181.8 16.0 all-gather.2
  220.1 31.9 all-reduce.8
  310.0 66.7 all-reduce.10
  378.2 16.0 all-gather.4
where the time goes:
time: 417 us
  waiting for transfers between devices  210 us (50%)
  blocking collectives  74.2 us (18%)
  matrix products  68.5 us (16%)
  other arithmetic  48.3 us (12%)
  between operations  14.3 us (3%)
    psum x2, waiting for transfers between devices, per_device(): wide = lax.psum(partial_wide, 'pix')  134 us
    psum x2, blocking collectives, per_device(): gram_left = lax.psum(gram_of(panel), 'pix')  74.2 us
    psum x2, waiting for transfers between devices, per_device(): panel = lax.psum(partial_left, 'gal')  66.9 us
    another operation x12, other arithmetic, orth_with(): factor = jnp.linalg.cholesky(gram)  26.1 us
    dot_general x2, matrix products, per_device(): lax.dot_general(left, wide, (((0,), (0,)), ((), ())), precision=HIGH)  25.6 us
    another operation x8, other arithmetic, orth_with(): return jax.scipy.linalg.solve_triangular(factor, panel, lower=True)  22.2 us
    dot_general x2, matrix products, per_device(): lax.dot_general(right, target, (((1,), (1,)), ((), ())), precision=HIGH)  16.9 us
    dot_general x2, matrix products, per_device(): partial_wide = jnp.dot(left, target, precision=HIGH)  14 us
  transfers between devices with their start and end apart: 6, of which 6 were waited for; matrix products, arithmetic and copies ran while one was open for 6% of the time, Pallas kernels for 0%

commit v1 on v0

v1 whole, which is shorter than its diff:
```python
import jax
import jax.numpy as jnp
from jax import lax
from jax.sharding import PartitionSpec as P

ITERS = 2


MU = 1.25
TAU = 0.6 / 1.25
HIGH = lax.Precision.HIGHEST
CORES = 2


def gram_of(panel):
    return lax.dot_general(panel, panel, (((1,), (1,)), ((), ())), precision=HIGH)


def apply_inverse(factor, panel):
    return jax.scipy.linalg.solve_triangular(factor, panel, lower=True)


def sum_exchange(value, axis, n):
    bit = 1
    while bit < n:
        value = value + lax.ppermute(value, axis, [(i, i ^ bit) for i in range(n)])
        bit *= 2
    return value


def sum_over_gal(value, axis, n):
    half = value.shape[0] // CORES
    core = lax.rem(lax.axis_index(axis), CORES)
    twin = [(i, i ^ 1) for i in range(n)]
    away = lax.dynamic_slice_in_dim(value, (1 - core) * half, half, 0)
    mine = lax.dynamic_slice_in_dim(value, core * half, half, 0)
    mine = mine + lax.ppermute(away, axis, twin)
    got = [
        lax.ppermute(mine, axis, [(i, (i + CORES * k) % n) for i in range(n)])
        for k in range(1, n // CORES)
    ]
    for piece in got:
        mine = mine + piece
    other = lax.ppermute(mine, axis, twin)
    first = jnp.where(core == 0, mine, other)
    second = jnp.where(core == 0, other, mine)
    return jnp.concatenate([first, second], axis=0)


def sum_over_pix(value, axis, n):
    part = value.shape[0] // n
    me = lax.axis_index(axis)
    total = lax.dynamic_slice_in_dim(value, me * part, part, 0)
    got = []
    for k in range(1, n):
        peer = lax.rem(me + k, n)
        piece = lax.dynamic_slice_in_dim(value, peer * part, part, 0)
        got.append(lax.ppermute(piece, axis, [(i, (i + k) % n) for i in range(n)]))
    for piece in got:
        total = total + piece
    whole = jnp.zeros_like(value)
    whole = lax.dynamic_update_slice_in_dim(whole, total, me * part, 0)
    for k in range(1, n):
        piece = lax.ppermute(total, axis, [(i, (i + k) % n) for i in range(n)])
        peer = lax.rem(me + n - k, n)
        whole = lax.dynamic_update_slice_in_dim(whole, piece, peer * part, 0)
    return whole


def solution(mesh):
    n_gal, n_pix = mesh.shape["gal"], mesh.shape["pix"]

    def per_device(observed, sparse_init, dual_init, right_init):
        sparse, scaled, right = (None, dual_init / MU, right_init)
        target = observed - sparse_init + scaled
        for step in range(ITERS):
            last = step == ITERS - 1
            partial_left = lax.dot_general(right, target, (((1,), (1,)), ((), ())), precision=HIGH)
            panel = sum_over_gal(partial_left, "gal", n_gal)
            gram_left = sum_exchange(gram_of(panel), "pix", n_pix)
            raw = sum_over_pix(jnp.dot(panel, target, precision=HIGH), "pix", n_pix)
            factor = jnp.linalg.cholesky(gram_left)
            left = apply_inverse(factor, panel)
            wide = apply_inverse(factor, raw)
            if last:
                gram_right = sum_exchange(gram_of(wide), "gal", n_gal)
                right = apply_inverse(jnp.linalg.cholesky(gram_right), wide)
            else:
                right = wide
            lowrank = lax.dot_general(left, wide, (((0,), (0,)), ((), ())), precision=HIGH)
            value = observed - lowrank + scaled
            scaled = jnp.clip(value, -TAU, TAU)
            sparse = value - scaled
            target = observed - sparse + scaled
        return (sparse, MU * scaled, left, right)

    return jax.shard_map(
        per_device,
        mesh=mesh,
        in_specs=(P("pix", "gal"), P("pix", "gal"), P("pix", "gal"), P(None, "gal")),
        out_specs=(P("pix", "gal"), P("pix", "gal"), P(None, "pix"), P(None, "gal")),
        check_vma=False,
    )
```

time: 417 us -> 170 us (0.41)
  waiting for transfers between devices: 210 us -> 22.2 us
  blocking collectives: 74.2 us -> 0 us
  starting transfers between devices: 0.42 us -> 61.8 us
  matrix products: 68.5 us -> 47.1 us
  between operations: 14.3 us -> 1.14 us
  other arithmetic: 48.3 us -> 36.4 us
    psum x4 -> x0, waiting for transfers between devices: 201 us -> none  [the longest x2 134 us: per_device(): wide = lax.psum(partial_wide, 'pix')]
    psum x2 -> x0, blocking collectives: 74.2 us -> none  [per_device(): gram_left = lax.psum(gram_of(panel), 'pix')]
    ppermute x0 -> x42, starting transfers between devices: none -> 61.8 us  [the longest x14 21.9 us: sum_over_pix(): piece = lax.ppermute(total, axis, [(i, (i + k) % n) for i in range(n)])]
    ppermute x0 -> x42, waiting for transfers between devices: none -> 22.2 us  [the longest x2 7.83 us: sum_over_gal(): lax.ppermute(mine, axis, [(i, (i + CORES * k) % n) for i in range(n)])]
    another operation x20 -> x15, other arithmetic: 48.3 us -> 36.2 us  [the longest x6 16.6 us: apply_inverse(): return jax.scipy.linalg.solve_triangular(factor, panel, lower=True)]
    all_gather x2 -> x0, waiting for transfers between devices: 9.22 us -> none  [per_device(): whole_wide = lax.all_gather(wide, 'gal', axis=1, tiled=True)]
    dot_general x4 -> x3, matrix products: 7.82 us -> 1.09 us  [gram_of(): lax.dot_general(panel, panel, (((1,), (1,)), ((), ())), precision=HIGH)]
    dot_general x2, matrix products: 25.6 us -> 19.7 us  [per_device(): lax.dot_general(left, wide, (((0,), (0,)), ((), ())), precision=HIGH)]
  transfers between devices with their start and end apart: 6 -> 42, of which waited for: 6 -> 15; matrix products, arithmetic and copies ran while one was open for 6% -> 21% of each run, Pallas kernels for 0% -> 0%
where the time goes in v1:
time: 170 us
  starting transfers between devices  61.8 us (36%)
  matrix products  47.1 us (28%)
  other arithmetic  36.4 us (21%)
  waiting for transfers between devices  22.2 us (13%)
    ppermute x14, starting transfers between devices, sum_over_pix(): piece = lax.ppermute(total, axis, [(i, (i + k) % n) for i in range(n)])  21.9 us
    ppermute x14, starting transfers between devices, sum_over_pix(): got.append(lax.ppermute(piece, axis, [(i, (i + k) % n) for i in range(n)]))  21.1 us
    dot_general x2, matrix products, per_device(): lax.dot_general(left, wide, (((0,), (0,)), ((), ())), precision=HIGH)  19.7 us
    another operation x6, other arithmetic, apply_inverse(): return jax.scipy.linalg.solve_triangular(factor, panel, lower=True)  16.6 us
    ppermute x8, starting transfers between devices, sum_exchange(): value = value + lax.ppermute(value, axis, [(i, i ^ bit) for i in range(n)])  13.4 us
    dot_general x2, matrix products, per_device(): lax.dot_general(right, target, (((1,), (1,)), ((), ())), precision=HIGH)  13.3 us
    another operation x6, other arithmetic, per_device(): factor = jnp.linalg.cholesky(gram_left)  13 us
    dot_general x2, matrix products, per_device(): raw = sum_over_pix(jnp.dot(panel, target, precision=HIGH), 'pix', n_pix)  10.3 us
  transfers between devices with their start and end apart: 42, of which 15 were waited for; matrix products, arithmetic and copies ran while one was open for 21% of the time, Pallas kernels for 0%

profile of v1, /device:TPU:0, one launch (start us, length us, event | category | flops | bytes accessed | tf_op | source)
XLA Modules:
  0.0 170.1 jit_solution(12791630266383593271)
XLA Ops:
  1.6 9.2 %fusion.29 = f32[1024,64]{0,1:T(8,128)S(1)} fusion(f32[64,1024]{1,0:T(8,128)S(1)} %copy-done, f32[1024,1024]{1,0:T(8,128)} %param.7, f32[1024,1024]{1,0:T(8,128)} %param.8, f32[1024,1024]{1,0:T(8,128)} %param.9), kind=kOutput, calls=%fused_computation.91 | convolution fusion | flops 808452096 | bytes 13107200 | tf_op jit(solution)/shard_map/dot_general | solution.py:78
  12.3 2.9 %collective-permute-start.1 = (f32[32,1024]{1,0:T(8,128)S(1)}, f32[32,1024]{1,0:T(8,128)S(1)}, u32[]{:S(2)}, u32[]{:S(2)}) collective-permute-start(f32[32,1024]{1,0:T(8,128)S(1)} %bitcast_add_fusion), channel_id=1, source_target_pairs={{0,16},{8,24},{16,0},{24,8},{1,17},{9,25},{17,1},{25,9},{2,18},{10... | collective-permute-start | bytes 393224 | tf_op jit(solution)/shard_map/ppermute | solution.py:39
  15.3 3.8 %collective-permute-done.1 = f32[32,1024]{1,0:T(8,128)S(1)} collective-permute-done((f32[32,1024]{1,0:T(8,128)S(1)}, f32[32,1024]{1,0:T(8,128)S(1)}, u32[]{:S(2)}, u32[]{:S(2)}) %collective-permute-start.1) | collective-permute-done | bytes 131104 | tf_op jit(solution)/shard_map/ppermute | solution.py:39
  19.2 1.3 collective-permute-done.2
  20.9 7.7 %fusion.5 = f32[64,1024]{1,0:T(8,128)S(1)} fusion(f32[32,1024]{1,0:T(8,128)S(1)} %get-tuple-element.29, f32[32,1024]{1,0:T(8,128)S(1)} %get-tuple-element.28, f32[1024,1024]{1,0:T(8,128)} %param.7, f32[1024,1024]{1,0:T(8,128)} %param.8, f32[1024,1024]{1,0:T(8,128)} %param.9), kind=kOutput, calls=%fused_computation.14 | convolution fusion | flops 808517632 | bytes 13107200 | tf_op jit(solution)/shard_map/dot_general | solution.py:81
  28.6 1.8 %collective-permute-start.3 = (f32[64,64]{0,1:T(8,128)S(1)}, f32[64,64]{0,1:T(8,128)S(1)}, u32[]{:S(2)}, u32[]{:S(2)}) collective-permute-start(f32[64,64]{0,1:T(8,128)S(1)} %fusion.6), channel_id=1, source_target_pairs={{0,1},{1,0},{2,3},{3,2},{4,5},{5,4},{6,7},{7,6},{8,9},{9,8},{10,11... | collective-permute-start | bytes 49160 | tf_op jit(solution)/shard_map/ppermute | solution.py:26
  30.4 3.6 %collective-permute-start.12 = (f32[8,1024]{1,0:T(8,128)S(1)}, f32[8,1024]{1,0:T(8,128)S(1)}, u32[]{:S(2)}, u32[]{:S(2)}) collective-permute-start(f32[8,1024]{1,0:T(8,128)S(1)} %get-tuple-element.22), channel_id=1, source_target_pairs={{0,7},{1,0},{2,1},{3,2},{4,3},{5,4},{6,5},{7,6},{8,15},{9,8},{10,9... | collective-permute-start | bytes 98312 | tf_op jit(solution)/shard_map/ppermute | solution.py:58
  34.5 1.6 collective-permute-start.4
  36.1 1.8 %collective-permute-start.10 = (f32[8,1024]{1,0:T(8,128)S(1)}, f32[8,1024]{1,0:T(8,128)S(1)}, u32[]{:S(2)}, u32[]{:S(2)}) collective-permute-start(f32[8,1024]{1,0:T(8,128)S(1)} %get-tuple-element.24), channel_id=1, source_target_pairs={{0,5},{1,6},{2,7},{3,0},{4,1},{5,2},{6,3},{7,4},{8,13},{9,14},{10,... | collective-permute-start | bytes 98312 | tf_op jit(solution)/shard_map/ppermute | solution.py:58
  38.6 1.5 collective-permute-start.8
  41.2 1.7 %collective-permute-start.6 = (f32[8,1024]{1,0:T(8,128)S(1)}, f32[8,1024]{1,0:T(8,128)S(1)}, u32[]{:S(2)}, u32[]{:S(2)}) collective-permute-start(f32[8,1024]{1,0:T(8,128)S(1)} %get-tuple-element.21), channel_id=1, source_target_pairs={{0,1},{1,2},{2,3},{3,4},{4,5},{5,6},{6,7},{7,0},{8,9},{9,10},{10,1... | collective-permute-start | bytes 98312 | tf_op jit(solution)/shard_map/ppermute | solution.py:58
  43.0 2.0 %collective-permute-start.5 = (f32[64,64]{0,1:T(8,128)S(1)}, f32[64,64]{0,1:T(8,128)S(1)}, u32[]{:S(2)}, u32[]{:S(2)}) collective-permute-start(f32[64,64]{0,1:T(8,128)S(1)} %add.224), channel_id=1, source_target_pairs={{0,4},{1,5},{2,6},{3,7},{4,0},{5,1},{6,2},{7,3},{8,12},{9,13},{10,... | collective-permute-start | bytes 49160 | tf_op jit(solution)/shard_map/ppermute | solution.py:26
  45.8 2.0 %collective-permute-done.6 = f32[8,1024]{1,0:T(8,128)S(1)} collective-permute-done((f32[8,1024]{1,0:T(8,128)S(1)}, f32[8,1024]{1,0:T(8,128)S(1)}, u32[]{:S(2)}, u32[]{:S(2)}) %collective-permute-start.6) | collective-permute-done | bytes 32800 | tf_op jit(solution)/shard_map/ppermute | solution.py:58
  48.6 2.3 %collective-permute-start.15 = (f32[8,1024]{1,0:T(8,128)S(1)}, f32[8,1024]{1,0:T(8,128)S(1)}, u32[]{:S(2)}, u32[]{:S(2)}) collective-permute-start(f32[8,1024]{1,0:T(8,128)S(1)} %get-tuple-element.9), channel_id=1, source_target_pairs={{0,3},{1,4},{2,5},{3,6},{4,7},{5,0},{6,1},{7,2},{8,11},{9,12},{10,... | collective-permute-start | bytes 98312 | tf_op jit(solution)/shard_map/ppermute | solution.py:64
  50.9 2.9 %collective-permute-start.16 = (f32[8,1024]{1,0:T(8,128)S(1)}, f32[8,1024]{1,0:T(8,128)S(1)}, u32[]{:S(2)}, u32[]{:S(2)}) collective-permute-start(f32[8,1024]{1,0:T(8,128)S(1)} %get-tuple-element.9), channel_id=1, source_target_pairs={{0,4},{1,5},{2,6},{3,7},{4,0},{5,1},{6,2},{7,3},{8,12},{9,13},{10,... | collective-permute-start | bytes 98312 | tf_op jit(solution)/shard_map/ppermute | solution.py:64
  54.6 5.8 %cholesky.59 = f32[64,64]{1,0:T(8,128)S(1)} custom-call(f32[64,64]{1,0:T(8,128)S(1)} %fusion.20), custom_call_target="Cholesky" | custom-call | tf_op jit(solution)/shard_map/jit(cholesky)/cholesky | solution.py:82
  61.8 4.9 %custom-call.9 = f32[1,64,64]{1,2,0:T(8,128)S(1)} custom-call(f32[1,64,64]{2,1,0:T(8,128)S(1)} %fusion.7), custom_call_target="InvertDiagBlocksLowerTriangular" | custom-call | tf_op jit(solution)/shard_map/jit(_solve_triangular)/triangular_solve | solution.py:20
  67.1 1.7 %collective-permute-start.18 = (f32[8,1024]{1,0:T(8,128)S(1)}, f32[8,1024]{1,0:T(8,128)S(1)}, u32[]{:S(2)}, u32[]{:S(2)}) collective-permute-start(f32[8,1024]{1,0:T(8,128)S(1)} %get-tuple-element.9), channel_id=1, source_target_pairs={{0,6},{1,7},{2,0},{3,1},{4,2},{5,3},{6,4},{7,5},{8,14},{9,15},{10,... | collective-permute-start | bytes 98312 | tf_op jit(solution)/shard_map/ppermute | solution.py:64
  68.9 2.5 %collective-permute-start.19 = (f32[8,1024]{1,0:T(8,128)S(1)}, f32[8,1024]{1,0:T(8,128)S(1)}, u32[]{:S(2)}, u32[]{:S(2)}) collective-permute-start(f32[8,1024]{1,0:T(8,128)S(1)} %get-tuple-element.9), channel_id=1, source_target_pairs={{0,7},{1,0},{2,1},{3,2},{4,3},{5,4},{6,5},{7,6},{8,15},{9,8},{10,9... | collective-permute-start | bytes 98312 | tf_op jit(solution)/shard_map/ppermute | solution.py:64
  71.5 1.5 collective-permute-done.19
  73.4 10.1 %clamp_add_fusion.1 = (f32[1024,1024]{1,0:T(8,128)S(1)}, f32[1024,1024]{1,0:T(8,128)}) fusion(f32[1024,1024]{1,0:T(8,128)} %param.7, f32[1024,1024]{1,0:T(8,128)} %param.9, f32[64,1024]{1,0:T(8,128)S(1)} %fusion.4, f32[64,1024]{1,0:T(8,128)S(1)} %fusion.18), kind=kOutput, calls=%fused_computation.3 | convolution fusion | flops 812646400 | bytes 17301504 | tf_op jit(solution)/shard_map/dot_general | solution.py:90
  83.5 4.1 %fusion.30 = f32[64,1024]{1,0:T(8,128)S(1)} fusion(f32[64,1024]{1,0:T(8,128)S(1)} %fusion.18, f32[1024,1024]{1,0:T(8,128)S(1)} %get-tuple-element.30), kind=kOutput, calls=%fused_computation.92 | convolution fusion | flops 805306368 | bytes 4718592 | tf_op jit(solution)/shard_map/dot_general | solution.py:78
  87.7 1.3 collective-permute-done.20
  89.1 1.6 collective-permute-start.21
  90.7 4.0 %collective-permute-done.21 = f32[32,1024]{1,0:T(8,128)S(1)} collective-permute-done((f32[32,1024]{1,0:T(8,128)S(1)}, f32[32,1024]{1,0:T(8,128)S(1)}, u32[]{:S(2)}, u32[]{:S(2)}) %collective-permute-start.21) | collective-permute-done | bytes 131104 | tf_op jit(solution)/shard_map/ppermute | solution.py:39
  94.8 1.3 collective-permute-done.22
  96.5 2.6 %fusion.1 = f32[64,1024]{1,0:T(8,128)S(1)} fusion(f32[1024,1024]{1,0:T(8,128)S(1)} %get-tuple-element.30, f32[32,1024]{1,0:T(8,128)S(1)} %get-tuple-element.20, f32[32,1024]{1,0:T(8,128)S(1)} %get-tuple-element.19), kind=kOutput, calls=%fused_computation.10 | convolution fusion | flops 805371904 | bytes 4718592 | tf_op jit(solution)/shard_map/dot_general | solution.py:81
  99.2 2.4 %collective-permute-start.23 = (f32[64,64]{0,1:T(8,128)S(1)}, f32[64,64]{0,1:T(8,128)S(1)}, u32[]{:S(2)}, u32[]{:S(2)}) collective-permute-start(f32[64,64]{0,1:T(8,128)S(1)} %fusion.3), channel_id=1, source_target_pairs={{0,1},{1,0},{2,3},{3,2},{4,5},{5,4},{6,7},{7,6},{8,9},{9,8},{10,11... | collective-permute-start | bytes 49160 | tf_op jit(solution)/shard_map/ppermute | solution.py:26
  101.7 2.7 %collective-permute-start.32 = (f32[8,1024]{1,0:T(8,128)S(1)}, f32[8,1024]{1,0:T(8,128)S(1)}, u32[]{:S(2)}, u32[]{:S(2)}) collective-permute-start(f32[8,1024]{1,0:T(8,128)S(1)} %get-tuple-element.13), channel_id=1, source_target_pairs={{0,7},{1,0},{2,1},{3,2},{4,3},{5,4},{6,5},{7,6},{8,15},{9,8},{10,9... | collective-permute-start | bytes 98312 | tf_op jit(solution)/shard_map/ppermute | solution.py:58
  105.0 1.5 collective-permute-start.24
  106.5 2.3 %collective-permute-start.30 = (f32[8,1024]{1,0:T(8,128)S(1)}, f32[8,1024]{1,0:T(8,128)S(1)}, u32[]{:S(2)}, u32[]{:S(2)}) collective-permute-start(f32[8,1024]{1,0:T(8,128)S(1)} %get-tuple-element.15), channel_id=1, source_target_pairs={{0,5},{1,6},{2,7},{3,0},{4,1},{5,2},{6,3},{7,4},{8,13},{9,14},{10,... | collective-permute-start | bytes 98312 | tf_op jit(solution)/shard_map/ppermute | solution.py:58
  108.7 1.5 collective-permute-start.29
  110.3 1.2 collective-permute-start.28
  111.5 1.9 %collective-permute-start.26 = (f32[8,1024]{1,0:T(8,128)S(1)}, f32[8,1024]{1,0:T(8,128)S(1)}, u32[]{:S(2)}, u32[]{:S(2)}) collective-permute-start(f32[8,1024]{1,0:T(8,128)S(1)} %get-tuple-element.12), channel_id=1, source_target_pairs={{0,1},{1,2},{2,3},{3,4},{4,5},{5,6},{6,7},{7,0},{8,9},{9,10},{10,1... | collective-permute-start | bytes 98312 | tf_op jit(solution)/shard_map/ppermute | solution.py:58
  113.4 2.5 %collective-permute-start.25 = (f32[64,64]{0,1:T(8,128)S(1)}, f32[64,64]{0,1:T(8,128)S(1)}, u32[]{:S(2)}, u32[]{:S(2)}) collective-permute-start(f32[64,64]{0,1:T(8,128)S(1)} %add.253), channel_id=1, source_target_pairs={{0,4},{1,5},{2,6},{3,7},{4,0},{5,1},{6,2},{7,3},{8,12},{9,13},{10,... | collective-permute-start | bytes 49160 | tf_op jit(solution)/shard_map/ppermute | solution.py:26
  117.2 1.4 collective-permute-done.26
  119.2 3.3 %collective-permute-start.35 = (f32[8,1024]{1,0:T(8,128)S(1)}, f32[8,1024]{1,0:T(8,128)S(1)}, u32[]{:S(2)}, u32[]{:S(2)}) collective-permute-start(f32[8,1024]{1,0:T(8,128)S(1)} %get-tuple-element.7), channel_id=1, source_target_pairs={{0,3},{1,4},{2,5},{3,6},{4,7},{5,0},{6,1},{7,2},{8,11},{9,12},{10,... | collective-permute-start | bytes 98312 | tf_op jit(solution)/shard_map/ppermute | solution.py:64
  122.6 1.9 %collective-permute-start.36 = (f32[8,1024]{1,0:T(8,128)S(1)}, f32[8,1024]{1,0:T(8,128)S(1)}, u32[]{:S(2)}, u32[]{:S(2)}) collective-permute-start(f32[8,1024]{1,0:T(8,128)S(1)} %get-tuple-element.7), channel_id=1, source_target_pairs={{0,4},{1,5},{2,6},{3,7},{4,0},{5,1},{6,2},{7,3},{8,12},{9,13},{10,... | collective-permute-start | bytes 98312 | tf_op jit(solution)/shard_map/ppermute | solution.py:64
  125.5 5.8 %cholesky.70 = f32[64,64]{1,0:T(8,128)S(1)} custom-call(f32[64,64]{1,0:T(8,128)S(1)} %fusion.16), custom_call_target="Cholesky" | custom-call | tf_op jit(solution)/shard_map/jit(cholesky)/cholesky | solution.py:82
  132.7 4.9 %custom-call.11 = f32[1,64,64]{1,2,0:T(8,128)S(1)} custom-call(f32[1,64,64]{2,1,0:T(8,128)S(1)} %fusion.8), custom_call_target="InvertDiagBlocksLowerTriangular" | custom-call | tf_op jit(solution)/shard_map/jit(_solve_triangular)/triangular_solve | solution.py:20
  137.6 1.6 collective-permute-start.38
  139.2 2.8 %collective-permute-start.39 = (f32[8,1024]{1,0:T(8,128)S(1)}, f32[8,1024]{1,0:T(8,128)S(1)}, u32[]{:S(2)}, u32[]{:S(2)}) collective-permute-start(f32[8,1024]{1,0:T(8,128)S(1)} %get-tuple-element.7), channel_id=1, source_target_pairs={{0,7},{1,0},{2,1},{3,2},{4,3},{5,4},{6,5},{7,6},{8,15},{9,8},{10,9... | collective-permute-start | bytes 98312 | tf_op jit(solution)/shard_map/ppermute | solution.py:64
  142.1 1.5 collective-permute-done.39
  145.7 1.5 collective-permute-start.41
  147.2 9.6 %clamp_multiply_fusion = (f32[1024,1024]{1,0:T(8,128)}, f32[1024,1024]{1,0:T(8,128)}) fusion(f32[1024,1024]{1,0:T(8,128)} %param.9, f32[1024,1024]{1,0:T(8,128)} %param.7, f32[1024,1024]{1,0:T(8,128)} %get-tuple-element.31, f32[64,1024]{1,0:T(8,128)S(1)} %fusion.2, f32[64,1024]{1,0:T(8,128)S(1)} %fusion.13), kind=kOutput, calls=%fused_computation | convolution fusion | flops 814743552 | bytes 21495808 | tf_op jit(solution)/shard_map/dot_general | solution.py:90
  156.9 5.8 %cholesky.81 = f32[64,64]{1,0:T(8,128)S(1)} custom-call(f32[64,64]{1,0:T(8,128)S(1)} %fusion.12), custom_call_target="Cholesky" | custom-call | tf_op jit(solution)/shard_map/jit(cholesky)/cholesky | solution.py:87
  164.1 4.9 %custom-call.13 = f32[1,64,64]{1,2,0:T(8,128)S(1)} custom-call(f32[1,64,64]{2,1,0:T(8,128)S(1)} %fusion.9), custom_call_target="InvertDiagBlocksLowerTriangular" | custom-call | tf_op jit(solution)/shard_map/jit(_solve_triangular)/triangular_solve | solution.py:20
  169.0 1.1 fusion.10
  (111 shorter events, 18.8 us)
Async XLA Ops:
  0.6 1.0 copy-start
  10.8 1.5 collective-permute-start
  12.3 6.8 %collective-permute-start.1 = (f32[32,1024]{1,0:T(8,128)S(1)}, f32[32,1024]{1,0:T(8,128)S(1)}, u32[]{:S(2)}, u32[]{:S(2)}) collective-permute-start(f32[32,1024]{1,0:T(8,128)S(1)} %bitcast_add_fusion), channel_id=1, source_target_pairs={{0,16},{8,24},{16,0},{24,8},{1,17},{9,25},{17,1},{25,9},{2,18},{10... | collective-permute-start | bytes 393224 | tf_op jit(solution)/shard_map/ppermute | solution.py:39
  19.1 1.4 collective-permute-start.2
  28.6 5.9 %collective-permute-start.3 = (f32[64,64]{0,1:T(8,128)S(1)}, f32[64,64]{0,1:T(8,128)S(1)}, u32[]{:S(2)}, u32[]{:S(2)}) collective-permute-start(f32[64,64]{0,1:T(8,128)S(1)} %fusion.6), channel_id=1, source_target_pairs={{0,1},{1,0},{2,3},{3,2},{4,5},{5,4},{6,7},{7,6},{8,9},{9,8},{10,11... | collective-permute-start | bytes 49160 | tf_op jit(solution)/shard_map/ppermute | solution.py:26
  30.4 9.7 %collective-permute-start.12 = (f32[8,1024]{1,0:T(8,128)S(1)}, f32[8,1024]{1,0:T(8,128)S(1)}, u32[]{:S(2)}, u32[]{:S(2)}) collective-permute-start(f32[8,1024]{1,0:T(8,128)S(1)} %get-tuple-element.22), channel_id=1, source_target_pairs={{0,7},{1,0},{2,1},{3,2},{4,3},{5,4},{6,5},{7,6},{8,15},{9,8},{10,9... | collective-permute-start | bytes 98312 | tf_op jit(solution)/shard_map/ppermute | solution.py:58
  34.0 7.2 %collective-permute-start.11 = (f32[8,1024]{1,0:T(8,128)S(1)}, f32[8,1024]{1,0:T(8,128)S(1)}, u32[]{:S(2)}, u32[]{:S(2)}) collective-permute-start(f32[8,1024]{1,0:T(8,128)S(1)} %get-tuple-element.23), channel_id=1, source_target_pairs={{0,6},{1,7},{2,0},{3,1},{4,2},{5,3},{6,4},{7,5},{8,14},{9,15},{10,... | collective-permute-start | bytes 98312 | tf_op jit(solution)/shard_map/ppermute | solution.py:58
  34.5 4.1 %collective-permute-start.4 = (f32[64,64]{0,1:T(8,128)S(1)}, f32[64,64]{0,1:T(8,128)S(1)}, u32[]{:S(2)}, u32[]{:S(2)}) collective-permute-start(f32[64,64]{0,1:T(8,128)S(1)} %add.223), channel_id=1, source_target_pairs={{0,2},{1,3},{2,0},{3,1},{4,6},{5,7},{6,4},{7,5},{8,10},{9,11},{10,... | collective-permute-start | bytes 49160 | tf_op jit(solution)/shard_map/ppermute | solution.py:26
  36.1 6.9 %collective-permute-start.10 = (f32[8,1024]{1,0:T(8,128)S(1)}, f32[8,1024]{1,0:T(8,128)S(1)}, u32[]{:S(2)}, u32[]{:S(2)}) collective-permute-start(f32[8,1024]{1,0:T(8,128)S(1)} %get-tuple-element.24), channel_id=1, source_target_pairs={{0,5},{1,6},{2,7},{3,0},{4,1},{5,2},{6,3},{7,4},{8,13},{9,14},{10,... | collective-permute-start | bytes 98312 | tf_op jit(solution)/shard_map/ppermute | solution.py:58
  37.9 7.1 %collective-permute-start.9 = (f32[8,1024]{1,0:T(8,128)S(1)}, f32[8,1024]{1,0:T(8,128)S(1)}, u32[]{:S(2)}, u32[]{:S(2)}) collective-permute-start(f32[8,1024]{1,0:T(8,128)S(1)} %get-tuple-element.25), channel_id=1, source_target_pairs={{0,4},{1,5},{2,6},{3,7},{4,0},{5,1},{6,2},{7,3},{8,12},{9,13},{10,... | collective-permute-start | bytes 98312 | tf_op jit(solution)/shard_map/ppermute | solution.py:58
  38.6 6.6 %collective-permute-start.8 = (f32[8,1024]{1,0:T(8,128)S(1)}, f32[8,1024]{1,0:T(8,128)S(1)}, u32[]{:S(2)}, u32[]{:S(2)}) collective-permute-start(f32[8,1024]{1,0:T(8,128)S(1)} %get-tuple-element.26), channel_id=1, source_target_pairs={{0,3},{1,4},{2,5},{3,6},{4,7},{5,0},{6,1},{7,2},{8,11},{9,12},{10,... | collective-permute-start | bytes 98312 | tf_op jit(solution)/shard_map/ppermute | solution.py:58
  40.1 5.7 %collective-permute-start.7 = (f32[8,1024]{1,0:T(8,128)S(1)}, f32[8,1024]{1,0:T(8,128)S(1)}, u32[]{:S(2)}, u32[]{:S(2)}) collective-permute-start(f32[8,1024]{1,0:T(8,128)S(1)} %get-tuple-element.27), channel_id=1, source_target_pairs={{0,2},{1,3},{2,4},{3,5},{4,6},{5,7},{6,0},{7,1},{8,10},{9,11},{10,... | collective-permute-start | bytes 98312 | tf_op jit(solution)/shard_map/ppermute | solution.py:58
  41.2 6.6 %collective-permute-start.6 = (f32[8,1024]{1,0:T(8,128)S(1)}, f32[8,1024]{1,0:T(8,128)S(1)}, u32[]{:S(2)}, u32[]{:S(2)}) collective-permute-start(f32[8,1024]{1,0:T(8,128)S(1)} %get-tuple-element.21), channel_id=1, source_target_pairs={{0,1},{1,2},{2,3},{3,4},{4,5},{5,6},{6,7},{7,0},{8,9},{9,10},{10,1... | collective-permute-start | bytes 98312 | tf_op jit(solution)/shard_map/ppermute | solution.py:58
  43.0 10.8 %collective-permute-start.5 = (f32[64,64]{0,1:T(8,128)S(1)}, f32[64,64]{0,1:T(8,128)S(1)}, u32[]{:S(2)}, u32[]{:S(2)}) collective-permute-start(f32[64,64]{0,1:T(8,128)S(1)} %add.224), channel_id=1, source_target_pairs={{0,4},{1,5},{2,6},{3,7},{4,0},{5,1},{6,2},{7,3},{8,12},{9,13},{10,... | collective-permute-start | bytes 49160 | tf_op jit(solution)/shard_map/ppermute | solution.py:26
  47.9 19.2 %collective-permute-start.13 = (f32[8,1024]{1,0:T(8,128)S(1)}, f32[8,1024]{1,0:T(8,128)S(1)}, u32[]{:S(2)}, u32[]{:S(2)}) collective-permute-start(f32[8,1024]{1,0:T(8,128)S(1)} %get-tuple-element.9), channel_id=1, source_target_pairs={{0,1},{1,2},{2,3},{3,4},{4,5},{5,6},{6,7},{7,0},{8,9},{9,10},{10,1... | collective-permute-start | bytes 98312 | tf_op jit(solution)/shard_map/ppermute | solution.py:64
  48.1 20.8 %collective-permute-start.14 = (f32[8,1024]{1,0:T(8,128)S(1)}, f32[8,1024]{1,0:T(8,128)S(1)}, u32[]{:S(2)}, u32[]{:S(2)}) collective-permute-start(f32[8,1024]{1,0:T(8,128)S(1)} %get-tuple-element.9), channel_id=1, source_target_pairs={{0,2},{1,3},{2,4},{3,5},{4,6},{5,7},{6,0},{7,1},{8,10},{9,11},{10,... | collective-permute-start | bytes 98312 | tf_op jit(solution)/shard_map/ppermute | solution.py:64
  48.6 22.8 %collective-permute-start.15 = (f32[8,1024]{1,0:T(8,128)S(1)}, f32[8,1024]{1,0:T(8,128)S(1)}, u32[]{:S(2)}, u32[]{:S(2)}) collective-permute-start(f32[8,1024]{1,0:T(8,128)S(1)} %get-tuple-element.9), channel_id=1, source_target_pairs={{0,3},{1,4},{2,5},{3,6},{4,7},{5,0},{6,1},{7,2},{8,11},{9,12},{10,... | collective-permute-start | bytes 98312 | tf_op jit(solution)/shard_map/ppermute | solution.py:64
  50.9 20.5 %collective-permute-start.16 = (f32[8,1024]{1,0:T(8,128)S(1)}, f32[8,1024]{1,0:T(8,128)S(1)}, u32[]{:S(2)}, u32[]{:S(2)}) collective-permute-start(f32[8,1024]{1,0:T(8,128)S(1)} %get-tuple-element.9), channel_id=1, source_target_pairs={{0,4},{1,5},{2,6},{3,7},{4,0},{5,1},{6,2},{7,3},{8,12},{9,13},{10,... | collective-permute-start | bytes 98312 | tf_op jit(solution)/shard_map/ppermute | solution.py:64
  53.8 17.6 %collective-permute-start.17 = (f32[8,1024]{1,0:T(8,128)S(1)}, f32[8,1024]{1,0:T(8,128)S(1)}, u32[]{:S(2)}, u32[]{:S(2)}) collective-permute-start(f32[8,1024]{1,0:T(8,128)S(1)} %get-tuple-element.9), channel_id=1, source_target_pairs={{0,5},{1,6},{2,7},{3,0},{4,1},{5,2},{6,3},{7,4},{8,13},{9,14},{10,... | collective-permute-start | bytes 98312 | tf_op jit(solution)/shard_map/ppermute | solution.py:64
  67.1 4.3 %collective-permute-start.18 = (f32[8,1024]{1,0:T(8,128)S(1)}, f32[8,1024]{1,0:T(8,128)S(1)}, u32[]{:S(2)}, u32[]{:S(2)}) collective-permute-start(f32[8,1024]{1,0:T(8,128)S(1)} %get-tuple-element.9), channel_id=1, source_target_pairs={{0,6},{1,7},{2,0},{3,1},{4,2},{5,3},{6,4},{7,5},{8,14},{9,15},{10,... | collective-permute-start | bytes 98312 | tf_op jit(solution)/shard_map/ppermute | solution.py:64
  68.9 4.1 %collective-permute-start.19 = (f32[8,1024]{1,0:T(8,128)S(1)}, f32[8,1024]{1,0:T(8,128)S(1)}, u32[]{:S(2)}, u32[]{:S(2)}) collective-permute-start(f32[8,1024]{1,0:T(8,128)S(1)} %get-tuple-element.9), channel_id=1, source_target_pairs={{0,7},{1,0},{2,1},{3,2},{4,3},{5,4},{6,5},{7,6},{8,15},{9,8},{10,9... | collective-permute-start | bytes 98312 | tf_op jit(solution)/shard_map/ppermute | solution.py:64
  87.7 1.4 collective-permute-start.20
  89.1 5.6 %collective-permute-start.21 = (f32[32,1024]{1,0:T(8,128)S(1)}, f32[32,1024]{1,0:T(8,128)S(1)}, u32[]{:S(2)}, u32[]{:S(2)}) collective-permute-start(f32[32,1024]{1,0:T(8,128)S(1)} %dynamic-slice_add_fusion), channel_id=1, source_target_pairs={{0,16},{8,24},{16,0},{24,8},{1,17},{9,25},{17,1},{25,9},{2,18},{10... | collective-permute-start | bytes 393224 | tf_op jit(solution)/shard_map/ppermute | solution.py:39
  94.7 1.4 collective-permute-start.22
  99.2 5.8 %collective-permute-start.23 = (f32[64,64]{0,1:T(8,128)S(1)}, f32[64,64]{0,1:T(8,128)S(1)}, u32[]{:S(2)}, u32[]{:S(2)}) collective-permute-start(f32[64,64]{0,1:T(8,128)S(1)} %fusion.3), channel_id=1, source_target_pairs={{0,1},{1,0},{2,3},{3,2},{4,5},{5,4},{6,7},{7,6},{8,9},{9,8},{10,11... | collective-permute-start | bytes 49160 | tf_op jit(solution)/shard_map/ppermute | solution.py:26
  101.7 9.8 %collective-permute-start.32 = (f32[8,1024]{1,0:T(8,128)S(1)}, f32[8,1024]{1,0:T(8,128)S(1)}, u32[]{:S(2)}, u32[]{:S(2)}) collective-permute-start(f32[8,1024]{1,0:T(8,128)S(1)} %get-tuple-element.13), channel_id=1, source_target_pairs={{0,7},{1,0},{2,1},{3,2},{4,3},{5,4},{6,5},{7,6},{8,15},{9,8},{10,9... | collective-permute-start | bytes 98312 | tf_op jit(solution)/shard_map/ppermute | solution.py:58
  104.4 7.1 %collective-permute-start.31 = (f32[8,1024]{1,0:T(8,128)S(1)}, f32[8,1024]{1,0:T(8,128)S(1)}, u32[]{:S(2)}, u32[]{:S(2)}) collective-permute-start(f32[8,1024]{1,0:T(8,128)S(1)} %get-tuple-element.14), channel_id=1, source_target_pairs={{0,6},{1,7},{2,0},{3,1},{4,2},{5,3},{6,4},{7,5},{8,14},{9,15},{10,... | collective-permute-start | bytes 98312 | tf_op jit(solution)/shard_map/ppermute | solution.py:58
  105.0 5.3 %collective-permute-start.24 = (f32[64,64]{0,1:T(8,128)S(1)}, f32[64,64]{0,1:T(8,128)S(1)}, u32[]{:S(2)}, u32[]{:S(2)}) collective-permute-start(f32[64,64]{0,1:T(8,128)S(1)} %add.252), channel_id=1, source_target_pairs={{0,2},{1,3},{2,0},{3,1},{4,6},{5,7},{6,4},{7,5},{8,10},{9,11},{10,... | collective-permute-start | bytes 49160 | tf_op jit(solution)/shard_map/ppermute | solution.py:26
  106.5 6.9 %collective-permute-start.30 = (f32[8,1024]{1,0:T(8,128)S(1)}, f32[8,1024]{1,0:T(8,128)S(1)}, u32[]{:S(2)}, u32[]{:S(2)}) collective-permute-start(f32[8,1024]{1,0:T(8,128)S(1)} %get-tuple-element.15), channel_id=1, source_target_pairs={{0,5},{1,6},{2,7},{3,0},{4,1},{5,2},{6,3},{7,4},{8,13},{9,14},{10,... | collective-permute-start | bytes 98312 | tf_op jit(solution)/shard_map/ppermute | solution.py:58
  108.7 7.1 %collective-permute-start.29 = (f32[8,1024]{1,0:T(8,128)S(1)}, f32[8,1024]{1,0:T(8,128)S(1)}, u32[]{:S(2)}, u32[]{:S(2)}) collective-permute-start(f32[8,1024]{1,0:T(8,128)S(1)} %get-tuple-element.16), channel_id=1, source_target_pairs={{0,4},{1,5},{2,6},{3,7},{4,0},{5,1},{6,2},{7,3},{8,12},{9,13},{10,... | collective-permute-start | bytes 98312 | tf_op jit(solution)/shard_map/ppermute | solution.py:58
  110.3 6.0 %collective-permute-start.28 = (f32[8,1024]{1,0:T(8,128)S(1)}, f32[8,1024]{1,0:T(8,128)S(1)}, u32[]{:S(2)}, u32[]{:S(2)}) collective-permute-start(f32[8,1024]{1,0:T(8,128)S(1)} %get-tuple-element.17), channel_id=1, source_target_pairs={{0,3},{1,4},{2,5},{3,6},{4,7},{5,0},{6,1},{7,2},{8,11},{9,12},{10,... | collective-permute-start | bytes 98312 | tf_op jit(solution)/shard_map/ppermute | solution.py:58
  111.5 5.7 %collective-permute-start.27 = (f32[8,1024]{1,0:T(8,128)S(1)}, f32[8,1024]{1,0:T(8,128)S(1)}, u32[]{:S(2)}, u32[]{:S(2)}) collective-permute-start(f32[8,1024]{1,0:T(8,128)S(1)} %get-tuple-element.18), channel_id=1, source_target_pairs={{0,2},{1,3},{2,4},{3,5},{4,6},{5,7},{6,0},{7,1},{8,10},{9,11},{10,... | collective-permute-start | bytes 98312 | tf_op jit(solution)/shard_map/ppermute | solution.py:58
  111.5 7.1 %collective-permute-start.26 = (f32[8,1024]{1,0:T(8,128)S(1)}, f32[8,1024]{1,0:T(8,128)S(1)}, u32[]{:S(2)}, u32[]{:S(2)}) collective-permute-start(f32[8,1024]{1,0:T(8,128)S(1)} %get-tuple-element.12), channel_id=1, source_target_pairs={{0,1},{1,2},{2,3},{3,4},{4,5},{5,6},{6,7},{7,0},{8,9},{9,10},{10,1... | collective-permute-start | bytes 98312 | tf_op jit(solution)/shard_map/ppermute | solution.py:58
  113.4 11.1 %collective-permute-start.25 = (f32[64,64]{0,1:T(8,128)S(1)}, f32[64,64]{0,1:T(8,128)S(1)}, u32[]{:S(2)}, u32[]{:S(2)}) collective-permute-start(f32[64,64]{0,1:T(8,128)S(1)} %add.253), channel_id=1, source_target_pairs={{0,4},{1,5},{2,6},{3,7},{4,0},{5,1},{6,2},{7,3},{8,12},{9,13},{10,... | collective-permute-start | bytes 49160 | tf_op jit(solution)/shard_map/ppermute | solution.py:26
  118.7 18.9 %collective-permute-start.33 = (f32[8,1024]{1,0:T(8,128)S(1)}, f32[8,1024]{1,0:T(8,128)S(1)}, u32[]{:S(2)}, u32[]{:S(2)}) collective-permute-start(f32[8,1024]{1,0:T(8,128)S(1)} %get-tuple-element.7), channel_id=1, source_target_pairs={{0,1},{1,2},{2,3},{3,4},{4,5},{5,6},{6,7},{7,0},{8,9},{9,10},{10,1... | collective-permute-start | bytes 98312 | tf_op jit(solution)/shard_map/ppermute | solution.py:64
  118.9 20.3 %collective-permute-start.34 = (f32[8,1024]{1,0:T(8,128)S(1)}, f32[8,1024]{1,0:T(8,128)S(1)}, u32[]{:S(2)}, u32[]{:S(2)}) collective-permute-start(f32[8,1024]{1,0:T(8,128)S(1)} %get-tuple-element.7), channel_id=1, source_target_pairs={{0,2},{1,3},{2,4},{3,5},{4,6},{5,7},{6,0},{7,1},{8,10},{9,11},{10,... | collective-permute-start | bytes 98312 | tf_op jit(solution)/shard_map/ppermute | solution.py:64
  119.2 22.8 %collective-permute-start.35 = (f32[8,1024]{1,0:T(8,128)S(1)}, f32[8,1024]{1,0:T(8,128)S(1)}, u32[]{:S(2)}, u32[]{:S(2)}) collective-permute-start(f32[8,1024]{1,0:T(8,128)S(1)} %get-tuple-element.7), channel_id=1, source_target_pairs={{0,3},{1,4},{2,5},{3,6},{4,7},{5,0},{6,1},{7,2},{8,11},{9,12},{10,... | collective-permute-start | bytes 98312 | tf_op jit(solution)/shard_map/ppermute | solution.py:64
  122.6 19.5 %collective-permute-start.36 = (f32[8,1024]{1,0:T(8,128)S(1)}, f32[8,1024]{1,0:T(8,128)S(1)}, u32[]{:S(2)}, u32[]{:S(2)}) collective-permute-start(f32[8,1024]{1,0:T(8,128)S(1)} %get-tuple-element.7), channel_id=1, source_target_pairs={{0,4},{1,5},{2,6},{3,7},{4,0},{5,1},{6,2},{7,3},{8,12},{9,13},{10,... | collective-permute-start | bytes 98312 | tf_op jit(solution)/shard_map/ppermute | solution.py:64
  124.5 17.6 %collective-permute-start.37 = (f32[8,1024]{1,0:T(8,128)S(1)}, f32[8,1024]{1,0:T(8,128)S(1)}, u32[]{:S(2)}, u32[]{:S(2)}) collective-permute-start(f32[8,1024]{1,0:T(8,128)S(1)} %get-tuple-element.7), channel_id=1, source_target_pairs={{0,5},{1,6},{2,7},{3,0},{4,1},{5,2},{6,3},{7,4},{8,13},{9,14},{10,... | collective-permute-start | bytes 98312 | tf_op jit(solution)/shard_map/ppermute | solution.py:64
  137.6 4.5 %collective-permute-start.38 = (f32[8,1024]{1,0:T(8,128)S(1)}, f32[8,1024]{1,0:T(8,128)S(1)}, u32[]{:S(2)}, u32[]{:S(2)}) collective-permute-start(f32[8,1024]{1,0:T(8,128)S(1)} %get-tuple-element.7), channel_id=1, source_target_pairs={{0,6},{1,7},{2,0},{3,1},{4,2},{5,3},{6,4},{7,5},{8,14},{9,15},{10,... | collective-permute-start | bytes 98312 | tf_op jit(solution)/shard_map/ppermute | solution.py:64
  139.2 4.4 %collective-permute-start.39 = (f32[8,1024]{1,0:T(8,128)S(1)}, f32[8,1024]{1,0:T(8,128)S(1)}, u32[]{:S(2)}, u32[]{:S(2)}) collective-permute-start(f32[8,1024]{1,0:T(8,128)S(1)} %get-tuple-element.7), channel_id=1, source_target_pairs={{0,7},{1,0},{2,1},{3,2},{4,3},{5,4},{6,5},{7,6},{8,15},{9,8},{10,9... | collective-permute-start | bytes 98312 | tf_op jit(solution)/shard_map/ppermute | solution.py:64
  144.4 1.3 collective-permute-start.40
  144.9 11.9 %copy-start.1 = (f32[64,1024]{1,0:T(8,128)}, f32[64,1024]{1,0:T(8,128)S(1)}, u32[]{:S(2)}) copy-start(f32[64,1024]{1,0:T(8,128)S(1)} %fusion.2) | copy-start | bytes 786436
  145.7 11.1 %collective-permute-start.41 = (f32[64,64]{0,1:T(8,128)S(1)}, f32[64,64]{0,1:T(8,128)S(1)}, u32[]{:S(2)}, u32[]{:S(2)}) collective-permute-start(f32[64,64]{0,1:T(8,128)S(1)} %add.263), channel_id=1, source_target_pairs={{0,16},{8,24},{16,0},{24,8},{1,17},{9,25},{17,1},{25,9},{2,18},{10... | collective-permute-start | bytes 49160 | tf_op jit(solution)/shard_map/ppermute | solution.py:26

commit v2 on v1

--- a/solution.py
+++ b/solution.py
@@ -48,23 +48,11 @@
 
 
 def sum_over_pix(value, axis, n):
-    part = value.shape[0] // n
-    me = lax.axis_index(axis)
-    total = lax.dynamic_slice_in_dim(value, me * part, part, 0)
-    got = []
-    for k in range(1, n):
-        peer = lax.rem(me + k, n)
-        piece = lax.dynamic_slice_in_dim(value, peer * part, part, 0)
-        got.append(lax.ppermute(piece, axis, [(i, (i + k) % n) for i in range(n)]))
-    for piece in got:
-        total = total + piece
-    whole = jnp.zeros_like(value)
-    whole = lax.dynamic_update_slice_in_dim(whole, total, me * part, 0)
-    for k in range(1, n):
-        piece = lax.ppermute(total, axis, [(i, (i + k) % n) for i in range(n)])
-        peer = lax.rem(me + n - k, n)
-        whole = lax.dynamic_update_slice_in_dim(whole, piece, peer * part, 0)
-    return whole
+    rows, columns = value.shape
+    got = lax.all_to_all(value, axis, 0, 0, tiled=True)
+    total = jnp.sum(got.reshape(n, rows // n, columns), axis=0)
+    total = jnp.broadcast_to(total[None], (n, rows // n, columns))
+    return lax.all_to_all(total.reshape(rows, columns), axis, 0, 0, tiled=True)
 
 
 def solution(mesh):
@@ -77,8 +65,9 @@
             last = step == ITERS - 1
             partial_left = lax.dot_general(right, target, (((1,), (1,)), ((), ())), precision=HIGH)
             panel = sum_over_gal(partial_left, "gal", n_gal)
-            gram_left = sum_exchange(gram_of(panel), "pix", n_pix)
-            raw = sum_over_pix(jnp.dot(panel, target, precision=HIGH), "pix", n_pix)
+            raw = jnp.dot(panel, target, precision=HIGH)
+            both = sum_over_pix(jnp.concatenate([raw, gram_of(panel)], axis=1), "pix", n_pix)
+            raw, gram_left = both[:, : raw.shape[1]], both[:, raw.shape[1] :]
             factor = jnp.linalg.cholesky(gram_left)
             left = apply_inverse(factor, panel)
             wide = apply_inverse(factor, raw)

time: 170 us -> 162 us (0.953)
  blocking collectives: 0 us -> 55.6 us
  starting transfers between devices: 61.8 us -> 6.86 us
  waiting for transfers between devices: 22.2 us -> 13.6 us
    all_to_all x0 -> x4, blocking collectives: none -> 55.6 us  [the longest x2 29.8 us: sum_over_pix(): got = lax.all_to_all(value, axis, 0, 0, tiled=True)]
    ppermute x28 -> x0, starting transfers between devices: 43.1 us -> none  [the longest x14 21.9 us: sum_over_pix(): piece = lax.ppermute(total, axis, [(i, (i + k) % n) for i in range(n)])]
    ppermute x8 -> x2, starting transfers between devices: 13.4 us -> 1.6 us  [sum_exchange(): value = value + lax.ppermute(value, axis, [(i, i ^ bit) for i in range(n)])]
    ppermute x28 -> x0, waiting for transfers between devices: 8.69 us -> none  [the longest x14 5.64 us: sum_over_pix(): got.append(lax.ppermute(piece, axis, [(i, (i + k) % n) for i in range(n)]))]
  transfers between devices with their start and end apart: 42 -> 8, of which waited for: 15 -> 7; matrix products, arithmetic and copies ran while one was open for 21% -> 6% of each run, Pallas kernels for 0% -> 0%
where the time goes in v2:
time: 162 us
  blocking collectives  55.6 us (34%)
  matrix products  47.2 us (29%)
  other arithmetic  36.4 us (22%)
  waiting for transfers between devices  13.6 us (8%)
  starting transfers between devices  6.86 us (4%)
    all_to_all x2, blocking collectives, sum_over_pix(): got = lax.all_to_all(value, axis, 0, 0, tiled=True)  29.8 us
    all_to_all x2, blocking collectives, sum_over_pix(): return lax.all_to_all(total.reshape(rows, columns), axis, 0, 0, tiled=True)  25.8 us
    dot_general x2, matrix products, per_device(): lax.dot_general(left, wide, (((0,), (0,)), ((), ())), precision=HIGH)  19.7 us
    another operation x6, other arithmetic, apply_inverse(): return jax.scipy.linalg.solve_triangular(factor, panel, lower=True)  16.6 us
    dot_general x2, matrix products, per_device(): lax.dot_general(right, target, (((1,), (1,)), ((), ())), precision=HIGH)  13.3 us
    another operation x6, other arithmetic, per_device(): factor = jnp.linalg.cholesky(gram_left)  13 us
    dot_general x2, matrix products, per_device(): raw = jnp.dot(panel, target, precision=HIGH)  10.3 us
    ppermute x2, waiting for transfers between devices, sum_over_gal(): lax.ppermute(mine, axis, [(i, (i + CORES * k) % n) for i in range(n)])  7.83 us
  transfers between devices with their start and end apart: 8, of which 7 were waited for; matrix products, arithmetic and copies ran while one was open for 6% of the time, Pallas kernels for 0%

profile of v2, /device:TPU:0, one launch (start us, length us, event | category | flops | bytes accessed | tf_op | source)
XLA Modules:
  0.0 161.9 jit_solution(2523990397152085079)
XLA Ops:
  0.7 0.9 copy-done
  1.6 9.2 %fusion.31 = f32[1024,64]{0,1:T(8,128)S(1)} fusion(f32[64,1024]{1,0:T(8,128)S(1)} %copy-done, f32[1024,1024]{1,0:T(8,128)} %param.7, f32[1024,1024]{1,0:T(8,128)} %param.8, f32[1024,1024]{1,0:T(8,128)} %param.9), kind=kOutput, calls=%fused_computation.63 | convolution fusion | flops 808452096 | bytes 13107200 | tf_op jit(solution)/shard_map/dot_general | solution.py:66
  10.8 0.5 collective-permute-start
  11.3 1.0 collective-permute-done
  12.3 2.9 %collective-permute-start.1 = (f32[32,1024]{1,0:T(8,128)S(1)}, f32[32,1024]{1,0:T(8,128)S(1)}, u32[]{:S(2)}, u32[]{:S(2)}) collective-permute-start(f32[32,1024]{1,0:T(8,128)S(1)} %bitcast_add_fusion), channel_id=1, source_target_pairs={{0,16},{8,24},{16,0},{24,8},{1,17},{9,25},{17,1},{25,9},{2,18},{10... | collective-permute-start | bytes 393224 | tf_op jit(solution)/shard_map/ppermute | solution.py:39
  15.3 3.8 %collective-permute-done.1 = f32[32,1024]{1,0:T(8,128)S(1)} collective-permute-done((f32[32,1024]{1,0:T(8,128)S(1)}, f32[32,1024]{1,0:T(8,128)S(1)}, u32[]{:S(2)}, u32[]{:S(2)}) %collective-permute-start.1) | collective-permute-done | bytes 131104 | tf_op jit(solution)/shard_map/ppermute | solution.py:39
  19.1 0.1 collective-permute-start.2
  19.2 1.3 collective-permute-done.2
  20.5 0.4 fusion.9
  20.9 7.7 %fusion.10 = f32[64,1024]{1,0:T(8,128)S(1)} fusion(f32[32,1024]{1,0:T(8,128)S(1)} %get-tuple-element.11, f32[32,1024]{1,0:T(8,128)S(1)} %get-tuple-element.10, f32[1024,1024]{1,0:T(8,128)} %param.7, f32[1024,1024]{1,0:T(8,128)} %param.8, f32[1024,1024]{1,0:T(8,128)} %param.9), kind=kOutput, calls=%fused_computation.21 | convolution fusion | flops 808517632 | bytes 13107200 | tf_op jit(solution)/shard_map/dot_general | solution.py:68
  28.6 16.5 %all_to_all.36 = f32[8,8,1088]{2,1,0:T(8,128)S(1)} all-to-all(f32[8,8,1088]{2,1,0:T(8,128)S(1)} %maximum_bitcast_fusion), channel_id=1, replica_groups=mesh['gal'=4,'pix'=8] {'pix'}, dimensions={0} | all-to-all | bytes 557056 | tf_op jit(solution)/shard_map/all_to_all | solution.py:52
  45.1 12.9 %all_to_all.37 = f32[8,8,1088]{2,1,0:T(8,128)S(1)} all-to-all(f32[8,8,1088]{2,1,0:T(8,128)S(1)} %broadcast_in_dim.4), channel_id=1, replica_groups=mesh['gal'=4,'pix'=8] {'pix'}, dimensions={0} | all-to-all | bytes 557056 | tf_op jit(solution)/shard_map/all_to_all | solution.py:55
  58.0 0.1 copy.21
  58.1 5.8 %cholesky.59 = f32[64,64]{1,0:T(8,128)S(1)} custom-call(f32[64,64]{1,0:T(8,128)S(1)} %fusion.22), custom_call_target="Cholesky" | custom-call | tf_op jit(solution)/shard_map/jit(cholesky)/cholesky | solution.py:71
  64.0 0.6 compare_reduce_fusion.2
  64.7 0.7 fusion.11
  65.3 4.9 %custom-call.9 = f32[1,64,64]{1,2,0:T(8,128)S(1)} custom-call(f32[1,64,64]{2,1,0:T(8,128)S(1)} %fusion.11), custom_call_target="InvertDiagBlocksLowerTriangular" | custom-call | tf_op jit(solution)/shard_map/jit(_solve_triangular)/triangular_solve | solution.py:20
  70.2 0.4 fusion.8
  70.7 0.4 fusion.3
  71.1 10.1 %clamp_add_fusion.1 = (f32[1024,1024]{1,0:T(8,128)S(1)}, f32[1024,1024]{1,0:T(8,128)}) fusion(f32[1024,1024]{1,0:T(8,128)} %param.7, f32[1024,1024]{1,0:T(8,128)} %param.9, f32[64,1024]{1,0:T(8,128)S(1)} %fusion.8, f32[64,1024]{1,0:T(8,128)S(1)} %fusion.3), kind=kOutput, calls=%fused_computation.3 | convolution fusion | flops 812646400 | bytes 17301504 | tf_op jit(solution)/shard_map/dot_general | solution.py:79
  81.2 4.1 %fusion.32 = f32[64,1024]{1,0:T(8,128)S(1)} fusion(f32[64,1024]{1,0:T(8,128)S(1)} %fusion.3, f32[1024,1024]{1,0:T(8,128)S(1)} %get-tuple-element.12), kind=kOutput, calls=%fused_computation.64 | convolution fusion | flops 805306368 | bytes 4718592 | tf_op jit(solution)/shard_map/dot_general | solution.py:66
  85.3 0.1 collective-permute-start.3
  85.4 1.3 collective-permute-done.3
  86.7 1.6 collective-permute-start.4
  88.3 4.0 %collective-permute-done.4 = f32[32,1024]{1,0:T(8,128)S(1)} collective-permute-done((f32[32,1024]{1,0:T(8,128)S(1)}, f32[32,1024]{1,0:T(8,128)S(1)}, u32[]{:S(2)}, u32[]{:S(2)}) %collective-permute-start.4) | collective-permute-done | bytes 131104 | tf_op jit(solution)/shard_map/ppermute | solution.py:39
  92.4 1.3 collective-permute-done.5
  93.8 0.4 fusion.6
  94.2 2.6 %fusion.7 = f32[64,1024]{1,0:T(8,128)S(1)} fusion(f32[1024,1024]{1,0:T(8,128)S(1)} %get-tuple-element.12, f32[32,1024]{1,0:T(8,128)S(1)} %get-tuple-element.9, f32[32,1024]{1,0:T(8,128)S(1)} %get-tuple-element.8), kind=kOutput, calls=%fused_computation.18 | convolution fusion | flops 805371904 | bytes 4718592 | tf_op jit(solution)/shard_map/dot_general | solution.py:68
  96.9 13.3 %all_to_all.38 = f32[8,8,1088]{2,1,0:T(8,128)S(1)} all-to-all(f32[8,8,1088]{2,1,0:T(8,128)S(1)} %maximum_bitcast_fusion.1), channel_id=1, replica_groups=mesh['gal'=4,'pix'=8] {'pix'}, dimensions={0} | all-to-all | bytes 557056 | tf_op jit(solution)/shard_map/all_to_all | solution.py:52
  110.2 12.9 %all_to_all.39 = f32[8,8,1088]{2,1,0:T(8,128)S(1)} all-to-all(f32[8,8,1088]{2,1,0:T(8,128)S(1)} %broadcast_in_dim.6), channel_id=1, replica_groups=mesh['gal'=4,'pix'=8] {'pix'}, dimensions={0} | all-to-all | bytes 557056 | tf_op jit(solution)/shard_map/all_to_all | solution.py:55
  123.1 0.1 copy.22
  123.2 5.8 %cholesky.70 = f32[64,64]{1,0:T(8,128)S(1)} custom-call(f32[64,64]{1,0:T(8,128)S(1)} %fusion.19), custom_call_target="Cholesky" | custom-call | tf_op jit(solution)/shard_map/jit(cholesky)/cholesky | solution.py:71
  129.1 0.6 compare_reduce_fusion.1
  129.8 0.7 fusion.12
  130.4 4.9 %custom-call.11 = f32[1,64,64]{1,2,0:T(8,128)S(1)} custom-call(f32[1,64,64]{2,1,0:T(8,128)S(1)} %fusion.12), custom_call_target="InvertDiagBlocksLowerTriangular" | custom-call | tf_op jit(solution)/shard_map/jit(_solve_triangular)/triangular_solve | solution.py:20
  135.3 0.4 fusion.1
  135.8 0.4 fusion.33
  136.1 0.1 collective-permute-start.6
  136.2 0.4 fusion.5
  136.6 0.8 collective-permute-done.6
  137.4 1.5 collective-permute-start.7
  138.9 9.6 %clamp_multiply_fusion = (f32[1024,1024]{1,0:T(8,128)}, f32[1024,1024]{1,0:T(8,128)}) fusion(f32[1024,1024]{1,0:T(8,128)} %param.9, f32[1024,1024]{1,0:T(8,128)} %param.7, f32[1024,1024]{1,0:T(8,128)} %get-tuple-element.13, f32[64,1024]{1,0:T(8,128)S(1)} %fusion.5, f32[64,1024]{1,0:T(8,128)S(1)} %fusion.1), kind=kOutput, calls=%fused_computation | convolution fusion | flops 814743552 | bytes 21495808 | tf_op jit(solution)/shard_map/dot_general | solution.py:79
  148.5 0.1 copy.19
  148.6 5.8 %cholesky.81 = f32[64,64]{1,0:T(8,128)S(1)} custom-call(f32[64,64]{1,0:T(8,128)S(1)} %fusion.16), custom_call_target="Cholesky" | custom-call | tf_op jit(solution)/shard_map/jit(cholesky)/cholesky | solution.py:76
  154.5 0.6 compare_reduce_fusion
  155.2 0.7 fusion.13
  155.8 4.9 %custom-call.13 = f32[1,64,64]{1,2,0:T(8,128)S(1)} custom-call(f32[1,64,64]{2,1,0:T(8,128)S(1)} %fusion.13), custom_call_target="InvertDiagBlocksLowerTriangular" | custom-call | tf_op jit(solution)/shard_map/jit(_solve_triangular)/triangular_solve | solution.py:20
  160.7 1.1 fusion.14
  (29 shorter events, 0.5 us)
Async XLA Ops:
  0.6 1.0 copy-start
  10.8 1.5 collective-permute-start
  12.3 6.8 %collective-permute-start.1 = (f32[32,1024]{1,0:T(8,128)S(1)}, f32[32,1024]{1,0:T(8,128)S(1)}, u32[]{:S(2)}, u32[]{:S(2)}) collective-permute-start(f32[32,1024]{1,0:T(8,128)S(1)} %bitcast_add_fusion), channel_id=1, source_target_pairs={{0,16},{8,24},{16,0},{24,8},{1,17},{9,25},{17,1},{25,9},{2,18},{10... | collective-permute-start | bytes 393224 | tf_op jit(solution)/shard_map/ppermute | solution.py:39
  19.1 1.4 collective-permute-start.2
  85.3 1.4 collective-permute-start.3
  86.7 5.6 %collective-permute-start.4 = (f32[32,1024]{1,0:T(8,128)S(1)}, f32[32,1024]{1,0:T(8,128)S(1)}, u32[]{:S(2)}, u32[]{:S(2)}) collective-permute-start(f32[32,1024]{1,0:T(8,128)S(1)} %dynamic-slice_add_fusion), channel_id=1, source_target_pairs={{0,16},{8,24},{16,0},{24,8},{1,17},{9,25},{17,1},{25,9},{2,18},{10... | collective-permute-start | bytes 393224 | tf_op jit(solution)/shard_map/ppermute | solution.py:39
  92.4 1.4 collective-permute-start.5
  136.1 1.3 collective-permute-start.6
  136.6 11.9 %copy-start.1 = (f32[64,1024]{1,0:T(8,128)}, f32[64,1024]{1,0:T(8,128)S(1)}, u32[]{:S(2)}) copy-start(f32[64,1024]{1,0:T(8,128)S(1)} %fusion.5) | copy-start | bytes 786436
  137.4 11.1 %collective-permute-start.7 = (f32[64,64]{0,1:T(8,128)S(1)}, f32[64,64]{0,1:T(8,128)S(1)}, u32[]{:S(2)}, u32[]{:S(2)}) collective-permute-start(f32[64,64]{0,1:T(8,128)S(1)} %add.57), channel_id=1, source_target_pairs={{0,16},{8,24},{16,0},{24,8},{1,17},{9,25},{17,1},{25,9},{2,18},{10... | collective-permute-start | bytes 49160 | tf_op jit(solution)/shard_map/ppermute | solution.py:26

commit v3 on v0

v3 whole, which is shorter than its diff:
```python
import jax
import jax.numpy as jnp
from jax import lax
from jax.experimental import pallas as pl
from jax.experimental.pallas import tpu as pltpu
from jax.sharding import PartitionSpec as P

ITERS = 2


MU = 1.25
TAU = 0.6 / 1.25
HIGH = lax.Precision.HIGHEST
CORES = 2
LANES = 128
F32, BF16 = jnp.float32, jnp.bfloat16
MIB = 1 << 20


def split(value):
    high = value.astype(BF16)
    return high, (value - high.astype(F32)).astype(BF16)


def dot(a, b, dims, precision=None):
    return lax.dot_general(a, b, (dims, ((), ())), precision=precision, preferred_element_type=F32)


def dot_nt(a, b):
    rows = a[0].shape[0]
    both = dot(jnp.concatenate(a, axis=0), b[0], ((1,), (1,)))
    return both[:rows] + both[rows:] + dot(a[0], b[1], ((1,), (1,)))


def dot_nn(a, b):
    rows = a[0].shape[0]
    both = dot(jnp.concatenate(a, axis=0), b[0], ((1,), (0,)))
    return both[:rows] + both[rows:] + dot(a[0], b[1], ((1,), (0,)))


def call(body, name, scalars, ins, outs, grid, scratch=(), aliases=None, cost=(0, 0), limit=24):
    return pl.pallas_call(
        body,
        name=name,
        grid_spec=pltpu.PrefetchScalarGridSpec(
            num_scalar_prefetch=1,
            grid=grid,
            in_specs=[
                pl.BlockSpec(block, index) if block else pl.BlockSpec(memory_space=pl.ANY)
                for _, block, index in ins
            ],
            out_specs=[pl.BlockSpec(block, index) for _, _, block, index in outs],
            scratch_shapes=list(scratch),
        ),
        out_shape=[jax.ShapeDtypeStruct(shape, dtype) for shape, dtype, _, _ in outs],
        input_output_aliases=aliases or {},
        compiler_params=pltpu.CompilerParams(vmem_limit_bytes=limit * MIB),
        cost_estimate=pl.CostEstimate(flops=cost[0], bytes_accessed=cost[1], transcendentals=0),
    )(scalars, *[array for array, _, _ in ins])


def unstack(ref):
    blocks = ref.shape[0] // 64
    return jnp.concatenate([ref[64 * t : 64 * (t + 1), :] for t in range(blocks)], axis=1)


def solution(mesh):
    n_gal, n_pix = mesh.shape["gal"], mesh.shape["pix"]
    levels = n_pix.bit_length() - 1

    def swap(value, axis, bit):
        n = mesh.shape[axis]
        return lax.ppermute(value, axis, [(i, i ^ bit) for i in range(n)])

    def per_device(observed, sparse_init, dual_init, right_init):
        rank = right_init.shape[0]
        n_rows, n_cols = observed.shape
        half = n_cols // 2
        tall = min(256, n_rows // 2)
        steps = n_rows // tall
        core = lax.rem(lax.axis_index("gal"), CORES)
        side = lax.rem(lax.axis_index("pix"), 2)
        scalars = jnp.stack([core, side]).astype(jnp.int32)
        stack_rows = rank * (half // LANES)
        gram_rows = rank * rank // LANES

        def gal_block(i, s):
            return lax.rem(i + (1 - s[0]) * (steps // 2), steps)

        def natural(p):
            return (tall, half), lambda i, s: (gal_block(i, s), (s[1] + p) % 2)

        block = (tall, half), lambda i, s: (i, 0)
        strip = (rank, tall), lambda i, s: (0, i)

        def whole(shape):
            return shape, lambda i, s: (0, 0)

        def first(right):
            def body(s, o0, o1, s0, s1, d0, d1, r0, r1, h0, l0, h1, l1, part):
                total = None
                for o, sp, d, r, h, l in ((o0, s0, d0, r0, h0, l0), (o1, s1, d1, r1, h1, l1)):
                    pair = split(o[...] - sp[...] + d[...] * (1 / MU))
                    h[...], l[...] = pair
                    term = dot_nt(split(r[...]), pair)
                    total = term if total is None else total + term
                part[...] = total

            def columns(p):
                return (rank, half), lambda i, s: (0, (s[1] + p) % 2)

            ins = [(a, *natural(p)) for a in (observed, sparse_init, dual_init) for p in (0, 1)]
            ins += [(right, *columns(p)) for p in (0, 1)]
            outs = [((n_rows, half), BF16, *block)] * 4 + [((rank, n_rows), F32, *strip)]
            cost = (6 * rank * n_rows * n_cols, 16 * n_rows * n_cols)
            h0, l0, h1, l1, part = call(body, "first", scalars, ins, outs, (steps,), cost=cost)
            return (h0, l0), (h1, l1), part

        def sum_gal(part):
            away, mine = jnp.split(part, 2, axis=1)
            mine = mine + swap(away, "gal", 1)
            got = [
                lax.ppermute(mine, "gal", [(i, (i + CORES * k) % n_gal) for i in range(n_gal)])
                for k in range(1, n_gal // CORES)
            ]
            for piece in got:
                mine = mine + piece
            return jnp.concatenate([swap(mine, "gal", 1), mine], axis=1)

        def multiply(panel, pair, with_gram):
            def body(s, whole_panel, panel, high, low, out, total):
                i = pl.program_id(0)
                term = dot_nn(split(panel[...]), (high[...], low[...]))

                @pl.when(i == 0)
                def _():
                    total[...] = term

                @pl.when(i > 0)
                def _():
                    total[...] += term

                @pl.when(i == steps - 1)
                def _():
                    for t in range(half // LANES):
                        out[rank * t : rank * (t + 1), :] = total[:, LANES * t : LANES * (t + 1)]
                    if with_gram:
                        gram = dot(whole_panel[...], whole_panel[...], ((1,), (1,)), HIGH)
                        packed = jnp.concatenate([gram[:gram_rows], gram[gram_rows:]], axis=1)
                        out[stack_rows : stack_rows + gram_rows, :] = packed

            rows = stack_rows + (gram_rows if with_gram else 0)
            ins = [(panel, *whole(panel.shape)), (panel, *strip), (pair[0], *block), (pair[1], *block)]
            outs = [((rows, LANES), F32, *whole((rows, LANES)))]
            cost = (3 * rank * n_rows * n_cols, 2 * n_rows * n_cols)
            scratch = [pltpu.VMEM((rank, half), F32)]
            return call(body, "multiply", scalars, ins, outs, (steps,), scratch, cost=cost)[0]

        def eliminate(one, two):
            def body(s, one, two, out):
                packed = one[...] + two[...]
                lane = lax.broadcasted_iota(jnp.int32, (8, LANES), 1)
                sub = lax.broadcasted_iota(jnp.int32, (8, LANES), 0)
                turned = pltpu.roll(packed, LANES // 2, 1)
                rows = []
                for j in range(rank // 8):
                    source = packed if 8 * j < gram_rows else turned
                    at = 8 * j % gram_rows
                    eye = jnp.where(lane - rank == sub + 8 * j, 1.0, 0.0)
                    rows.append(jnp.where(lane < rank, source[at : at + 8], eye))
                for k in range(rank):
                    r, at = divmod(k, 8)
                    pivot_row = rows[r][at : at + 1, :]
                    pivot = pivot_row[:, k : k + 1]
                    scaled = pivot_row * (1.0 / pivot)
                    out[k : k + 1, :] = (pivot_row * lax.rsqrt(pivot))[:, rank:]
                    for j in range(r, rank // 8):
                        column = rows[j][:, k : k + 1]
                        if j == r:
                            column = jnp.where(sub[:, :1] > at, column, 0.0)
                        rows[j] = rows[j] - column * scaled

            shape = (gram_rows, LANES)
            ins = [(one, *whole(shape)), (two, *whole(shape))]
            outs = [((rank, rank), F32, *whole((rank, rank)))]
            cost = (10**9, 20 * MIB)
            return call(body, "eliminate", scalars, ins, outs, (1,), cost=cost)[0]

        def sum_pix(send, own):
            got = swap(send, "pix", 1)
            value, gram = own + got[:stack_rows], send[stack_rows:] + got[stack_rows:]
            me = lax.axis_index("pix")
            for level in range(1, levels - 1):
                mine = lax.rem(me >> level, 2)
                rows = value.shape[0] // 2
                away = lax.dynamic_slice_in_dim(value, (1 - mine) * rows, rows, 0)
                value = lax.dynamic_slice_in_dim(value, mine * rows, rows, 0)
                got = swap(jnp.concatenate([away, gram], axis=0), "pix", 1 << level)
                value, gram = value + got[:rows], gram + got[rows:]
            rows = value.shape[0]
            got = swap(jnp.concatenate([value, gram], axis=0), "pix", 1 << (levels - 1))
            value = value + got[:rows]
            inverse = eliminate(gram, got[rows:])
            for level in range(levels - 2, 0, -1):
                mine = lax.rem(me >> level, 2)
                got = swap(value, "pix", 1 << level)
                low = jnp.where(mine == 0, value, got)
                high = jnp.where(mine == 0, got, value)
                value = jnp.concatenate([low, high], axis=0)
            return inverse, value, swap(value, "pix", 1)

        def prepare(s, inverse, panel, stacked, wide):
            @pl.when(pl.program_id(0) == 0)
            def _():
                wide[...] = dot(inverse[...], unstack(stacked), ((1,), (0,)), HIGH)

            left = dot(inverse[...], panel[...], ((1,), (0,)), HIGH)
            left_high, left_low = split(left)
            wide_high, wide_low = split(wide[...])
            lowrank = dot(
                jnp.concatenate([left_high, left_low, left_high], axis=0),
                jnp.concatenate([wide_high, wide_high, wide_low], axis=0),
                ((0,), (0,)),
            )
            return left, (wide_high, wide_low), lowrank

        def middle(p, inverse, panel, stacked, part):
            def body(s, inverse, panel, stacked, o, d, *rest):
                before = rest[0] if p else None
                base, high, low, after, wide = rest[p:]
                _, right, lowrank = prepare(s, inverse, panel, stacked, wide)
                value = o[...] + d[...] * (1 / MU) - lowrank
                scaled = jnp.clip(value, -TAU, TAU)
                base[...] = o[...] + scaled
                pair = split(o[...] + 2.0 * scaled - value)
                high[...], low[...] = pair
                term = dot_nt(right, pair)
                after[...] = before[...] + term if p else term

            ins = [(inverse, *whole(inverse.shape)), (panel, *strip), (stacked, *whole(stacked.shape))]
            ins += [(observed, *natural(p)), (dual_init, *natural(p))]
            ins += [(part, *strip)] * p
            outs = [((n_rows, half), F32, *block)] + [((n_rows, half), BF16, *block)] * 2
            outs += [((rank, n_rows), F32, *strip)]
            cost = (9 * rank * n_rows * n_cols, 8 * n_rows * n_cols)
            scratch = [pltpu.VMEM((rank, half), F32)]
            base, high, low, part = call(body, "middle", scalars, ins, outs, (steps,), scratch, cost=cost)
            return base, (high, low), part

        def final(p, inverse, panel, stacked, base, before):
            def body(s, inverse, panel, stacked, base, *rest):
                sparse, dual, left_out, wide = rest[3 * p :]
                left, _, lowrank = prepare(s, inverse, panel, stacked, wide)
                value = base[...] - lowrank
                scaled = jnp.clip(value, -TAU, TAU)
                sparse[...] = value - scaled
                dual[...] = MU * scaled
                left_out[...] = left

            ins = [(inverse, *whole(inverse.shape)), (panel, *strip), (stacked, *whole(stacked.shape))]
            ins += [(base, *block)]
            out_strip = (rank, tall), lambda i, s: (0, gal_block(i, s))
            outs = [((n_rows, n_cols), F32, *natural(p))] * 2 + [((rank, n_rows), F32, *out_strip)]
            aliases = {}
            if p:
                ins += [(a, None, None) for a in before]
                aliases = {5: 0, 6: 1, 7: 2}
            cost = (3 * rank * n_rows * n_cols, 6 * n_rows * n_cols)
            scratch = [pltpu.VMEM((rank, half), F32)]
            return call(body, "final", scalars, ins, outs, (steps,), scratch, aliases, cost)

        def widen(inverse, own, other):
            def body(s, inverse, own, other, wide, out):
                gram = None
                for p, stacked in enumerate((own, other)):
                    value = dot(inverse[...], unstack(stacked), ((1,), (0,)), HIGH)
                    wide[:, half * p : half * (p + 1)] = value
                    term = dot(value, value, ((1,), (1,)), HIGH)
                    gram = term if gram is None else gram + term
                out[...] = jnp.concatenate([gram[:gram_rows], gram[gram_rows:]], axis=1)

            ins = [(a, *whole(a.shape)) for a in (inverse, own, other)]
            outs = [((rank, n_cols), F32, *whole((rank, n_cols)))]
            outs += [((gram_rows, LANES), F32, *whole((gram_rows, LANES)))]
            return call(body, "widen", scalars, ins, outs, (1,), cost=(10**8, MIB))

        def finish(inverse, wide):
            def body(s, inverse, wide, out):
                for p in (0, 1):
                    at = pl.multiple_of(lax.rem(s[1] + p, 2) * half, half)
                    value = wide[:, half * p : half * (p + 1)]
                    out[:, pl.ds(at, half)] = dot(inverse[...], value, ((1,), (0,)), HIGH)

            ins = [(a, *whole(a.shape)) for a in (inverse, wide)]
            outs = [((rank, n_cols), F32, *whole((rank, n_cols)))]
            return call(body, "finish", scalars, ins, outs, (1,), cost=(10**8, MIB))[0]

        own, other, part = first(right_init)
        base = None
        for step in range(ITERS):
            panel = sum_gal(part)
            send = multiply(panel, other, True)
            inverse, own_wide, other_wide = sum_pix(send, multiply(panel, own, False))
            if step < ITERS - 1:
                base0, own, part = middle(0, inverse, panel, own_wide, None)
                base1, other, part = middle(1, inverse, panel, other_wide, part)
            else:
                outs = final(0, inverse, panel, own_wide, base0, None)
                wide, gram = widen(inverse, own_wide, other_wide)
                bit = 1
                while 2 * bit < n_gal:
                    gram = gram + swap(gram, "gal", bit)
                    bit *= 2
                got = swap(gram, "gal", bit)
                sparse, dual, left = final(1, inverse, panel, other_wide, base1, outs)
                right = finish(eliminate(gram, got), wide)
        return sparse, dual, left, right

    return jax.shard_map(
        per_device,
        mesh=mesh,
        in_specs=(P("pix", "gal"), P("pix", "gal"), P("pix", "gal"), P(None, "gal")),
        out_specs=(P("pix", "gal"), P("pix", "gal"), P(None, "pix"), P(None, "gal")),
        check_vma=False,
    )
```

time: 417 us -> 122 us (0.29)
  waiting for transfers between devices: 210 us -> 34.7 us
  blocking collectives: 74.2 us -> 0 us
  matrix products: 68.5 us -> 0 us
  Pallas kernels: 0 us -> 51 us
  other arithmetic: 48.3 us -> 0.36 us
  starting transfers between devices: 0.42 us -> 24.6 us
  between operations: 14.3 us -> 0.89 us
  local copies, waits for them, and re-layouts: 1.24 us -> 9.76 us
    psum x4 -> x0, waiting for transfers between devices: 201 us -> none  [the longest x2 134 us: per_device(): wide = lax.psum(partial_wide, 'pix')]
    psum x2 -> x0, blocking collectives: 74.2 us -> none  [per_device(): gram_left = lax.psum(gram_of(panel), 'pix')]
    dot_general x10 -> x0, matrix products: 64.2 us -> none  [the longest x2 25.6 us: per_device(): lax.dot_general(left, wide, (((0,), (0,)), ((), ())), precision=HIGH)]
    pallas_call x0 -> x14, Pallas kernels: none -> 51 us  [call(): pl.pallas_call(body, name=name, grid_spec=pltpu.PrefetchScalarGridSpec(nu...]
    another operation x20 -> x1, other arithmetic: 48.3 us -> 0.08 us  [per_device(): scalars = jnp.stack([core, side]).astype(jnp.int32)]
    ppermute x0 -> x18, waiting for transfers between devices: none -> 34.7 us  [the longest x16 26.8 us: swap(): return lax.ppermute(value, axis, [(i, i ^ bit) for i in range(n)])]
    ppermute x0 -> x18, starting transfers between devices: none -> 24.6 us  [the longest x16 20.1 us: swap(): return lax.ppermute(value, axis, [(i, i ^ bit) for i in range(n)])]
    all_gather x2 -> x0, waiting for transfers between devices: 9.22 us -> none  [per_device(): whole_wide = lax.all_gather(wide, 'gal', axis=1, tiled=True)]
  transfers between devices with their start and end apart: 6 -> 18, of which waited for: 6 -> 14; matrix products, arithmetic and copies ran while one was open for 6% -> 0% of each run, Pallas kernels for 0% -> 24%
where the time goes in v3:
time: 122 us; the launch traced here: 121 us
  Pallas kernels  51 us (42%)
  waiting for transfers between devices  34.7 us (28%)
  starting transfers between devices  24.6 us (20%)
  local copies, waits for them, and re-layouts  9.76 us (8%)
    pallas_call x14, Pallas kernels, call(): pl.pallas_call(body, name=name, grid_spec=pltpu.PrefetchScalarGridSpec(nu...  51 us
    ppermute x16, waiting for transfers between devices, swap(): return lax.ppermute(value, axis, [(i, i ^ bit) for i in range(n)])  26.8 us
    ppermute x16, starting transfers between devices, swap(): return lax.ppermute(value, axis, [(i, i ^ bit) for i in range(n)])  20.1 us
    unnamed x12, local copies, waits for them, and re-layouts  9.71 us
    ppermute x2, waiting for transfers between devices, sum_gal(): lax.ppermute(mine, 'gal', [(i, (i + CORES * k) % n_gal) for i in range(n_...  7.84 us
    ppermute x2, starting transfers between devices, sum_gal(): lax.ppermute(mine, 'gal', [(i, (i + CORES * k) % n_gal) for i in range(n_...  4.52 us
  transfers between devices with their start and end apart: 18, of which 14 were waited for; matrix products, arithmetic and copies ran while one was open for 0% of the time, Pallas kernels for 24%

profile of v3, /device:TPU:0, one launch (start us, length us, event | category | flops | bytes accessed | tf_op | source)
XLA Modules:
  0.0 121.4 jit_solution(6241012473046780381)
XLA Ops:
  0.6 0.1 pad_add_fusion.s
  0.7 2.2 %copy-done = f32[1024,1024]{1,0:T(8,128)S(1)} copy-done((f32[1024,1024]{1,0:T(8,128)S(1)}, f32[1024,1024]{1,0:T(8,128)}, u32[]{:S(2)}) %copy-start) | copy-done | bytes 4194328
  2.9 2.2 %copy-done.2 = f32[1024,1024]{1,0:T(8,128)S(1)} copy-done((f32[1024,1024]{1,0:T(8,128)S(1)}, f32[1024,1024]{1,0:T(8,128)}, u32[]{:S(2)}) %copy-start.2) | copy-done | bytes 4194328
  5.1 2.2 %copy-done.4 = f32[1024,1024]{1,0:T(8,128)S(1)} copy-done((f32[1024,1024]{1,0:T(8,128)S(1)}, f32[1024,1024]{1,0:T(8,128)}, u32[]{:S(2)}) %copy-start.4) | copy-done | bytes 4194328
  7.3 0.9 copy-done.5
  8.2 4.1 %first.1 = (bf16[1024,512]{1,0:T(8,128)(2,1)S(1)}, bf16[1024,512]{1,0:T(8,128)(2,1)S(1)}, bf16[1024,512]{1,0:T(8,128)(2,1)S(1)}, bf16[1024,512]{1,0:T(8,128)(2,1)S(1)}, f32[64,1024]{1,0:T(8,128)S(1)}) custom-call(s32[2]{0:T(128)S(1)} %pad_add_fusion.s, f32[1024,1024]{1,0:T(8,128)S(1)} %copy-done, f32[1024,1024]{1,0:T(8,128)S(1)} %copy-done, ...), custom_call_target="tpu_custom_call" | custom-call | flops 402653184 | bytes 16777216 | tf_op jit(solution)/shard_map/first/pallas_call | solution.py:42
  12.4 0.5 collective-permute-start
  12.9 1.0 collective-permute-done
  13.9 2.9 %collective-permute-start.1 = (f32[64,512]{1,0:T(8,128)S(1)}, f32[64,512]{1,0:T(8,128)S(1)}, u32[]{:S(2)}, u32[]{:S(2)}) collective-permute-start(f32[64,512]{1,0:T(8,128)S(1)} %slice_add_fusion.3), channel_id=1, source_target_pairs={{0,16},{8,24},{16,0},{24,8},{1,17},{9,25},{17,1},{25,9},{2,18},{10... | collective-permute-start | bytes 393224 | tf_op jit(solution)/shard_map/ppermute | solution.py:123
  16.8 3.8 %collective-permute-done.1 = f32[64,512]{1,0:T(8,128)S(1)} collective-permute-done((f32[64,512]{1,0:T(8,128)S(1)}, f32[64,512]{1,0:T(8,128)S(1)}, u32[]{:S(2)}, u32[]{:S(2)}) %collective-permute-start.1) | collective-permute-done | bytes 131104 | tf_op jit(solution)/shard_map/ppermute | solution.py:123
  20.7 1.3 %collective-permute-done.2 = f32[64,512]{1,0:T(8,128)S(1)} collective-permute-done((f32[64,512]{1,0:T(8,128)S(1)}, f32[64,512]{1,0:T(8,128)S(1)}, u32[]{:S(2)}, u32[]{:S(2)}) %collective-permute-start.2) | collective-permute-done | bytes 131104 | tf_op jit(solution)/shard_map/ppermute | solution.py:73
  22.1 2.0 %multiply.4 = f32[288,128]{1,0:T(8,128)S(1)} custom-call(s32[2]{0:T(128)S(1)} %pad_add_fusion.s, f32[64,1024]{1,0:T(8,128)S(1)} %pad_maximum_fusion.whole_panel.panel, f32[64,1024]{1,0:T(8,128)S(1)} %pad_maximum_fusion.whole_panel.panel, bf16[1024,512]{1,0:T(8,128)(2,1)S(1)} %get-tuple-element.26.high, bf16[1024,512]{1,0:T(8,128)(2,1)S(1)} %get-tuple-element.27.low), custom_call_target="tpu_custom_call" | custom-call | flops 201326592 | bytes 2097152 | tf_op jit(solution)/shard_map/multiply/pallas_call | solution.py:42
  24.1 1.7 %collective-permute-start.3 = (f32[288,128]{1,0:T(8,128)S(1)}, f32[288,128]{1,0:T(8,128)S(1)}, u32[]{:S(2)}, u32[]{:S(2)}) collective-permute-start(f32[288,128]{1,0:T(8,128)S(1)} %multiply.4), channel_id=1, source_target_pairs={{0,1},{1,0},{2,3},{3,2},{4,5},{5,4},{6,7},{7,6},{8,9},{9,8},{10,11... | collective-permute-start | bytes 442376 | tf_op jit(solution)/shard_map/ppermute | solution.py:73
  25.8 1.6 %multiply.5 = f32[256,128]{1,0:T(8,128)S(1)} custom-call(s32[2]{0:T(128)S(1)} %pad_add_fusion.s, f32[64,1024]{1,0:T(8,128)S(1)} %pad_maximum_fusion.whole_panel.panel, f32[64,1024]{1,0:T(8,128)S(1)} %pad_maximum_fusion.whole_panel.panel, bf16[1024,512]{1,0:T(8,128)(2,1)S(1)} %get-tuple-element.28.high, bf16[1024,512]{1,0:T(8,128)(2,1)S(1)} %get-tuple-element.29.low), custom_call_target="tpu_custom_call" | custom-call | flops 201326592 | bytes 2097152 | tf_op jit(solution)/shard_map/multiply/pallas_call | solution.py:42
  27.4 2.6 %collective-permute-done.3 = f32[288,128]{1,0:T(8,128)S(1)} collective-permute-done((f32[288,128]{1,0:T(8,128)S(1)}, f32[288,128]{1,0:T(8,128)S(1)}, u32[]{:S(2)}, u32[]{:S(2)}) %collective-permute-start.3) | collective-permute-done | bytes 147488 | tf_op jit(solution)/shard_map/ppermute | solution.py:73
  30.1 1.9 %collective-permute-start.4 = (f32[160,128]{1,0:T(8,128)S(1)}, f32[160,128]{1,0:T(8,128)S(1)}, u32[]{:S(2)}, u32[]{:S(2)}) collective-permute-start(f32[160,128]{1,0:T(8,128)S(1)} %pad_maximum_fusion.4), channel_id=1, source_target_pairs={{0,2},{1,3},{2,0},{3,1},{4,6},{5,7},{6,4},{7,5},{8,10},{9,11},{10,... | collective-permute-start | bytes 245768 | tf_op jit(solution)/shard_map/ppermute | solution.py:73
  31.9 2.6 %collective-permute-done.4 = f32[160,128]{1,0:T(8,128)S(1)} collective-permute-done((f32[160,128]{1,0:T(8,128)S(1)}, f32[160,128]{1,0:T(8,128)S(1)}, u32[]{:S(2)}, u32[]{:S(2)}) %collective-permute-start.4) | collective-permute-done | bytes 81952 | tf_op jit(solution)/shard_map/ppermute | solution.py:73
  34.6 2.9 %collective-permute-start.5 = (f32[160,128]{1,0:T(8,128)S(1)}, f32[160,128]{1,0:T(8,128)S(1)}, u32[]{:S(2)}, u32[]{:S(2)}) collective-permute-start(f32[160,128]{1,0:T(8,128)S(1)} %pad_maximum_fusion.5), channel_id=1, source_target_pairs={{0,4},{1,5},{2,6},{3,7},{4,0},{5,1},{6,2},{7,3},{8,12},{9,13},{10,... | collective-permute-start | bytes 245768 | tf_op jit(solution)/shard_map/ppermute | solution.py:73
  37.5 2.5 %collective-permute-done.5 = f32[160,128]{1,0:T(8,128)S(1)} collective-permute-done((f32[160,128]{1,0:T(8,128)S(1)}, f32[160,128]{1,0:T(8,128)S(1)}, u32[]{:S(2)}, u32[]{:S(2)}) %collective-permute-start.5) | collective-permute-done | bytes 81952 | tf_op jit(solution)/shard_map/ppermute | solution.py:73
  40.0 1.9 %collective-permute-start.6 = (f32[128,128]{1,0:T(8,128)S(1)}, f32[128,128]{1,0:T(8,128)S(1)}, u32[]{:S(2)}, u32[]{:S(2)}) collective-permute-start(f32[128,128]{1,0:T(8,128)S(1)} %slice_add_fusion.6), channel_id=1, source_target_pairs={{0,2},{1,3},{2,0},{3,1},{4,6},{5,7},{6,4},{7,5},{8,10},{9,11},{10,... | collective-permute-start | bytes 196616 | tf_op jit(solution)/shard_map/ppermute | solution.py:73
  41.9 2.5 %collective-permute-done.6 = f32[128,128]{1,0:T(8,128)S(1)} collective-permute-done((f32[128,128]{1,0:T(8,128)S(1)}, f32[128,128]{1,0:T(8,128)S(1)}, u32[]{:S(2)}, u32[]{:S(2)}) %collective-permute-start.6) | collective-permute-done | bytes 65568 | tf_op jit(solution)/shard_map/ppermute | solution.py:73
  44.4 1.8 %collective-permute-start.7 = (f32[256,128]{1,0:T(8,128)S(1)}, f32[256,128]{1,0:T(8,128)S(1)}, u32[]{:S(2)}, u32[]{:S(2)}) collective-permute-start(f32[256,128]{1,0:T(8,128)S(1)} %pad_maximum_fusion.2.stacked), channel_id=1, source_target_pairs={{0,1},{1,0},{2,3},{3,2},{4,5},{5,4},{6,7},{7,6},{8,9},{9,8},{10,11... | collective-permute-start | bytes 393224 | tf_op jit(solution)/shard_map/ppermute | solution.py:73
  46.2 6.2 %eliminate.3.inverse = f32[64,64]{1,0:T(8,128)S(1)} custom-call(s32[2]{0:T(128)S(1)} %pad_add_fusion.s, f32[32,128]{1,0:T(8,128)S(1)} %slice_add_fusion.10.one, f32[32,128]{1,0:T(8,128)S(1)} %slice.61.two), custom_call_target="tpu_custom_call" | custom-call | flops 1000000000 | bytes 20971520 | tf_op jit(solution)/shard_map/eliminate/pallas_call | solution.py:42
  52.5 2.2 %copy-done.3 = f32[1024,1024]{1,0:T(8,128)S(1)} copy-done((f32[1024,1024]{1,0:T(8,128)S(1)}, f32[1024,1024]{1,0:T(8,128)}, u32[]{:S(2)}) %copy-start.3) | copy-done | bytes 4194328
  54.6 4.5 %middle.2 = (f32[1024,512]{1,0:T(8,128)S(1)}, bf16[1024,512]{1,0:T(8,128)(2,1)S(1)}, bf16[1024,512]{1,0:T(8,128)(2,1)S(1)}, f32[64,1024]{1,0:T(8,128)S(1)}) custom-call(s32[2]{0:T(128)S(1)} %pad_add_fusion.s, f32[64,64]{1,0:T(8,128)S(1)} %eliminate.3.inverse, f32[64,1024]{1,0:T(8,128)S(1)} %pad_maximum_fusion.whole_panel.panel, ...), custom_call_target="tpu_custom_call" | custom-call | flops 603979776 | bytes 8388608 | tf_op jit(solution)/shard_map/middle/pallas_call | solution.py:42
  59.2 4.6 %middle.3 = (f32[1024,512]{1,0:T(8,128)S(1)}, bf16[1024,512]{1,0:T(8,128)(2,1)S(1)}, bf16[1024,512]{1,0:T(8,128)(2,1)S(1)}, f32[64,1024]{1,0:T(8,128)S(1)}) custom-call(s32[2]{0:T(128)S(1)} %pad_add_fusion.s, f32[64,64]{1,0:T(8,128)S(1)} %eliminate.3.inverse, f32[64,1024]{1,0:T(8,128)S(1)} %pad_maximum_fusion.whole_panel.panel, ...), custom_call_target="tpu_custom_call" | custom-call | flops 603979776 | bytes 8388608 | tf_op jit(solution)/shard_map/middle/pallas_call | solution.py:42
  63.8 1.3 %collective-permute-done.8 = f32[64,512]{1,0:T(8,128)S(1)} collective-permute-done((f32[64,512]{1,0:T(8,128)S(1)}, f32[64,512]{1,0:T(8,128)S(1)}, u32[]{:S(2)}, u32[]{:S(2)}) %collective-permute-start.8) | collective-permute-done | bytes 131104 | tf_op jit(solution)/shard_map/ppermute | solution.py:73
  65.2 1.6 %collective-permute-start.9 = (f32[64,512]{1,0:T(8,128)S(1)}, f32[64,512]{1,0:T(8,128)S(1)}, u32[]{:S(2)}, u32[]{:S(2)}) collective-permute-start(f32[64,512]{1,0:T(8,128)S(1)} %slice_add_fusion.2), channel_id=1, source_target_pairs={{0,16},{8,24},{16,0},{24,8},{1,17},{9,25},{17,1},{25,9},{2,18},{10... | collective-permute-start | bytes 393224 | tf_op jit(solution)/shard_map/ppermute | solution.py:123
  66.8 4.0 %collective-permute-done.9 = f32[64,512]{1,0:T(8,128)S(1)} collective-permute-done((f32[64,512]{1,0:T(8,128)S(1)}, f32[64,512]{1,0:T(8,128)S(1)}, u32[]{:S(2)}, u32[]{:S(2)}) %collective-permute-start.9) | collective-permute-done | bytes 131104 | tf_op jit(solution)/shard_map/ppermute | solution.py:123
  70.9 1.3 %collective-permute-done.10 = f32[64,512]{1,0:T(8,128)S(1)} collective-permute-done((f32[64,512]{1,0:T(8,128)S(1)}, f32[64,512]{1,0:T(8,128)S(1)}, u32[]{:S(2)}, u32[]{:S(2)}) %collective-permute-start.10) | collective-permute-done | bytes 131104 | tf_op jit(solution)/shard_map/ppermute | solution.py:73
  72.3 2.0 %multiply.6 = f32[288,128]{1,0:T(8,128)S(1)} custom-call(s32[2]{0:T(128)S(1)} %pad_add_fusion.s, f32[64,1024]{1,0:T(8,128)S(1)} %pad_maximum_fusion.1.whole_panel.panel, f32[64,1024]{1,0:T(8,128)S(1)} %pad_maximum_fusion.1.whole_panel.panel, bf16[1024,512]{1,0:T(8,128)(2,1)S(1)} %get-tuple-element.32.high, bf16[1024,512]{1,0:T(8,128)(2,1)S(1)} %get-tuple-element.33.low), custom_call_target="tpu_custom_call" | custom-call | flops 201326592 | bytes 2097152 | tf_op jit(solution)/shard_map/multiply/pallas_call | solution.py:42
  74.3 0.3 collective-permute-start.11
  74.6 1.6 %multiply.7 = f32[256,128]{1,0:T(8,128)S(1)} custom-call(s32[2]{0:T(128)S(1)} %pad_add_fusion.s, f32[64,1024]{1,0:T(8,128)S(1)} %pad_maximum_fusion.1.whole_panel.panel, f32[64,1024]{1,0:T(8,128)S(1)} %pad_maximum_fusion.1.whole_panel.panel, bf16[1024,512]{1,0:T(8,128)(2,1)S(1)} %get-tuple-element.34.high, bf16[1024,512]{1,0:T(8,128)(2,1)S(1)} %get-tuple-element.35.low), custom_call_target="tpu_custom_call" | custom-call | flops 201326592 | bytes 2097152 | tf_op jit(solution)/shard_map/multiply/pallas_call | solution.py:42
  76.2 4.0 %collective-permute-done.11 = f32[288,128]{1,0:T(8,128)S(1)} collective-permute-done((f32[288,128]{1,0:T(8,128)S(1)}, f32[288,128]{1,0:T(8,128)S(1)}, u32[]{:S(2)}, u32[]{:S(2)}) %collective-permute-start.11) | collective-permute-done | bytes 147488 | tf_op jit(solution)/shard_map/ppermute | solution.py:73
  80.3 1.6 %collective-permute-start.12 = (f32[160,128]{1,0:T(8,128)S(1)}, f32[160,128]{1,0:T(8,128)S(1)}, u32[]{:S(2)}, u32[]{:S(2)}) collective-permute-start(f32[160,128]{1,0:T(8,128)S(1)} %pad_maximum_fusion.6), channel_id=1, source_target_pairs={{0,2},{1,3},{2,0},{3,1},{4,6},{5,7},{6,4},{7,5},{8,10},{9,11},{10,... | collective-permute-start | bytes 245768 | tf_op jit(solution)/shard_map/ppermute | solution.py:73
  81.9 2.9 %collective-permute-done.12 = f32[160,128]{1,0:T(8,128)S(1)} collective-permute-done((f32[160,128]{1,0:T(8,128)S(1)}, f32[160,128]{1,0:T(8,128)S(1)}, u32[]{:S(2)}, u32[]{:S(2)}) %collective-permute-start.12) | collective-permute-done | bytes 81952 | tf_op jit(solution)/shard_map/ppermute | solution.py:73
  84.8 3.0 %collective-permute-start.13 = (f32[160,128]{1,0:T(8,128)S(1)}, f32[160,128]{1,0:T(8,128)S(1)}, u32[]{:S(2)}, u32[]{:S(2)}) collective-permute-start(f32[160,128]{1,0:T(8,128)S(1)} %pad_maximum_fusion.7), channel_id=1, source_target_pairs={{0,4},{1,5},{2,6},{3,7},{4,0},{5,1},{6,2},{7,3},{8,12},{9,13},{10,... | collective-permute-start | bytes 245768 | tf_op jit(solution)/shard_map/ppermute | solution.py:73
  87.8 2.4 %collective-permute-done.13 = f32[160,128]{1,0:T(8,128)S(1)} collective-permute-done((f32[160,128]{1,0:T(8,128)S(1)}, f32[160,128]{1,0:T(8,128)S(1)}, u32[]{:S(2)}, u32[]{:S(2)}) %collective-permute-start.13) | collective-permute-done | bytes 81952 | tf_op jit(solution)/shard_map/ppermute | solution.py:73
  90.2 2.1 %collective-permute-start.14 = (f32[128,128]{1,0:T(8,128)S(1)}, f32[128,128]{1,0:T(8,128)S(1)}, u32[]{:S(2)}, u32[]{:S(2)}) collective-permute-start(f32[128,128]{1,0:T(8,128)S(1)} %slice_add_fusion.4), channel_id=1, source_target_pairs={{0,2},{1,3},{2,0},{3,1},{4,6},{5,7},{6,4},{7,5},{8,10},{9,11},{10,... | collective-permute-start | bytes 196616 | tf_op jit(solution)/shard_map/ppermute | solution.py:73
  92.3 2.2 %collective-permute-done.14 = f32[128,128]{1,0:T(8,128)S(1)} collective-permute-done((f32[128,128]{1,0:T(8,128)S(1)}, f32[128,128]{1,0:T(8,128)S(1)}, u32[]{:S(2)}, u32[]{:S(2)}) %collective-permute-start.14) | collective-permute-done | bytes 65568 | tf_op jit(solution)/shard_map/ppermute | solution.py:73
  94.6 0.6 collective-permute-start.15
  95.2 6.2 %eliminate.4.inverse = f32[64,64]{1,0:T(8,128)S(1)} custom-call(s32[2]{0:T(128)S(1)} %pad_add_fusion.s, f32[32,128]{1,0:T(8,128)S(1)} %slice_add_fusion.8.one, f32[32,128]{1,0:T(8,128)S(1)} %slice.68.two), custom_call_target="tpu_custom_call" | custom-call | flops 1000000000 | bytes 20971520 | tf_op jit(solution)/shard_map/eliminate/pallas_call | solution.py:42
  101.4 1.5 %widen.1 = (f32[64,1024]{1,0:T(8,128)S(1)}, f32[32,128]{1,0:T(8,128)S(1)}) custom-call(s32[2]{0:T(128)S(1)} %pad_add_fusion.s, f32[64,64]{1,0:T(8,128)S(1)} %eliminate.4.inverse, f32[256,128]{1,0:T(8,128)S(1)} %pad_maximum_fusion.3.stacked.own, f32[256,128]{1,0:T(8,128)S(1)} %collective-permute-done.15.stacked.other), custom_call_target="tpu_custom_call" | custom-call | flops 100000000 | bytes 1048576 | tf_op jit(solution)/shard_map/widen/pallas_call | solution.py:42
  103.0 4.4 %final.2 = (f32[1024,1024]{1,0:T(8,128)}, f32[1024,1024]{1,0:T(8,128)}, f32[64,1024]{1,0:T(8,128)}) custom-call(s32[2]{0:T(128)S(1)} %pad_add_fusion.s, f32[64,64]{1,0:T(8,128)S(1)} %eliminate.4.inverse, f32[64,1024]{1,0:T(8,128)S(1)} %pad_maximum_fusion.1.whole_panel.panel, f32[256,128]{1,0:T(8,128)S(1)} %pad_maximum_fusion.3.stacked.own, ...), custom_call_target="tpu_custom_call" | custom-call | flops 201326592 | bytes 6291456 | tf_op jit(solution)/shard_map/final/pallas_call | solution.py:42
  107.5 1.6 %collective-permute-start.17 = (f32[32,128]{1,0:T(8,128)S(1)}, f32[32,128]{1,0:T(8,128)S(1)}, u32[]{:S(2)}, u32[]{:S(2)}) collective-permute-start(f32[32,128]{1,0:T(8,128)S(1)} %add.69.one), channel_id=1, source_target_pairs={{0,16},{8,24},{16,0},{24,8},{1,17},{9,25},{17,1},{25,9},{2,18},{10... | collective-permute-start | bytes 49160 | tf_op jit(solution)/shard_map/ppermute | solution.py:73
  109.1 4.4 %final.3 = (f32[1024,1024]{1,0:T(8,128)}, f32[1024,1024]{1,0:T(8,128)}, f32[64,1024]{1,0:T(8,128)}) custom-call(s32[2]{0:T(128)S(1)} %pad_add_fusion.s, f32[64,64]{1,0:T(8,128)S(1)} %eliminate.4.inverse, f32[64,1024]{1,0:T(8,128)S(1)} %pad_maximum_fusion.1.whole_panel.panel, ...), custom_call_target="tpu_custom_call", output_to_operand_aliasing={{0}: (5, {}), {1}: (6, {}), {2}: (7, {})} | custom-call | flops 201326592 | bytes 6291456 | tf_op jit(solution)/shard_map/final/pallas_call | solution.py:42
  113.5 6.2 %eliminate.5.inverse = f32[64,64]{1,0:T(8,128)S(1)} custom-call(s32[2]{0:T(128)S(1)} %pad_add_fusion.s, f32[32,128]{1,0:T(8,128)S(1)} %add.69.one, f32[32,128]{1,0:T(8,128)S(1)} %collective-permute-done.17.two), custom_call_target="tpu_custom_call" | custom-call | flops 1000000000 | bytes 20971520 | tf_op jit(solution)/shard_map/eliminate/pallas_call | solution.py:42
  119.7 1.6 %finish.1 = f32[64,1024]{1,0:T(8,128)} custom-call(s32[2]{0:T(128)S(1)} %pad_add_fusion.s, f32[64,64]{1,0:T(8,128)S(1)} %eliminate.5.inverse, f32[64,1024]{1,0:T(8,128)S(1)} %get-tuple-element.45.wide), custom_call_target="tpu_custom_call" | custom-call | flops 100000000 | bytes 1048576 | tf_op jit(solution)/shard_map/finish/pallas_call | solution.py:42
  (46 shorter events, 0.6 us)
Async XLA Ops:
  0.7 2.2 %copy-start = (f32[1024,1024]{1,0:T(8,128)S(1)}, f32[1024,1024]{1,0:T(8,128)}, u32[]{:S(2)}) copy-start(f32[1024,1024]{1,0:T(8,128)} %o.3) | copy-start | bytes 12582916
  2.9 2.2 %copy-start.2 = (f32[1024,1024]{1,0:T(8,128)S(1)}, f32[1024,1024]{1,0:T(8,128)}, u32[]{:S(2)}) copy-start(f32[1024,1024]{1,0:T(8,128)} %d.3) | copy-start | bytes 12582916
  5.1 2.2 %copy-start.4 = (f32[1024,1024]{1,0:T(8,128)S(1)}, f32[1024,1024]{1,0:T(8,128)}, u32[]{:S(2)}) copy-start(f32[1024,1024]{1,0:T(8,128)} %s1_.1) | copy-start | bytes 12582916
  7.3 0.9 copy-start.5
  12.4 1.5 %collective-permute-start = (f32[64,512]{1,0:T(8,128)S(1)}, f32[64,512]{1,0:T(8,128)S(1)}, u32[]{:S(2)}, u32[]{:S(2)}) collective-permute-start(f32[64,512]{1,0:T(8,128)S(1)} %split.13), channel_id=1, source_target_pairs={{0,8},{8,0},{16,24},{24,16},{1,9},{9,1},{17,25},{25,17},{2,10},{10... | collective-permute-start | bytes 393224 | tf_op jit(solution)/shard_map/ppermute | solution.py:73
  13.9 6.8 %collective-permute-start.1 = (f32[64,512]{1,0:T(8,128)S(1)}, f32[64,512]{1,0:T(8,128)S(1)}, u32[]{:S(2)}, u32[]{:S(2)}) collective-permute-start(f32[64,512]{1,0:T(8,128)S(1)} %slice_add_fusion.3), channel_id=1, source_target_pairs={{0,16},{8,24},{16,0},{24,8},{1,17},{9,25},{17,1},{25,9},{2,18},{10... | collective-permute-start | bytes 393224 | tf_op jit(solution)/shard_map/ppermute | solution.py:123
  20.7 1.4 %collective-permute-start.2 = (f32[64,512]{1,0:T(8,128)S(1)}, f32[64,512]{1,0:T(8,128)S(1)}, u32[]{:S(2)}, u32[]{:S(2)}) collective-permute-start(f32[64,512]{1,0:T(8,128)S(1)} %add.54), channel_id=1, source_target_pairs={{0,8},{8,0},{16,24},{24,16},{1,9},{9,1},{17,25},{25,17},{2,10},{10... | collective-permute-start | bytes 393224 | tf_op jit(solution)/shard_map/ppermute | solution.py:73
  24.1 5.9 %collective-permute-start.3 = (f32[288,128]{1,0:T(8,128)S(1)}, f32[288,128]{1,0:T(8,128)S(1)}, u32[]{:S(2)}, u32[]{:S(2)}) collective-permute-start(f32[288,128]{1,0:T(8,128)S(1)} %multiply.4), channel_id=1, source_target_pairs={{0,1},{1,0},{2,3},{3,2},{4,5},{5,4},{6,7},{7,6},{8,9},{9,8},{10,11... | collective-permute-start | bytes 442376 | tf_op jit(solution)/shard_map/ppermute | solution.py:73
  30.1 4.5 %collective-permute-start.4 = (f32[160,128]{1,0:T(8,128)S(1)}, f32[160,128]{1,0:T(8,128)S(1)}, u32[]{:S(2)}, u32[]{:S(2)}) collective-permute-start(f32[160,128]{1,0:T(8,128)S(1)} %pad_maximum_fusion.4), channel_id=1, source_target_pairs={{0,2},{1,3},{2,0},{3,1},{4,6},{5,7},{6,4},{7,5},{8,10},{9,11},{10,... | collective-permute-start | bytes 245768 | tf_op jit(solution)/shard_map/ppermute | solution.py:73
  34.6 5.4 %collective-permute-start.5 = (f32[160,128]{1,0:T(8,128)S(1)}, f32[160,128]{1,0:T(8,128)S(1)}, u32[]{:S(2)}, u32[]{:S(2)}) collective-permute-start(f32[160,128]{1,0:T(8,128)S(1)} %pad_maximum_fusion.5), channel_id=1, source_target_pairs={{0,4},{1,5},{2,6},{3,7},{4,0},{5,1},{6,2},{7,3},{8,12},{9,13},{10,... | collective-permute-start | bytes 245768 | tf_op jit(solution)/shard_map/ppermute | solution.py:73
  40.0 4.3 %collective-permute-start.6 = (f32[128,128]{1,0:T(8,128)S(1)}, f32[128,128]{1,0:T(8,128)S(1)}, u32[]{:S(2)}, u32[]{:S(2)}) collective-permute-start(f32[128,128]{1,0:T(8,128)S(1)} %slice_add_fusion.6), channel_id=1, source_target_pairs={{0,2},{1,3},{2,0},{3,1},{4,6},{5,7},{6,4},{7,5},{8,10},{9,11},{10,... | collective-permute-start | bytes 196616 | tf_op jit(solution)/shard_map/ppermute | solution.py:73
  41.9 10.6 %copy-start.1 = (f32[1024,1024]{1,0:T(8,128)S(1)}, f32[1024,1024]{1,0:T(8,128)}, u32[]{:S(2)}) copy-start(f32[1024,1024]{1,0:T(8,128)} %o.3) | copy-start | bytes 12582916
  44.4 14.8 %collective-permute-start.7 = (f32[256,128]{1,0:T(8,128)S(1)}, f32[256,128]{1,0:T(8,128)S(1)}, u32[]{:S(2)}, u32[]{:S(2)}) collective-permute-start(f32[256,128]{1,0:T(8,128)S(1)} %pad_maximum_fusion.2.stacked), channel_id=1, source_target_pairs={{0,1},{1,0},{2,3},{3,2},{4,5},{5,4},{6,7},{7,6},{8,9},{9,8},{10,11... | collective-permute-start | bytes 393224 | tf_op jit(solution)/shard_map/ppermute | solution.py:73
  52.4 2.2 %copy-start.3 = (f32[1024,1024]{1,0:T(8,128)S(1)}, f32[1024,1024]{1,0:T(8,128)}, u32[]{:S(2)}) copy-start(f32[1024,1024]{1,0:T(8,128)} %d.3) | copy-start | bytes 12582916
  63.8 1.4 %collective-permute-start.8 = (f32[64,512]{1,0:T(8,128)S(1)}, f32[64,512]{1,0:T(8,128)S(1)}, u32[]{:S(2)}, u32[]{:S(2)}) collective-permute-start(f32[64,512]{1,0:T(8,128)S(1)} %split.15), channel_id=1, source_target_pairs={{0,8},{8,0},{16,24},{24,16},{1,9},{9,1},{17,25},{25,17},{2,10},{10... | collective-permute-start | bytes 393224 | tf_op jit(solution)/shard_map/ppermute | solution.py:73
  65.2 5.6 %collective-permute-start.9 = (f32[64,512]{1,0:T(8,128)S(1)}, f32[64,512]{1,0:T(8,128)S(1)}, u32[]{:S(2)}, u32[]{:S(2)}) collective-permute-start(f32[64,512]{1,0:T(8,128)S(1)} %slice_add_fusion.2), channel_id=1, source_target_pairs={{0,16},{8,24},{16,0},{24,8},{1,17},{9,25},{17,1},{25,9},{2,18},{10... | collective-permute-start | bytes 393224 | tf_op jit(solution)/shard_map/ppermute | solution.py:123
  70.8 1.4 %collective-permute-start.10 = (f32[64,512]{1,0:T(8,128)S(1)}, f32[64,512]{1,0:T(8,128)S(1)}, u32[]{:S(2)}, u32[]{:S(2)}) collective-permute-start(f32[64,512]{1,0:T(8,128)S(1)} %add.63), channel_id=1, source_target_pairs={{0,8},{8,0},{16,24},{24,16},{1,9},{9,1},{17,25},{25,17},{2,10},{10... | collective-permute-start | bytes 393224 | tf_op jit(solution)/shard_map/ppermute | solution.py:73
  74.3 5.9 %collective-permute-start.11 = (f32[288,128]{1,0:T(8,128)S(1)}, f32[288,128]{1,0:T(8,128)S(1)}, u32[]{:S(2)}, u32[]{:S(2)}) collective-permute-start(f32[288,128]{1,0:T(8,128)S(1)} %multiply.6), channel_id=1, source_target_pairs={{0,1},{1,0},{2,3},{3,2},{4,5},{5,4},{6,7},{7,6},{8,9},{9,8},{10,11... | collective-permute-start | bytes 442376 | tf_op jit(solution)/shard_map/ppermute | solution.py:73
  80.3 4.5 %collective-permute-start.12 = (f32[160,128]{1,0:T(8,128)S(1)}, f32[160,128]{1,0:T(8,128)S(1)}, u32[]{:S(2)}, u32[]{:S(2)}) collective-permute-start(f32[160,128]{1,0:T(8,128)S(1)} %pad_maximum_fusion.6), channel_id=1, source_target_pairs={{0,2},{1,3},{2,0},{3,1},{4,6},{5,7},{6,4},{7,5},{8,10},{9,11},{10,... | collective-permute-start | bytes 245768 | tf_op jit(solution)/shard_map/ppermute | solution.py:73
  84.8 5.4 %collective-permute-start.13 = (f32[160,128]{1,0:T(8,128)S(1)}, f32[160,128]{1,0:T(8,128)S(1)}, u32[]{:S(2)}, u32[]{:S(2)}) collective-permute-start(f32[160,128]{1,0:T(8,128)S(1)} %pad_maximum_fusion.7), channel_id=1, source_target_pairs={{0,4},{1,5},{2,6},{3,7},{4,0},{5,1},{6,2},{7,3},{8,12},{9,13},{10,... | collective-permute-start | bytes 245768 | tf_op jit(solution)/shard_map/ppermute | solution.py:73
  90.2 4.3 %collective-permute-start.14 = (f32[128,128]{1,0:T(8,128)S(1)}, f32[128,128]{1,0:T(8,128)S(1)}, u32[]{:S(2)}, u32[]{:S(2)}) collective-permute-start(f32[128,128]{1,0:T(8,128)S(1)} %slice_add_fusion.4), channel_id=1, source_target_pairs={{0,2},{1,3},{2,0},{3,1},{4,6},{5,7},{6,4},{7,5},{8,10},{9,11},{10,... | collective-permute-start | bytes 196616 | tf_op jit(solution)/shard_map/ppermute | solution.py:73
  94.6 6.8 %collective-permute-start.15 = (f32[256,128]{1,0:T(8,128)S(1)}, f32[256,128]{1,0:T(8,128)S(1)}, u32[]{:S(2)}, u32[]{:S(2)}) collective-permute-start(f32[256,128]{1,0:T(8,128)S(1)} %pad_maximum_fusion.3.stacked.own), channel_id=1, source_target_pairs={{0,1},{1,0},{2,3},{3,2},{4,5},{5,4},{6,7},{7,6},{8,9},{9,8},{10,11... | collective-permute-start | bytes 393224 | tf_op jit(solution)/shard_map/ppermute | solution.py:73
  103.0 4.5 %collective-permute-start.16 = (f32[32,128]{1,0:T(8,128)S(1)}, f32[32,128]{1,0:T(8,128)S(1)}, u32[]{:S(2)}, u32[]{:S(2)}) collective-permute-start(f32[32,128]{1,0:T(8,128)S(1)} %get-tuple-element.44), channel_id=1, source_target_pairs={{0,8},{8,0},{16,24},{24,16},{1,9},{9,1},{17,25},{25,17},{2,10},{10... | collective-permute-start | bytes 49160 | tf_op jit(solution)/shard_map/ppermute | solution.py:73
  107.5 6.0 %collective-permute-start.17 = (f32[32,128]{1,0:T(8,128)S(1)}, f32[32,128]{1,0:T(8,128)S(1)}, u32[]{:S(2)}, u32[]{:S(2)}) collective-permute-start(f32[32,128]{1,0:T(8,128)S(1)} %add.69.one), channel_id=1, source_target_pairs={{0,16},{8,24},{16,0},{24,8},{1,17},{9,25},{17,1},{25,9},{2,18},{10... | collective-permute-start | bytes 49160 | tf_op jit(solution)/shard_map/ppermute | solution.py:73

commit v4 on v0

v4 whole, which is shorter than its diff:
```python
import jax
import jax.numpy as jnp
from jax import lax
from jax.experimental import pallas as pl
from jax.experimental.pallas import tpu as pltpu
from jax.sharding import PartitionSpec as P

ITERS = 2


MU = 1.25
TAU = 0.6 / 1.25
HIGH = lax.Precision.HIGHEST
CORES = 2
LANES = 128
F32, BF16 = jnp.float32, jnp.bfloat16
MIB = 1 << 20


def split(value):
    high = value.astype(BF16)
    return high, (value - high.astype(F32)).astype(BF16)


def dot(a, b, dims, precision=None):
    return lax.dot_general(a, b, (dims, ((), ())), precision=precision, preferred_element_type=F32)


def dot_nt(a, b):
    rows = a[0].shape[0]
    both = dot(jnp.concatenate(a, axis=0), b[0], ((1,), (1,)))
    return both[:rows] + both[rows:] + dot(a[0], b[1], ((1,), (1,)))


def dot_nn(a, b):
    rows = a[0].shape[0]
    both = dot(jnp.concatenate(a, axis=0), b[0], ((1,), (0,)))
    return both[:rows] + both[rows:] + dot(a[0], b[1], ((1,), (0,)))


def call(body, name, ins, outs, scratch=(), aliases=None, cost=(0, 0), limit=24):
    return pl.pallas_call(
        body,
        name=name,
        in_specs=[pl.BlockSpec(memory_space=space) for _, space in ins],
        out_specs=[pl.BlockSpec(memory_space=space) for _, _, space in outs],
        out_shape=[jax.ShapeDtypeStruct(shape, dtype) for shape, dtype, _ in outs],
        scratch_shapes=list(scratch),
        input_output_aliases=aliases or {},
        compiler_params=pltpu.CompilerParams(vmem_limit_bytes=limit * MIB),
        cost_estimate=pl.CostEstimate(flops=cost[0], bytes_accessed=cost[1], transcendentals=0),
    )(*[pltpu.with_memory_space_constraint(a, pltpu.HBM) if m is pltpu.HBM else a for a, m in ins])


def invert(packed, out):
    gram_rows, rank = packed.shape[0], out.shape[0]
    full = (8, LANES)
    lane = lax.broadcasted_iota(jnp.int32, full, 1)
    sub = lax.broadcasted_iota(jnp.int32, full, 0)
    turned = pltpu.roll(packed, LANES // 2, 1)
    rows = []
    for j in range(rank // 8):
        source = packed if 8 * j < gram_rows else turned
        at = 8 * j % gram_rows
        eye = jnp.where(lane - rank == sub + 8 * j, 1.0, 0.0)
        rows.append(jnp.where(lane < rank, source[at : at + 8], eye))
    wide = 4
    for k in range(0, rank, wide):
        r, at = divmod(k, 8)
        after = range(r if at + wide < 8 else r + 1, rank // 8)
        lines = [jnp.broadcast_to(rows[r][at + p : at + p + 1, :], full) for p in range(wide)]
        core = {
            (p, q): jnp.broadcast_to(lines[p][:, k + q : k + q + 1], full)
            for p in range(wide)
            for q in range(p, wide)
        }
        columns = {
            (j, p): jnp.broadcast_to(rows[j][:, k + p : k + p + 1], full) for j in after for p in range(wide)
        }
        for p in range(wide):
            inverse = 1.0 / core[p, p]
            factors = [core[p, q] * inverse for q in range(p + 1, wide)]
            for q, factor in zip(range(p + 1, wide), factors):
                for t in range(q, wide):
                    core[q, t] = core[q, t] - factor * core[p, t]
            scaled = lines[p] * inverse
            for q in range(p + 1, wide):
                lines[q] = lines[q] - core[p, q] * scaled
            for j in after:
                column = columns[j, p]
                if j == r:
                    column = jnp.where(sub >= at + wide, column, 0.0)
                rows[j] = rows[j] - column * scaled
                for q, factor in zip(range(p + 1, wide), factors):
                    columns[j, q] = columns[j, q] - factor * columns[j, p]
            done = lines[p] * lax.rsqrt(core[p, p])
            out[k + p : k + p + 1, :] = done[0:1, rank:]


def unstack(ref):
    blocks = ref.shape[0] // 64
    return jnp.concatenate([ref[64 * t : 64 * (t + 1), :] for t in range(blocks)], axis=1)


def solution(mesh):
    n_gal, n_pix = mesh.shape["gal"], mesh.shape["pix"]
    levels = n_pix.bit_length() - 1

    def swap(value, axis, bit):
        n = mesh.shape[axis]
        return lax.ppermute(value, axis, [(i, i ^ bit) for i in range(n)])

    def per_device(observed, sparse_init, dual_init, right_init):
        rank = right_init.shape[0]
        n_rows, n_cols = observed.shape
        half = n_cols // 2
        tall = min(256, n_rows // 2)
        steps = n_rows // tall
        core = lax.rem(lax.axis_index("gal"), CORES)
        side = lax.rem(lax.axis_index("pix"), 2)
        scalars = jnp.stack([core, side]).astype(jnp.int32)
        stack_rows = rank * (half // LANES)
        gram_rows = rank * rank // LANES
        where = (scalars, pltpu.SMEM)

        def gal_at(i, s):
            turn = (1 - s[0]) * (steps // 2)
            return pl.multiple_of(lax.rem(i + turn, steps) * tall, tall)

        def pix_at(p, s):
            return pl.multiple_of(lax.rem(s[1] + p, 2) * half, half)

        def chunk(i):
            return slice(tall * i, tall * (i + 1))

        def first(right):
            def body(s, o_in, s_in, d_in, r_in, o0, o1, d0, d1, h0, l0, h1, l1, part, s0, s1, right, r_sem, sems):
                moves = {}
                right_move = pltpu.make_async_copy(r_in, right, r_sem)
                right_move.start()
                for i in range(steps):
                    for p, targets in enumerate(((o0, s0, d0), (o1, s1, d1))):
                        for a, (source, target) in enumerate(zip((o_in, s_in, d_in), targets)):
                            block = source.at[pl.ds(gal_at(i, s), tall), pl.ds(pix_at(p, s), half)]
                            move = pltpu.make_async_copy(block, target.at[chunk(i), :], sems.at[i, p, a])
                            move.start()
                            moves[i, p, a] = move
                right_move.wait()
                rights = [split(right[:, pl.ds(pix_at(p, s), half)]) for p in (0, 1)]
                for i in range(steps):
                    total = None
                    for p, (o, sp, d, h, l) in enumerate(((o0, s0, d0, h0, l0), (o1, s1, d1, h1, l1))):
                        for a in range(3):
                            moves[i, p, a].wait()
                        pair = split(o[chunk(i), :] - sp[chunk(i), :] + d[chunk(i), :] * (1 / MU))
                        h[chunk(i), :], l[chunk(i), :] = pair
                        term = dot_nt(rights[p], pair)
                        total = term if total is None else total + term
                    part[:, chunk(i)] = total

            ins = [where] + [(a, pltpu.HBM) for a in (observed, sparse_init, dual_init, right)]
            outs = [((n_rows, half), F32, pltpu.VMEM)] * 4 + [((n_rows, half), BF16, pltpu.VMEM)] * 4
            outs += [((rank, n_rows), F32, pltpu.VMEM)]
            scratch = [pltpu.VMEM((n_rows, half), F32)] * 2 + [pltpu.VMEM((rank, n_cols), F32)]
            scratch += [pltpu.SemaphoreType.DMA(()), pltpu.SemaphoreType.DMA((steps, 2, 3))]
            cost = (6 * rank * n_rows * n_cols, 16 * n_rows * n_cols)
            got = call(body, "first", ins, outs, scratch, cost=cost)
            return got[0:2], got[2:4], got[4:6], got[6:8], got[8]

        def sum_gal(part):
            away, mine = jnp.split(part, 2, axis=1)
            mine = mine + swap(away, "gal", 1)
            got = [
                lax.ppermute(mine, "gal", [(i, (i + CORES * k) % n_gal) for i in range(n_gal)])
                for k in range(1, n_gal // CORES)
            ]
            for piece in got:
                mine = mine + piece
            return jnp.concatenate([swap(mine, "gal", 1), mine], axis=1)

        def multiply(panel, pair, with_gram):
            def body(panel, high, low, out):
                total = dot_nn(split(panel[...]), (high[...], low[...]))
                for t in range(half // LANES):
                    out[rank * t : rank * (t + 1), :] = total[:, LANES * t : LANES * (t + 1)]
                if with_gram:
                    gram = dot(panel[...], panel[...], ((1,), (1,)), HIGH)
                    packed = jnp.concatenate([gram[:gram_rows], gram[gram_rows:]], axis=1)
                    out[stack_rows : stack_rows + gram_rows, :] = packed

            rows = stack_rows + (gram_rows if with_gram else 0)
            ins = [(panel, pltpu.VMEM), (pair[0], pltpu.VMEM), (pair[1], pltpu.VMEM)]
            outs = [((rows, LANES), F32, pltpu.VMEM)]
            cost = (3 * rank * n_rows * n_cols, 2 * n_rows * n_cols)
            return call(body, "multiply", ins, outs, cost=cost)[0]

        def eliminate(one, two):
            def body(one, two, out):
                invert(one[...] + two[...], out)

            ins = [(one, pltpu.VMEM), (two, pltpu.VMEM)]
            outs = [((rank, rank), F32, pltpu.VMEM)]
            return call(body, "eliminate", ins, outs, cost=(10**8, 8 * MIB))[0]

        def sum_pix(send, own):
            got = swap(send, "pix", 1)
            value, gram = own + got[:stack_rows], send[stack_rows:] + got[stack_rows:]
            me = lax.axis_index("pix")
            for level in range(1, levels - 1):
                mine = lax.rem(me >> level, 2)
                rows = value.shape[0] // 2
                away = lax.dynamic_slice_in_dim(value, (1 - mine) * rows, rows, 0)
                value = lax.dynamic_slice_in_dim(value, mine * rows, rows, 0)
                got = swap(jnp.concatenate([away, gram], axis=0), "pix", 1 << level)
                value, gram = value + got[:rows], gram + got[rows:]
            rows = value.shape[0]
            got = swap(jnp.concatenate([value, gram], axis=0), "pix", 1 << (levels - 1))
            value = value + got[:rows]
            inverse = eliminate(gram, got[rows:])
            for level in range(levels - 2, 0, -1):
                mine = lax.rem(me >> level, 2)
                got = swap(value, "pix", 1 << level)
                low = jnp.where(mine == 0, value, got)
                high = jnp.where(mine == 0, got, value)
                value = jnp.concatenate([low, high], axis=0)
            value, inverse = lax.optimization_barrier((value, inverse))
            return inverse, value, swap(value, "pix", 1)

        def halves(inverse, panel, stacked):
            left = dot(inverse[...], panel[...], ((1,), (0,)), HIGH)
            wide = dot(inverse[...], unstack(stacked), ((1,), (0,)), HIGH)
            left_high, left_low = split(left)
            wide_high, wide_low = split(wide)
            tops = jnp.concatenate([left_high, left_low, left_high], axis=0)
            return left, (wide_high, wide_low), tops, jnp.concatenate([wide_high, wide_high, wide_low], axis=0)

        def middle(inverse, panel, stacked, o, d, before):
            adds = before is not None

            def body(inverse, panel, stacked, o, d, *rest):
                base, high, low, after = rest[adds:]
                _, right, tops, wides = halves(inverse, panel, stacked)
                for i in range(steps):
                    lowrank = dot(tops[:, chunk(i)], wides, ((0,), (0,)))
                    seen = o[chunk(i), :]
                    value = seen + d[chunk(i), :] * (1 / MU) - lowrank
                    scaled = jnp.clip(value, -TAU, TAU)
                    base[chunk(i), :] = seen + scaled
                    pair = split(seen + 2.0 * scaled - value)
                    high[chunk(i), :], low[chunk(i), :] = pair
                    term = dot_nt(right, pair)
                    after[:, chunk(i)] = rest[0][:, chunk(i)] + term if adds else term

            arrays = [inverse, panel, stacked, o, d] + [before] * adds
            outs = [((n_rows, half), F32, pltpu.VMEM)] + [((n_rows, half), BF16, pltpu.VMEM)] * 2
            outs += [((rank, n_rows), F32, pltpu.VMEM)]
            cost = (9 * rank * n_rows * n_cols, 4 * n_rows * n_cols)
            base, high, low, part = call(body, "middle", [(a, pltpu.VMEM) for a in arrays], outs, cost=cost)
            return base, (high, low), part

        def final(p, inverse, panel, stacked, base, before):
            def body(s, inverse, panel, stacked, base, *rest):
                sparse, dual, *outs, sparse_part, dual_part, left_part, sems = rest[2 * p :]
                left, _, tops, wides = halves(inverse, panel, stacked)
                moves = []
                if not p:
                    for i in range(steps):
                        left_part[:, pl.ds(gal_at(i, s), tall)] = left[:, chunk(i)]
                    moves.append(pltpu.make_async_copy(left_part, outs[0], sems.at[steps, 0]))
                    moves[0].start()
                for i in range(steps):
                    value = base[chunk(i), :] - dot(tops[:, chunk(i)], wides, ((0,), (0,)))
                    scaled = jnp.clip(value, -TAU, TAU)
                    sparse_part[chunk(i), :] = value - scaled
                    dual_part[chunk(i), :] = MU * scaled
                    for a, (source, target) in enumerate(((sparse_part, sparse), (dual_part, dual))):
                        block = target.at[pl.ds(gal_at(i, s), tall), pl.ds(pix_at(p, s), half)]
                        move = pltpu.make_async_copy(source.at[chunk(i), :], block, sems.at[i, a])
                        move.start()
                        moves.append(move)
                for move in moves:
                    move.wait()

            ins = [where] + [(a, pltpu.VMEM) for a in (inverse, panel, stacked, base)]
            outs = [((n_rows, n_cols), F32, pltpu.HBM)] * 2
            aliases = {}
            if p:
                ins += [(a, pltpu.HBM) for a in before[:2]]
                aliases = {5: 0, 6: 1}
            else:
                outs += [((rank, n_rows), F32, pltpu.HBM)]
            scratch = [pltpu.VMEM((n_rows, half), F32)] * 2 + [pltpu.VMEM((rank, n_rows), F32)]
            scratch += [pltpu.SemaphoreType.DMA((steps + 1, 2))]
            cost = (3 * rank * n_rows * n_cols, 4 * n_rows * n_cols)
            return call(body, "final", ins, outs, scratch, aliases, cost)

        def widen(inverse, own, other):
            def body(inverse, own, other, wide, out):
                gram = None
                for p, stacked in enumerate((own, other)):
                    value = dot(inverse[...], unstack(stacked), ((1,), (0,)), HIGH)
                    wide[:, half * p : half * (p + 1)] = value
                    term = dot(value, value, ((1,), (1,)), HIGH)
                    gram = term if gram is None else gram + term
                out[...] = jnp.concatenate([gram[:gram_rows], gram[gram_rows:]], axis=1)

            ins = [(a, pltpu.VMEM) for a in (inverse, own, other)]
            outs = [((rank, n_cols), F32, pltpu.VMEM), ((gram_rows, LANES), F32, pltpu.VMEM)]
            return call(body, "widen", ins, outs, cost=(10**8, MIB))

        def finish(one, two, wide):
            def body(s, one, two, wide, out, inverse, right, sem):
                invert(one[...] + two[...], inverse)
                for p in (0, 1):
                    value = wide[:, half * p : half * (p + 1)]
                    right[:, pl.ds(pix_at(p, s), half)] = dot(inverse[...], value, ((1,), (0,)), HIGH)
                move = pltpu.make_async_copy(right, out, sem)
                move.start()
                move.wait()

            ins = [where] + [(a, pltpu.VMEM) for a in (one, two, wide)]
            outs = [((rank, n_cols), F32, pltpu.HBM)]
            scratch = [pltpu.VMEM((rank, rank), F32), pltpu.VMEM((rank, n_cols), F32), pltpu.SemaphoreType.DMA(())]
            return call(body, "finish", ins, outs, scratch, cost=(10**8, 8 * MIB))[0]

        seen, pulls, own, other, part = first(right_init)
        base = [None, None]
        for step in range(ITERS):
            panel = sum_gal(part)
            send = multiply(panel, other, True)
            inverse, own_wide, other_wide = sum_pix(send, multiply(panel, own, False))
            if step < ITERS - 1:
                base[0], own, part = middle(inverse, panel, own_wide, seen[0], pulls[0], None)
                base[1], other, part = middle(inverse, panel, other_wide, seen[1], pulls[1], part)
            else:
                outs = final(0, inverse, panel, own_wide, base[0], None)
                other_wide, outs = lax.optimization_barrier((other_wide, outs))
                wide, gram = widen(inverse, own_wide, other_wide)
                bit = 1
                while 2 * bit < n_gal:
                    gram = gram + swap(gram, "gal", bit)
                    bit *= 2
                got = swap(gram, "gal", bit)
                sparse, dual = final(1, inverse, panel, other_wide, base[1], outs)
                left = outs[2]
                right = finish(gram, got, wide)
        return sparse, dual, left, right

    return jax.shard_map(
        per_device,
        mesh=mesh,
        in_specs=(P("pix", "gal"), P("pix", "gal"), P("pix", "gal"), P(None, "gal")),
        out_specs=(P("pix", "gal"), P("pix", "gal"), P(None, "pix"), P(None, "gal")),
        check_vma=False,
    )
```

time: 417 us -> 102 us (0.24)
  waiting for transfers between devices: 210 us -> 33.2 us
  blocking collectives: 74.2 us -> 0 us
  matrix products: 68.5 us -> 0 us
  other arithmetic: 48.3 us -> 1.98 us
  Pallas kernels: 0 us -> 32.6 us
  starting transfers between devices: 0.42 us -> 24.7 us
  between operations: 14.3 us -> 1.1 us
  local copies, waits for them, and re-layouts: 1.24 us -> 8.45 us
    psum x4 -> x0, waiting for transfers between devices: 201 us -> none  [the longest x2 134 us: per_device(): wide = lax.psum(partial_wide, 'pix')]
    psum x2 -> x0, blocking collectives: 74.2 us -> none  [per_device(): gram_left = lax.psum(gram_of(panel), 'pix')]
    dot_general x10 -> x0, matrix products: 64.2 us -> none  [the longest x2 25.6 us: per_device(): lax.dot_general(left, wide, (((0,), (0,)), ((), ())), precision=HIGH)]
    another operation x20 -> x1, other arithmetic: 48.3 us -> 0.08 us  [per_device(): scalars = jnp.stack([core, side]).astype(jnp.int32)]
    ppermute x0 -> x18, waiting for transfers between devices: none -> 33.2 us  [the longest x16 25.4 us: swap(): return lax.ppermute(value, axis, [(i, i ^ bit) for i in range(n)])]
    pallas_call x0 -> x13, Pallas kernels: none -> 32.6 us  [call(): pl.pallas_call(body, name=name, in_specs=[pl.BlockSpec(memory_space=space...]
    ppermute x0 -> x18, starting transfers between devices: none -> 24.7 us  [the longest x16 20.2 us: swap(): return lax.ppermute(value, axis, [(i, i ^ bit) for i in range(n)])]
    all_gather x2 -> x0, waiting for transfers between devices: 9.22 us -> none  [per_device(): whole_wide = lax.all_gather(wide, 'gal', axis=1, tiled=True)]
  transfers between devices with their start and end apart: 6 -> 18, of which waited for: 6 -> 14; matrix products, arithmetic and copies ran while one was open for 6% -> 0% of each run, Pallas kernels for 0% -> 15%
where the time goes in v4:
time: 102 us
  waiting for transfers between devices  33.2 us (33%)
  Pallas kernels  32.6 us (32%)
  starting transfers between devices  24.7 us (24%)
  local copies, waits for them, and re-layouts  8.45 us (8%)
  other arithmetic  1.98 us (2%)
  between operations  1.1 us (1%)
    pallas_call x13, Pallas kernels, call(): pl.pallas_call(body, name=name, in_specs=[pl.BlockSpec(memory_space=space...  32.6 us
    ppermute x16, waiting for transfers between devices, swap(): return lax.ppermute(value, axis, [(i, i ^ bit) for i in range(n)])  25.4 us
    ppermute x16, starting transfers between devices, swap(): return lax.ppermute(value, axis, [(i, i ^ bit) for i in range(n)])  20.2 us
    unnamed x20, local copies, waits for them, and re-layouts  8.4 us
    ppermute x2, waiting for transfers between devices, sum_gal(): lax.ppermute(mine, 'gal', [(i, (i + CORES * k) % n_gal) for i in range(n_...  7.83 us
    ppermute x2, starting transfers between devices, sum_gal(): lax.ppermute(mine, 'gal', [(i, (i + CORES * k) % n_gal) for i in range(n_...  4.53 us
  transfers between devices with their start and end apart: 18, of which 14 were waited for; matrix products, arithmetic and copies ran while one was open for 0% of the time, Pallas kernels for 15%

profile of v4, /device:TPU:0, one launch (start us, length us, event | category | flops | bytes accessed | tf_op | source)
XLA Modules:
  0.0 102.1 jit_solution(1383792182264783205)
XLA Ops:
  0.7 8.5 %first.1 = (f32[1024,512]{1,0:T(8,128)S(1)}, f32[1024,512]{1,0:T(8,128)S(1)}, f32[1024,512]{1,0:T(8,128)S(1)}, f32[1024,512]{1,0:T(8,128)S(1)}, bf16[1024,512]{1...) custom-call(s32[2]{0:T(128)S(1)} %pad_add_fusion.s, ...), custom_call_target="tpu_custom_call" | custom-call | flops 402653184 | bytes 16777216 | tf_op jit(solution)/shard_map/first/pallas_call | solution.py:42
  9.2 1.3 %copy-done = f32[1024,512]{1,0:T(8,128)} copy-done((f32[1024,512]{1,0:T(8,128)}, f32[1024,512]{1,0:T(8,128)S(1)}, u32[]{:S(2)}) %copy-start) | copy-done | bytes 2097176
  10.5 1.3 %copy-done.2 = f32[1024,512]{1,0:T(8,128)} copy-done((f32[1024,512]{1,0:T(8,128)}, f32[1024,512]{1,0:T(8,128)S(1)}, u32[]{:S(2)}) %copy-start.2) | copy-done | bytes 2097176
  11.9 1.3 %copy-done.4 = f32[1024,512]{1,0:T(8,128)} copy-done((f32[1024,512]{1,0:T(8,128)}, f32[1024,512]{1,0:T(8,128)S(1)}, u32[]{:S(2)}) %copy-start.4) | copy-done | bytes 2097176
  13.2 0.5 collective-permute-start
  13.7 1.0 collective-permute-done
  14.7 2.9 %collective-permute-start.1 = (f32[64,512]{1,0:T(8,128)S(1)}, f32[64,512]{1,0:T(8,128)S(1)}, u32[]{:S(2)}, u32[]{:S(2)}) collective-permute-start(f32[64,512]{1,0:T(8,128)S(1)} %slice_add_fusion.3), channel_id=1, source_target_pairs={{0,16},{8,24},{16,0},{24,8},{1,17},{9,25},{17,1},{25,9},{2,18},{10... | collective-permute-start | bytes 393224 | tf_op jit(solution)/shard_map/ppermute | solution.py:174
  17.7 3.8 %collective-permute-done.1 = f32[64,512]{1,0:T(8,128)S(1)} collective-permute-done((f32[64,512]{1,0:T(8,128)S(1)}, f32[64,512]{1,0:T(8,128)S(1)}, u32[]{:S(2)}, u32[]{:S(2)}) %collective-permute-start.1) | collective-permute-done | bytes 131104 | tf_op jit(solution)/shard_map/ppermute | solution.py:174
  21.6 1.3 %collective-permute-done.2 = f32[64,512]{1,0:T(8,128)S(1)} collective-permute-done((f32[64,512]{1,0:T(8,128)S(1)}, f32[64,512]{1,0:T(8,128)S(1)}, u32[]{:S(2)}, u32[]{:S(2)}) %collective-permute-start.2) | collective-permute-done | bytes 131104 | tf_op jit(solution)/shard_map/ppermute | solution.py:111
  22.9 0.7 multiply.5
  23.7 1.7 %collective-permute-start.3 = (f32[288,128]{1,0:T(8,128)S(1)}, f32[288,128]{1,0:T(8,128)}, u32[]{:S(2)}, u32[]{:S(2)}) collective-permute-start(f32[288,128]{1,0:T(8,128)S(1)} %multiply.5), channel_id=1, source_target_pairs={{0,1},{1,0},{2,3},{3,2},{4,5},{5,4},{6,7},{7,6},{8,9},{9,8},{10,11... | collective-permute-start | bytes 442376 | tf_op jit(solution)/shard_map/ppermute | solution.py:111
  25.4 1.2 %copy-done.7 = bf16[1024,512]{1,0:T(8,128)(2,1)S(1)} copy-done((bf16[1024,512]{1,0:T(8,128)(2,1)S(1)}, bf16[1024,512]{1,0:T(8,128)(2,1)}, u32[]{:S(2)}) %copy-start.7) | copy-done | bytes 1048600
  27.1 2.6 %collective-permute-done.3 = f32[288,128]{1,0:T(8,128)} collective-permute-done((f32[288,128]{1,0:T(8,128)S(1)}, f32[288,128]{1,0:T(8,128)}, u32[]{:S(2)}, u32[]{:S(2)}) %collective-permute-start.3) | collective-permute-done | bytes 147488 | tf_op jit(solution)/shard_map/ppermute | solution.py:111
  29.7 0.9 slice_add_fusion.1
  30.6 0.7 slice_add_fusion.11
  31.4 1.9 %collective-permute-start.4 = (f32[160,128]{1,0:T(8,128)S(1)}, f32[160,128]{1,0:T(8,128)S(1)}, u32[]{:S(2)}, u32[]{:S(2)}) collective-permute-start(f32[160,128]{1,0:T(8,128)S(1)} %pad_maximum_fusion.4), channel_id=1, source_target_pairs={{0,2},{1,3},{2,0},{3,1},{4,6},{5,7},{6,4},{7,5},{8,10},{9,11},{10,... | collective-permute-start | bytes 245768 | tf_op jit(solution)/shard_map/ppermute | solution.py:111
  33.2 2.6 %collective-permute-done.4 = f32[160,128]{1,0:T(8,128)S(1)} collective-permute-done((f32[160,128]{1,0:T(8,128)S(1)}, f32[160,128]{1,0:T(8,128)S(1)}, u32[]{:S(2)}, u32[]{:S(2)}) %collective-permute-start.4) | collective-permute-done | bytes 81952 | tf_op jit(solution)/shard_map/ppermute | solution.py:111
  35.9 2.9 %collective-permute-start.5 = (f32[160,128]{1,0:T(8,128)S(1)}, f32[160,128]{1,0:T(8,128)S(1)}, u32[]{:S(2)}, u32[]{:S(2)}) collective-permute-start(f32[160,128]{1,0:T(8,128)S(1)} %pad_maximum_fusion.5), channel_id=1, source_target_pairs={{0,4},{1,5},{2,6},{3,7},{4,0},{5,1},{6,2},{7,3},{8,12},{9,13},{10,... | collective-permute-start | bytes 245768 | tf_op jit(solution)/shard_map/ppermute | solution.py:111
  38.8 2.5 %collective-permute-done.5 = f32[160,128]{1,0:T(8,128)S(1)} collective-permute-done((f32[160,128]{1,0:T(8,128)S(1)}, f32[160,128]{1,0:T(8,128)S(1)}, u32[]{:S(2)}, u32[]{:S(2)}) %collective-permute-start.5) | collective-permute-done | bytes 81952 | tf_op jit(solution)/shard_map/ppermute | solution.py:111
  41.3 1.9 %collective-permute-start.6 = (f32[128,128]{1,0:T(8,128)S(1)}, f32[128,128]{1,0:T(8,128)S(1)}, u32[]{:S(2)}, u32[]{:S(2)}) collective-permute-start(f32[128,128]{1,0:T(8,128)S(1)} %slice_add_fusion.6), channel_id=1, source_target_pairs={{0,2},{1,3},{2,0},{3,1},{4,6},{5,7},{6,4},{7,5},{8,10},{9,11},{10,... | collective-permute-start | bytes 196616 | tf_op jit(solution)/shard_map/ppermute | solution.py:111
  43.2 2.8 %eliminate.2.inverse = f32[64,64]{1,0:T(8,128)S(1)} custom-call(f32[32,128]{1,0:T(8,128)S(1)} %slice_add_fusion.10.one, f32[32,128]{1,0:T(8,128)S(1)} %slice.62.two), custom_call_target="tpu_custom_call" | custom-call | flops 100000000 | bytes 8388608 | tf_op jit(solution)/shard_map/eliminate/pallas_call | solution.py:42
  46.0 1.6 %collective-permute-start.7 = (f32[256,128]{1,0:T(8,128)S(1)}, f32[256,128]{1,0:T(8,128)S(1)}, u32[]{:S(2)}, u32[]{:S(2)}) collective-permute-start(f32[256,128]{1,0:T(8,128)S(1)} %pad_maximum_fusion.2.stacked), channel_id=1, source_target_pairs={{0,1},{1,0},{2,3},{3,2},{4,5},{5,4},{6,7},{7,6},{8,9},{9,8},{10,11... | collective-permute-start | bytes 393224 | tf_op jit(solution)/shard_map/ppermute | solution.py:111
  47.6 1.6 %copy-done.3 = f32[1024,512]{1,0:T(8,128)S(1)} copy-done((f32[1024,512]{1,0:T(8,128)S(1)}, f32[1024,512]{1,0:T(8,128)}, u32[]{:S(2)}) %copy-start.3) | copy-done | bytes 2097176
  49.2 1.6 %copy-done.5 = f32[1024,512]{1,0:T(8,128)S(1)} copy-done((f32[1024,512]{1,0:T(8,128)S(1)}, f32[1024,512]{1,0:T(8,128)}, u32[]{:S(2)}) %copy-start.5) | copy-done | bytes 2097176
  50.8 2.0 %middle.2 = (f32[1024,512]{1,0:T(8,128)S(1)}, bf16[1024,512]{1,0:T(8,128)(2,1)S(1)}, bf16[1024,512]{1,0:T(8,128)(2,1)S(1)}, f32[64,1024]{1,0:T(8,128)S(1)}) custom-call(f32[64,64]{1,0:T(8,128)S(1)} %eliminate.2.inverse, f32[64,1024]{1,0:T(8,128)S(1)} %pad_maximum_fusion.panel, f32[256,128]{1,0:T(8,128)S(1)} %pad_maximum_fusion.2.stacked, ...), custom_call_target="tpu_custom_call" | custom-call | flops 603979776 | bytes 4194304 | tf_op jit(solution)/shard_map/middle/pallas_call | solution.py:42
  52.8 2.0 %middle.3 = (f32[1024,512]{1,0:T(8,128)S(1)}, bf16[1024,512]{1,0:T(8,128)(2,1)S(1)}, bf16[1024,512]{1,0:T(8,128)(2,1)S(1)}, f32[64,1024]{1,0:T(8,128)S(1)}) custom-call(f32[64,64]{1,0:T(8,128)S(1)} %eliminate.2.inverse, f32[64,1024]{1,0:T(8,128)S(1)} %pad_maximum_fusion.panel, f32[256,128]{1,0:T(8,128)S(1)} %collective-permute-done.7.stacked, ...), custom_call_target="tpu_custom_call" | custom-call | flops 603979776 | bytes 4194304 | tf_op jit(solution)/shard_map/middle/pallas_call | solution.py:42
  54.9 1.3 %collective-permute-done.8 = f32[64,512]{1,0:T(8,128)S(1)} collective-permute-done((f32[64,512]{1,0:T(8,128)S(1)}, f32[64,512]{1,0:T(8,128)S(1)}, u32[]{:S(2)}, u32[]{:S(2)}) %collective-permute-start.8) | collective-permute-done | bytes 131104 | tf_op jit(solution)/shard_map/ppermute | solution.py:111
  56.3 1.6 %collective-permute-start.9 = (f32[64,512]{1,0:T(8,128)S(1)}, f32[64,512]{1,0:T(8,128)S(1)}, u32[]{:S(2)}, u32[]{:S(2)}) collective-permute-start(f32[64,512]{1,0:T(8,128)S(1)} %slice_add_fusion.2), channel_id=1, source_target_pairs={{0,16},{8,24},{16,0},{24,8},{1,17},{9,25},{17,1},{25,9},{2,18},{10... | collective-permute-start | bytes 393224 | tf_op jit(solution)/shard_map/ppermute | solution.py:174
  57.9 4.0 %collective-permute-done.9 = f32[64,512]{1,0:T(8,128)S(1)} collective-permute-done((f32[64,512]{1,0:T(8,128)S(1)}, f32[64,512]{1,0:T(8,128)S(1)}, u32[]{:S(2)}, u32[]{:S(2)}) %collective-permute-start.9) | collective-permute-done | bytes 131104 | tf_op jit(solution)/shard_map/ppermute | solution.py:174
  62.0 1.3 %collective-permute-done.10 = f32[64,512]{1,0:T(8,128)S(1)} collective-permute-done((f32[64,512]{1,0:T(8,128)S(1)}, f32[64,512]{1,0:T(8,128)S(1)}, u32[]{:S(2)}, u32[]{:S(2)}) %collective-permute-start.10) | collective-permute-done | bytes 131104 | tf_op jit(solution)/shard_map/ppermute | solution.py:111
  63.4 0.7 multiply.7
  64.1 0.5 collective-permute-start.11
  64.6 0.4 multiply.6
  65.1 4.9 %collective-permute-done.11 = f32[288,128]{1,0:T(8,128)S(1)} collective-permute-done((f32[288,128]{1,0:T(8,128)S(1)}, f32[288,128]{1,0:T(8,128)S(1)}, u32[]{:S(2)}, u32[]{:S(2)}) %collective-permute-start.11) | collective-permute-done | bytes 147488 | tf_op jit(solution)/shard_map/ppermute | solution.py:111
  70.1 1.5 %collective-permute-start.12 = (f32[160,128]{1,0:T(8,128)S(1)}, f32[160,128]{1,0:T(8,128)S(1)}, u32[]{:S(2)}, u32[]{:S(2)}) collective-permute-start(f32[160,128]{1,0:T(8,128)S(1)} %pad_maximum_fusion.6), channel_id=1, source_target_pairs={{0,2},{1,3},{2,0},{3,1},{4,6},{5,7},{6,4},{7,5},{8,10},{9,11},{10,... | collective-permute-start | bytes 245768 | tf_op jit(solution)/shard_map/ppermute | solution.py:111
  71.6 3.0 %collective-permute-done.12 = f32[160,128]{1,0:T(8,128)S(1)} collective-permute-done((f32[160,128]{1,0:T(8,128)S(1)}, f32[160,128]{1,0:T(8,128)S(1)}, u32[]{:S(2)}, u32[]{:S(2)}) %collective-permute-start.12) | collective-permute-done | bytes 81952 | tf_op jit(solution)/shard_map/ppermute | solution.py:111
  74.6 3.4 %collective-permute-start.13 = (f32[160,128]{1,0:T(8,128)S(1)}, f32[160,128]{1,0:T(8,128)S(1)}, u32[]{:S(2)}, u32[]{:S(2)}) collective-permute-start(f32[160,128]{1,0:T(8,128)S(1)} %pad_maximum_fusion.7), channel_id=1, source_target_pairs={{0,4},{1,5},{2,6},{3,7},{4,0},{5,1},{6,2},{7,3},{8,12},{9,13},{10,... | collective-permute-start | bytes 245768 | tf_op jit(solution)/shard_map/ppermute | solution.py:111
  78.1 2.4 %collective-permute-done.13 = f32[160,128]{1,0:T(8,128)S(1)} collective-permute-done((f32[160,128]{1,0:T(8,128)S(1)}, f32[160,128]{1,0:T(8,128)S(1)}, u32[]{:S(2)}, u32[]{:S(2)}) %collective-permute-start.13) | collective-permute-done | bytes 81952 | tf_op jit(solution)/shard_map/ppermute | solution.py:111
  80.5 1.9 %collective-permute-start.14 = (f32[128,128]{1,0:T(8,128)S(1)}, f32[128,128]{1,0:T(8,128)S(1)}, u32[]{:S(2)}, u32[]{:S(2)}) collective-permute-start(f32[128,128]{1,0:T(8,128)S(1)} %slice_add_fusion.4), channel_id=1, source_target_pairs={{0,2},{1,3},{2,0},{3,1},{4,6},{5,7},{6,4},{7,5},{8,10},{9,11},{10,... | collective-permute-start | bytes 196616 | tf_op jit(solution)/shard_map/ppermute | solution.py:111
  82.4 2.8 %eliminate.3.inverse = f32[64,64]{1,0:T(8,128)S(1)} custom-call(f32[32,128]{1,0:T(8,128)S(1)} %slice_add_fusion.8.one, f32[32,128]{1,0:T(8,128)S(1)} %slice.69.two), custom_call_target="tpu_custom_call" | custom-call | flops 100000000 | bytes 8388608 | tf_op jit(solution)/shard_map/eliminate/pallas_call | solution.py:42
  85.3 0.6 collective-permute-start.15
  85.9 3.3 %final.2 = (f32[1024,1024]{1,0:T(8,128)}, f32[1024,1024]{1,0:T(8,128)}, f32[64,1024]{1,0:T(8,128)}) custom-call(s32[2]{0:T(128)S(1)} %copy-done.9, f32[64,64]{1,0:T(8,128)S(1)} %eliminate.3.inverse, f32[64,1024]{1,0:T(8,128)S(1)} %pad_maximum_fusion.1.panel, f32[256,128]{1,0:T(8,128)S(1)} %pad_maximum_fusion.3.stacked.own, ...), custom_call_target="tpu_custom_call" | custom-call | flops 201326592 | bytes 4194304 | tf_op jit(solution)/shard_map/final/pallas_call | solution.py:42
  89.2 1.1 %collective-permute-done.15.stacked.other = f32[256,128]{1,0:T(8,128)S(1)} collective-permute-done((f32[256,128]{1,0:T(8,128)S(1)}, f32[256,128]{1,0:T(8,128)S(1)}, u32[]{:S(2)}, u32[]{:S(2)}) %collective-permute-start.15) | collective-permute-done | bytes 131104 | tf_op jit(solution)/shard_map/ppermute | solution.py:111
  90.3 1.2 %widen.1 = (f32[64,1024]{1,0:T(8,128)S(1)}, f32[32,128]{1,0:T(8,128)S(1)}) custom-call(f32[64,64]{1,0:T(8,128)S(1)} %eliminate.3.inverse, f32[256,128]{1,0:T(8,128)S(1)} %pad_maximum_fusion.3.stacked.own, f32[256,128]{1,0:T(8,128)S(1)} %collective-permute-done.15.stacked.other), custom_call_target="tpu_custom_call" | custom-call | flops 100000000 | bytes 1048576 | tf_op jit(solution)/shard_map/widen/pallas_call | solution.py:42
  91.5 1.2 %collective-permute-done.16 = f32[32,128]{1,0:T(8,128)S(1)} collective-permute-done((f32[32,128]{1,0:T(8,128)S(1)}, f32[32,128]{1,0:T(8,128)S(1)}, u32[]{:S(2)}, u32[]{:S(2)}) %collective-permute-start.16) | collective-permute-done | bytes 16416 | tf_op jit(solution)/shard_map/ppermute | solution.py:111
  92.7 1.5 %collective-permute-start.17 = (f32[32,128]{1,0:T(8,128)S(1)}, f32[32,128]{1,0:T(8,128)S(1)}, u32[]{:S(2)}, u32[]{:S(2)}) collective-permute-start(f32[32,128]{1,0:T(8,128)S(1)} %add.69.one), channel_id=1, source_target_pairs={{0,16},{8,24},{16,0},{24,8},{1,17},{9,25},{17,1},{25,9},{2,18},{10... | collective-permute-start | bytes 49160 | tf_op jit(solution)/shard_map/ppermute | solution.py:111
  94.2 3.3 %final.3 = (f32[1024,1024]{1,0:T(8,128)}, f32[1024,1024]{1,0:T(8,128)}) custom-call(s32[2]{0:T(128)S(1)} %copy-done.9, f32[64,64]{1,0:T(8,128)S(1)} %eliminate.3.inverse, f32[64,1024]{1,0:T(8,128)S(1)} %pad_maximum_fusion.1.panel, f32[256,128]{1,0:T(8,128)S(1)} %collective-permute-done.15.stacked.other, ...), custom_call_target="tpu_custom_call", output_to_operand_aliasing={{0}: (5, {}), {1}: (6, {})} | custom-call | flops 201326592 | bytes 4194304 | tf_op jit(solution)/shard_map/final/pallas_call | solution.py:42
  97.5 4.4 %finish.1 = f32[64,1024]{1,0:T(8,128)} custom-call(s32[2]{0:T(128)S(1)} %copy-done.9, f32[32,128]{1,0:T(8,128)S(1)} %add.69.one, f32[32,128]{1,0:T(8,128)S(1)} %collective-permute-done.17.two, f32[64,1024]{1,0:T(8,128)S(1)} %get-tuple-element.67.wide), custom_call_target="tpu_custom_call" | custom-call | flops 100000000 | bytes 8388608 | tf_op jit(solution)/shard_map/finish/pallas_call | solution.py:42
  (53 shorter events, 1.1 us)
Async XLA Ops:
  0.7 8.5 %copy-start.8 = (s32[2]{0:T(128)}, s32[2]{0:T(128)S(1)}, u32[]{:S(2)}) copy-start(s32[2]{0:T(128)S(1)} %pad_add_fusion.s) | copy-start | bytes 28
  9.2 1.3 %copy-start = (f32[1024,512]{1,0:T(8,128)}, f32[1024,512]{1,0:T(8,128)S(1)}, u32[]{:S(2)}) copy-start(f32[1024,512]{1,0:T(8,128)S(1)} %get-tuple-element.44.d) | copy-start | bytes 6291460
  10.5 1.3 %copy-start.2 = (f32[1024,512]{1,0:T(8,128)}, f32[1024,512]{1,0:T(8,128)S(1)}, u32[]{:S(2)}) copy-start(f32[1024,512]{1,0:T(8,128)S(1)} %get-tuple-element.45.o) | copy-start | bytes 6291460
  11.9 1.3 %copy-start.4 = (f32[1024,512]{1,0:T(8,128)}, f32[1024,512]{1,0:T(8,128)S(1)}, u32[]{:S(2)}) copy-start(f32[1024,512]{1,0:T(8,128)S(1)} %get-tuple-element.46.d) | copy-start | bytes 6291460
  13.2 8.4 %copy-start.6 = (bf16[1024,512]{1,0:T(8,128)(2,1)}, bf16[1024,512]{1,0:T(8,128)(2,1)S(1)}, u32[]{:S(2)}) copy-start(bf16[1024,512]{1,0:T(8,128)(2,1)S(1)} %get-tuple-element.38.low) | copy-start | bytes 3145732
  13.2 1.5 %collective-permute-start = (f32[64,512]{1,0:T(8,128)S(1)}, f32[64,512]{1,0:T(8,128)S(1)}, u32[]{:S(2)}, u32[]{:S(2)}) collective-permute-start(f32[64,512]{1,0:T(8,128)S(1)} %split.13), channel_id=1, source_target_pairs={{0,8},{8,0},{16,24},{24,16},{1,9},{9,1},{17,25},{25,17},{2,10},{10... | collective-permute-start | bytes 393224 | tf_op jit(solution)/shard_map/ppermute | solution.py:111
  14.7 6.8 %collective-permute-start.1 = (f32[64,512]{1,0:T(8,128)S(1)}, f32[64,512]{1,0:T(8,128)S(1)}, u32[]{:S(2)}, u32[]{:S(2)}) collective-permute-start(f32[64,512]{1,0:T(8,128)S(1)} %slice_add_fusion.3), channel_id=1, source_target_pairs={{0,16},{8,24},{16,0},{24,8},{1,17},{9,25},{17,1},{25,9},{2,18},{10... | collective-permute-start | bytes 393224 | tf_op jit(solution)/shard_map/ppermute | solution.py:174
  21.5 1.4 %collective-permute-start.2 = (f32[64,512]{1,0:T(8,128)S(1)}, f32[64,512]{1,0:T(8,128)S(1)}, u32[]{:S(2)}, u32[]{:S(2)}) collective-permute-start(f32[64,512]{1,0:T(8,128)S(1)} %add.54), channel_id=1, source_target_pairs={{0,8},{8,0},{16,24},{24,16},{1,9},{9,1},{17,25},{25,17},{2,10},{10... | collective-permute-start | bytes 393224 | tf_op jit(solution)/shard_map/ppermute | solution.py:111
  23.7 6.0 %collective-permute-start.3 = (f32[288,128]{1,0:T(8,128)S(1)}, f32[288,128]{1,0:T(8,128)}, u32[]{:S(2)}, u32[]{:S(2)}) collective-permute-start(f32[288,128]{1,0:T(8,128)S(1)} %multiply.5), channel_id=1, source_target_pairs={{0,1},{1,0},{2,3},{3,2},{4,5},{5,4},{6,7},{7,6},{8,9},{9,8},{10,11... | collective-permute-start | bytes 442376 | tf_op jit(solution)/shard_map/ppermute | solution.py:111
  25.4 1.2 %copy-start.7 = (bf16[1024,512]{1,0:T(8,128)(2,1)S(1)}, bf16[1024,512]{1,0:T(8,128)(2,1)}, u32[]{:S(2)}) copy-start(bf16[1024,512]{1,0:T(8,128)(2,1)} %copy-done.6) | copy-start | bytes 3145732
  31.4 4.5 %collective-permute-start.4 = (f32[160,128]{1,0:T(8,128)S(1)}, f32[160,128]{1,0:T(8,128)S(1)}, u32[]{:S(2)}, u32[]{:S(2)}) collective-permute-start(f32[160,128]{1,0:T(8,128)S(1)} %pad_maximum_fusion.4), channel_id=1, source_target_pairs={{0,2},{1,3},{2,0},{3,1},{4,6},{5,7},{6,4},{7,5},{8,10},{9,11},{10,... | collective-permute-start | bytes 245768 | tf_op jit(solution)/shard_map/ppermute | solution.py:111
  35.9 5.4 %collective-permute-start.5 = (f32[160,128]{1,0:T(8,128)S(1)}, f32[160,128]{1,0:T(8,128)S(1)}, u32[]{:S(2)}, u32[]{:S(2)}) collective-permute-start(f32[160,128]{1,0:T(8,128)S(1)} %pad_maximum_fusion.5), channel_id=1, source_target_pairs={{0,4},{1,5},{2,6},{3,7},{4,0},{5,1},{6,2},{7,3},{8,12},{9,13},{10,... | collective-permute-start | bytes 245768 | tf_op jit(solution)/shard_map/ppermute | solution.py:111
  41.3 4.7 %collective-permute-start.6 = (f32[128,128]{1,0:T(8,128)S(1)}, f32[128,128]{1,0:T(8,128)S(1)}, u32[]{:S(2)}, u32[]{:S(2)}) collective-permute-start(f32[128,128]{1,0:T(8,128)S(1)} %slice_add_fusion.6), channel_id=1, source_target_pairs={{0,2},{1,3},{2,0},{3,1},{4,6},{5,7},{6,4},{7,5},{8,10},{9,11},{10,... | collective-permute-start | bytes 196616 | tf_op jit(solution)/shard_map/ppermute | solution.py:111
  43.2 9.6 %copy-start.1 = (f32[1024,512]{1,0:T(8,128)S(1)}, f32[1024,512]{1,0:T(8,128)}, u32[]{:S(2)}) copy-start(f32[1024,512]{1,0:T(8,128)} %copy-done) | copy-start | bytes 6291460
  46.0 6.8 %collective-permute-start.7 = (f32[256,128]{1,0:T(8,128)S(1)}, f32[256,128]{1,0:T(8,128)S(1)}, u32[]{:S(2)}, u32[]{:S(2)}) collective-permute-start(f32[256,128]{1,0:T(8,128)S(1)} %pad_maximum_fusion.2.stacked), channel_id=1, source_target_pairs={{0,1},{1,0},{2,3},{3,2},{4,5},{5,4},{6,7},{7,6},{8,9},{9,8},{10,11... | collective-permute-start | bytes 393224 | tf_op jit(solution)/shard_map/ppermute | solution.py:111
  47.6 1.6 %copy-start.3 = (f32[1024,512]{1,0:T(8,128)S(1)}, f32[1024,512]{1,0:T(8,128)}, u32[]{:S(2)}) copy-start(f32[1024,512]{1,0:T(8,128)} %copy-done.2) | copy-start | bytes 6291460
  49.2 1.6 %copy-start.5 = (f32[1024,512]{1,0:T(8,128)S(1)}, f32[1024,512]{1,0:T(8,128)}, u32[]{:S(2)}) copy-start(f32[1024,512]{1,0:T(8,128)} %copy-done.4) | copy-start | bytes 6291460
  54.8 1.4 %collective-permute-start.8 = (f32[64,512]{1,0:T(8,128)S(1)}, f32[64,512]{1,0:T(8,128)S(1)}, u32[]{:S(2)}, u32[]{:S(2)}) collective-permute-start(f32[64,512]{1,0:T(8,128)S(1)} %split.15), channel_id=1, source_target_pairs={{0,8},{8,0},{16,24},{24,16},{1,9},{9,1},{17,25},{25,17},{2,10},{10... | collective-permute-start | bytes 393224 | tf_op jit(solution)/shard_map/ppermute | solution.py:111
  56.3 29.6 %copy-start.9 = (s32[2]{0:T(128)S(1)}, s32[2]{0:T(128)}, u32[]{:S(2)}) copy-start(s32[2]{0:T(128)} %copy-done.8) | copy-start | bytes 28
  56.3 5.6 %collective-permute-start.9 = (f32[64,512]{1,0:T(8,128)S(1)}, f32[64,512]{1,0:T(8,128)S(1)}, u32[]{:S(2)}, u32[]{:S(2)}) collective-permute-start(f32[64,512]{1,0:T(8,128)S(1)} %slice_add_fusion.2), channel_id=1, source_target_pairs={{0,16},{8,24},{16,0},{24,8},{1,17},{9,25},{17,1},{25,9},{2,18},{10... | collective-permute-start | bytes 393224 | tf_op jit(solution)/shard_map/ppermute | solution.py:174
  61.9 1.4 %collective-permute-start.10 = (f32[64,512]{1,0:T(8,128)S(1)}, f32[64,512]{1,0:T(8,128)S(1)}, u32[]{:S(2)}, u32[]{:S(2)}) collective-permute-start(f32[64,512]{1,0:T(8,128)S(1)} %add.63), channel_id=1, source_target_pairs={{0,8},{8,0},{16,24},{24,16},{1,9},{9,1},{17,25},{25,17},{2,10},{10... | collective-permute-start | bytes 393224 | tf_op jit(solution)/shard_map/ppermute | solution.py:111
  64.1 5.9 %collective-permute-start.11 = (f32[288,128]{1,0:T(8,128)S(1)}, f32[288,128]{1,0:T(8,128)S(1)}, u32[]{:S(2)}, u32[]{:S(2)}) collective-permute-start(f32[288,128]{1,0:T(8,128)S(1)} %multiply.7), channel_id=1, source_target_pairs={{0,1},{1,0},{2,3},{3,2},{4,5},{5,4},{6,7},{7,6},{8,9},{9,8},{10,11... | collective-permute-start | bytes 442376 | tf_op jit(solution)/shard_map/ppermute | solution.py:111
  70.1 4.5 %collective-permute-start.12 = (f32[160,128]{1,0:T(8,128)S(1)}, f32[160,128]{1,0:T(8,128)S(1)}, u32[]{:S(2)}, u32[]{:S(2)}) collective-permute-start(f32[160,128]{1,0:T(8,128)S(1)} %pad_maximum_fusion.6), channel_id=1, source_target_pairs={{0,2},{1,3},{2,0},{3,1},{4,6},{5,7},{6,4},{7,5},{8,10},{9,11},{10,... | collective-permute-start | bytes 245768 | tf_op jit(solution)/shard_map/ppermute | solution.py:111
  74.6 5.9 %collective-permute-start.13 = (f32[160,128]{1,0:T(8,128)S(1)}, f32[160,128]{1,0:T(8,128)S(1)}, u32[]{:S(2)}, u32[]{:S(2)}) collective-permute-start(f32[160,128]{1,0:T(8,128)S(1)} %pad_maximum_fusion.7), channel_id=1, source_target_pairs={{0,4},{1,5},{2,6},{3,7},{4,0},{5,1},{6,2},{7,3},{8,12},{9,13},{10,... | collective-permute-start | bytes 245768 | tf_op jit(solution)/shard_map/ppermute | solution.py:111
  80.5 4.7 %collective-permute-start.14 = (f32[128,128]{1,0:T(8,128)S(1)}, f32[128,128]{1,0:T(8,128)S(1)}, u32[]{:S(2)}, u32[]{:S(2)}) collective-permute-start(f32[128,128]{1,0:T(8,128)S(1)} %slice_add_fusion.4), channel_id=1, source_target_pairs={{0,2},{1,3},{2,0},{3,1},{4,6},{5,7},{6,4},{7,5},{8,10},{9,11},{10,... | collective-permute-start | bytes 196616 | tf_op jit(solution)/shard_map/ppermute | solution.py:111
  85.3 5.0 %collective-permute-start.15 = (f32[256,128]{1,0:T(8,128)S(1)}, f32[256,128]{1,0:T(8,128)S(1)}, u32[]{:S(2)}, u32[]{:S(2)}) collective-permute-start(f32[256,128]{1,0:T(8,128)S(1)} %pad_maximum_fusion.3.stacked.own), channel_id=1, source_target_pairs={{0,1},{1,0},{2,3},{3,2},{4,5},{5,4},{6,7},{7,6},{8,9},{9,8},{10,11... | collective-permute-start | bytes 393224 | tf_op jit(solution)/shard_map/ppermute | solution.py:111
  91.5 1.2 %collective-permute-start.16 = (f32[32,128]{1,0:T(8,128)S(1)}, f32[32,128]{1,0:T(8,128)S(1)}, u32[]{:S(2)}, u32[]{:S(2)}) collective-permute-start(f32[32,128]{1,0:T(8,128)S(1)} %get-tuple-element.66), channel_id=1, source_target_pairs={{0,8},{8,0},{16,24},{24,16},{1,9},{9,1},{17,25},{25,17},{2,10},{10... | collective-permute-start | bytes 49160 | tf_op jit(solution)/shard_map/ppermute | solution.py:111
  92.7 4.9 %collective-permute-start.17 = (f32[32,128]{1,0:T(8,128)S(1)}, f32[32,128]{1,0:T(8,128)S(1)}, u32[]{:S(2)}, u32[]{:S(2)}) collective-permute-start(f32[32,128]{1,0:T(8,128)S(1)} %add.69.one), channel_id=1, source_target_pairs={{0,16},{8,24},{16,0},{24,8},{1,17},{9,25},{17,1},{25,9},{2,18},{10... | collective-permute-start | bytes 49160 | tf_op jit(solution)/shard_map/ppermute | solution.py:111

commit v5 on v4

v5 whole, which is shorter than its diff:
```python
import jax
import jax.numpy as jnp
from jax import lax
from jax.experimental import pallas as pl
from jax.experimental.pallas import tpu as pltpu
from jax.sharding import PartitionSpec as P

ITERS = 2


MU = 1.25
TAU = 0.6 / 1.25
HIGH = lax.Precision.HIGHEST
CORES = 2
LANES = 128
F32, BF16 = jnp.float32, jnp.bfloat16
MIB = 1 << 20


def split(value):
    high = value.astype(BF16)
    return high, (value - high.astype(F32)).astype(BF16)


def dot(a, b, dims, precision=None):
    return lax.dot_general(a, b, (dims, ((), ())), precision=precision, preferred_element_type=F32)


def dot_nt(a, b):
    rows = a[0].shape[0]
    both = dot(jnp.concatenate(a, axis=0), b[0], ((1,), (1,)))
    return both[:rows] + both[rows:] + dot(a[0], b[1], ((1,), (1,)))


def dot_nn(a, b):
    rows = a[0].shape[0]
    both = dot(jnp.concatenate(a, axis=0), b[0], ((1,), (0,)))
    return both[:rows] + both[rows:] + dot(a[0], b[1], ((1,), (0,)))


def call(body, name, ins, outs, scratch=(), aliases=None, cost=(0, 0), limit=16):
    return pl.pallas_call(
        body,
        name=name,
        in_specs=[pl.BlockSpec(memory_space=space) for _, space in ins],
        out_specs=[pl.BlockSpec(memory_space=space) for _, _, space in outs],
        out_shape=[jax.ShapeDtypeStruct(shape, dtype) for shape, dtype, _ in outs],
        scratch_shapes=list(scratch),
        input_output_aliases=aliases or {},
        compiler_params=pltpu.CompilerParams(vmem_limit_bytes=limit * MIB),
        cost_estimate=pl.CostEstimate(flops=cost[0], bytes_accessed=cost[1], transcendentals=0),
    )(*[pltpu.with_memory_space_constraint(a, pltpu.HBM) if m is pltpu.HBM else a for a, m in ins])


def invert(packed, out):
    gram_rows, rank = packed.shape[0], out.shape[0]
    full = (8, LANES)
    lane = lax.broadcasted_iota(jnp.int32, full, 1)
    sub = lax.broadcasted_iota(jnp.int32, full, 0)
    turned = pltpu.roll(packed, LANES // 2, 1)
    rows = []
    for j in range(rank // 8):
        source = packed if 8 * j < gram_rows else turned
        at = 8 * j % gram_rows
        eye = jnp.where(lane - rank == sub + 8 * j, 1.0, 0.0)
        rows.append(jnp.where(lane < rank, source[at : at + 8], eye))
    wide = 4
    for k in range(0, rank, wide):
        r, at = divmod(k, 8)
        after = range(r if at + wide < 8 else r + 1, rank // 8)
        lines = [jnp.broadcast_to(rows[r][at + p : at + p + 1, :], full) for p in range(wide)]
        core = {
            (p, q): jnp.broadcast_to(lines[p][:, k + q : k + q + 1], full)
            for p in range(wide)
            for q in range(p, wide)
        }
        columns = {
            (j, p): jnp.broadcast_to(rows[j][:, k + p : k + p + 1], full) for j in after for p in range(wide)
        }
        for p in range(wide):
            inverse = 1.0 / core[p, p]
            factors = [core[p, q] * inverse for q in range(p + 1, wide)]
            for q, factor in zip(range(p + 1, wide), factors):
                for t in range(q, wide):
                    core[q, t] = core[q, t] - factor * core[p, t]
            scaled = lines[p] * inverse
            for q in range(p + 1, wide):
                lines[q] = lines[q] - core[p, q] * scaled
            for j in after:
                column = columns[j, p]
                if j == r:
                    column = jnp.where(sub >= at + wide, column, 0.0)
                rows[j] = rows[j] - column * scaled
                for q, factor in zip(range(p + 1, wide), factors):
                    columns[j, q] = columns[j, q] - factor * columns[j, p]
            done = lines[p] * lax.rsqrt(core[p, p])
            out[k + p : k + p + 1, :] = done[0:1, rank:]


def pack(gram):
    rows = gram.shape[0] // 2
    return jnp.concatenate([gram[:rows], gram[rows:]], axis=1)


def unstack(ref):
    blocks = ref.shape[0] // 64
    return jnp.concatenate([ref[64 * t : 64 * (t + 1), :] for t in range(blocks)], axis=1)


def solution(mesh):
    n_gal, n_pix = mesh.shape["gal"], mesh.shape["pix"]
    levels = n_pix.bit_length() - 1

    def swap(value, axis, bit):
        n = mesh.shape[axis]
        return lax.ppermute(value, axis, [(i, i ^ bit) for i in range(n)])

    def per_device(observed, sparse_init, dual_init, right_init):
        rank = right_init.shape[0]
        n_rows, n_cols = observed.shape
        half = n_cols // 2
        tall = min(256, n_rows // 2)
        steps = n_rows // tall
        core = lax.rem(lax.axis_index("gal"), CORES)
        bits = [lax.rem(lax.axis_index("pix") >> level, 2) for level in range(levels)]
        scalars = jnp.stack([core] + bits).astype(jnp.int32)
        stack_rows = rank * (half // LANES)
        gram_rows = rank * rank // LANES
        where = (scalars, pltpu.SMEM)

        def gal_at(i, s):
            turn = (1 - s[0]) * (steps // 2)
            return pl.multiple_of(lax.rem(i + turn, steps) * tall, tall)

        def pix_at(p, s):
            return pl.multiple_of(lax.rem(s[1] + p, 2) * half, half)

        def chunk(i):
            return slice(tall * i, tall * (i + 1))

        def join(pair):
            return jnp.concatenate([half[...] for half in pair], axis=1)

        def small(body, name, ins, rows, scratch=()):
            outs = [((n, LANES), F32, pltpu.VMEM) for n in rows]
            return call(body, name, ins, outs, scratch, cost=(10**5, 10**6), limit=4)

        def add(*arrays):
            def body(*refs):
                *ins, out = refs
                total = ins[0][...]
                for ref in ins[1:]:
                    total = total + ref[...]
                out[...] = total

            out = (arrays[0].shape, F32, pltpu.VMEM)
            return call(body, "add", [(a, pltpu.VMEM) for a in arrays], [out], cost=(10**5, 10**6), limit=4)[0]

        def first(right):
            def body(s, o_in, s_in, d_in, r_in, o, d, h0, l0, h1, l1, away, mine, sp, right, r_sem, sems):
                right_move = pltpu.make_async_copy(r_in, right, r_sem)
                right_move.start()
                moves = {}
                for i in range(steps):
                    for a, (source, target) in enumerate(((o_in, o), (s_in, sp), (d_in, d))):
                        block = source.at[pl.ds(gal_at(i, s), tall), :]
                        move = pltpu.make_async_copy(block, target.at[chunk(i), :], sems.at[i, a])
                        move.start(priority=(i + a) % 2)
                        moves[i, a] = move
                right_move.wait()
                rights = [split(right[:, pl.ds(pix_at(p, s), half)]) for p in (0, 1)]
                for i in range(steps):
                    total = None
                    for a in range(3):
                        moves[i, a].wait()
                    for p, (h, l) in enumerate(((h0, l0), (h1, l1))):
                        at = chunk(i), pl.ds(pix_at(p, s), half)
                        pair = split(o[at] - sp[at] + d[at] * (1 / MU))
                        h[chunk(i), :], l[chunk(i), :] = pair
                        term = dot_nt(rights[p], pair)
                        total = term if total is None else total + term
                    out = away if i < steps // 2 else mine
                    out[:, chunk(i % (steps // 2))] = total

            ins = [where] + [(a, pltpu.HBM) for a in (observed, sparse_init, dual_init, right)]
            outs = [((n_rows, n_cols), F32, pltpu.VMEM)] * 2 + [((n_rows, half), BF16, pltpu.VMEM)] * 4
            outs += [((rank, n_rows // 2), F32, pltpu.VMEM)] * 2
            scratch = [pltpu.VMEM((n_rows, n_cols), F32), pltpu.VMEM((rank, n_cols), F32)]
            scratch += [pltpu.SemaphoreType.DMA(()), pltpu.SemaphoreType.DMA((steps, 3))]
            cost = (6 * rank * n_rows * n_cols, 16 * n_rows * n_cols)
            got = call(body, "first", ins, outs, scratch, cost=cost)
            return got[0], got[1], got[2:4], got[4:6], got[6:8]

        def sum_gal(part):
            away, mine = part
            mine = add(mine, swap(away, "gal", 1))
            got = [
                lax.ppermute(mine, "gal", [(i, (i + CORES * k) % n_gal) for i in range(n_gal)])
                for k in range(1, n_gal // CORES)
            ]
            mine = add(mine, *got)
            return swap(mine, "gal", 1), mine

        def multiply(panel, pair, with_gram):
            def body(away, mine, high, low, out):
                panel = join((away, mine))
                total = dot_nn(split(panel), (high[...], low[...]))
                for t in range(half // LANES):
                    out[rank * t : rank * (t + 1), :] = total[:, LANES * t : LANES * (t + 1)]
                if with_gram:
                    gram = dot(panel, panel, ((1,), (1,)), HIGH)
                    out[stack_rows : stack_rows + gram_rows, :] = pack(gram)

            rows = stack_rows + (gram_rows if with_gram else 0)
            ins = [(a, pltpu.VMEM) for a in (*panel, *pair)]
            outs = [((rows, LANES), F32, pltpu.VMEM)]
            cost = (3 * rank * n_rows * n_cols, 2 * n_rows * n_cols)
            return call(body, "multiply", ins, outs, cost=cost)[0]

        def eliminate(one, two):
            def body(one, two, out):
                invert(one[-gram_rows:, :] + two[-gram_rows:, :], out)

            ins = [(one, pltpu.VMEM), (two, pltpu.VMEM)]
            outs = [((rank, rank), F32, pltpu.VMEM)]
            return call(body, "eliminate", ins, outs, cost=(10**8, 8 * MIB), limit=4)[0]

        def fold(level, value, sent, got):
            rows = value.shape[0]
            last = level == levels - 1
            keep = rows if last else rows // 2

            def body(s, value, sent, got, *outs):
                message = outs[-1]
                if last:
                    message[:rows, :] = value[...] + got[:rows, :]
                else:
                    for mine, out in ((s[1 + level], outs[0]), (1 - s[1 + level], message)):
                        at = pl.ds(pl.multiple_of(mine * keep, keep), keep)
                        out[:keep, :] = value[at, :] + got[at, :]
                message[keep:, :] = sent[rows_of(sent), :] + got[rows_of(got), :]

            def rows_of(ref):
                return slice(ref.shape[0] - gram_rows, ref.shape[0])

            ins = [where] + [(a, pltpu.VMEM) for a in (value, sent, got)]
            outs = small(body, "fold", ins, [keep + gram_rows] if last else [keep, keep + gram_rows])
            return outs[0], outs[-1]

        def unfold(level, value, got):
            rows = value.shape[0]

            def body(s, value, got, out):
                for mine, ref in ((s[1 + level], value), (1 - s[1 + level], got)):
                    out[pl.ds(pl.multiple_of(mine * rows, rows), rows), :] = ref[...]

            ins = [where, (value, pltpu.VMEM), (got, pltpu.VMEM)]
            return small(body, "unfold", ins, [2 * rows])[0]

        def top(one, two):
            rows = one.shape[0] - gram_rows

            def body(one, two, out):
                out[...] = one[:rows, :] + two[:rows, :]

            return small(body, "top", [(one, pltpu.VMEM), (two, pltpu.VMEM)], [rows])[0]

        def sum_pix(send, own):
            value, sent = own, send
            for level in range(1, levels):
                value, sent = fold(level, value, sent, swap(sent, "pix", 1 << (level - 1)))
            got = swap(sent, "pix", 1 << (levels - 1))
            value = top(sent, got)
            inverse = eliminate(sent, got)
            for level in range(levels - 2, 0, -1):
                value = unfold(level, value, swap(value, "pix", 1 << level))
            value, inverse = lax.optimization_barrier((value, inverse))
            return inverse, value, swap(value, "pix", 1)

        def halves(inverse, panel, stacked):
            left = dot(inverse[...], join(panel), ((1,), (0,)), HIGH)
            wide = dot(inverse[...], unstack(stacked), ((1,), (0,)), HIGH)
            left_high, left_low = split(left)
            wide_high, wide_low = split(wide)
            tops = jnp.concatenate([left_high, left_low, left_high], axis=0)
            return left, wide, (wide_high, wide_low), tops, jnp.concatenate([wide_high, wide_high, wide_low], axis=0)

        def middle(p, inverse, panel, stacked, o, d, before):
            def body(s, inverse, away, mine, stacked, o, d, *rest):
                base, high, low, *after = rest[2 * p :]
                _, _, right, tops, wides = halves(inverse, (away, mine), stacked)
                for i in range(steps):
                    lowrank = dot(tops[:, chunk(i)], wides, ((0,), (0,)))
                    at = chunk(i), pl.ds(pix_at(p, s), half)
                    seen = o[at]
                    value = seen + d[at] * (1 / MU) - lowrank
                    scaled = jnp.clip(value, -TAU, TAU)
                    base[chunk(i), :] = seen + scaled
                    pair = split(seen + 2.0 * scaled - value)
                    high[chunk(i), :], low[chunk(i), :] = pair
                    term = dot_nt(right, pair)
                    side, block = divmod(i, steps // 2)
                    after[side][:, chunk(block)] = rest[side][:, chunk(block)] + term if p else term

            arrays = [inverse, *panel, stacked, o, d] + (list(before) if p else [])
            outs = [((n_rows, half), F32, pltpu.VMEM)] + [((n_rows, half), BF16, pltpu.VMEM)] * 2
            outs += [((rank, n_rows // 2), F32, pltpu.VMEM)] * 2
            cost = (9 * rank * n_rows * n_cols, 4 * n_rows * n_cols)
            ins = [where] + [(a, pltpu.VMEM) for a in arrays]
            base, high, low, *part = call(body, "middle", ins, outs, cost=cost)
            return base, (high, low), part

        def final(p, inverse, panel, stacked, base, before):
            def body(s, inverse, away, mine, stacked, base, *rest):
                sparse, dual, *outs, sparse_part, dual_part, left_part, sems = rest[2 * p :]
                left, wide, _, tops, wides = halves(inverse, (away, mine), stacked)
                moves = []
                if not p:
                    outs[1][...] = wide
                    outs[2][...] = pack(dot(wide, wide, ((1,), (1,)), HIGH))
                    for i in range(steps):
                        left_part[:, pl.ds(gal_at(i, s), tall)] = left[:, chunk(i)]
                    moves.append(pltpu.make_async_copy(left_part, outs[0], sems.at[steps, 0]))
                    moves[0].start()
                for i in range(steps):
                    value = base[chunk(i), :] - dot(tops[:, chunk(i)], wides, ((0,), (0,)))
                    scaled = jnp.clip(value, -TAU, TAU)
                    sparse_part[chunk(i), :] = value - scaled
                    dual_part[chunk(i), :] = MU * scaled
                    for a, (source, target) in enumerate(((sparse_part, sparse), (dual_part, dual))):
                        block = target.at[pl.ds(gal_at(i, s), tall), pl.ds(pix_at(p, s), half)]
                        move = pltpu.make_async_copy(source.at[chunk(i), :], block, sems.at[i, a])
                        move.start(priority=(i + a) % 2)
                        moves.append(move)
                for move in moves:
                    move.wait()

            ins = [where] + [(a, pltpu.VMEM) for a in (inverse, *panel, stacked, base)]
            outs = [((n_rows, n_cols), F32, pltpu.HBM)] * 2
            aliases = {}
            if p:
                ins += [(a, pltpu.HBM) for a in before[:2]]
                aliases = {6: 0, 7: 1}
            else:
                outs += [((rank, n_rows), F32, pltpu.HBM), ((rank, half), F32, pltpu.VMEM)]
                outs += [((gram_rows, LANES), F32, pltpu.VMEM)]
            scratch = [pltpu.VMEM((n_rows, half), F32)] * 2 + [pltpu.VMEM((rank, n_rows), F32)]
            scratch += [pltpu.SemaphoreType.DMA((steps + 1, 2))]
            cost = (3 * rank * n_rows * n_cols, 4 * n_rows * n_cols)
            return call(body, "final", ins, outs, scratch, aliases, cost)

        def widen(inverse, other, gram):
            def body(inverse, stacked, gram, wide, out):
                wide[...] = dot(inverse[...], unstack(stacked), ((1,), (0,)), HIGH)
                out[...] = gram[...] + pack(dot(wide[...], wide[...], ((1,), (1,)), HIGH))

            ins = [(a, pltpu.VMEM) for a in (inverse, other, gram)]
            outs = [((rank, half), F32, pltpu.VMEM), ((gram_rows, LANES), F32, pltpu.VMEM)]
            return call(body, "widen", ins, outs, cost=(10**8, MIB), limit=8)

        def finish(one, two, wide):
            def body(s, one, two, own, other, out, inverse, right, sem):
                invert(one[...] + two[...], inverse)
                for p, value in enumerate((own, other)):
                    right[:, pl.ds(pix_at(p, s), half)] = dot(inverse[...], value[...], ((1,), (0,)), HIGH)
                move = pltpu.make_async_copy(right, out, sem)
                move.start()
                move.wait()

            ins = [where] + [(a, pltpu.VMEM) for a in (one, two, *wide)]
            outs = [((rank, n_cols), F32, pltpu.HBM)]
            scratch = [pltpu.VMEM((rank, rank), F32), pltpu.VMEM((rank, n_cols), F32), pltpu.SemaphoreType.DMA(())]
            return call(body, "finish", ins, outs, scratch, cost=(10**8, 8 * MIB))[0]

        seen, pulls, own, other, part = first(right_init)
        base = [None, None]
        for step in range(ITERS):
            panel = sum_gal(part)
            send = multiply(panel, other, True)
            inverse, own_wide, other_wide = sum_pix(send, multiply(panel, own, False))
            if step < ITERS - 1:
                base[0], own, part = middle(0, inverse, panel, own_wide, seen, pulls, None)
                base[1], other, part = middle(1, inverse, panel, other_wide, seen, pulls, part)
            else:
                outs = final(0, inverse, panel, own_wide, base[0], None)
                other_wide, outs = lax.optimization_barrier((other_wide, outs))
                wide, gram = widen(inverse, other_wide, outs[4])
                bit = 1
                while 2 * bit < n_gal:
                    gram = add(gram, swap(gram, "gal", bit))
                    bit *= 2
                got = swap(gram, "gal", bit)
                sparse, dual = final(1, inverse, panel, other_wide, base[1], outs)
                left = outs[2]
                right = finish(gram, got, (outs[3], wide))
        return sparse, dual, left, right

    return jax.shard_map(
        per_device,
        mesh=mesh,
        in_specs=(P("pix", "gal"), P("pix", "gal"), P("pix", "gal"), P(None, "gal")),
        out_specs=(P("pix", "gal"), P("pix", "gal"), P(None, "pix"), P(None, "gal")),
        check_vma=False,
    )
```

time: 102 us -> 96.3 us (0.944)
  local copies, waits for them, and re-layouts: 8.45 us -> 0 us
  Pallas kernels: 32.6 us -> 35.2 us
  starting transfers between devices: 24.7 us -> 26.6 us
  other arithmetic: 1.98 us -> 0.08 us
    unnamed x20 -> x0, local copies, waits for them, and re-layouts: 8.4 us -> none
    pallas_call x13 -> x26, Pallas kernels: 32.6 us -> 35.2 us  [call(): pl.pallas_call(body, name=name, in_specs=[pl.BlockSpec(memory_space=space...]
    ppermute x16, starting transfers between devices: 20.2 us -> 22.1 us  [swap(): return lax.ppermute(value, axis, [(i, i ^ bit) for i in range(n)])]
    add x15 -> x0, other arithmetic: 1.79 us -> none  [the longest x4 1.66 us: sum_pix(): value, gram = (own + got[:stack_rows], send[stack_rows:] + got[stack_rows:])]
  transfers between devices with their start and end apart: 18 -> 18, of which waited for: 14 -> 15; matrix products, arithmetic and copies ran while one was open for 0% -> 0% of each run, Pallas kernels for 15% -> 16%
where the time goes in v5:
time: 96.3 us; the launch traced here: 96.2 us
  Pallas kernels  35.2 us (37%)
  waiting for transfers between devices  33.3 us (35%)
  starting transfers between devices  26.6 us (28%)
  between operations  0.97 us (1%)
    pallas_call x26, Pallas kernels, call(): pl.pallas_call(body, name=name, in_specs=[pl.BlockSpec(memory_space=space...  35.2 us
    ppermute x16, waiting for transfers between devices, swap(): return lax.ppermute(value, axis, [(i, i ^ bit) for i in range(n)])  25.4 us
    ppermute x16, starting transfers between devices, swap(): return lax.ppermute(value, axis, [(i, i ^ bit) for i in range(n)])  22.1 us
    ppermute x2, waiting for transfers between devices, sum_gal(): lax.ppermute(mine, 'gal', [(i, (i + CORES * k) % n_gal) for i in range(n_...  7.83 us
    ppermute x2, starting transfers between devices, sum_gal(): lax.ppermute(mine, 'gal', [(i, (i + CORES * k) % n_gal) for i in range(n_...  4.53 us
  transfers between devices with their start and end apart: 18, of which 15 were waited for; matrix products, arithmetic and copies ran while one was open for 0% of the time, Pallas kernels for 16%

profile of v5, /device:TPU:0, one launch (start us, length us, event | category | flops | bytes accessed | tf_op | source)
XLA Modules:
  0.0 96.2 jit_solution(16735189246782680360)
XLA Ops:
  0.7 6.9 %first.1 = (f32[1024,1024]{1,0:T(8,128)S(1)}, f32[1024,1024]{1,0:T(8,128)S(1)}, bf16[1024,512]{1,0:T(8,128)(2,1)S(1)}, bf16[1024,512]{1,0:T(8,128)(2,1)S(1)}, bf...) custom-call(s32[4]{0:T(128)S(1)} %pad_add_fusion.s, ...), custom_call_target="tpu_custom_call" | custom-call | flops 402653184 | bytes 16777216 | tf_op jit(solution)/shard_map/first/pallas_call | solution.py:42
  7.6 0.5 collective-permute-start
  8.1 1.0 %collective-permute-done.refs_1_ = f32[64,512]{1,0:T(8,128)S(1)} collective-permute-done((f32[64,512]{1,0:T(8,128)S(1)}, f32[64,512]{1,0:T(8,128)S(1)}, u32[]{:S(2)}, u32[]{:S(2)}) %collective-permute-start) | collective-permute-done | bytes 131104 | tf_op jit(solution)/shard_map/ppermute | solution.py:116
  9.1 2.9 %collective-permute-start.1 = (f32[64,512]{1,0:T(8,128)S(1)}, f32[64,512]{1,0:T(8,128)S(1)}, u32[]{:S(2)}, u32[]{:S(2)}) collective-permute-start(f32[64,512]{1,0:T(8,128)S(1)} %add.11.refs_0_), channel_id=1, source_target_pairs={{0,16},{8,24},{16,0},{24,8},{1,17},{9,25},{17,1},{25,9},{2,18},{10... | collective-permute-start | bytes 393224 | tf_op jit(solution)/shard_map/ppermute | solution.py:198
  12.1 3.8 %collective-permute-done.1.refs_1_ = f32[64,512]{1,0:T(8,128)S(1)} collective-permute-done((f32[64,512]{1,0:T(8,128)S(1)}, f32[64,512]{1,0:T(8,128)S(1)}, u32[]{:S(2)}, u32[]{:S(2)}) %collective-permute-start.1) | collective-permute-done | bytes 131104 | tf_op jit(solution)/shard_map/ppermute | solution.py:198
  16.0 1.3 %collective-permute-done.2.away = f32[64,512]{1,0:T(8,128)S(1)} collective-permute-done((f32[64,512]{1,0:T(8,128)S(1)}, f32[64,512]{1,0:T(8,128)S(1)}, u32[]{:S(2)}, u32[]{:S(2)}) %collective-permute-start.2) | collective-permute-done | bytes 131104 | tf_op jit(solution)/shard_map/ppermute | solution.py:116
  17.3 0.7 multiply.5.sent
  18.0 1.7 %collective-permute-start.3 = (f32[288,128]{1,0:T(8,128)S(1)}, f32[288,128]{1,0:T(8,128)S(1)}, u32[]{:S(2)}, u32[]{:S(2)}) collective-permute-start(f32[288,128]{1,0:T(8,128)S(1)} %multiply.5.sent), channel_id=1, source_target_pairs={{0,1},{1,0},{2,3},{3,2},{4,5},{5,4},{6,7},{7,6},{8,9},{9,8},{10,11... | collective-permute-start | bytes 442376 | tf_op jit(solution)/shard_map/ppermute | solution.py:116
  19.7 0.4 multiply.4.value
  20.2 3.7 %collective-permute-done.3.got = f32[288,128]{1,0:T(8,128)S(1)} collective-permute-done((f32[288,128]{1,0:T(8,128)S(1)}, f32[288,128]{1,0:T(8,128)S(1)}, u32[]{:S(2)}, u32[]{:S(2)}) %collective-permute-start.3) | collective-permute-done | bytes 147488 | tf_op jit(solution)/shard_map/ppermute | solution.py:116
  23.9 0.6 fold.4
  24.5 1.9 %collective-permute-start.4 = (f32[160,128]{1,0:T(8,128)S(1)}, f32[160,128]{1,0:T(8,128)S(1)}, u32[]{:S(2)}, u32[]{:S(2)}) collective-permute-start(f32[160,128]{1,0:T(8,128)S(1)} %get-tuple-element.52.sent), channel_id=1, source_target_pairs={{0,2},{1,3},{2,0},{3,1},{4,6},{5,7},{6,4},{7,5},{8,10},{9,11},{10,... | collective-permute-start | bytes 245768 | tf_op jit(solution)/shard_map/ppermute | solution.py:116
  26.3 2.6 %collective-permute-done.4.got = f32[160,128]{1,0:T(8,128)S(1)} collective-permute-done((f32[160,128]{1,0:T(8,128)S(1)}, f32[160,128]{1,0:T(8,128)S(1)}, u32[]{:S(2)}, u32[]{:S(2)}) %collective-permute-start.4) | collective-permute-done | bytes 81952 | tf_op jit(solution)/shard_map/ppermute | solution.py:116
  29.0 0.6 fold.5.one
  29.5 2.9 %collective-permute-start.5 = (f32[160,128]{1,0:T(8,128)S(1)}, f32[160,128]{1,0:T(8,128)S(1)}, u32[]{:S(2)}, u32[]{:S(2)}) collective-permute-start(f32[160,128]{1,0:T(8,128)S(1)} %fold.5.one), channel_id=1, source_target_pairs={{0,4},{1,5},{2,6},{3,7},{4,0},{5,1},{6,2},{7,3},{8,12},{9,13},{10,... | collective-permute-start | bytes 245768 | tf_op jit(solution)/shard_map/ppermute | solution.py:116
  32.4 2.5 %collective-permute-done.5.two = f32[160,128]{1,0:T(8,128)S(1)} collective-permute-done((f32[160,128]{1,0:T(8,128)S(1)}, f32[160,128]{1,0:T(8,128)S(1)}, u32[]{:S(2)}, u32[]{:S(2)}) %collective-permute-start.5) | collective-permute-done | bytes 81952 | tf_op jit(solution)/shard_map/ppermute | solution.py:116
  35.0 1.9 %collective-permute-start.6 = (f32[128,128]{1,0:T(8,128)S(1)}, f32[128,128]{1,0:T(8,128)S(1)}, u32[]{:S(2)}, u32[]{:S(2)}) collective-permute-start(f32[128,128]{1,0:T(8,128)S(1)} %top.2.value), channel_id=1, source_target_pairs={{0,2},{1,3},{2,0},{3,1},{4,6},{5,7},{6,4},{7,5},{8,10},{9,11},{10,... | collective-permute-start | bytes 196616 | tf_op jit(solution)/shard_map/ppermute | solution.py:116
  36.8 2.8 %eliminate.2.inverse = f32[64,64]{1,0:T(8,128)S(1)} custom-call(f32[160,128]{1,0:T(8,128)S(1)} %fold.5.one, f32[160,128]{1,0:T(8,128)S(1)} %collective-permute-done.5.two), custom_call_target="tpu_custom_call" | custom-call | flops 100000000 | bytes 8388608 | tf_op jit(solution)/shard_map/eliminate/pallas_call | solution.py:42
  39.6 0.6 unfold.2.stacked
  40.2 1.6 %collective-permute-start.7 = (f32[256,128]{1,0:T(8,128)S(1)}, f32[256,128]{1,0:T(8,128)S(1)}, u32[]{:S(2)}, u32[]{:S(2)}) collective-permute-start(f32[256,128]{1,0:T(8,128)S(1)} %unfold.2.stacked), channel_id=1, source_target_pairs={{0,1},{1,0},{2,3},{3,2},{4,5},{5,4},{6,7},{7,6},{8,9},{9,8},{10,11... | collective-permute-start | bytes 393224 | tf_op jit(solution)/shard_map/ppermute | solution.py:116
  41.7 2.6 %middle.2 = (f32[1024,512]{1,0:T(8,128)S(1)}, bf16[1024,512]{1,0:T(8,128)(2,1)S(1)}, bf16[1024,512]{1,0:T(8,128)(2,1)S(1)}, f32[64,512]{1,0:T(8,128)S(1)}, f32[64,512]{1,0:T(8,128)S(1)}) custom-call(s32[4]{0:T(128)S(1)} %pad_add_fusion.s, f32[64,64]{1,0:T(8,128)S(1)} %eliminate.2.inverse, f32[64,512]{1,0:T(8,128)S(1)} %collective-permute-done.2.away, ...), custom_call_target="tpu_custom_call" | custom-call | flops 603979776 | bytes 4194304 | tf_op jit(solution)/shard_map/middle/pallas_call | solution.py:42
  44.3 0.9 collective-permute-done.7.stacked
  45.2 2.6 %middle.3 = (f32[1024,512]{1,0:T(8,128)S(1)}, bf16[1024,512]{1,0:T(8,128)(2,1)S(1)}, bf16[1024,512]{1,0:T(8,128)(2,1)S(1)}, f32[64,512]{1,0:T(8,128)S(1)}, f32[64,512]{1,0:T(8,128)S(1)}) custom-call(s32[4]{0:T(128)S(1)} %pad_add_fusion.s, f32[64,64]{1,0:T(8,128)S(1)} %eliminate.2.inverse, f32[64,512]{1,0:T(8,128)S(1)} %collective-permute-done.2.away, ...), custom_call_target="tpu_custom_call" | custom-call | flops 603979776 | bytes 4194304 | tf_op jit(solution)/shard_map/middle/pallas_call | solution.py:42
  47.9 1.3 %collective-permute-done.8.refs_1_ = f32[64,512]{1,0:T(8,128)S(1)} collective-permute-done((f32[64,512]{1,0:T(8,128)S(1)}, f32[64,512]{1,0:T(8,128)S(1)}, u32[]{:S(2)}, u32[]{:S(2)}) %collective-permute-start.8) | collective-permute-done | bytes 131104 | tf_op jit(solution)/shard_map/ppermute | solution.py:116
  49.2 1.6 %collective-permute-start.9 = (f32[64,512]{1,0:T(8,128)S(1)}, f32[64,512]{1,0:T(8,128)S(1)}, u32[]{:S(2)}, u32[]{:S(2)}) collective-permute-start(f32[64,512]{1,0:T(8,128)S(1)} %add.13.refs_0_), channel_id=1, source_target_pairs={{0,16},{8,24},{16,0},{24,8},{1,17},{9,25},{17,1},{25,9},{2,18},{10... | collective-permute-start | bytes 393224 | tf_op jit(solution)/shard_map/ppermute | solution.py:198
  50.8 4.0 %collective-permute-done.9.refs_1_ = f32[64,512]{1,0:T(8,128)S(1)} collective-permute-done((f32[64,512]{1,0:T(8,128)S(1)}, f32[64,512]{1,0:T(8,128)S(1)}, u32[]{:S(2)}, u32[]{:S(2)}) %collective-permute-start.9) | collective-permute-done | bytes 131104 | tf_op jit(solution)/shard_map/ppermute | solution.py:198
  54.9 1.3 %collective-permute-done.10.away = f32[64,512]{1,0:T(8,128)S(1)} collective-permute-done((f32[64,512]{1,0:T(8,128)S(1)}, f32[64,512]{1,0:T(8,128)S(1)}, u32[]{:S(2)}, u32[]{:S(2)}) %collective-permute-start.10) | collective-permute-done | bytes 131104 | tf_op jit(solution)/shard_map/ppermute | solution.py:116
  56.3 0.7 multiply.7.sent
  57.0 1.5 %collective-permute-start.11 = (f32[288,128]{1,0:T(8,128)S(1)}, f32[288,128]{1,0:T(8,128)S(1)}, u32[]{:S(2)}, u32[]{:S(2)}) collective-permute-start(f32[288,128]{1,0:T(8,128)S(1)} %multiply.7.sent), channel_id=1, source_target_pairs={{0,1},{1,0},{2,3},{3,2},{4,5},{5,4},{6,7},{7,6},{8,9},{9,8},{10,11... | collective-permute-start | bytes 442376 | tf_op jit(solution)/shard_map/ppermute | solution.py:116
  58.5 0.4 multiply.6.value
  58.9 4.0 %collective-permute-done.11.got = f32[288,128]{1,0:T(8,128)S(1)} collective-permute-done((f32[288,128]{1,0:T(8,128)S(1)}, f32[288,128]{1,0:T(8,128)S(1)}, u32[]{:S(2)}, u32[]{:S(2)}) %collective-permute-start.11) | collective-permute-done | bytes 147488 | tf_op jit(solution)/shard_map/ppermute | solution.py:116
  62.9 0.6 fold.6
  63.5 1.5 %collective-permute-start.12 = (f32[160,128]{1,0:T(8,128)S(1)}, f32[160,128]{1,0:T(8,128)S(1)}, u32[]{:S(2)}, u32[]{:S(2)}) collective-permute-start(f32[160,128]{1,0:T(8,128)S(1)} %get-tuple-element.66.sent), channel_id=1, source_target_pairs={{0,2},{1,3},{2,0},{3,1},{4,6},{5,7},{6,4},{7,5},{8,10},{9,11},{10,... | collective-permute-start | bytes 245768 | tf_op jit(solution)/shard_map/ppermute | solution.py:116
  65.0 3.0 %collective-permute-done.12.got = f32[160,128]{1,0:T(8,128)S(1)} collective-permute-done((f32[160,128]{1,0:T(8,128)S(1)}, f32[160,128]{1,0:T(8,128)S(1)}, u32[]{:S(2)}, u32[]{:S(2)}) %collective-permute-start.12) | collective-permute-done | bytes 81952 | tf_op jit(solution)/shard_map/ppermute | solution.py:116
  68.0 0.6 fold.7.one
  68.5 3.4 %collective-permute-start.13 = (f32[160,128]{1,0:T(8,128)S(1)}, f32[160,128]{1,0:T(8,128)S(1)}, u32[]{:S(2)}, u32[]{:S(2)}) collective-permute-start(f32[160,128]{1,0:T(8,128)S(1)} %fold.7.one), channel_id=1, source_target_pairs={{0,4},{1,5},{2,6},{3,7},{4,0},{5,1},{6,2},{7,3},{8,12},{9,13},{10,... | collective-permute-start | bytes 245768 | tf_op jit(solution)/shard_map/ppermute | solution.py:116
  72.0 2.4 %collective-permute-done.13.two = f32[160,128]{1,0:T(8,128)S(1)} collective-permute-done((f32[160,128]{1,0:T(8,128)S(1)}, f32[160,128]{1,0:T(8,128)S(1)}, u32[]{:S(2)}, u32[]{:S(2)}) %collective-permute-start.13) | collective-permute-done | bytes 81952 | tf_op jit(solution)/shard_map/ppermute | solution.py:116
  74.4 1.9 %collective-permute-start.14 = (f32[128,128]{1,0:T(8,128)S(1)}, f32[128,128]{1,0:T(8,128)S(1)}, u32[]{:S(2)}, u32[]{:S(2)}) collective-permute-start(f32[128,128]{1,0:T(8,128)S(1)} %top.3.value), channel_id=1, source_target_pairs={{0,2},{1,3},{2,0},{3,1},{4,6},{5,7},{6,4},{7,5},{8,10},{9,11},{10,... | collective-permute-start | bytes 196616 | tf_op jit(solution)/shard_map/ppermute | solution.py:116
  76.4 2.8 %eliminate.3.inverse = f32[64,64]{1,0:T(8,128)S(1)} custom-call(f32[160,128]{1,0:T(8,128)S(1)} %fold.7.one, f32[160,128]{1,0:T(8,128)S(1)} %collective-permute-done.13.two), custom_call_target="tpu_custom_call" | custom-call | flops 100000000 | bytes 8388608 | tf_op jit(solution)/shard_map/eliminate/pallas_call | solution.py:42
  79.2 0.6 unfold.3.stacked
  79.7 1.6 %collective-permute-start.15 = (f32[256,128]{1,0:T(8,128)S(1)}, f32[256,128]{1,0:T(8,128)S(1)}, u32[]{:S(2)}, u32[]{:S(2)}) collective-permute-start(f32[256,128]{1,0:T(8,128)S(1)} %unfold.3.stacked), channel_id=1, source_target_pairs={{0,1},{1,0},{2,3},{3,2},{4,5},{5,4},{6,7},{7,6},{8,9},{9,8},{10,11... | collective-permute-start | bytes 393224 | tf_op jit(solution)/shard_map/ppermute | solution.py:116
  81.3 3.4 %final.2 = (f32[1024,1024]{1,0:T(8,128)}, f32[1024,1024]{1,0:T(8,128)}, f32[64,1024]{1,0:T(8,128)}, f32[64,512]{1,0:T(8,128)S(1)}, f32[32,128]{1,0:T(8,128)S(1)}) custom-call(s32[4]{0:T(128)S(1)} %pad_add_fusion.s, f32[64,64]{1,0:T(8,128)S(1)} %eliminate.3.inverse, f32[64,512]{1,0:T(8,128)S(1)} %collective-permute-done.10.away, f32[64,512]{1,0:T(8,128)S(1)} %add.14.mine, ...), custom_call_target="tpu_custom_call" | custom-call | flops 201326592 | bytes 4194304 | tf_op jit(solution)/shard_map/final/pallas_call | solution.py:42
  84.7 0.1 collective-permute-done.15.stacked
  84.8 0.8 widen.1
  85.6 1.2 %collective-permute-done.16.refs_1_ = f32[32,128]{1,0:T(8,128)S(1)} collective-permute-done((f32[32,128]{1,0:T(8,128)S(1)}, f32[32,128]{1,0:T(8,128)S(1)}, u32[]{:S(2)}, u32[]{:S(2)}) %collective-permute-start.16) | collective-permute-done | bytes 16416 | tf_op jit(solution)/shard_map/ppermute | solution.py:116
  86.7 1.5 %collective-permute-start.17 = (f32[32,128]{1,0:T(8,128)S(1)}, f32[32,128]{1,0:T(8,128)S(1)}, u32[]{:S(2)}, u32[]{:S(2)}) collective-permute-start(f32[32,128]{1,0:T(8,128)S(1)} %add.15.one), channel_id=1, source_target_pairs={{0,16},{8,24},{16,0},{24,8},{1,17},{9,25},{17,1},{25,9},{2,18},{10... | collective-permute-start | bytes 49160 | tf_op jit(solution)/shard_map/ppermute | solution.py:116
  88.3 3.3 %final.3 = (f32[1024,1024]{1,0:T(8,128)}, f32[1024,1024]{1,0:T(8,128)}) custom-call(s32[4]{0:T(128)S(1)} %pad_add_fusion.s, f32[64,64]{1,0:T(8,128)S(1)} %eliminate.3.inverse, f32[64,512]{1,0:T(8,128)S(1)} %collective-permute-done.10.away, f32[64,512]{1,0:T(8,128)S(1)} %add.14.mine, ...), custom_call_target="tpu_custom_call", output_to_operand_aliasing={{0}: (6, {}), {1}: (7, {})} | custom-call | flops 201326592 | bytes 4194304 | tf_op jit(solution)/shard_map/final/pallas_call | solution.py:42
  91.6 4.4 %finish.1 = f32[64,1024]{1,0:T(8,128)} custom-call(s32[4]{0:T(128)S(1)} %pad_add_fusion.s, f32[32,128]{1,0:T(8,128)S(1)} %add.15.one, f32[32,128]{1,0:T(8,128)S(1)} %collective-permute-done.17.two, f32[64,512]{1,0:T(8,128)S(1)} %get-tuple-element.84.own, f32[64,512]{1,0:T(8,128)S(1)} %get-tuple-element.85.other), custom_call_target="tpu_custom_call" | custom-call | flops 100000000 | bytes 8388608 | tf_op jit(solution)/shard_map/finish/pallas_call | solution.py:42
  (15 shorter events, 0.4 us)
Async XLA Ops:
  7.6 1.5 %collective-permute-start = (f32[64,512]{1,0:T(8,128)S(1)}, f32[64,512]{1,0:T(8,128)S(1)}, u32[]{:S(2)}, u32[]{:S(2)}) collective-permute-start(f32[64,512]{1,0:T(8,128)S(1)} %get-tuple-element.46), channel_id=1, source_target_pairs={{0,8},{8,0},{16,24},{24,16},{1,9},{9,1},{17,25},{25,17},{2,10},{10... | collective-permute-start | bytes 393224 | tf_op jit(solution)/shard_map/ppermute | solution.py:116
  9.1 6.8 %collective-permute-start.1 = (f32[64,512]{1,0:T(8,128)S(1)}, f32[64,512]{1,0:T(8,128)S(1)}, u32[]{:S(2)}, u32[]{:S(2)}) collective-permute-start(f32[64,512]{1,0:T(8,128)S(1)} %add.11.refs_0_), channel_id=1, source_target_pairs={{0,16},{8,24},{16,0},{24,8},{1,17},{9,25},{17,1},{25,9},{2,18},{10... | collective-permute-start | bytes 393224 | tf_op jit(solution)/shard_map/ppermute | solution.py:198
  15.9 1.4 %collective-permute-start.2 = (f32[64,512]{1,0:T(8,128)S(1)}, f32[64,512]{1,0:T(8,128)S(1)}, u32[]{:S(2)}, u32[]{:S(2)}) collective-permute-start(f32[64,512]{1,0:T(8,128)S(1)} %add.12.mine), channel_id=1, source_target_pairs={{0,8},{8,0},{16,24},{24,16},{1,9},{9,1},{17,25},{25,17},{2,10},{10... | collective-permute-start | bytes 393224 | tf_op jit(solution)/shard_map/ppermute | solution.py:116
  18.0 5.9 %collective-permute-start.3 = (f32[288,128]{1,0:T(8,128)S(1)}, f32[288,128]{1,0:T(8,128)S(1)}, u32[]{:S(2)}, u32[]{:S(2)}) collective-permute-start(f32[288,128]{1,0:T(8,128)S(1)} %multiply.5.sent), channel_id=1, source_target_pairs={{0,1},{1,0},{2,3},{3,2},{4,5},{5,4},{6,7},{7,6},{8,9},{9,8},{10,11... | collective-permute-start | bytes 442376 | tf_op jit(solution)/shard_map/ppermute | solution.py:116
  24.5 4.5 %collective-permute-start.4 = (f32[160,128]{1,0:T(8,128)S(1)}, f32[160,128]{1,0:T(8,128)S(1)}, u32[]{:S(2)}, u32[]{:S(2)}) collective-permute-start(f32[160,128]{1,0:T(8,128)S(1)} %get-tuple-element.52.sent), channel_id=1, source_target_pairs={{0,2},{1,3},{2,0},{3,1},{4,6},{5,7},{6,4},{7,5},{8,10},{9,11},{10,... | collective-permute-start | bytes 245768 | tf_op jit(solution)/shard_map/ppermute | solution.py:116
  29.5 5.4 %collective-permute-start.5 = (f32[160,128]{1,0:T(8,128)S(1)}, f32[160,128]{1,0:T(8,128)S(1)}, u32[]{:S(2)}, u32[]{:S(2)}) collective-permute-start(f32[160,128]{1,0:T(8,128)S(1)} %fold.5.one), channel_id=1, source_target_pairs={{0,4},{1,5},{2,6},{3,7},{4,0},{5,1},{6,2},{7,3},{8,12},{9,13},{10,... | collective-permute-start | bytes 245768 | tf_op jit(solution)/shard_map/ppermute | solution.py:116
  35.0 4.7 %collective-permute-start.6 = (f32[128,128]{1,0:T(8,128)S(1)}, f32[128,128]{1,0:T(8,128)S(1)}, u32[]{:S(2)}, u32[]{:S(2)}) collective-permute-start(f32[128,128]{1,0:T(8,128)S(1)} %top.2.value), channel_id=1, source_target_pairs={{0,2},{1,3},{2,0},{3,1},{4,6},{5,7},{6,4},{7,5},{8,10},{9,11},{10,... | collective-permute-start | bytes 196616 | tf_op jit(solution)/shard_map/ppermute | solution.py:116
  40.2 5.0 %collective-permute-start.7 = (f32[256,128]{1,0:T(8,128)S(1)}, f32[256,128]{1,0:T(8,128)S(1)}, u32[]{:S(2)}, u32[]{:S(2)}) collective-permute-start(f32[256,128]{1,0:T(8,128)S(1)} %unfold.2.stacked), channel_id=1, source_target_pairs={{0,1},{1,0},{2,3},{3,2},{4,5},{5,4},{6,7},{7,6},{8,9},{9,8},{10,11... | collective-permute-start | bytes 393224 | tf_op jit(solution)/shard_map/ppermute | solution.py:116
  47.8 1.4 %collective-permute-start.8 = (f32[64,512]{1,0:T(8,128)S(1)}, f32[64,512]{1,0:T(8,128)S(1)}, u32[]{:S(2)}, u32[]{:S(2)}) collective-permute-start(f32[64,512]{1,0:T(8,128)S(1)} %get-tuple-element.60), channel_id=1, source_target_pairs={{0,8},{8,0},{16,24},{24,16},{1,9},{9,1},{17,25},{25,17},{2,10},{10... | collective-permute-start | bytes 393224 | tf_op jit(solution)/shard_map/ppermute | solution.py:116
  49.2 5.6 %collective-permute-start.9 = (f32[64,512]{1,0:T(8,128)S(1)}, f32[64,512]{1,0:T(8,128)S(1)}, u32[]{:S(2)}, u32[]{:S(2)}) collective-permute-start(f32[64,512]{1,0:T(8,128)S(1)} %add.13.refs_0_), channel_id=1, source_target_pairs={{0,16},{8,24},{16,0},{24,8},{1,17},{9,25},{17,1},{25,9},{2,18},{10... | collective-permute-start | bytes 393224 | tf_op jit(solution)/shard_map/ppermute | solution.py:198
  54.9 1.4 %collective-permute-start.10 = (f32[64,512]{1,0:T(8,128)S(1)}, f32[64,512]{1,0:T(8,128)S(1)}, u32[]{:S(2)}, u32[]{:S(2)}) collective-permute-start(f32[64,512]{1,0:T(8,128)S(1)} %add.14.mine), channel_id=1, source_target_pairs={{0,8},{8,0},{16,24},{24,16},{1,9},{9,1},{17,25},{25,17},{2,10},{10... | collective-permute-start | bytes 393224 | tf_op jit(solution)/shard_map/ppermute | solution.py:116
  57.0 5.9 %collective-permute-start.11 = (f32[288,128]{1,0:T(8,128)S(1)}, f32[288,128]{1,0:T(8,128)S(1)}, u32[]{:S(2)}, u32[]{:S(2)}) collective-permute-start(f32[288,128]{1,0:T(8,128)S(1)} %multiply.7.sent), channel_id=1, source_target_pairs={{0,1},{1,0},{2,3},{3,2},{4,5},{5,4},{6,7},{7,6},{8,9},{9,8},{10,11... | collective-permute-start | bytes 442376 | tf_op jit(solution)/shard_map/ppermute | solution.py:116
  63.5 4.5 %collective-permute-start.12 = (f32[160,128]{1,0:T(8,128)S(1)}, f32[160,128]{1,0:T(8,128)S(1)}, u32[]{:S(2)}, u32[]{:S(2)}) collective-permute-start(f32[160,128]{1,0:T(8,128)S(1)} %get-tuple-element.66.sent), channel_id=1, source_target_pairs={{0,2},{1,3},{2,0},{3,1},{4,6},{5,7},{6,4},{7,5},{8,10},{9,11},{10,... | collective-permute-start | bytes 245768 | tf_op jit(solution)/shard_map/ppermute | solution.py:116
  68.5 5.9 %collective-permute-start.13 = (f32[160,128]{1,0:T(8,128)S(1)}, f32[160,128]{1,0:T(8,128)S(1)}, u32[]{:S(2)}, u32[]{:S(2)}) collective-permute-start(f32[160,128]{1,0:T(8,128)S(1)} %fold.7.one), channel_id=1, source_target_pairs={{0,4},{1,5},{2,6},{3,7},{4,0},{5,1},{6,2},{7,3},{8,12},{9,13},{10,... | collective-permute-start | bytes 245768 | tf_op jit(solution)/shard_map/ppermute | solution.py:116
  74.4 4.7 %collective-permute-start.14 = (f32[128,128]{1,0:T(8,128)S(1)}, f32[128,128]{1,0:T(8,128)S(1)}, u32[]{:S(2)}, u32[]{:S(2)}) collective-permute-start(f32[128,128]{1,0:T(8,128)S(1)} %top.3.value), channel_id=1, source_target_pairs={{0,2},{1,3},{2,0},{3,1},{4,6},{5,7},{6,4},{7,5},{8,10},{9,11},{10,... | collective-permute-start | bytes 196616 | tf_op jit(solution)/shard_map/ppermute | solution.py:116
  79.7 5.0 %collective-permute-start.15 = (f32[256,128]{1,0:T(8,128)S(1)}, f32[256,128]{1,0:T(8,128)S(1)}, u32[]{:S(2)}, u32[]{:S(2)}) collective-permute-start(f32[256,128]{1,0:T(8,128)S(1)} %unfold.3.stacked), channel_id=1, source_target_pairs={{0,1},{1,0},{2,3},{3,2},{4,5},{5,4},{6,7},{7,6},{8,9},{9,8},{10,11... | collective-permute-start | bytes 393224 | tf_op jit(solution)/shard_map/ppermute | solution.py:116
  85.5 1.2 %collective-permute-start.16 = (f32[32,128]{1,0:T(8,128)S(1)}, f32[32,128]{1,0:T(8,128)S(1)}, u32[]{:S(2)}, u32[]{:S(2)}) collective-permute-start(f32[32,128]{1,0:T(8,128)S(1)} %get-tuple-element.83.refs_0_), channel_id=1, source_target_pairs={{0,8},{8,0},{16,24},{24,16},{1,9},{9,1},{17,25},{25,17},{2,10},{10... | collective-permute-start | bytes 49160 | tf_op jit(solution)/shard_map/ppermute | solution.py:116
  86.7 4.8 %collective-permute-start.17 = (f32[32,128]{1,0:T(8,128)S(1)}, f32[32,128]{1,0:T(8,128)S(1)}, u32[]{:S(2)}, u32[]{:S(2)}) collective-permute-start(f32[32,128]{1,0:T(8,128)S(1)} %add.15.one), channel_id=1, source_target_pairs={{0,16},{8,24},{16,0},{24,8},{1,17},{9,25},{17,1},{25,9},{2,18},{10... | collective-permute-start | bytes 49160 | tf_op jit(solution)/shard_map/ppermute | solution.py:116

commit v6 on v5

--- a/solution.py
+++ b/solution.py
@@ -121,12 +121,12 @@
         half = n_cols // 2
         tall = min(256, n_rows // 2)
         steps = n_rows // tall
-        core = lax.rem(lax.axis_index("gal"), CORES)
-        bits = [lax.rem(lax.axis_index("pix") >> level, 2) for level in range(levels)]
-        scalars = jnp.stack([core] + bits).astype(jnp.int32)
         stack_rows = rank * (half // LANES)
         gram_rows = rank * rank // LANES
-        where = (scalars, pltpu.SMEM)
+
+        def place():
+            pix = lax.axis_index("pix")
+            return [lax.rem(lax.axis_index("gal"), CORES)] + [lax.rem(pix >> level, 2) for level in range(levels)]
 
         def gal_at(i, s):
             turn = (1 - s[0]) * (steps // 2)
@@ -157,7 +157,8 @@
             return call(body, "add", [(a, pltpu.VMEM) for a in arrays], [out], cost=(10**5, 10**6), limit=4)[0]
 
         def first(right):
-            def body(s, o_in, s_in, d_in, r_in, o, d, h0, l0, h1, l1, away, mine, sp, right, r_sem, sems):
+            def body(o_in, s_in, d_in, r_in, o, d, h0, l0, h1, l1, away, mine, sp, right, r_sem, sems):
+                s = place()
                 right_move = pltpu.make_async_copy(r_in, right, r_sem)
                 right_move.start()
                 moves = {}
@@ -182,7 +183,7 @@
                     out = away if i < steps // 2 else mine
                     out[:, chunk(i % (steps // 2))] = total
 
-            ins = [where] + [(a, pltpu.HBM) for a in (observed, sparse_init, dual_init, right)]
+            ins = [(a, pltpu.HBM) for a in (observed, sparse_init, dual_init, right)]
             outs = [((n_rows, n_cols), F32, pltpu.VMEM)] * 2 + [((n_rows, half), BF16, pltpu.VMEM)] * 4
             outs += [((rank, n_rows // 2), F32, pltpu.VMEM)] * 2
             scratch = [pltpu.VMEM((n_rows, n_cols), F32), pltpu.VMEM((rank, n_cols), F32)]
@@ -230,7 +231,8 @@
             last = level == levels - 1
             keep = rows if last else rows // 2
 
-            def body(s, value, sent, got, *outs):
+            def body(value, sent, got, *outs):
+                s = place()
                 message = outs[-1]
                 if last:
                     message[:rows, :] = value[...] + got[:rows, :]
@@ -243,18 +245,19 @@
             def rows_of(ref):
                 return slice(ref.shape[0] - gram_rows, ref.shape[0])
 
-            ins = [where] + [(a, pltpu.VMEM) for a in (value, sent, got)]
+            ins = [(a, pltpu.VMEM) for a in (value, sent, got)]
             outs = small(body, "fold", ins, [keep + gram_rows] if last else [keep, keep + gram_rows])
             return outs[0], outs[-1]
 
         def unfold(level, value, got):
             rows = value.shape[0]
 
-            def body(s, value, got, out):
+            def body(value, got, out):
+                s = place()
                 for mine, ref in ((s[1 + level], value), (1 - s[1 + level], got)):
                     out[pl.ds(pl.multiple_of(mine * rows, rows), rows), :] = ref[...]
 
-            ins = [where, (value, pltpu.VMEM), (got, pltpu.VMEM)]
+            ins = [(value, pltpu.VMEM), (got, pltpu.VMEM)]
             return small(body, "unfold", ins, [2 * rows])[0]
 
         def top(one, two):
@@ -286,7 +289,8 @@
             return left, wide, (wide_high, wide_low), tops, jnp.concatenate([wide_high, wide_high, wide_low], axis=0)
 
         def middle(p, inverse, panel, stacked, o, d, before):
-            def body(s, inverse, away, mine, stacked, o, d, *rest):
+            def body(inverse, away, mine, stacked, o, d, *rest):
+                s = place()
                 base, high, low, *after = rest[2 * p :]
                 _, _, right, tops, wides = halves(inverse, (away, mine), stacked)
                 for i in range(steps):
@@ -306,12 +310,13 @@
             outs = [((n_rows, half), F32, pltpu.VMEM)] + [((n_rows, half), BF16, pltpu.VMEM)] * 2
             outs += [((rank, n_rows // 2), F32, pltpu.VMEM)] * 2
             cost = (9 * rank * n_rows * n_cols, 4 * n_rows * n_cols)
-            ins = [where] + [(a, pltpu.VMEM) for a in arrays]
+            ins = [(a, pltpu.VMEM) for a in arrays]
             base, high, low, *part = call(body, "middle", ins, outs, cost=cost)
             return base, (high, low), part
 
         def final(p, inverse, panel, stacked, base, before):
-            def body(s, inverse, away, mine, stacked, base, *rest):
+            def body(inverse, away, mine, stacked, base, *rest):
+                s = place()
                 sparse, dual, *outs, sparse_part, dual_part, left_part, sems = rest[2 * p :]
                 left, wide, _, tops, wides = halves(inverse, (away, mine), stacked)
                 moves = []
@@ -335,12 +340,12 @@
                 for move in moves:
                     move.wait()
 
-            ins = [where] + [(a, pltpu.VMEM) for a in (inverse, *panel, stacked, base)]
+            ins = [(a, pltpu.VMEM) for a in (inverse, *panel, stacked, base)]
             outs = [((n_rows, n_cols), F32, pltpu.HBM)] * 2
             aliases = {}
             if p:
                 ins += [(a, pltpu.HBM) for a in before[:2]]
-                aliases = {6: 0, 7: 1}
+                aliases = {5: 0, 6: 1}
             else:
                 outs += [((rank, n_rows), F32, pltpu.HBM), ((rank, half), F32, pltpu.VMEM)]
                 outs += [((gram_rows, LANES), F32, pltpu.VMEM)]
@@ -359,7 +364,8 @@
             return call(body, "widen", ins, outs, cost=(10**8, MIB), limit=8)
 
         def finish(one, two, wide):
-            def body(s, one, two, own, other, out, inverse, right, sem):
+            def body(one, two, own, other, out, inverse, right, sem):
+                s = place()
                 invert(one[...] + two[...], inverse)
                 for p, value in enumerate((own, other)):
                     right[:, pl.ds(pix_at(p, s), half)] = dot(inverse[...], value[...], ((1,), (0,)), HIGH)
@@ -367,7 +373,7 @@
                 move.start()
                 move.wait()
 
-            ins = [where] + [(a, pltpu.VMEM) for a in (one, two, *wide)]
+            ins = [(a, pltpu.VMEM) for a in (one, two, *wide)]
             outs = [((rank, n_cols), F32, pltpu.HBM)]
             scratch = [pltpu.VMEM((rank, rank), F32), pltpu.VMEM((rank, n_cols), F32), pltpu.SemaphoreType.DMA(())]
             return call(body, "finish", ins, outs, scratch, cost=(10**8, 8 * MIB))[0]

time: 96.3 us -> 90.7 us (0.942)
  Pallas kernels: 35.2 us -> 28.6 us
  waiting for transfers between devices: 33.3 us -> 34.4 us
    pallas_call x26, Pallas kernels: 35.2 us -> 28.6 us  [call(): pl.pallas_call(body, name=name, in_specs=[pl.BlockSpec(memory_space=space...]
    ppermute x16, waiting for transfers between devices: 25.4 us -> 26.6 us  [swap(): return lax.ppermute(value, axis, [(i, i ^ bit) for i in range(n)])]
where the time goes in v6:
time: 90.7 us; the launch traced here: 90.5 us
  waiting for transfers between devices  34.4 us (38%)
  Pallas kernels  28.6 us (32%)
  starting transfers between devices  26.6 us (29%)
  between operations  0.95 us (1%)
    pallas_call x26, Pallas kernels, call(): pl.pallas_call(body, name=name, in_specs=[pl.BlockSpec(memory_space=space...  28.6 us
    ppermute x16, waiting for transfers between devices, swap(): return lax.ppermute(value, axis, [(i, i ^ bit) for i in range(n)])  26.6 us
    ppermute x16, starting transfers between devices, swap(): return lax.ppermute(value, axis, [(i, i ^ bit) for i in range(n)])  22.1 us
    ppermute x2, waiting for transfers between devices, sum_gal(): lax.ppermute(mine, 'gal', [(i, (i + CORES * k) % n_gal) for i in range(n_...  7.84 us
    ppermute x2, starting transfers between devices, sum_gal(): lax.ppermute(mine, 'gal', [(i, (i + CORES * k) % n_gal) for i in range(n_...  4.53 us
  transfers between devices with their start and end apart: 18, of which 15 were waited for; matrix products, arithmetic and copies ran while one was open for 0% of the time, Pallas kernels for 16%

profile of v6, /device:TPU:0, one launch (start us, length us, event | category | flops | bytes accessed | tf_op | source)
XLA Modules:
  0.0 90.5 jit_solution(5122024690440477990)
XLA Ops:
  0.6 6.3 %first.1 = (f32[1024,1024]{1,0:T(8,128)S(1)}, f32[1024,1024]{1,0:T(8,128)S(1)}, bf16[1024,512]{1,0:T(8,128)(2,1)S(1)}, bf16[1024,512]{1,0:T(8,128)(2,1)S(1)}, bf...) custom-call(f32[1024,1024]{1,0:T(8,128)} %o_in.1, ...), custom_call_target="tpu_custom_call" | custom-call | flops 402653184 | bytes 16777216 | tf_op jit(solution)/shard_map/first/pallas_call | solution.py:42
  6.9 0.5 collective-permute-start
  7.4 1.0 %collective-permute-done.refs_1_ = f32[64,512]{1,0:T(8,128)S(1)} collective-permute-done((f32[64,512]{1,0:T(8,128)S(1)}, f32[64,512]{1,0:T(8,128)S(1)}, u32[]{:S(2)}, u32[]{:S(2)}) %collective-permute-start) | collective-permute-done | bytes 131104 | tf_op jit(solution)/shard_map/ppermute | solution.py:116
  8.4 2.9 %collective-permute-start.1 = (f32[64,512]{1,0:T(8,128)S(1)}, f32[64,512]{1,0:T(8,128)S(1)}, u32[]{:S(2)}, u32[]{:S(2)}) collective-permute-start(f32[64,512]{1,0:T(8,128)S(1)} %add.5.refs_0_), channel_id=1, source_target_pairs={{0,16},{8,24},{16,0},{24,8},{1,17},{9,25},{17,1},{25,9},{2,18},{10... | collective-permute-start | bytes 393224 | tf_op jit(solution)/shard_map/ppermute | solution.py:199
  11.4 3.8 %collective-permute-done.1.refs_1_ = f32[64,512]{1,0:T(8,128)S(1)} collective-permute-done((f32[64,512]{1,0:T(8,128)S(1)}, f32[64,512]{1,0:T(8,128)S(1)}, u32[]{:S(2)}, u32[]{:S(2)}) %collective-permute-start.1) | collective-permute-done | bytes 131104 | tf_op jit(solution)/shard_map/ppermute | solution.py:199
  15.2 0.1 collective-permute-start.2
  15.3 1.3 %collective-permute-done.2.away = f32[64,512]{1,0:T(8,128)S(1)} collective-permute-done((f32[64,512]{1,0:T(8,128)S(1)}, f32[64,512]{1,0:T(8,128)S(1)}, u32[]{:S(2)}, u32[]{:S(2)}) %collective-permute-start.2) | collective-permute-done | bytes 131104 | tf_op jit(solution)/shard_map/ppermute | solution.py:116
  16.6 0.7 multiply.5.sent
  17.3 1.7 %collective-permute-start.3 = (f32[288,128]{1,0:T(8,128)S(1)}, f32[288,128]{1,0:T(8,128)S(1)}, u32[]{:S(2)}, u32[]{:S(2)}) collective-permute-start(f32[288,128]{1,0:T(8,128)S(1)} %multiply.5.sent), channel_id=1, source_target_pairs={{0,1},{1,0},{2,3},{3,2},{4,5},{5,4},{6,7},{7,6},{8,9},{9,8},{10,11... | collective-permute-start | bytes 442376 | tf_op jit(solution)/shard_map/ppermute | solution.py:116
  19.0 0.4 multiply.4.value
  19.5 3.8 %collective-permute-done.3.got = f32[288,128]{1,0:T(8,128)S(1)} collective-permute-done((f32[288,128]{1,0:T(8,128)S(1)}, f32[288,128]{1,0:T(8,128)S(1)}, u32[]{:S(2)}, u32[]{:S(2)}) %collective-permute-start.3) | collective-permute-done | bytes 147488 | tf_op jit(solution)/shard_map/ppermute | solution.py:116
  23.2 1.9 %collective-permute-start.4 = (f32[160,128]{1,0:T(8,128)S(1)}, f32[160,128]{1,0:T(8,128)S(1)}, u32[]{:S(2)}, u32[]{:S(2)}) collective-permute-start(f32[160,128]{1,0:T(8,128)S(1)} %get-tuple-element.52.sent), channel_id=1, source_target_pairs={{0,2},{1,3},{2,0},{3,1},{4,6},{5,7},{6,4},{7,5},{8,10},{9,11},{10,... | collective-permute-start | bytes 245768 | tf_op jit(solution)/shard_map/ppermute | solution.py:116
  25.1 2.6 %collective-permute-done.4.got = f32[160,128]{1,0:T(8,128)S(1)} collective-permute-done((f32[160,128]{1,0:T(8,128)S(1)}, f32[160,128]{1,0:T(8,128)S(1)}, u32[]{:S(2)}, u32[]{:S(2)}) %collective-permute-start.4) | collective-permute-done | bytes 81952 | tf_op jit(solution)/shard_map/ppermute | solution.py:116
  27.8 2.9 %collective-permute-start.5 = (f32[160,128]{1,0:T(8,128)S(1)}, f32[160,128]{1,0:T(8,128)S(1)}, u32[]{:S(2)}, u32[]{:S(2)}) collective-permute-start(f32[160,128]{1,0:T(8,128)S(1)} %fold.5.one), channel_id=1, source_target_pairs={{0,4},{1,5},{2,6},{3,7},{4,0},{5,1},{6,2},{7,3},{8,12},{9,13},{10,... | collective-permute-start | bytes 245768 | tf_op jit(solution)/shard_map/ppermute | solution.py:116
  30.6 2.5 %collective-permute-done.5.two = f32[160,128]{1,0:T(8,128)S(1)} collective-permute-done((f32[160,128]{1,0:T(8,128)S(1)}, f32[160,128]{1,0:T(8,128)S(1)}, u32[]{:S(2)}, u32[]{:S(2)}) %collective-permute-start.5) | collective-permute-done | bytes 81952 | tf_op jit(solution)/shard_map/ppermute | solution.py:116
  33.2 1.9 %collective-permute-start.6 = (f32[128,128]{1,0:T(8,128)S(1)}, f32[128,128]{1,0:T(8,128)S(1)}, u32[]{:S(2)}, u32[]{:S(2)}) collective-permute-start(f32[128,128]{1,0:T(8,128)S(1)} %top.2.value), channel_id=1, source_target_pairs={{0,2},{1,3},{2,0},{3,1},{4,6},{5,7},{6,4},{7,5},{8,10},{9,11},{10,... | collective-permute-start | bytes 196616 | tf_op jit(solution)/shard_map/ppermute | solution.py:116
  35.0 2.8 %eliminate.2.inverse = f32[64,64]{1,0:T(8,128)S(1)} custom-call(f32[160,128]{1,0:T(8,128)S(1)} %fold.5.one, f32[160,128]{1,0:T(8,128)S(1)} %collective-permute-done.5.two), custom_call_target="tpu_custom_call" | custom-call | flops 100000000 | bytes 8388608 | tf_op jit(solution)/shard_map/eliminate/pallas_call | solution.py:42
  37.8 0.0 collective-permute-done.6.got
  37.9 1.5 %collective-permute-start.7 = (f32[256,128]{1,0:T(8,128)S(1)}, f32[256,128]{1,0:T(8,128)S(1)}, u32[]{:S(2)}, u32[]{:S(2)}) collective-permute-start(f32[256,128]{1,0:T(8,128)S(1)} %unfold.2.stacked), channel_id=1, source_target_pairs={{0,1},{1,0},{2,3},{3,2},{4,5},{5,4},{6,7},{7,6},{8,9},{9,8},{10,11... | collective-permute-start | bytes 393224 | tf_op jit(solution)/shard_map/ppermute | solution.py:116
  39.4 2.0 %middle.2 = (f32[1024,512]{1,0:T(8,128)S(1)}, bf16[1024,512]{1,0:T(8,128)(2,1)S(1)}, bf16[1024,512]{1,0:T(8,128)(2,1)S(1)}, f32[64,512]{1,0:T(8,128)S(1)}, f32[64,512]{1,0:T(8,128)S(1)}) custom-call(f32[64,64]{1,0:T(8,128)S(1)} %eliminate.2.inverse, f32[64,512]{1,0:T(8,128)S(1)} %collective-permute-done.2.away, f32[64,512]{1,0:T(8,128)S(1)} %add.6.mine, ...), custom_call_target="tpu_custom_call" | custom-call | flops 603979776 | bytes 4194304 | tf_op jit(solution)/shard_map/middle/pallas_call | solution.py:42
  41.4 1.5 %collective-permute-done.7.stacked = f32[256,128]{1,0:T(8,128)S(1)} collective-permute-done((f32[256,128]{1,0:T(8,128)S(1)}, f32[256,128]{1,0:T(8,128)S(1)}, u32[]{:S(2)}, u32[]{:S(2)}) %collective-permute-start.7) | collective-permute-done | bytes 131104 | tf_op jit(solution)/shard_map/ppermute | solution.py:116
  42.9 2.0 %middle.3 = (f32[1024,512]{1,0:T(8,128)S(1)}, bf16[1024,512]{1,0:T(8,128)(2,1)S(1)}, bf16[1024,512]{1,0:T(8,128)(2,1)S(1)}, f32[64,512]{1,0:T(8,128)S(1)}, f32[64,512]{1,0:T(8,128)S(1)}) custom-call(f32[64,64]{1,0:T(8,128)S(1)} %eliminate.2.inverse, f32[64,512]{1,0:T(8,128)S(1)} %collective-permute-done.2.away, f32[64,512]{1,0:T(8,128)S(1)} %add.6.mine, ...), custom_call_target="tpu_custom_call" | custom-call | flops 603979776 | bytes 4194304 | tf_op jit(solution)/shard_map/middle/pallas_call | solution.py:42
  44.9 0.1 collective-permute-start.8
  45.0 1.3 %collective-permute-done.8.refs_1_ = f32[64,512]{1,0:T(8,128)S(1)} collective-permute-done((f32[64,512]{1,0:T(8,128)S(1)}, f32[64,512]{1,0:T(8,128)S(1)}, u32[]{:S(2)}, u32[]{:S(2)}) %collective-permute-start.8) | collective-permute-done | bytes 131104 | tf_op jit(solution)/shard_map/ppermute | solution.py:116
  46.4 1.6 %collective-permute-start.9 = (f32[64,512]{1,0:T(8,128)S(1)}, f32[64,512]{1,0:T(8,128)S(1)}, u32[]{:S(2)}, u32[]{:S(2)}) collective-permute-start(f32[64,512]{1,0:T(8,128)S(1)} %add.7.refs_0_), channel_id=1, source_target_pairs={{0,16},{8,24},{16,0},{24,8},{1,17},{9,25},{17,1},{25,9},{2,18},{10... | collective-permute-start | bytes 393224 | tf_op jit(solution)/shard_map/ppermute | solution.py:199
  47.9 4.0 %collective-permute-done.9.refs_1_ = f32[64,512]{1,0:T(8,128)S(1)} collective-permute-done((f32[64,512]{1,0:T(8,128)S(1)}, f32[64,512]{1,0:T(8,128)S(1)}, u32[]{:S(2)}, u32[]{:S(2)}) %collective-permute-start.9) | collective-permute-done | bytes 131104 | tf_op jit(solution)/shard_map/ppermute | solution.py:199
  52.0 0.1 collective-permute-start.10
  52.1 1.3 %collective-permute-done.10.away = f32[64,512]{1,0:T(8,128)S(1)} collective-permute-done((f32[64,512]{1,0:T(8,128)S(1)}, f32[64,512]{1,0:T(8,128)S(1)}, u32[]{:S(2)}, u32[]{:S(2)}) %collective-permute-start.10) | collective-permute-done | bytes 131104 | tf_op jit(solution)/shard_map/ppermute | solution.py:116
  53.4 0.7 multiply.7.sent
  54.1 1.5 %collective-permute-start.11 = (f32[288,128]{1,0:T(8,128)S(1)}, f32[288,128]{1,0:T(8,128)S(1)}, u32[]{:S(2)}, u32[]{:S(2)}) collective-permute-start(f32[288,128]{1,0:T(8,128)S(1)} %multiply.7.sent), channel_id=1, source_target_pairs={{0,1},{1,0},{2,3},{3,2},{4,5},{5,4},{6,7},{7,6},{8,9},{9,8},{10,11... | collective-permute-start | bytes 442376 | tf_op jit(solution)/shard_map/ppermute | solution.py:116
  55.6 0.4 multiply.6.value
  56.0 4.0 %collective-permute-done.11.got = f32[288,128]{1,0:T(8,128)S(1)} collective-permute-done((f32[288,128]{1,0:T(8,128)S(1)}, f32[288,128]{1,0:T(8,128)S(1)}, u32[]{:S(2)}, u32[]{:S(2)}) %collective-permute-start.11) | collective-permute-done | bytes 147488 | tf_op jit(solution)/shard_map/ppermute | solution.py:116
  60.0 1.5 %collective-permute-start.12 = (f32[160,128]{1,0:T(8,128)S(1)}, f32[160,128]{1,0:T(8,128)S(1)}, u32[]{:S(2)}, u32[]{:S(2)}) collective-permute-start(f32[160,128]{1,0:T(8,128)S(1)} %get-tuple-element.66.sent), channel_id=1, source_target_pairs={{0,2},{1,3},{2,0},{3,1},{4,6},{5,7},{6,4},{7,5},{8,10},{9,11},{10,... | collective-permute-start | bytes 245768 | tf_op jit(solution)/shard_map/ppermute | solution.py:116
  61.6 3.0 %collective-permute-done.12.got = f32[160,128]{1,0:T(8,128)S(1)} collective-permute-done((f32[160,128]{1,0:T(8,128)S(1)}, f32[160,128]{1,0:T(8,128)S(1)}, u32[]{:S(2)}, u32[]{:S(2)}) %collective-permute-start.12) | collective-permute-done | bytes 81952 | tf_op jit(solution)/shard_map/ppermute | solution.py:116
  64.6 3.4 %collective-permute-start.13 = (f32[160,128]{1,0:T(8,128)S(1)}, f32[160,128]{1,0:T(8,128)S(1)}, u32[]{:S(2)}, u32[]{:S(2)}) collective-permute-start(f32[160,128]{1,0:T(8,128)S(1)} %fold.7.one), channel_id=1, source_target_pairs={{0,4},{1,5},{2,6},{3,7},{4,0},{5,1},{6,2},{7,3},{8,12},{9,13},{10,... | collective-permute-start | bytes 245768 | tf_op jit(solution)/shard_map/ppermute | solution.py:116
  68.0 2.4 %collective-permute-done.13.two = f32[160,128]{1,0:T(8,128)S(1)} collective-permute-done((f32[160,128]{1,0:T(8,128)S(1)}, f32[160,128]{1,0:T(8,128)S(1)}, u32[]{:S(2)}, u32[]{:S(2)}) %collective-permute-start.13) | collective-permute-done | bytes 81952 | tf_op jit(solution)/shard_map/ppermute | solution.py:116
  70.4 1.9 %collective-permute-start.14 = (f32[128,128]{1,0:T(8,128)S(1)}, f32[128,128]{1,0:T(8,128)S(1)}, u32[]{:S(2)}, u32[]{:S(2)}) collective-permute-start(f32[128,128]{1,0:T(8,128)S(1)} %top.3.value), channel_id=1, source_target_pairs={{0,2},{1,3},{2,0},{3,1},{4,6},{5,7},{6,4},{7,5},{8,10},{9,11},{10,... | collective-permute-start | bytes 196616 | tf_op jit(solution)/shard_map/ppermute | solution.py:116
  72.4 2.8 %eliminate.3.inverse = f32[64,64]{1,0:T(8,128)S(1)} custom-call(f32[160,128]{1,0:T(8,128)S(1)} %fold.7.one, f32[160,128]{1,0:T(8,128)S(1)} %collective-permute-done.13.two), custom_call_target="tpu_custom_call" | custom-call | flops 100000000 | bytes 8388608 | tf_op jit(solution)/shard_map/eliminate/pallas_call | solution.py:42
  75.2 0.0 collective-permute-done.14.got
  75.2 1.6 %collective-permute-start.15 = (f32[256,128]{1,0:T(8,128)S(1)}, f32[256,128]{1,0:T(8,128)S(1)}, u32[]{:S(2)}, u32[]{:S(2)}) collective-permute-start(f32[256,128]{1,0:T(8,128)S(1)} %unfold.3.stacked), channel_id=1, source_target_pairs={{0,1},{1,0},{2,3},{3,2},{4,5},{5,4},{6,7},{7,6},{8,9},{9,8},{10,11... | collective-permute-start | bytes 393224 | tf_op jit(solution)/shard_map/ppermute | solution.py:116
  76.8 2.9 %final.2 = (f32[1024,1024]{1,0:T(8,128)}, f32[1024,1024]{1,0:T(8,128)}, f32[64,1024]{1,0:T(8,128)}, f32[64,512]{1,0:T(8,128)S(1)}, f32[32,128]{1,0:T(8,128)S(1)}) custom-call(f32[64,64]{1,0:T(8,128)S(1)} %eliminate.3.inverse, f32[64,512]{1,0:T(8,128)S(1)} %collective-permute-done.10.away, f32[64,512]{1,0:T(8,128)S(1)} %add.8.mine, ...), custom_call_target="tpu_custom_call" | custom-call | flops 201326592 | bytes 4194304 | tf_op jit(solution)/shard_map/final/pallas_call | solution.py:42
  79.6 0.6 collective-permute-done.15.stacked
  80.2 0.8 widen.1
  81.0 0.0 collective-permute-start.16
  81.0 1.2 %collective-permute-done.16.refs_1_ = f32[32,128]{1,0:T(8,128)S(1)} collective-permute-done((f32[32,128]{1,0:T(8,128)S(1)}, f32[32,128]{1,0:T(8,128)S(1)}, u32[]{:S(2)}, u32[]{:S(2)}) %collective-permute-start.16) | collective-permute-done | bytes 16416 | tf_op jit(solution)/shard_map/ppermute | solution.py:116
  82.2 1.5 %collective-permute-start.17 = (f32[32,128]{1,0:T(8,128)S(1)}, f32[32,128]{1,0:T(8,128)S(1)}, u32[]{:S(2)}, u32[]{:S(2)}) collective-permute-start(f32[32,128]{1,0:T(8,128)S(1)} %add.9.one), channel_id=1, source_target_pairs={{0,16},{8,24},{16,0},{24,8},{1,17},{9,25},{17,1},{25,9},{2,18},{10... | collective-permute-start | bytes 49160 | tf_op jit(solution)/shard_map/ppermute | solution.py:116
  83.7 2.8 %final.3 = (f32[1024,1024]{1,0:T(8,128)}, f32[1024,1024]{1,0:T(8,128)}) custom-call(f32[64,64]{1,0:T(8,128)S(1)} %eliminate.3.inverse, f32[64,512]{1,0:T(8,128)S(1)} %collective-permute-done.10.away, f32[64,512]{1,0:T(8,128)S(1)} %add.8.mine, f32[256,128]{1,0:T(8,128)S(1)} %collective-permute-done.15.stacked, ...), custom_call_target="tpu_custom_call", output_to_operand_aliasing={{0}: (5, {}), {1}: (6, {})} | custom-call | flops 201326592 | bytes 4194304 | tf_op jit(solution)/shard_map/final/pallas_call | solution.py:42
  86.5 3.8 %finish.1 = f32[64,1024]{1,0:T(8,128)} custom-call(f32[32,128]{1,0:T(8,128)S(1)} %add.9.one, f32[32,128]{1,0:T(8,128)S(1)} %collective-permute-done.17.two, f32[64,512]{1,0:T(8,128)S(1)} %get-tuple-element.84.own, f32[64,512]{1,0:T(8,128)S(1)} %get-tuple-element.85.other), custom_call_target="tpu_custom_call" | custom-call | flops 100000000 | bytes 8388608 | tf_op jit(solution)/shard_map/finish/pallas_call | solution.py:42
  (14 shorter events, 0.2 us)
Async XLA Ops:
  6.9 1.5 %collective-permute-start = (f32[64,512]{1,0:T(8,128)S(1)}, f32[64,512]{1,0:T(8,128)S(1)}, u32[]{:S(2)}, u32[]{:S(2)}) collective-permute-start(f32[64,512]{1,0:T(8,128)S(1)} %get-tuple-element.46), channel_id=1, source_target_pairs={{0,8},{8,0},{16,24},{24,16},{1,9},{9,1},{17,25},{25,17},{2,10},{10... | collective-permute-start | bytes 393224 | tf_op jit(solution)/shard_map/ppermute | solution.py:116
  8.4 6.8 %collective-permute-start.1 = (f32[64,512]{1,0:T(8,128)S(1)}, f32[64,512]{1,0:T(8,128)S(1)}, u32[]{:S(2)}, u32[]{:S(2)}) collective-permute-start(f32[64,512]{1,0:T(8,128)S(1)} %add.5.refs_0_), channel_id=1, source_target_pairs={{0,16},{8,24},{16,0},{24,8},{1,17},{9,25},{17,1},{25,9},{2,18},{10... | collective-permute-start | bytes 393224 | tf_op jit(solution)/shard_map/ppermute | solution.py:199
  15.2 1.4 %collective-permute-start.2 = (f32[64,512]{1,0:T(8,128)S(1)}, f32[64,512]{1,0:T(8,128)S(1)}, u32[]{:S(2)}, u32[]{:S(2)}) collective-permute-start(f32[64,512]{1,0:T(8,128)S(1)} %add.6.mine), channel_id=1, source_target_pairs={{0,8},{8,0},{16,24},{24,16},{1,9},{9,1},{17,25},{25,17},{2,10},{10... | collective-permute-start | bytes 393224 | tf_op jit(solution)/shard_map/ppermute | solution.py:116
  17.3 5.9 %collective-permute-start.3 = (f32[288,128]{1,0:T(8,128)S(1)}, f32[288,128]{1,0:T(8,128)S(1)}, u32[]{:S(2)}, u32[]{:S(2)}) collective-permute-start(f32[288,128]{1,0:T(8,128)S(1)} %multiply.5.sent), channel_id=1, source_target_pairs={{0,1},{1,0},{2,3},{3,2},{4,5},{5,4},{6,7},{7,6},{8,9},{9,8},{10,11... | collective-permute-start | bytes 442376 | tf_op jit(solution)/shard_map/ppermute | solution.py:116
  23.2 4.5 %collective-permute-start.4 = (f32[160,128]{1,0:T(8,128)S(1)}, f32[160,128]{1,0:T(8,128)S(1)}, u32[]{:S(2)}, u32[]{:S(2)}) collective-permute-start(f32[160,128]{1,0:T(8,128)S(1)} %get-tuple-element.52.sent), channel_id=1, source_target_pairs={{0,2},{1,3},{2,0},{3,1},{4,6},{5,7},{6,4},{7,5},{8,10},{9,11},{10,... | collective-permute-start | bytes 245768 | tf_op jit(solution)/shard_map/ppermute | solution.py:116
  27.8 5.4 %collective-permute-start.5 = (f32[160,128]{1,0:T(8,128)S(1)}, f32[160,128]{1,0:T(8,128)S(1)}, u32[]{:S(2)}, u32[]{:S(2)}) collective-permute-start(f32[160,128]{1,0:T(8,128)S(1)} %fold.5.one), channel_id=1, source_target_pairs={{0,4},{1,5},{2,6},{3,7},{4,0},{5,1},{6,2},{7,3},{8,12},{9,13},{10,... | collective-permute-start | bytes 245768 | tf_op jit(solution)/shard_map/ppermute | solution.py:116
  33.2 4.7 %collective-permute-start.6 = (f32[128,128]{1,0:T(8,128)S(1)}, f32[128,128]{1,0:T(8,128)S(1)}, u32[]{:S(2)}, u32[]{:S(2)}) collective-permute-start(f32[128,128]{1,0:T(8,128)S(1)} %top.2.value), channel_id=1, source_target_pairs={{0,2},{1,3},{2,0},{3,1},{4,6},{5,7},{6,4},{7,5},{8,10},{9,11},{10,... | collective-permute-start | bytes 196616 | tf_op jit(solution)/shard_map/ppermute | solution.py:116
  37.9 5.0 %collective-permute-start.7 = (f32[256,128]{1,0:T(8,128)S(1)}, f32[256,128]{1,0:T(8,128)S(1)}, u32[]{:S(2)}, u32[]{:S(2)}) collective-permute-start(f32[256,128]{1,0:T(8,128)S(1)} %unfold.2.stacked), channel_id=1, source_target_pairs={{0,1},{1,0},{2,3},{3,2},{4,5},{5,4},{6,7},{7,6},{8,9},{9,8},{10,11... | collective-permute-start | bytes 393224 | tf_op jit(solution)/shard_map/ppermute | solution.py:116
  44.9 1.4 %collective-permute-start.8 = (f32[64,512]{1,0:T(8,128)S(1)}, f32[64,512]{1,0:T(8,128)S(1)}, u32[]{:S(2)}, u32[]{:S(2)}) collective-permute-start(f32[64,512]{1,0:T(8,128)S(1)} %get-tuple-element.60), channel_id=1, source_target_pairs={{0,8},{8,0},{16,24},{24,16},{1,9},{9,1},{17,25},{25,17},{2,10},{10... | collective-permute-start | bytes 393224 | tf_op jit(solution)/shard_map/ppermute | solution.py:116
  46.4 5.6 %collective-permute-start.9 = (f32[64,512]{1,0:T(8,128)S(1)}, f32[64,512]{1,0:T(8,128)S(1)}, u32[]{:S(2)}, u32[]{:S(2)}) collective-permute-start(f32[64,512]{1,0:T(8,128)S(1)} %add.7.refs_0_), channel_id=1, source_target_pairs={{0,16},{8,24},{16,0},{24,8},{1,17},{9,25},{17,1},{25,9},{2,18},{10... | collective-permute-start | bytes 393224 | tf_op jit(solution)/shard_map/ppermute | solution.py:199
  52.0 1.4 %collective-permute-start.10 = (f32[64,512]{1,0:T(8,128)S(1)}, f32[64,512]{1,0:T(8,128)S(1)}, u32[]{:S(2)}, u32[]{:S(2)}) collective-permute-start(f32[64,512]{1,0:T(8,128)S(1)} %add.8.mine), channel_id=1, source_target_pairs={{0,8},{8,0},{16,24},{24,16},{1,9},{9,1},{17,25},{25,17},{2,10},{10... | collective-permute-start | bytes 393224 | tf_op jit(solution)/shard_map/ppermute | solution.py:116
  54.1 5.9 %collective-permute-start.11 = (f32[288,128]{1,0:T(8,128)S(1)}, f32[288,128]{1,0:T(8,128)S(1)}, u32[]{:S(2)}, u32[]{:S(2)}) collective-permute-start(f32[288,128]{1,0:T(8,128)S(1)} %multiply.7.sent), channel_id=1, source_target_pairs={{0,1},{1,0},{2,3},{3,2},{4,5},{5,4},{6,7},{7,6},{8,9},{9,8},{10,11... | collective-permute-start | bytes 442376 | tf_op jit(solution)/shard_map/ppermute | solution.py:116
  60.0 4.5 %collective-permute-start.12 = (f32[160,128]{1,0:T(8,128)S(1)}, f32[160,128]{1,0:T(8,128)S(1)}, u32[]{:S(2)}, u32[]{:S(2)}) collective-permute-start(f32[160,128]{1,0:T(8,128)S(1)} %get-tuple-element.66.sent), channel_id=1, source_target_pairs={{0,2},{1,3},{2,0},{3,1},{4,6},{5,7},{6,4},{7,5},{8,10},{9,11},{10,... | collective-permute-start | bytes 245768 | tf_op jit(solution)/shard_map/ppermute | solution.py:116
  64.6 5.9 %collective-permute-start.13 = (f32[160,128]{1,0:T(8,128)S(1)}, f32[160,128]{1,0:T(8,128)S(1)}, u32[]{:S(2)}, u32[]{:S(2)}) collective-permute-start(f32[160,128]{1,0:T(8,128)S(1)} %fold.7.one), channel_id=1, source_target_pairs={{0,4},{1,5},{2,6},{3,7},{4,0},{5,1},{6,2},{7,3},{8,12},{9,13},{10,... | collective-permute-start | bytes 245768 | tf_op jit(solution)/shard_map/ppermute | solution.py:116
  70.4 4.7 %collective-permute-start.14 = (f32[128,128]{1,0:T(8,128)S(1)}, f32[128,128]{1,0:T(8,128)S(1)}, u32[]{:S(2)}, u32[]{:S(2)}) collective-permute-start(f32[128,128]{1,0:T(8,128)S(1)} %top.3.value), channel_id=1, source_target_pairs={{0,2},{1,3},{2,0},{3,1},{4,6},{5,7},{6,4},{7,5},{8,10},{9,11},{10,... | collective-permute-start | bytes 196616 | tf_op jit(solution)/shard_map/ppermute | solution.py:116
  75.2 5.0 %collective-permute-start.15 = (f32[256,128]{1,0:T(8,128)S(1)}, f32[256,128]{1,0:T(8,128)S(1)}, u32[]{:S(2)}, u32[]{:S(2)}) collective-permute-start(f32[256,128]{1,0:T(8,128)S(1)} %unfold.3.stacked), channel_id=1, source_target_pairs={{0,1},{1,0},{2,3},{3,2},{4,5},{5,4},{6,7},{7,6},{8,9},{9,8},{10,11... | collective-permute-start | bytes 393224 | tf_op jit(solution)/shard_map/ppermute | solution.py:116
  81.0 1.2 %collective-permute-start.16 = (f32[32,128]{1,0:T(8,128)S(1)}, f32[32,128]{1,0:T(8,128)S(1)}, u32[]{:S(2)}, u32[]{:S(2)}) collective-permute-start(f32[32,128]{1,0:T(8,128)S(1)} %get-tuple-element.83.refs_0_), channel_id=1, source_target_pairs={{0,8},{8,0},{16,24},{24,16},{1,9},{9,1},{17,25},{25,17},{2,10},{10... | collective-permute-start | bytes 49160 | tf_op jit(solution)/shard_map/ppermute | solution.py:116
  82.2 4.3 %collective-permute-start.17 = (f32[32,128]{1,0:T(8,128)S(1)}, f32[32,128]{1,0:T(8,128)S(1)}, u32[]{:S(2)}, u32[]{:S(2)}) collective-permute-start(f32[32,128]{1,0:T(8,128)S(1)} %add.9.one), channel_id=1, source_target_pairs={{0,16},{8,24},{16,0},{24,8},{1,17},{9,25},{17,1},{25,9},{2,18},{10... | collective-permute-start | bytes 49160 | tf_op jit(solution)/shard_map/ppermute | solution.py:116

commit v7 on v6

--- a/solution.py
+++ b/solution.py
@@ -12,6 +12,7 @@
 TAU = 0.6 / 1.25
 HIGH = lax.Precision.HIGHEST
 CORES = 2
+STREAMS = 2
 LANES = 128
 F32, BF16 = jnp.float32, jnp.bfloat16
 MIB = 1 << 20
@@ -102,9 +103,13 @@
     return jnp.concatenate([gram[:rows], gram[rows:]], axis=1)
 
 
-def unstack(ref):
-    blocks = ref.shape[0] // 64
-    return jnp.concatenate([ref[64 * t : 64 * (t + 1), :] for t in range(blocks)], axis=1)
+def unstack(ref, rank):
+    part, rows = rank // STREAMS, ref.shape[0] // STREAMS
+    parts = []
+    for at in range(0, STREAMS * rows, rows):
+        blocks = [ref[at + t : at + t + part, :] for t in range(0, rows, part)]
+        parts.append(jnp.concatenate(blocks, axis=1))
+    return jnp.concatenate(parts, axis=0)
 
 
 def solution(mesh):
@@ -121,7 +126,8 @@
         half = n_cols // 2
         tall = min(256, n_rows // 2)
         steps = n_rows // tall
-        stack_rows = rank * (half // LANES)
+        part_rank = rank // STREAMS
+        part_rows = part_rank * (half // LANES)
         gram_rows = rank * rank // LANES
 
         def place():
@@ -139,7 +145,11 @@
             return slice(tall * i, tall * (i + 1))
 
         def join(pair):
-            return jnp.concatenate([half[...] for half in pair], axis=1)
+            rows = [jnp.concatenate([pair[at][...], pair[at + 1][...]], axis=1) for at in range(0, len(pair), 2)]
+            return jnp.concatenate(rows, axis=0)
+
+        def part_of(k):
+            return slice(part_rank * k, part_rank * (k + 1))
 
         def small(body, name, ins, rows, scratch=()):
             outs = [((n, LANES), F32, pltpu.VMEM) for n in rows]
@@ -157,8 +167,9 @@
             return call(body, "add", [(a, pltpu.VMEM) for a in arrays], [out], cost=(10**5, 10**6), limit=4)[0]
 
         def first(right):
-            def body(o_in, s_in, d_in, r_in, o, d, h0, l0, h1, l1, away, mine, sp, right, r_sem, sems):
-                s = place()
+            def body(o_in, s_in, d_in, r_in, o, d, h0, l0, h1, l1, *rest):
+                s = place()
+                *parts, sp, right, r_sem, sems = rest
                 right_move = pltpu.make_async_copy(r_in, right, r_sem)
                 right_move.start()
                 moves = {}
@@ -180,19 +191,22 @@
                         h[chunk(i), :], l[chunk(i), :] = pair
                         term = dot_nt(rights[p], pair)
                         total = term if total is None else total + term
-                    out = away if i < steps // 2 else mine
-                    out[:, chunk(i % (steps // 2))] = total
+                    side, block = divmod(i, steps // 2)
+                    for k in range(STREAMS):
+                        parts[2 * k + side][:, chunk(block)] = total[part_of(k)]
 
             ins = [(a, pltpu.HBM) for a in (observed, sparse_init, dual_init, right)]
             outs = [((n_rows, n_cols), F32, pltpu.VMEM)] * 2 + [((n_rows, half), BF16, pltpu.VMEM)] * 4
-            outs += [((rank, n_rows // 2), F32, pltpu.VMEM)] * 2
+            outs += [((part_rank, n_rows // 2), F32, pltpu.VMEM)] * (2 * STREAMS)
             scratch = [pltpu.VMEM((n_rows, n_cols), F32), pltpu.VMEM((rank, n_cols), F32)]
             scratch += [pltpu.SemaphoreType.DMA(()), pltpu.SemaphoreType.DMA((steps, 3))]
             cost = (6 * rank * n_rows * n_cols, 16 * n_rows * n_cols)
             got = call(body, "first", ins, outs, scratch, cost=cost)
-            return got[0], got[1], got[2:4], got[4:6], got[6:8]
+            return got[0], got[1], got[2:4], got[4:6], got[6:]
 
         def sum_gal(part):
+            if len(part) > 2:
+                return *sum_gal(part[:2]), *sum_gal(part[2:])
             away, mine = part
             mine = add(mine, swap(away, "gal", 1))
             got = [
@@ -202,21 +216,24 @@
             mine = add(mine, *got)
             return swap(mine, "gal", 1), mine
 
-        def multiply(panel, pair, with_gram):
-            def body(away, mine, high, low, out):
-                panel = join((away, mine))
-                total = dot_nn(split(panel), (high[...], low[...]))
-                for t in range(half // LANES):
-                    out[rank * t : rank * (t + 1), :] = total[:, LANES * t : LANES * (t + 1)]
-                if with_gram:
-                    gram = dot(panel, panel, ((1,), (1,)), HIGH)
-                    out[stack_rows : stack_rows + gram_rows, :] = pack(gram)
-
-            rows = stack_rows + (gram_rows if with_gram else 0)
-            ins = [(a, pltpu.VMEM) for a in (*panel, *pair)]
-            outs = [((rows, LANES), F32, pltpu.VMEM)]
+        def multiply(panel, pair, streams, gram_too, after=()):
+            def body(*refs):
+                *parts, high, low = refs[: len(panel) + 2]
+                outs = refs[len(panel) + 2 + len(after) :]
+                total = dot_nn(split(join(parts[-2 * streams :])), (high[...], low[...]))
+                for k, out in enumerate(outs):
+                    for t in range(half // LANES):
+                        out[part_of(t), :] = total[part_of(k), LANES * t : LANES * (t + 1)]
+                if gram_too:
+                    whole = join(parts)
+                    outs[-1][part_rows:, :] = pack(dot(whole, whole, ((1,), (1,)), HIGH))
+
+            ins = [(a, pltpu.VMEM) for a in (*panel, *pair, *after)]
+            outs = [((part_rows, LANES), F32, pltpu.VMEM)] * streams
+            if gram_too:
+                outs[-1] = ((part_rows + gram_rows, LANES), F32, pltpu.VMEM)
             cost = (3 * rank * n_rows * n_cols, 2 * n_rows * n_cols)
-            return call(body, "multiply", ins, outs, cost=cost)[0]
+            return call(body, "multiply", ins, outs, cost=cost)
 
         def eliminate(one, two):
             def body(one, two, out):
@@ -228,6 +245,7 @@
 
         def fold(level, value, sent, got):
             rows = value.shape[0]
+            extra = sent.shape[0] - got_rows(level)
             last = level == levels - 1
             keep = rows if last else rows // 2
 
@@ -240,41 +258,49 @@
                     for mine, out in ((s[1 + level], outs[0]), (1 - s[1 + level], message)):
                         at = pl.ds(pl.multiple_of(mine * keep, keep), keep)
                         out[:keep, :] = value[at, :] + got[at, :]
-                message[keep:, :] = sent[rows_of(sent), :] + got[rows_of(got), :]
-
-            def rows_of(ref):
-                return slice(ref.shape[0] - gram_rows, ref.shape[0])
+                if extra:
+                    message[keep:, :] = sent[rows:, :] + got[rows:, :]
 
             ins = [(a, pltpu.VMEM) for a in (value, sent, got)]
-            outs = small(body, "fold", ins, [keep + gram_rows] if last else [keep, keep + gram_rows])
+            outs = small(body, "fold", ins, [keep + extra] if last else [keep, keep + extra])
             return outs[0], outs[-1]
 
+        def got_rows(level):
+            return part_rows >> (level - 1)
+
+        def merge(sent, got):
+            rows = got_rows(levels - 1)
+
+            def body(*refs):
+                *ins, out = refs
+                for k in range(STREAMS):
+                    out[rows * k : rows * (k + 1), :] = ins[2 * k][:rows, :] + ins[2 * k + 1][:rows, :]
+
+            ins = [(a, pltpu.VMEM) for pair in zip(sent, got) for a in pair]
+            return small(body, "merge", ins, [rows * STREAMS])[0]
+
         def unfold(level, value, got):
-            rows = value.shape[0]
+            rows = value.shape[0] // STREAMS
 
             def body(value, got, out):
                 s = place()
                 for mine, ref in ((s[1 + level], value), (1 - s[1 + level], got)):
-                    out[pl.ds(pl.multiple_of(mine * rows, rows), rows), :] = ref[...]
+                    for k in range(STREAMS):
+                        at = pl.multiple_of(mine * rows + 2 * rows * k, rows)
+                        out[pl.ds(at, rows), :] = ref[rows * k : rows * (k + 1), :]
 
             ins = [(value, pltpu.VMEM), (got, pltpu.VMEM)]
-            return small(body, "unfold", ins, [2 * rows])[0]
-
-        def top(one, two):
-            rows = one.shape[0] - gram_rows
-
-            def body(one, two, out):
-                out[...] = one[:rows, :] + two[:rows, :]
-
-            return small(body, "top", [(one, pltpu.VMEM), (two, pltpu.VMEM)], [rows])[0]
-
-        def sum_pix(send, own):
-            value, sent = own, send
+            return small(body, "unfold", ins, [2 * STREAMS * rows])[0]
+
+        def sum_pix(sends, owns):
+            values, sents = list(owns), list(sends)
             for level in range(1, levels):
-                value, sent = fold(level, value, sent, swap(sent, "pix", 1 << (level - 1)))
-            got = swap(sent, "pix", 1 << (levels - 1))
-            value = top(sent, got)
-            inverse = eliminate(sent, got)
+                for k in range(STREAMS):
+                    got = swap(sents[k], "pix", 1 << (level - 1))
+                    values[k], sents[k] = fold(level, values[k], sents[k], got)
+            gots = [swap(sent, "pix", 1 << (levels - 1)) for sent in sents]
+            value = merge(sents, gots)
+            inverse = eliminate(sents[-1], gots[-1])
             for level in range(levels - 2, 0, -1):
                 value = unfold(level, value, swap(value, "pix", 1 << level))
             value, inverse = lax.optimization_barrier((value, inverse))
@@ -282,17 +308,20 @@
 
         def halves(inverse, panel, stacked):
             left = dot(inverse[...], join(panel), ((1,), (0,)), HIGH)
-            wide = dot(inverse[...], unstack(stacked), ((1,), (0,)), HIGH)
+            wide = dot(inverse[...], unstack(stacked, rank), ((1,), (0,)), HIGH)
             left_high, left_low = split(left)
             wide_high, wide_low = split(wide)
             tops = jnp.concatenate([left_high, left_low, left_high], axis=0)
             return left, wide, (wide_high, wide_low), tops, jnp.concatenate([wide_high, wide_high, wide_low], axis=0)
 
         def middle(p, inverse, panel, stacked, o, d, before):
-            def body(inverse, away, mine, stacked, o, d, *rest):
-                s = place()
-                base, high, low, *after = rest[2 * p :]
-                _, _, right, tops, wides = halves(inverse, (away, mine), stacked)
+            n = len(panel)
+
+            def body(inverse, *rest):
+                s = place()
+                parts, (stacked, o, d, *rest) = rest[:n], rest[n:]
+                base, high, low, *after = rest[n * p :]
+                _, _, right, tops, wides = halves(inverse, parts, stacked)
                 for i in range(steps):
                     lowrank = dot(tops[:, chunk(i)], wides, ((0,), (0,)))
                     at = chunk(i), pl.ds(pix_at(p, s), half)
@@ -304,21 +333,27 @@
                     high[chunk(i), :], low[chunk(i), :] = pair
                     term = dot_nt(right, pair)
                     side, block = divmod(i, steps // 2)
-                    after[side][:, chunk(block)] = rest[side][:, chunk(block)] + term if p else term
+                    for k in range(STREAMS):
+                        at = 2 * k + side, (slice(None), chunk(block))
+                        new = term[part_of(k)]
+                        after[at[0]][at[1]] = rest[at[0]][at[1]] + new if p else new
 
             arrays = [inverse, *panel, stacked, o, d] + (list(before) if p else [])
             outs = [((n_rows, half), F32, pltpu.VMEM)] + [((n_rows, half), BF16, pltpu.VMEM)] * 2
-            outs += [((rank, n_rows // 2), F32, pltpu.VMEM)] * 2
+            outs += [((part_rank, n_rows // 2), F32, pltpu.VMEM)] * n
             cost = (9 * rank * n_rows * n_cols, 4 * n_rows * n_cols)
             ins = [(a, pltpu.VMEM) for a in arrays]
             base, high, low, *part = call(body, "middle", ins, outs, cost=cost)
             return base, (high, low), part
 
         def final(p, inverse, panel, stacked, base, before):
-            def body(inverse, away, mine, stacked, base, *rest):
-                s = place()
+            n = len(panel)
+
+            def body(inverse, *rest):
+                s = place()
+                parts, (stacked, base, *rest) = rest[:n], rest[n:]
                 sparse, dual, *outs, sparse_part, dual_part, left_part, sems = rest[2 * p :]
-                left, wide, _, tops, wides = halves(inverse, (away, mine), stacked)
+                left, wide, _, tops, wides = halves(inverse, parts, stacked)
                 moves = []
                 if not p:
                     outs[1][...] = wide
@@ -345,7 +380,7 @@
             aliases = {}
             if p:
                 ins += [(a, pltpu.HBM) for a in before[:2]]
-                aliases = {5: 0, 6: 1}
+                aliases = {n + 3: 0, n + 4: 1}
             else:
                 outs += [((rank, n_rows), F32, pltpu.HBM), ((rank, half), F32, pltpu.VMEM)]
                 outs += [((gram_rows, LANES), F32, pltpu.VMEM)]
@@ -356,7 +391,7 @@
 
         def widen(inverse, other, gram):
             def body(inverse, stacked, gram, wide, out):
-                wide[...] = dot(inverse[...], unstack(stacked), ((1,), (0,)), HIGH)
+                wide[...] = dot(inverse[...], unstack(stacked, rank), ((1,), (0,)), HIGH)
                 out[...] = gram[...] + pack(dot(wide[...], wide[...], ((1,), (1,)), HIGH))
 
             ins = [(a, pltpu.VMEM) for a in (inverse, other, gram)]
@@ -382,8 +417,9 @@
         base = [None, None]
         for step in range(ITERS):
             panel = sum_gal(part)
-            send = multiply(panel, other, True)
-            inverse, own_wide, other_wide = sum_pix(send, multiply(panel, own, False))
+            sends = multiply(panel[:2], other, 1, False)
+            sends += multiply(panel, other, 1, True, sends)
+            inverse, own_wide, other_wide = sum_pix(sends, multiply(panel, own, STREAMS, False))
             if step < ITERS - 1:
                 base[0], own, part = middle(0, inverse, panel, own_wide, seen, pulls, None)
                 base[1], other, part = middle(1, inverse, panel, other_wide, seen, pulls, part)

time: 90.7 us -> 90.7 us (level)
  waiting for transfers between devices: 34.4 us -> 31.1 us
  starting transfers between devices: 26.6 us -> 28.9 us
    ppermute x16 -> x26, waiting for transfers between devices: 26.6 us -> 23.6 us  [swap(): return lax.ppermute(value, axis, [(i, i ^ bit) for i in range(n)])]
    ppermute x16 -> x26, starting transfers between devices: 22.1 us -> 23.7 us  [swap(): return lax.ppermute(value, axis, [(i, i ^ bit) for i in range(n)])]
    pallas_call x26 -> x36, Pallas kernels: 28.6 us -> 29.5 us  [call(): pl.pallas_call(body, name=name, in_specs=[pl.BlockSpec(memory_space=space...]
    ppermute x2 -> x4, starting transfers between devices: 4.53 us -> 5.23 us  [sum_gal(): lax.ppermute(mine, 'gal', [(i, (i + CORES * k) % n_gal) for i in range(n_...]
    ppermute x2 -> x4, waiting for transfers between devices: 7.84 us -> 7.57 us  [sum_gal(): lax.ppermute(mine, 'gal', [(i, (i + CORES * k) % n_gal) for i in range(n_...]
  transfers between devices with their start and end apart: 18 -> 30, of which waited for: 15 -> 20; matrix products, arithmetic and copies ran while one was open for 0% -> 0% of each run, Pallas kernels for 16% -> 17%
where the time goes in v7:
time: 90.7 us; the launch traced here: 90.5 us
  waiting for transfers between devices  31.1 us (34%)
  Pallas kernels  29.5 us (33%)
  starting transfers between devices  28.9 us (32%)
  between operations  1.01 us (1%)
    pallas_call x36, Pallas kernels, call(): pl.pallas_call(body, name=name, in_specs=[pl.BlockSpec(memory_space=space...  29.5 us
    ppermute x26, starting transfers between devices, swap(): return lax.ppermute(value, axis, [(i, i ^ bit) for i in range(n)])  23.7 us
    ppermute x26, waiting for transfers between devices, swap(): return lax.ppermute(value, axis, [(i, i ^ bit) for i in range(n)])  23.6 us
    ppermute x4, waiting for transfers between devices, sum_gal(): lax.ppermute(mine, 'gal', [(i, (i + CORES * k) % n_gal) for i in range(n_...  7.57 us
    ppermute x4, starting transfers between devices, sum_gal(): lax.ppermute(mine, 'gal', [(i, (i + CORES * k) % n_gal) for i in range(n_...  5.23 us
  transfers between devices with their start and end apart: 30, of which 20 were waited for; matrix products, arithmetic and copies ran while one was open for 0% of the time, Pallas kernels for 17%

profile of v7, /device:TPU:0, one launch (start us, length us, event | category | flops | bytes accessed | tf_op | source)
XLA Modules:
  0.0 90.5 jit_solution(16725715553875896294)
XLA Ops:
  0.6 6.3 %first.1 = (f32[1024,1024]{1,0:T(8,128)S(1)}, f32[1024,1024]{1,0:T(8,128)S(1)}, bf16[1024,512]{1,0:T(8,128)(2,1)S(1)}, bf16[1024,512]{1,0:T(8,128)(2,1)S(1)}, bf...) custom-call(f32[1024,1024]{1,0:T(8,128)} %o_in.1, ...), custom_call_target="tpu_custom_call" | custom-call | flops 402653184 | bytes 16777216 | tf_op jit(solution)/shard_map/first/pallas_call | solution.py:43
  6.9 0.5 collective-permute-start
  7.5 0.8 collective-permute-done.refs_1_
  8.3 2.9 %collective-permute-start.1 = (f32[32,512]{1,0:T(8,128)S(1)}, f32[32,512]{1,0:T(8,128)S(1)}, u32[]{:S(2)}, u32[]{:S(2)}) collective-permute-start(f32[32,512]{1,0:T(8,128)S(1)} %add.9.refs_0_), channel_id=1, source_target_pairs={{0,16},{8,24},{16,0},{24,8},{1,17},{9,25},{17,1},{25,9},{2,18},{10... | collective-permute-start | bytes 196616 | tf_op jit(solution)/shard_map/ppermute | solution.py:213
  11.4 2.3 %collective-permute-done.1.refs_1_ = f32[32,512]{1,0:T(8,128)S(1)} collective-permute-done((f32[32,512]{1,0:T(8,128)S(1)}, f32[32,512]{1,0:T(8,128)S(1)}, u32[]{:S(2)}, u32[]{:S(2)}) %collective-permute-start.1) | collective-permute-done | bytes 65568 | tf_op jit(solution)/shard_map/ppermute | solution.py:213
  13.8 1.8 %collective-permute-done.4.refs_1_ = f32[32,512]{1,0:T(8,128)S(1)} collective-permute-done((f32[32,512]{1,0:T(8,128)S(1)}, f32[32,512]{1,0:T(8,128)S(1)}, u32[]{:S(2)}, u32[]{:S(2)}) %collective-permute-start.4) | collective-permute-done | bytes 65568 | tf_op jit(solution)/shard_map/ppermute | solution.py:213
  16.2 0.8 collective-permute-done.5.refs_2_.rest_2_
  17.0 0.7 multiply.8.sent
  17.7 1.5 %collective-permute-start.9 = (f32[160,128]{1,0:T(8,128)S(1)}, f32[160,128]{1,0:T(8,128)S(1)}, u32[]{:S(2)}, u32[]{:S(2)}) collective-permute-start(f32[160,128]{1,0:T(8,128)S(1)} %multiply.8.sent), channel_id=1, source_target_pairs={{0,1},{1,0},{2,3},{3,2},{4,5},{5,4},{6,7},{7,6},{8,9},{9,8},{10,11... | collective-permute-start | bytes 245768 | tf_op jit(solution)/shard_map/ppermute | solution.py:121
  19.2 0.5 collective-permute-start.6
  20.2 2.6 %collective-permute-done.9.got = f32[160,128]{1,0:T(8,128)S(1)} collective-permute-done((f32[160,128]{1,0:T(8,128)S(1)}, f32[160,128]{1,0:T(8,128)S(1)}, u32[]{:S(2)}, u32[]{:S(2)}) %collective-permute-start.9) | collective-permute-done | bytes 81952 | tf_op jit(solution)/shard_map/ppermute | solution.py:121
  22.8 1.6 %collective-permute-start.10 = (f32[96,128]{1,0:T(8,128)S(1)}, f32[96,128]{1,0:T(8,128)S(1)}, u32[]{:S(2)}, u32[]{:S(2)}) collective-permute-start(f32[96,128]{1,0:T(8,128)S(1)} %get-tuple-element.72.sent), channel_id=1, source_target_pairs={{0,2},{1,3},{2,0},{3,1},{4,6},{5,7},{6,4},{7,5},{8,10},{9,11},{10,... | collective-permute-start | bytes 147464 | tf_op jit(solution)/shard_map/ppermute | solution.py:121
  24.4 0.8 collective-permute-start.7
  25.2 1.7 %collective-permute-done.10.got = f32[96,128]{1,0:T(8,128)S(1)} collective-permute-done((f32[96,128]{1,0:T(8,128)S(1)}, f32[96,128]{1,0:T(8,128)S(1)}, u32[]{:S(2)}, u32[]{:S(2)}) %collective-permute-start.10) | collective-permute-done | bytes 49184 | tf_op jit(solution)/shard_map/ppermute | solution.py:121
  26.9 2.7 %collective-permute-start.11 = (f32[96,128]{1,0:T(8,128)S(1)}, f32[96,128]{1,0:T(8,128)S(1)}, u32[]{:S(2)}, u32[]{:S(2)}) collective-permute-start(f32[96,128]{1,0:T(8,128)S(1)} %fold.11.refs_2_.one), channel_id=1, source_target_pairs={{0,4},{1,5},{2,6},{3,7},{4,0},{5,1},{6,2},{7,3},{8,12},{9,13},{10,... | collective-permute-start | bytes 147464 | tf_op jit(solution)/shard_map/ppermute | solution.py:121
  29.6 1.4 %collective-permute-start.8 = (f32[64,128]{1,0:T(8,128)S(1)}, f32[64,128]{1,0:T(8,128)S(1)}, u32[]{:S(2)}, u32[]{:S(2)}) collective-permute-start(f32[64,128]{1,0:T(8,128)S(1)} %fold.9.refs_0_), channel_id=1, source_target_pairs={{0,4},{1,5},{2,6},{3,7},{4,0},{5,1},{6,2},{7,3},{8,12},{9,13},{10,... | collective-permute-start | bytes 98312 | tf_op jit(solution)/shard_map/ppermute | solution.py:121
  31.0 3.5 %collective-permute-done.8.refs_1_ = f32[64,128]{1,0:T(8,128)S(1)} collective-permute-done((f32[64,128]{1,0:T(8,128)S(1)}, f32[64,128]{1,0:T(8,128)S(1)}, u32[]{:S(2)}, u32[]{:S(2)}) %collective-permute-start.8) | collective-permute-done | bytes 32800 | tf_op jit(solution)/shard_map/ppermute | solution.py:121
  34.5 1.7 %collective-permute-start.12 = (f32[128,128]{1,0:T(8,128)S(1)}, f32[128,128]{1,0:T(8,128)S(1)}, u32[]{:S(2)}, u32[]{:S(2)}) collective-permute-start(f32[128,128]{1,0:T(8,128)S(1)} %merge.2.value), channel_id=1, source_target_pairs={{0,2},{1,3},{2,0},{3,1},{4,6},{5,7},{6,4},{7,5},{8,10},{9,11},{10,... | collective-permute-start | bytes 196616 | tf_op jit(solution)/shard_map/ppermute | solution.py:121
  36.2 2.8 %eliminate.2.inverse = f32[64,64]{1,0:T(8,128)S(1)} custom-call(f32[96,128]{1,0:T(8,128)S(1)} %fold.11.refs_2_.one, f32[96,128]{1,0:T(8,128)S(1)} %collective-permute-done.11.refs_3_.two), custom_call_target="tpu_custom_call" | custom-call | flops 100000000 | bytes 8388608 | tf_op jit(solution)/shard_map/eliminate/pallas_call | solution.py:43
  39.0 1.7 %collective-permute-start.13 = (f32[256,128]{1,0:T(8,128)S(1)}, f32[256,128]{1,0:T(8,128)S(1)}, u32[]{:S(2)}, u32[]{:S(2)}) collective-permute-start(f32[256,128]{1,0:T(8,128)S(1)} %unfold.2.rest_4_), channel_id=1, source_target_pairs={{0,1},{1,0},{2,3},{3,2},{4,5},{5,4},{6,7},{7,6},{8,9},{9,8},{10,11... | collective-permute-start | bytes 393224 | tf_op jit(solution)/shard_map/ppermute | solution.py:121
  40.6 2.0 %middle.2 = (f32[1024,512]{1,0:T(8,128)S(1)}, bf16[1024,512]{1,0:T(8,128)(2,1)S(1)}, bf16[1024,512]{1,0:T(8,128)(2,1)S(1)}, f32[32,512]{1,0:T(8,128)S(1)}, f32[3...) custom-call(f32[64,64]{1,0:T(8,128)S(1)} %eliminate.2.inverse, ...), custom_call_target="tpu_custom_call" | custom-call | flops 603979776 | bytes 4194304 | tf_op jit(solution)/shard_map/middle/pallas_call | solution.py:43
  42.6 1.4 %collective-permute-done.13.rest_4_ = f32[256,128]{1,0:T(8,128)S(1)} collective-permute-done((f32[256,128]{1,0:T(8,128)S(1)}, f32[256,128]{1,0:T(8,128)S(1)}, u32[]{:S(2)}, u32[]{:S(2)}) %collective-permute-start.13) | collective-permute-done | bytes 131104 | tf_op jit(solution)/shard_map/ppermute | solution.py:121
  44.0 2.0 %middle.3 = (f32[1024,512]{1,0:T(8,128)S(1)}, bf16[1024,512]{1,0:T(8,128)(2,1)S(1)}, bf16[1024,512]{1,0:T(8,128)(2,1)S(1)}, f32[32,512]{1,0:T(8,128)S(1)}, f32[3...) custom-call(f32[64,64]{1,0:T(8,128)S(1)} %eliminate.2.inverse, ...), custom_call_target="tpu_custom_call" | custom-call | flops 603979776 | bytes 4194304 | tf_op jit(solution)/shard_map/middle/pallas_call | solution.py:43
  46.6 0.7 collective-permute-done.14.refs_1_
  47.4 1.3 %collective-permute-start.15 = (f32[32,512]{1,0:T(8,128)S(1)}, f32[32,512]{1,0:T(8,128)S(1)}, u32[]{:S(2)}, u32[]{:S(2)}) collective-permute-start(f32[32,512]{1,0:T(8,128)S(1)} %add.13.refs_0_), channel_id=1, source_target_pairs={{0,16},{8,24},{16,0},{24,8},{1,17},{9,25},{17,1},{25,9},{2,18},{10... | collective-permute-start | bytes 196616 | tf_op jit(solution)/shard_map/ppermute | solution.py:213
  48.7 0.9 collective-permute-start.18
  49.5 2.6 %collective-permute-done.15.refs_1_ = f32[32,512]{1,0:T(8,128)S(1)} collective-permute-done((f32[32,512]{1,0:T(8,128)S(1)}, f32[32,512]{1,0:T(8,128)S(1)}, u32[]{:S(2)}, u32[]{:S(2)}) %collective-permute-start.15) | collective-permute-done | bytes 65568 | tf_op jit(solution)/shard_map/ppermute | solution.py:213
  52.3 0.8 collective-permute-done.18.refs_1_
  54.4 0.7 multiply.11.sent
  55.2 1.6 %collective-permute-start.23 = (f32[160,128]{1,0:T(8,128)S(1)}, f32[160,128]{1,0:T(8,128)S(1)}, u32[]{:S(2)}, u32[]{:S(2)}) collective-permute-start(f32[160,128]{1,0:T(8,128)S(1)} %multiply.11.sent), channel_id=1, source_target_pairs={{0,1},{1,0},{2,3},{3,2},{4,5},{5,4},{6,7},{7,6},{8,9},{9,8},{10,11... | collective-permute-start | bytes 245768 | tf_op jit(solution)/shard_map/ppermute | solution.py:121
  57.6 2.5 %collective-permute-done.23.got = f32[160,128]{1,0:T(8,128)S(1)} collective-permute-done((f32[160,128]{1,0:T(8,128)S(1)}, f32[160,128]{1,0:T(8,128)S(1)}, u32[]{:S(2)}, u32[]{:S(2)}) %collective-permute-start.23) | collective-permute-done | bytes 81952 | tf_op jit(solution)/shard_map/ppermute | solution.py:121
  60.2 1.5 %collective-permute-start.24 = (f32[96,128]{1,0:T(8,128)S(1)}, f32[96,128]{1,0:T(8,128)S(1)}, u32[]{:S(2)}, u32[]{:S(2)}) collective-permute-start(f32[96,128]{1,0:T(8,128)S(1)} %get-tuple-element.94.sent), channel_id=1, source_target_pairs={{0,2},{1,3},{2,0},{3,1},{4,6},{5,7},{6,4},{7,5},{8,10},{9,11},{10,... | collective-permute-start | bytes 147464 | tf_op jit(solution)/shard_map/ppermute | solution.py:121
  61.7 0.9 collective-permute-start.21
  62.6 1.7 %collective-permute-done.24.got = f32[96,128]{1,0:T(8,128)S(1)} collective-permute-done((f32[96,128]{1,0:T(8,128)S(1)}, f32[96,128]{1,0:T(8,128)S(1)}, u32[]{:S(2)}, u32[]{:S(2)}) %collective-permute-start.24) | collective-permute-done | bytes 49184 | tf_op jit(solution)/shard_map/ppermute | solution.py:121
  64.3 1.1 %collective-permute-start.25 = (f32[96,128]{1,0:T(8,128)S(1)}, f32[96,128]{1,0:T(8,128)S(1)}, u32[]{:S(2)}, u32[]{:S(2)}) collective-permute-start(f32[96,128]{1,0:T(8,128)S(1)} %fold.15.refs_2_.one), channel_id=1, source_target_pairs={{0,4},{1,5},{2,6},{3,7},{4,0},{5,1},{6,2},{7,3},{8,12},{9,13},{10,... | collective-permute-start | bytes 147464 | tf_op jit(solution)/shard_map/ppermute | solution.py:121
  65.5 0.8 collective-permute-done.21.got
  66.3 1.2 %collective-permute-start.22 = (f32[64,128]{1,0:T(8,128)S(1)}, f32[64,128]{1,0:T(8,128)S(1)}, u32[]{:S(2)}, u32[]{:S(2)}) collective-permute-start(f32[64,128]{1,0:T(8,128)S(1)} %fold.13.refs_0_), channel_id=1, source_target_pairs={{0,4},{1,5},{2,6},{3,7},{4,0},{5,1},{6,2},{7,3},{8,12},{9,13},{10,... | collective-permute-start | bytes 98312 | tf_op jit(solution)/shard_map/ppermute | solution.py:121
  67.4 4.0 %collective-permute-done.22.refs_1_ = f32[64,128]{1,0:T(8,128)S(1)} collective-permute-done((f32[64,128]{1,0:T(8,128)S(1)}, f32[64,128]{1,0:T(8,128)S(1)}, u32[]{:S(2)}, u32[]{:S(2)}) %collective-permute-start.22) | collective-permute-done | bytes 32800 | tf_op jit(solution)/shard_map/ppermute | solution.py:121
  71.4 0.6 collective-permute-start.26
  72.0 3.0 %eliminate.3.inverse = f32[64,64]{1,0:T(8,128)S(1)} custom-call(f32[96,128]{1,0:T(8,128)S(1)} %fold.15.refs_2_.one, f32[96,128]{1,0:T(8,128)S(1)} %collective-permute-done.25.refs_3_.two), custom_call_target="tpu_custom_call" | custom-call | flops 100000000 | bytes 8388608 | tf_op jit(solution)/shard_map/eliminate/pallas_call | solution.py:43
  75.0 0.8 collective-permute-done.26.got
  75.8 1.8 %collective-permute-start.27 = (f32[256,128]{1,0:T(8,128)S(1)}, f32[256,128]{1,0:T(8,128)S(1)}, u32[]{:S(2)}, u32[]{:S(2)}) collective-permute-start(f32[256,128]{1,0:T(8,128)S(1)} %unfold.3.rest_4_), channel_id=1, source_target_pairs={{0,1},{1,0},{2,3},{3,2},{4,5},{5,4},{6,7},{7,6},{8,9},{9,8},{10,11... | collective-permute-start | bytes 393224 | tf_op jit(solution)/shard_map/ppermute | solution.py:121
  77.6 2.9 %final.2 = (f32[1024,1024]{1,0:T(8,128)}, f32[1024,1024]{1,0:T(8,128)}, f32[64,1024]{1,0:T(8,128)}, f32[64,512]{1,0:T(8,128)S(1)}, f32[32,128]{1,0:T(8,128)S(1)}) custom-call(f32[64,64]{1,0:T(8,128)S(1)} %eliminate.3.inverse, f32[32,512]{1,0:T(8,128)S(1)} %collective-permute-done.16.refs_0_.rest_0_, f32[32,512]{1,0:T(8,128)S(1)} %add.14.refs_1_.rest_1_, ...), custom_call_target="tpu_custom_call" | custom-call | flops 201326592 | bytes 4194304 | tf_op jit(solution)/shard_map/final/pallas_call | solution.py:43
  80.8 0.6 widen.1
  81.4 1.2 %collective-permute-done.28.refs_1_ = f32[32,128]{1,0:T(8,128)S(1)} collective-permute-done((f32[32,128]{1,0:T(8,128)S(1)}, f32[32,128]{1,0:T(8,128)S(1)}, u32[]{:S(2)}, u32[]{:S(2)}) %collective-permute-start.28) | collective-permute-done | bytes 16416 | tf_op jit(solution)/shard_map/ppermute | solution.py:121
  82.6 1.1 %collective-permute-start.29 = (f32[32,128]{1,0:T(8,128)S(1)}, f32[32,128]{1,0:T(8,128)S(1)}, u32[]{:S(2)}, u32[]{:S(2)}) collective-permute-start(f32[32,128]{1,0:T(8,128)S(1)} %add.17.one), channel_id=1, source_target_pairs={{0,16},{8,24},{16,0},{24,8},{1,17},{9,25},{17,1},{25,9},{2,18},{10... | collective-permute-start | bytes 49160 | tf_op jit(solution)/shard_map/ppermute | solution.py:121
  83.7 2.8 %final.3 = (f32[1024,1024]{1,0:T(8,128)}, f32[1024,1024]{1,0:T(8,128)}) custom-call(f32[64,64]{1,0:T(8,128)S(1)} %eliminate.3.inverse, f32[32,512]{1,0:T(8,128)S(1)} %collective-permute-done.16.refs_0_.rest_0_, f32[32,512]{1,0:T(8,128)S(1)} %add.14.refs_1_.rest_1_, ...), custom_call_target="tpu_custom_call", output_to_operand_aliasing={{0}: (7, {}), {1}: (8, {})} | custom-call | flops 201326592 | bytes 4194304 | tf_op jit(solution)/shard_map/final/pallas_call | solution.py:43
  86.5 3.8 %finish.1 = f32[64,1024]{1,0:T(8,128)} custom-call(f32[32,128]{1,0:T(8,128)S(1)} %add.17.one, f32[32,128]{1,0:T(8,128)S(1)} %collective-permute-done.29.two, f32[64,512]{1,0:T(8,128)S(1)} %get-tuple-element.112.own, f32[64,512]{1,0:T(8,128)S(1)} %get-tuple-element.113.other), custom_call_target="tpu_custom_call" | custom-call | flops 100000000 | bytes 8388608 | tf_op jit(solution)/shard_map/finish/pallas_call | solution.py:43
  (48 shorter events, 4.7 us)
Async XLA Ops:
  6.9 1.4 %collective-permute-start = (f32[32,512]{1,0:T(8,128)S(1)}, f32[32,512]{1,0:T(8,128)S(1)}, u32[]{:S(2)}, u32[]{:S(2)}) collective-permute-start(f32[32,512]{1,0:T(8,128)S(1)} %get-tuple-element.60), channel_id=1, source_target_pairs={{0,8},{8,0},{16,24},{24,16},{1,9},{9,1},{17,25},{25,17},{2,10},{10... | collective-permute-start | bytes 196616 | tf_op jit(solution)/shard_map/ppermute | solution.py:121
  7.4 3.9 %collective-permute-start.3 = (f32[32,512]{1,0:T(8,128)S(1)}, f32[32,512]{1,0:T(8,128)S(1)}, u32[]{:S(2)}, u32[]{:S(2)}) collective-permute-start(f32[32,512]{1,0:T(8,128)S(1)} %get-tuple-element.62), channel_id=1, source_target_pairs={{0,8},{8,0},{16,24},{24,16},{1,9},{9,1},{17,25},{25,17},{2,10},{10... | collective-permute-start | bytes 196616 | tf_op jit(solution)/shard_map/ppermute | solution.py:121
  8.3 5.3 %collective-permute-start.1 = (f32[32,512]{1,0:T(8,128)S(1)}, f32[32,512]{1,0:T(8,128)S(1)}, u32[]{:S(2)}, u32[]{:S(2)}) collective-permute-start(f32[32,512]{1,0:T(8,128)S(1)} %add.9.refs_0_), channel_id=1, source_target_pairs={{0,16},{8,24},{16,0},{24,8},{1,17},{9,25},{17,1},{25,9},{2,18},{10... | collective-permute-start | bytes 196616 | tf_op jit(solution)/shard_map/ppermute | solution.py:213
  11.3 4.3 %collective-permute-start.4 = (f32[32,512]{1,0:T(8,128)S(1)}, f32[32,512]{1,0:T(8,128)S(1)}, u32[]{:S(2)}, u32[]{:S(2)}) collective-permute-start(f32[32,512]{1,0:T(8,128)S(1)} %add.11.refs_0_), channel_id=1, source_target_pairs={{0,16},{8,24},{16,0},{24,8},{1,17},{9,25},{17,1},{25,9},{2,18},{10... | collective-permute-start | bytes 196616 | tf_op jit(solution)/shard_map/ppermute | solution.py:213
  13.7 2.0 %collective-permute-start.2 = (f32[32,512]{1,0:T(8,128)S(1)}, f32[32,512]{1,0:T(8,128)S(1)}, u32[]{:S(2)}, u32[]{:S(2)}) collective-permute-start(f32[32,512]{1,0:T(8,128)S(1)} %add.10.refs_1_.rest_1_), channel_id=1, source_target_pairs={{0,8},{8,0},{16,24},{24,16},{1,9},{9,1},{17,25},{25,17},{2,10},{10... | collective-permute-start | bytes 196616 | tf_op jit(solution)/shard_map/ppermute | solution.py:121
  15.6 1.3 %collective-permute-start.5 = (f32[32,512]{1,0:T(8,128)S(1)}, f32[32,512]{1,0:T(8,128)S(1)}, u32[]{:S(2)}, u32[]{:S(2)}) collective-permute-start(f32[32,512]{1,0:T(8,128)S(1)} %add.12.refs_3_.rest_3_), channel_id=1, source_target_pairs={{0,8},{8,0},{16,24},{24,16},{1,9},{9,1},{17,25},{25,17},{2,10},{10... | collective-permute-start | bytes 196616 | tf_op jit(solution)/shard_map/ppermute | solution.py:121
  17.7 5.1 %collective-permute-start.9 = (f32[160,128]{1,0:T(8,128)S(1)}, f32[160,128]{1,0:T(8,128)S(1)}, u32[]{:S(2)}, u32[]{:S(2)}) collective-permute-start(f32[160,128]{1,0:T(8,128)S(1)} %multiply.8.sent), channel_id=1, source_target_pairs={{0,1},{1,0},{2,3},{3,2},{4,5},{5,4},{6,7},{7,6},{8,9},{9,8},{10,11... | collective-permute-start | bytes 245768 | tf_op jit(solution)/shard_map/ppermute | solution.py:121
  19.2 5.2 %collective-permute-start.6 = (f32[128,128]{1,0:T(8,128)S(1)}, f32[128,128]{1,0:T(8,128)S(1)}, u32[]{:S(2)}, u32[]{:S(2)}) collective-permute-start(f32[128,128]{1,0:T(8,128)S(1)} %multiply.7.sent.refs_6_), channel_id=1, source_target_pairs={{0,1},{1,0},{2,3},{3,2},{4,5},{5,4},{6,7},{7,6},{8,9},{9,8},{10,11... | collective-permute-start | bytes 196616 | tf_op jit(solution)/shard_map/ppermute | solution.py:121
  22.8 4.2 %collective-permute-start.10 = (f32[96,128]{1,0:T(8,128)S(1)}, f32[96,128]{1,0:T(8,128)S(1)}, u32[]{:S(2)}, u32[]{:S(2)}) collective-permute-start(f32[96,128]{1,0:T(8,128)S(1)} %get-tuple-element.72.sent), channel_id=1, source_target_pairs={{0,2},{1,3},{2,0},{3,1},{4,6},{5,7},{6,4},{7,5},{8,10},{9,11},{10,... | collective-permute-start | bytes 147464 | tf_op jit(solution)/shard_map/ppermute | solution.py:121
  24.4 5.2 %collective-permute-start.7 = (f32[64,128]{1,0:T(8,128)S(1)}, f32[64,128]{1,0:T(8,128)S(1)}, u32[]{:S(2)}, u32[]{:S(2)}) collective-permute-start(f32[64,128]{1,0:T(8,128)S(1)} %get-tuple-element.69.sent), channel_id=1, source_target_pairs={{0,2},{1,3},{2,0},{3,1},{4,6},{5,7},{6,4},{7,5},{8,10},{9,11},{10,... | collective-permute-start | bytes 98312 | tf_op jit(solution)/shard_map/ppermute | solution.py:121
  26.9 7.5 %collective-permute-start.11 = (f32[96,128]{1,0:T(8,128)S(1)}, f32[96,128]{1,0:T(8,128)S(1)}, u32[]{:S(2)}, u32[]{:S(2)}) collective-permute-start(f32[96,128]{1,0:T(8,128)S(1)} %fold.11.refs_2_.one), channel_id=1, source_target_pairs={{0,4},{1,5},{2,6},{3,7},{4,0},{5,1},{6,2},{7,3},{8,12},{9,13},{10,... | collective-permute-start | bytes 147464 | tf_op jit(solution)/shard_map/ppermute | solution.py:121
  29.6 4.9 %collective-permute-start.8 = (f32[64,128]{1,0:T(8,128)S(1)}, f32[64,128]{1,0:T(8,128)S(1)}, u32[]{:S(2)}, u32[]{:S(2)}) collective-permute-start(f32[64,128]{1,0:T(8,128)S(1)} %fold.9.refs_0_), channel_id=1, source_target_pairs={{0,4},{1,5},{2,6},{3,7},{4,0},{5,1},{6,2},{7,3},{8,12},{9,13},{10,... | collective-permute-start | bytes 98312 | tf_op jit(solution)/shard_map/ppermute | solution.py:121
  34.5 4.5 %collective-permute-start.12 = (f32[128,128]{1,0:T(8,128)S(1)}, f32[128,128]{1,0:T(8,128)S(1)}, u32[]{:S(2)}, u32[]{:S(2)}) collective-permute-start(f32[128,128]{1,0:T(8,128)S(1)} %merge.2.value), channel_id=1, source_target_pairs={{0,2},{1,3},{2,0},{3,1},{4,6},{5,7},{6,4},{7,5},{8,10},{9,11},{10,... | collective-permute-start | bytes 196616 | tf_op jit(solution)/shard_map/ppermute | solution.py:121
  39.0 5.0 %collective-permute-start.13 = (f32[256,128]{1,0:T(8,128)S(1)}, f32[256,128]{1,0:T(8,128)S(1)}, u32[]{:S(2)}, u32[]{:S(2)}) collective-permute-start(f32[256,128]{1,0:T(8,128)S(1)} %unfold.2.rest_4_), channel_id=1, source_target_pairs={{0,1},{1,0},{2,3},{3,2},{4,5},{5,4},{6,7},{7,6},{8,9},{9,8},{10,11... | collective-permute-start | bytes 393224 | tf_op jit(solution)/shard_map/ppermute | solution.py:121
  46.0 1.3 %collective-permute-start.14 = (f32[32,512]{1,0:T(8,128)S(1)}, f32[32,512]{1,0:T(8,128)S(1)}, u32[]{:S(2)}, u32[]{:S(2)}) collective-permute-start(f32[32,512]{1,0:T(8,128)S(1)} %get-tuple-element.82), channel_id=1, source_target_pairs={{0,8},{8,0},{16,24},{24,16},{1,9},{9,1},{17,25},{25,17},{2,10},{10... | collective-permute-start | bytes 196616 | tf_op jit(solution)/shard_map/ppermute | solution.py:121
  46.1 2.5 %collective-permute-start.17 = (f32[32,512]{1,0:T(8,128)S(1)}, f32[32,512]{1,0:T(8,128)S(1)}, u32[]{:S(2)}, u32[]{:S(2)}) collective-permute-start(f32[32,512]{1,0:T(8,128)S(1)} %get-tuple-element.84), channel_id=1, source_target_pairs={{0,8},{8,0},{16,24},{24,16},{1,9},{9,1},{17,25},{25,17},{2,10},{10... | collective-permute-start | bytes 196616 | tf_op jit(solution)/shard_map/ppermute | solution.py:121
  47.4 4.8 %collective-permute-start.15 = (f32[32,512]{1,0:T(8,128)S(1)}, f32[32,512]{1,0:T(8,128)S(1)}, u32[]{:S(2)}, u32[]{:S(2)}) collective-permute-start(f32[32,512]{1,0:T(8,128)S(1)} %add.13.refs_0_), channel_id=1, source_target_pairs={{0,16},{8,24},{16,0},{24,8},{1,17},{9,25},{17,1},{25,9},{2,18},{10... | collective-permute-start | bytes 196616 | tf_op jit(solution)/shard_map/ppermute | solution.py:213
  48.7 4.4 %collective-permute-start.18 = (f32[32,512]{1,0:T(8,128)S(1)}, f32[32,512]{1,0:T(8,128)S(1)}, u32[]{:S(2)}, u32[]{:S(2)}) collective-permute-start(f32[32,512]{1,0:T(8,128)S(1)} %add.15.refs_0_), channel_id=1, source_target_pairs={{0,16},{8,24},{16,0},{24,8},{1,17},{9,25},{17,1},{25,9},{2,18},{10... | collective-permute-start | bytes 196616 | tf_op jit(solution)/shard_map/ppermute | solution.py:213
  52.2 1.3 %collective-permute-start.16 = (f32[32,512]{1,0:T(8,128)S(1)}, f32[32,512]{1,0:T(8,128)S(1)}, u32[]{:S(2)}, u32[]{:S(2)}) collective-permute-start(f32[32,512]{1,0:T(8,128)S(1)} %add.14.refs_1_.rest_1_), channel_id=1, source_target_pairs={{0,8},{8,0},{16,24},{24,16},{1,9},{9,1},{17,25},{25,17},{2,10},{10... | collective-permute-start | bytes 196616 | tf_op jit(solution)/shard_map/ppermute | solution.py:121
  53.1 1.3 %collective-permute-start.19 = (f32[32,512]{1,0:T(8,128)S(1)}, f32[32,512]{1,0:T(8,128)S(1)}, u32[]{:S(2)}, u32[]{:S(2)}) collective-permute-start(f32[32,512]{1,0:T(8,128)S(1)} %add.16.refs_3_.rest_3_), channel_id=1, source_target_pairs={{0,8},{8,0},{16,24},{24,16},{1,9},{9,1},{17,25},{25,17},{2,10},{10... | collective-permute-start | bytes 196616 | tf_op jit(solution)/shard_map/ppermute | solution.py:121
  55.2 5.0 %collective-permute-start.23 = (f32[160,128]{1,0:T(8,128)S(1)}, f32[160,128]{1,0:T(8,128)S(1)}, u32[]{:S(2)}, u32[]{:S(2)}) collective-permute-start(f32[160,128]{1,0:T(8,128)S(1)} %multiply.11.sent), channel_id=1, source_target_pairs={{0,1},{1,0},{2,3},{3,2},{4,5},{5,4},{6,7},{7,6},{8,9},{9,8},{10,11... | collective-permute-start | bytes 245768 | tf_op jit(solution)/shard_map/ppermute | solution.py:121
  56.8 5.0 %collective-permute-start.20 = (f32[128,128]{1,0:T(8,128)S(1)}, f32[128,128]{1,0:T(8,128)S(1)}, u32[]{:S(2)}, u32[]{:S(2)}) collective-permute-start(f32[128,128]{1,0:T(8,128)S(1)} %multiply.10.sent.refs_6_), channel_id=1, source_target_pairs={{0,1},{1,0},{2,3},{3,2},{4,5},{5,4},{6,7},{7,6},{8,9},{9,8},{10,11... | collective-permute-start | bytes 196616 | tf_op jit(solution)/shard_map/ppermute | solution.py:121
  60.2 4.2 %collective-permute-start.24 = (f32[96,128]{1,0:T(8,128)S(1)}, f32[96,128]{1,0:T(8,128)S(1)}, u32[]{:S(2)}, u32[]{:S(2)}) collective-permute-start(f32[96,128]{1,0:T(8,128)S(1)} %get-tuple-element.94.sent), channel_id=1, source_target_pairs={{0,2},{1,3},{2,0},{3,1},{4,6},{5,7},{6,4},{7,5},{8,10},{9,11},{10,... | collective-permute-start | bytes 147464 | tf_op jit(solution)/shard_map/ppermute | solution.py:121
  61.7 4.5 %collective-permute-start.21 = (f32[64,128]{1,0:T(8,128)S(1)}, f32[64,128]{1,0:T(8,128)S(1)}, u32[]{:S(2)}, u32[]{:S(2)}) collective-permute-start(f32[64,128]{1,0:T(8,128)S(1)} %get-tuple-element.91.sent), channel_id=1, source_target_pairs={{0,2},{1,3},{2,0},{3,1},{4,6},{5,7},{6,4},{7,5},{8,10},{9,11},{10,... | collective-permute-start | bytes 98312 | tf_op jit(solution)/shard_map/ppermute | solution.py:121
  64.3 7.1 %collective-permute-start.25 = (f32[96,128]{1,0:T(8,128)S(1)}, f32[96,128]{1,0:T(8,128)S(1)}, u32[]{:S(2)}, u32[]{:S(2)}) collective-permute-start(f32[96,128]{1,0:T(8,128)S(1)} %fold.15.refs_2_.one), channel_id=1, source_target_pairs={{0,4},{1,5},{2,6},{3,7},{4,0},{5,1},{6,2},{7,3},{8,12},{9,13},{10,... | collective-permute-start | bytes 147464 | tf_op jit(solution)/shard_map/ppermute | solution.py:121
  66.3 5.1 %collective-permute-start.22 = (f32[64,128]{1,0:T(8,128)S(1)}, f32[64,128]{1,0:T(8,128)S(1)}, u32[]{:S(2)}, u32[]{:S(2)}) collective-permute-start(f32[64,128]{1,0:T(8,128)S(1)} %fold.13.refs_0_), channel_id=1, source_target_pairs={{0,4},{1,5},{2,6},{3,7},{4,0},{5,1},{6,2},{7,3},{8,12},{9,13},{10,... | collective-permute-start | bytes 98312 | tf_op jit(solution)/shard_map/ppermute | solution.py:121
  71.4 4.3 %collective-permute-start.26 = (f32[128,128]{1,0:T(8,128)S(1)}, f32[128,128]{1,0:T(8,128)S(1)}, u32[]{:S(2)}, u32[]{:S(2)}) collective-permute-start(f32[128,128]{1,0:T(8,128)S(1)} %merge.3.value), channel_id=1, source_target_pairs={{0,2},{1,3},{2,0},{3,1},{4,6},{5,7},{6,4},{7,5},{8,10},{9,11},{10,... | collective-permute-start | bytes 196616 | tf_op jit(solution)/shard_map/ppermute | solution.py:121
  75.8 5.0 %collective-permute-start.27 = (f32[256,128]{1,0:T(8,128)S(1)}, f32[256,128]{1,0:T(8,128)S(1)}, u32[]{:S(2)}, u32[]{:S(2)}) collective-permute-start(f32[256,128]{1,0:T(8,128)S(1)} %unfold.3.rest_4_), channel_id=1, source_target_pairs={{0,1},{1,0},{2,3},{3,2},{4,5},{5,4},{6,7},{7,6},{8,9},{9,8},{10,11... | collective-permute-start | bytes 393224 | tf_op jit(solution)/shard_map/ppermute | solution.py:121
  81.4 1.2 %collective-permute-start.28 = (f32[32,128]{1,0:T(8,128)S(1)}, f32[32,128]{1,0:T(8,128)S(1)}, u32[]{:S(2)}, u32[]{:S(2)}) collective-permute-start(f32[32,128]{1,0:T(8,128)S(1)} %get-tuple-element.111.refs_0_), channel_id=1, source_target_pairs={{0,8},{8,0},{16,24},{24,16},{1,9},{9,1},{17,25},{25,17},{2,10},{10... | collective-permute-start | bytes 49160 | tf_op jit(solution)/shard_map/ppermute | solution.py:121
  82.6 3.9 %collective-permute-start.29 = (f32[32,128]{1,0:T(8,128)S(1)}, f32[32,128]{1,0:T(8,128)S(1)}, u32[]{:S(2)}, u32[]{:S(2)}) collective-permute-start(f32[32,128]{1,0:T(8,128)S(1)} %add.17.one), channel_id=1, source_target_pairs={{0,16},{8,24},{16,0},{24,8},{1,17},{9,25},{17,1},{25,9},{2,18},{10... | collective-permute-start | bytes 49160 | tf_op jit(solution)/shard_map/ppermute | solution.py:121

commit v8 on v6

--- a/solution.py
+++ b/solution.py
@@ -121,7 +121,7 @@
         half = n_cols // 2
         tall = min(256, n_rows // 2)
         steps = n_rows // tall
-        stack_rows = rank * (half // LANES)
+        quarter = rank * (half // LANES) // 2
         gram_rows = rank * rank // LANES
 
         def place():
@@ -202,21 +202,40 @@
             mine = add(mine, *got)
             return swap(mine, "gal", 1), mine
 
-        def multiply(panel, pair, with_gram):
-            def body(away, mine, high, low, out):
+        def multiply_other(panel, pair):
+            def body(away, mine, high, low, straight, across, stack):
+                s = place()
                 panel = join((away, mine))
-                total = dot_nn(split(panel), (high[...], low[...]))
-                for t in range(half // LANES):
-                    out[rank * t : rank * (t + 1), :] = total[:, LANES * t : LANES * (t + 1)]
-                if with_gram:
-                    gram = dot(panel, panel, ((1,), (1,)), HIGH)
-                    out[stack_rows : stack_rows + gram_rows, :] = pack(gram)
-
-            rows = stack_rows + (gram_rows if with_gram else 0)
+                put_stack(dot_nn(split(panel), (high[...], low[...])), stack)
+                gram = pack(dot(panel, panel, ((1,), (1,)), HIGH))
+                for side, out in ((s[2], straight), (1 - s[2], across)):
+                    out[:quarter, :] = stack[rows_at(side), :]
+                    out[quarter:, :] = gram
+
             ins = [(a, pltpu.VMEM) for a in (*panel, *pair)]
-            outs = [((rows, LANES), F32, pltpu.VMEM)]
+            outs = [((quarter + gram_rows, LANES), F32, pltpu.VMEM)] * 2
             cost = (3 * rank * n_rows * n_cols, 2 * n_rows * n_cols)
-            return call(body, "multiply", ins, outs, cost=cost)[0]
+            return call(body, "multiply_other", ins, outs, [pltpu.VMEM((2 * quarter, LANES), F32)], cost=cost)
+
+        def multiply_own(panel, pair, sent):
+            def body(away, mine, high, low, sent, keep, out, stack):
+                s = place()
+                put_stack(dot_nn(split(join((away, mine))), (high[...], low[...])), stack)
+                keep[...] = stack[rows_at(s[2]), :]
+                out[:quarter, :] = stack[rows_at(1 - s[2]), :]
+                out[quarter:, :] = sent[quarter:, :]
+
+            ins = [(a, pltpu.VMEM) for a in (*panel, *pair, sent)]
+            outs = [((rows, LANES), F32, pltpu.VMEM) for rows in (quarter, quarter + gram_rows)]
+            cost = (3 * rank * n_rows * n_cols, 2 * n_rows * n_cols)
+            return call(body, "multiply_own", ins, outs, [pltpu.VMEM((2 * quarter, LANES), F32)], cost=cost)
+
+        def put_stack(value, stack):
+            for t in range(half // LANES):
+                stack[rank * t : rank * (t + 1), :] = value[:, LANES * t : LANES * (t + 1)]
+
+        def rows_at(side):
+            return pl.ds(pl.multiple_of(side * quarter, quarter), quarter)
 
         def eliminate(one, two):
             def body(one, two, out):
@@ -226,36 +245,38 @@
             outs = [((rank, rank), F32, pltpu.VMEM)]
             return call(body, "eliminate", ins, outs, cost=(10**8, 8 * MIB), limit=4)[0]
 
-        def fold(level, value, sent, got):
-            rows = value.shape[0]
-            last = level == levels - 1
-            keep = rows if last else rows // 2
-
-            def body(value, sent, got, *outs):
-                s = place()
-                message = outs[-1]
-                if last:
-                    message[:rows, :] = value[...] + got[:rows, :]
-                else:
-                    for mine, out in ((s[1 + level], outs[0]), (1 - s[1 + level], message)):
-                        at = pl.ds(pl.multiple_of(mine * keep, keep), keep)
-                        out[:keep, :] = value[at, :] + got[at, :]
-                message[keep:, :] = sent[rows_of(sent), :] + got[rows_of(got), :]
-
-            def rows_of(ref):
-                return slice(ref.shape[0] - gram_rows, ref.shape[0])
-
-            ins = [(a, pltpu.VMEM) for a in (value, sent, got)]
-            outs = small(body, "fold", ins, [keep + gram_rows] if last else [keep, keep + gram_rows])
-            return outs[0], outs[-1]
+        def collect(keep, sent, gots):
+            rows = keep.shape[0]
+
+            def body(keep, sent, *refs):
+                *gots, out = refs
+                top, low = keep[...], sent[rows:, :]
+                for got in gots:
+                    top, low = top + got[:rows, :], low + got[rows:, :]
+                out[:rows, :] = top
+                out[rows:, :] = low
+
+            ins = [(a, pltpu.VMEM) for a in (keep, sent, *gots)]
+            return small(body, "collect", ins, [rows + gram_rows])[0]
+
+        def divide(level, total):
+            rows = (total.shape[0] - gram_rows) // 2
+
+            def body(total, keep, out):
+                s = place()
+                for side, ref in ((s[1 + level], keep), (1 - s[1 + level], out)):
+                    ref[:rows, :] = total[pl.ds(pl.multiple_of(side * rows, rows), rows), :]
+                out[rows:, :] = total[2 * rows :, :]
+
+            return small(body, "divide", [(total, pltpu.VMEM)], [rows, rows + gram_rows])
 
         def unfold(level, value, got):
             rows = value.shape[0]
 
             def body(value, got, out):
                 s = place()
-                for mine, ref in ((s[1 + level], value), (1 - s[1 + level], got)):
-                    out[pl.ds(pl.multiple_of(mine * rows, rows), rows), :] = ref[...]
+                for side, ref in ((s[1 + level], value), (1 - s[1 + level], got)):
+                    out[pl.ds(pl.multiple_of(side * rows, rows), rows), :] = ref[...]
 
             ins = [(value, pltpu.VMEM), (got, pltpu.VMEM)]
             return small(body, "unfold", ins, [2 * rows])[0]
@@ -268,17 +289,21 @@
 
             return small(body, "top", [(one, pltpu.VMEM), (two, pltpu.VMEM)], [rows])[0]
 
-        def sum_pix(send, own):
-            value, sent = own, send
-            for level in range(1, levels):
-                value, sent = fold(level, value, sent, swap(sent, "pix", 1 << (level - 1)))
-            got = swap(sent, "pix", 1 << (levels - 1))
-            value = top(sent, got)
-            inverse = eliminate(sent, got)
-            for level in range(levels - 2, 0, -1):
+        def sum_pix(panel, own, other):
+            straight, across = multiply_other(panel, other)
+            gots = [swap(straight, "pix", 1), swap(across, "pix", 3)]
+            keep, beside = multiply_own(panel, own, straight)
+            total = collect(keep, straight, gots + [swap(beside, "pix", 2)])
+            for level in range(2, levels - 1):
+                keep, sent = divide(level, total)
+                total = collect(keep, sent, [swap(sent, "pix", 1 << level)])
+            got = swap(total, "pix", 1 << (levels - 1))
+            value = top(total, got)
+            inverse = eliminate(total, got)
+            for level in range(levels - 2, 1, -1):
                 value = unfold(level, value, swap(value, "pix", 1 << level))
-            value, inverse = lax.optimization_barrier((value, inverse))
-            return inverse, value, swap(value, "pix", 1)
+            beside, straight, across = [swap(value, "pix", bit) for bit in (2, 1, 3)]
+            return inverse, unfold(1, value, beside), unfold(1, straight, across)
 
         def halves(inverse, panel, stacked):
             left = dot(inverse[...], join(panel), ((1,), (0,)), HIGH)
@@ -286,13 +311,13 @@
             left_high, left_low = split(left)
             wide_high, wide_low = split(wide)
             tops = jnp.concatenate([left_high, left_low, left_high], axis=0)
-            return left, wide, (wide_high, wide_low), tops, jnp.concatenate([wide_high, wide_high, wide_low], axis=0)
+            return left, (wide_high, wide_low), tops, jnp.concatenate([wide_high, wide_high, wide_low], axis=0)
 
         def middle(p, inverse, panel, stacked, o, d, before):
             def body(inverse, away, mine, stacked, o, d, *rest):
                 s = place()
                 base, high, low, *after = rest[2 * p :]
-                _, _, right, tops, wides = halves(inverse, (away, mine), stacked)
+                _, right, tops, wides = halves(inverse, (away, mine), stacked)
                 for i in range(steps):
                     lowrank = dot(tops[:, chunk(i)], wides, ((0,), (0,)))
                     at = chunk(i), pl.ds(pix_at(p, s), half)
@@ -318,11 +343,9 @@
             def body(inverse, away, mine, stacked, base, *rest):
                 s = place()
                 sparse, dual, *outs, sparse_part, dual_part, left_part, sems = rest[2 * p :]
-                left, wide, _, tops, wides = halves(inverse, (away, mine), stacked)
+                left, _, tops, wides = halves(inverse, (away, mine), stacked)
                 moves = []
                 if not p:
-                    outs[1][...] = wide
-                    outs[2][...] = pack(dot(wide, wide, ((1,), (1,)), HIGH))
                     for i in range(steps):
                         left_part[:, pl.ds(gal_at(i, s), tall)] = left[:, chunk(i)]
                     moves.append(pltpu.make_async_copy(left_part, outs[0], sems.at[steps, 0]))
@@ -347,20 +370,23 @@
                 ins += [(a, pltpu.HBM) for a in before[:2]]
                 aliases = {5: 0, 6: 1}
             else:
-                outs += [((rank, n_rows), F32, pltpu.HBM), ((rank, half), F32, pltpu.VMEM)]
-                outs += [((gram_rows, LANES), F32, pltpu.VMEM)]
+                outs += [((rank, n_rows), F32, pltpu.HBM)]
             scratch = [pltpu.VMEM((n_rows, half), F32)] * 2 + [pltpu.VMEM((rank, n_rows), F32)]
             scratch += [pltpu.SemaphoreType.DMA((steps + 1, 2))]
             cost = (3 * rank * n_rows * n_cols, 4 * n_rows * n_cols)
             return call(body, "final", ins, outs, scratch, aliases, cost)
 
-        def widen(inverse, other, gram):
-            def body(inverse, stacked, gram, wide, out):
-                wide[...] = dot(inverse[...], unstack(stacked), ((1,), (0,)), HIGH)
-                out[...] = gram[...] + pack(dot(wide[...], wide[...], ((1,), (1,)), HIGH))
-
-            ins = [(a, pltpu.VMEM) for a in (inverse, other, gram)]
-            outs = [((rank, half), F32, pltpu.VMEM), ((gram_rows, LANES), F32, pltpu.VMEM)]
+        def widen(inverse, own, other):
+            def body(inverse, own, other, wide_own, wide_other, out):
+                grams = []
+                for stacked, wide in ((own, wide_own), (other, wide_other)):
+                    value = dot(inverse[...], unstack(stacked), ((1,), (0,)), HIGH)
+                    wide[...] = value
+                    grams.append(dot(value, value, ((1,), (1,)), HIGH))
+                out[...] = pack(grams[0] + grams[1])
+
+            ins = [(a, pltpu.VMEM) for a in (inverse, own, other)]
+            outs = [((rank, half), F32, pltpu.VMEM)] * 2 + [((gram_rows, LANES), F32, pltpu.VMEM)]
             return call(body, "widen", ins, outs, cost=(10**8, MIB), limit=8)
 
         def finish(one, two, wide):
@@ -382,15 +408,13 @@
         base = [None, None]
         for step in range(ITERS):
             panel = sum_gal(part)
-            send = multiply(panel, other, True)
-            inverse, own_wide, other_wide = sum_pix(send, multiply(panel, own, False))
+            inverse, own_wide, other_wide = sum_pix(panel, own, other)
             if step < ITERS - 1:
                 base[0], own, part = middle(0, inverse, panel, own_wide, seen, pulls, None)
                 base[1], other, part = middle(1, inverse, panel, other_wide, seen, pulls, part)
             else:
+                *wide, gram = widen(inverse, own_wide, other_wide)
                 outs = final(0, inverse, panel, own_wide, base[0], None)
-                other_wide, outs = lax.optimization_barrier((other_wide, outs))
-                wide, gram = widen(inverse, other_wide, outs[4])
                 bit = 1
                 while 2 * bit < n_gal:
                     gram = add(gram, swap(gram, "gal", bit))
@@ -398,7 +422,7 @@
                 got = swap(gram, "gal", bit)
                 sparse, dual = final(1, inverse, panel, other_wide, base[1], outs)
                 left = outs[2]
-                right = finish(gram, got, (outs[3], wide))
+                right = finish(gram, got, wide)
         return sparse, dual, left, right
 
     return jax.shard_map(

time: 90.7 us -> 85.8 us (0.946)
  waiting for transfers between devices: 34.4 us -> 29.3 us
    ppermute x16 -> x20, waiting for transfers between devices: 26.6 us -> 21.5 us  [swap(): return lax.ppermute(value, axis, [(i, i ^ bit) for i in range(n)])]
    ppermute x16 -> x20, starting transfers between devices: 22.1 us -> 21.8 us  [swap(): return lax.ppermute(value, axis, [(i, i ^ bit) for i in range(n)])]
  transfers between devices with their start and end apart: 18 -> 22, of which waited for: 15 -> 15; matrix products, arithmetic and copies ran while one was open for 0% -> 0% of each run, Pallas kernels for 16% -> 14%
where the time goes in v8:
time: 85.8 us; the launch traced here: 85.7 us
  waiting for transfers between devices  29.3 us (34%)
  Pallas kernels  29 us (34%)
  starting transfers between devices  26.3 us (31%)
  between operations  0.99 us (1%)
    pallas_call x26, Pallas kernels, call(): pl.pallas_call(body, name=name, in_specs=[pl.BlockSpec(memory_space=space...  29 us
    ppermute x20, starting transfers between devices, swap(): return lax.ppermute(value, axis, [(i, i ^ bit) for i in range(n)])  21.8 us
    ppermute x20, waiting for transfers between devices, swap(): return lax.ppermute(value, axis, [(i, i ^ bit) for i in range(n)])  21.5 us
    ppermute x2, waiting for transfers between devices, sum_gal(): lax.ppermute(mine, 'gal', [(i, (i + CORES * k) % n_gal) for i in range(n_...  7.83 us
    ppermute x2, starting transfers between devices, sum_gal(): lax.ppermute(mine, 'gal', [(i, (i + CORES * k) % n_gal) for i in range(n_...  4.53 us
  transfers between devices with their start and end apart: 22, of which 15 were waited for; matrix products, arithmetic and copies ran while one was open for 0% of the time, Pallas kernels for 14%

profile of v8, /device:TPU:0, one launch (start us, length us, event | category | flops | bytes accessed | tf_op | source)
XLA Modules:
  0.0 85.7 jit_solution(10380299037262075794)
XLA Ops:
  0.6 6.3 %first.1 = (f32[1024,1024]{1,0:T(8,128)S(1)}, f32[1024,1024]{1,0:T(8,128)S(1)}, bf16[1024,512]{1,0:T(8,128)(2,1)S(1)}, bf16[1024,512]{1,0:T(8,128)(2,1)S(1)}, bf...) custom-call(f32[1024,1024]{1,0:T(8,128)} %o_in.1, ...), custom_call_target="tpu_custom_call" | custom-call | flops 402653184 | bytes 16777216 | tf_op jit(solution)/shard_map/first/pallas_call | solution.py:42
  6.9 0.5 collective-permute-start
  7.4 1.0 %collective-permute-done.refs_1_ = f32[64,512]{1,0:T(8,128)S(1)} collective-permute-done((f32[64,512]{1,0:T(8,128)S(1)}, f32[64,512]{1,0:T(8,128)S(1)}, u32[]{:S(2)}, u32[]{:S(2)}) %collective-permute-start) | collective-permute-done | bytes 131104 | tf_op jit(solution)/shard_map/ppermute | solution.py:116
  8.4 2.9 %collective-permute-start.1 = (f32[64,512]{1,0:T(8,128)S(1)}, f32[64,512]{1,0:T(8,128)S(1)}, u32[]{:S(2)}, u32[]{:S(2)}) collective-permute-start(f32[64,512]{1,0:T(8,128)S(1)} %add.5.refs_0_), channel_id=1, source_target_pairs={{0,16},{8,24},{16,0},{24,8},{1,17},{9,25},{17,1},{25,9},{2,18},{10... | collective-permute-start | bytes 393224 | tf_op jit(solution)/shard_map/ppermute | solution.py:199
  11.4 3.8 %collective-permute-done.1.refs_1_ = f32[64,512]{1,0:T(8,128)S(1)} collective-permute-done((f32[64,512]{1,0:T(8,128)S(1)}, f32[64,512]{1,0:T(8,128)S(1)}, u32[]{:S(2)}, u32[]{:S(2)}) %collective-permute-start.1) | collective-permute-done | bytes 131104 | tf_op jit(solution)/shard_map/ppermute | solution.py:199
  15.2 0.1 collective-permute-start.2
  15.3 1.3 %collective-permute-done.2.away = f32[64,512]{1,0:T(8,128)S(1)} collective-permute-done((f32[64,512]{1,0:T(8,128)S(1)}, f32[64,512]{1,0:T(8,128)S(1)}, u32[]{:S(2)}, u32[]{:S(2)}) %collective-permute-start.2) | collective-permute-done | bytes 131104 | tf_op jit(solution)/shard_map/ppermute | solution.py:116
  16.6 0.7 multiply_other.2
  17.3 1.7 %collective-permute-start.3 = (f32[160,128]{1,0:T(8,128)S(1)}, f32[160,128]{1,0:T(8,128)S(1)}, u32[]{:S(2)}, u32[]{:S(2)}) collective-permute-start(f32[160,128]{1,0:T(8,128)S(1)} %get-tuple-element.44.sent), channel_id=1, source_target_pairs={{0,1},{1,0},{2,3},{3,2},{4,5},{5,4},{6,7},{7,6},{8,9},{9,8},{10,11... | collective-permute-start | bytes 245768 | tf_op jit(solution)/shard_map/ppermute | solution.py:116
  19.1 1.5 %collective-permute-start.4 = (f32[160,128]{1,0:T(8,128)S(1)}, f32[160,128]{1,0:T(8,128)S(1)}, u32[]{:S(2)}, u32[]{:S(2)}) collective-permute-start(f32[160,128]{1,0:T(8,128)S(1)} %get-tuple-element.46), channel_id=1, source_target_pairs={{0,3},{1,2},{2,1},{3,0},{4,7},{5,6},{6,5},{7,4},{8,11},{9,10},{10,... | collective-permute-start | bytes 245768 | tf_op jit(solution)/shard_map/ppermute | solution.py:116
  20.6 0.5 multiply_own.2
  21.1 0.3 collective-permute-start.5
  21.4 1.5 %collective-permute-done.3.refs_0_ = f32[160,128]{1,0:T(8,128)S(1)} collective-permute-done((f32[160,128]{1,0:T(8,128)S(1)}, f32[160,128]{1,0:T(8,128)S(1)}, u32[]{:S(2)}, u32[]{:S(2)}) %collective-permute-start.3) | collective-permute-done | bytes 81952 | tf_op jit(solution)/shard_map/ppermute | solution.py:116
  22.9 1.7 %collective-permute-done.4.refs_1_ = f32[160,128]{1,0:T(8,128)S(1)} collective-permute-done((f32[160,128]{1,0:T(8,128)S(1)}, f32[160,128]{1,0:T(8,128)S(1)}, u32[]{:S(2)}, u32[]{:S(2)}) %collective-permute-start.4) | collective-permute-done | bytes 81952 | tf_op jit(solution)/shard_map/ppermute | solution.py:116
  24.6 1.0 %collective-permute-done.5.refs_2_ = f32[160,128]{1,0:T(8,128)S(1)} collective-permute-done((f32[160,128]{1,0:T(8,128)S(1)}, f32[160,128]{1,0:T(8,128)S(1)}, u32[]{:S(2)}, u32[]{:S(2)}) %collective-permute-start.5) | collective-permute-done | bytes 81952 | tf_op jit(solution)/shard_map/ppermute | solution.py:116
  25.6 2.7 %collective-permute-start.6 = (f32[160,128]{1,0:T(8,128)S(1)}, f32[160,128]{1,0:T(8,128)S(1)}, u32[]{:S(2)}, u32[]{:S(2)}) collective-permute-start(f32[160,128]{1,0:T(8,128)S(1)} %collect.2.one), channel_id=1, source_target_pairs={{0,4},{1,5},{2,6},{3,7},{4,0},{5,1},{6,2},{7,3},{8,12},{9,13},{10,... | collective-permute-start | bytes 245768 | tf_op jit(solution)/shard_map/ppermute | solution.py:116
  28.3 3.6 %collective-permute-done.6.two = f32[160,128]{1,0:T(8,128)S(1)} collective-permute-done((f32[160,128]{1,0:T(8,128)S(1)}, f32[160,128]{1,0:T(8,128)S(1)}, u32[]{:S(2)}, u32[]{:S(2)}) %collective-permute-start.6) | collective-permute-done | bytes 81952 | tf_op jit(solution)/shard_map/ppermute | solution.py:116
  31.9 0.3 collective-permute-start.9
  32.2 1.4 %collective-permute-start.7 = (f32[128,128]{1,0:T(8,128)S(1)}, f32[128,128]{1,0:T(8,128)S(1)}, u32[]{:S(2)}, u32[]{:S(2)}) collective-permute-start(f32[128,128]{1,0:T(8,128)S(1)} %top.2.value), channel_id=1, source_target_pairs={{0,1},{1,0},{2,3},{3,2},{4,5},{5,4},{6,7},{7,6},{8,9},{9,8},{10,11... | collective-permute-start | bytes 196616 | tf_op jit(solution)/shard_map/ppermute | solution.py:116
  33.7 1.8 %collective-permute-start.8 = (f32[128,128]{1,0:T(8,128)S(1)}, f32[128,128]{1,0:T(8,128)S(1)}, u32[]{:S(2)}, u32[]{:S(2)}) collective-permute-start(f32[128,128]{1,0:T(8,128)S(1)} %top.2.value), channel_id=1, source_target_pairs={{0,3},{1,2},{2,1},{3,0},{4,7},{5,6},{6,5},{7,4},{8,11},{9,10},{10,... | collective-permute-start | bytes 196616 | tf_op jit(solution)/shard_map/ppermute | solution.py:116
  35.5 2.8 %eliminate.2.inverse = f32[64,64]{1,0:T(8,128)S(1)} custom-call(f32[160,128]{1,0:T(8,128)S(1)} %collect.2.one, f32[160,128]{1,0:T(8,128)S(1)} %collective-permute-done.6.two), custom_call_target="tpu_custom_call" | custom-call | flops 100000000 | bytes 8388608 | tf_op jit(solution)/shard_map/eliminate/pallas_call | solution.py:42
  38.3 0.6 collective-permute-done.8.got
  38.9 2.0 %middle.2 = (f32[1024,512]{1,0:T(8,128)S(1)}, bf16[1024,512]{1,0:T(8,128)(2,1)S(1)}, bf16[1024,512]{1,0:T(8,128)(2,1)S(1)}, f32[64,512]{1,0:T(8,128)S(1)}, f32[64,512]{1,0:T(8,128)S(1)}) custom-call(f32[64,64]{1,0:T(8,128)S(1)} %eliminate.2.inverse, f32[64,512]{1,0:T(8,128)S(1)} %collective-permute-done.2.away, f32[64,512]{1,0:T(8,128)S(1)} %add.6.mine, ...), custom_call_target="tpu_custom_call" | custom-call | flops 603979776 | bytes 4194304 | tf_op jit(solution)/shard_map/middle/pallas_call | solution.py:42
  40.9 2.0 %middle.3 = (f32[1024,512]{1,0:T(8,128)S(1)}, bf16[1024,512]{1,0:T(8,128)(2,1)S(1)}, bf16[1024,512]{1,0:T(8,128)(2,1)S(1)}, f32[64,512]{1,0:T(8,128)S(1)}, f32[64,512]{1,0:T(8,128)S(1)}) custom-call(f32[64,64]{1,0:T(8,128)S(1)} %eliminate.2.inverse, f32[64,512]{1,0:T(8,128)S(1)} %collective-permute-done.2.away, f32[64,512]{1,0:T(8,128)S(1)} %add.6.mine, ...), custom_call_target="tpu_custom_call" | custom-call | flops 603979776 | bytes 4194304 | tf_op jit(solution)/shard_map/middle/pallas_call | solution.py:42
  43.0 1.3 %collective-permute-done.10.refs_1_ = f32[64,512]{1,0:T(8,128)S(1)} collective-permute-done((f32[64,512]{1,0:T(8,128)S(1)}, f32[64,512]{1,0:T(8,128)S(1)}, u32[]{:S(2)}, u32[]{:S(2)}) %collective-permute-start.10) | collective-permute-done | bytes 131104 | tf_op jit(solution)/shard_map/ppermute | solution.py:116
  44.3 1.6 %collective-permute-start.11 = (f32[64,512]{1,0:T(8,128)S(1)}, f32[64,512]{1,0:T(8,128)S(1)}, u32[]{:S(2)}, u32[]{:S(2)}) collective-permute-start(f32[64,512]{1,0:T(8,128)S(1)} %add.7.refs_0_), channel_id=1, source_target_pairs={{0,16},{8,24},{16,0},{24,8},{1,17},{9,25},{17,1},{25,9},{2,18},{10... | collective-permute-start | bytes 393224 | tf_op jit(solution)/shard_map/ppermute | solution.py:199
  45.9 4.0 %collective-permute-done.11.refs_1_ = f32[64,512]{1,0:T(8,128)S(1)} collective-permute-done((f32[64,512]{1,0:T(8,128)S(1)}, f32[64,512]{1,0:T(8,128)S(1)}, u32[]{:S(2)}, u32[]{:S(2)}) %collective-permute-start.11) | collective-permute-done | bytes 131104 | tf_op jit(solution)/shard_map/ppermute | solution.py:199
  50.0 0.1 collective-permute-start.12
  50.0 1.3 %collective-permute-done.12.away = f32[64,512]{1,0:T(8,128)S(1)} collective-permute-done((f32[64,512]{1,0:T(8,128)S(1)}, f32[64,512]{1,0:T(8,128)S(1)}, u32[]{:S(2)}, u32[]{:S(2)}) %collective-permute-start.12) | collective-permute-done | bytes 131104 | tf_op jit(solution)/shard_map/ppermute | solution.py:116
  51.4 0.7 multiply_other.3
  52.1 1.1 %collective-permute-start.13 = (f32[160,128]{1,0:T(8,128)S(1)}, f32[160,128]{1,0:T(8,128)S(1)}, u32[]{:S(2)}, u32[]{:S(2)}) collective-permute-start(f32[160,128]{1,0:T(8,128)S(1)} %get-tuple-element.58.sent), channel_id=1, source_target_pairs={{0,1},{1,0},{2,3},{3,2},{4,5},{5,4},{6,7},{7,6},{8,9},{9,8},{10,11... | collective-permute-start | bytes 245768 | tf_op jit(solution)/shard_map/ppermute | solution.py:116
  53.2 2.3 %collective-permute-start.14 = (f32[160,128]{1,0:T(8,128)S(1)}, f32[160,128]{1,0:T(8,128)S(1)}, u32[]{:S(2)}, u32[]{:S(2)}) collective-permute-start(f32[160,128]{1,0:T(8,128)S(1)} %get-tuple-element.60), channel_id=1, source_target_pairs={{0,3},{1,2},{2,1},{3,0},{4,7},{5,6},{6,5},{7,4},{8,11},{9,10},{10,... | collective-permute-start | bytes 245768 | tf_op jit(solution)/shard_map/ppermute | solution.py:116
  55.5 0.5 multiply_own.3
  56.0 0.2 collective-permute-start.15
  56.2 0.5 collective-permute-done.13.refs_0_
  56.6 2.4 %collective-permute-done.14.refs_1_ = f32[160,128]{1,0:T(8,128)S(1)} collective-permute-done((f32[160,128]{1,0:T(8,128)S(1)}, f32[160,128]{1,0:T(8,128)S(1)}, u32[]{:S(2)}, u32[]{:S(2)}) %collective-permute-start.14) | collective-permute-done | bytes 81952 | tf_op jit(solution)/shard_map/ppermute | solution.py:116
  59.0 1.4 %collective-permute-done.15.refs_2_ = f32[160,128]{1,0:T(8,128)S(1)} collective-permute-done((f32[160,128]{1,0:T(8,128)S(1)}, f32[160,128]{1,0:T(8,128)S(1)}, u32[]{:S(2)}, u32[]{:S(2)}) %collective-permute-start.15) | collective-permute-done | bytes 81952 | tf_op jit(solution)/shard_map/ppermute | solution.py:116
  60.5 2.5 %collective-permute-start.16 = (f32[160,128]{1,0:T(8,128)S(1)}, f32[160,128]{1,0:T(8,128)S(1)}, u32[]{:S(2)}, u32[]{:S(2)}) collective-permute-start(f32[160,128]{1,0:T(8,128)S(1)} %collect.3.one), channel_id=1, source_target_pairs={{0,4},{1,5},{2,6},{3,7},{4,0},{5,1},{6,2},{7,3},{8,12},{9,13},{10,... | collective-permute-start | bytes 245768 | tf_op jit(solution)/shard_map/ppermute | solution.py:116
  63.0 3.8 %collective-permute-done.16.two = f32[160,128]{1,0:T(8,128)S(1)} collective-permute-done((f32[160,128]{1,0:T(8,128)S(1)}, f32[160,128]{1,0:T(8,128)S(1)}, u32[]{:S(2)}, u32[]{:S(2)}) %collective-permute-start.16) | collective-permute-done | bytes 81952 | tf_op jit(solution)/shard_map/ppermute | solution.py:116
  66.8 0.3 collective-permute-start.19
  67.1 0.6 collective-permute-start.17
  67.7 2.7 %collective-permute-start.18 = (f32[128,128]{1,0:T(8,128)S(1)}, f32[128,128]{1,0:T(8,128)S(1)}, u32[]{:S(2)}, u32[]{:S(2)}) collective-permute-start(f32[128,128]{1,0:T(8,128)S(1)} %top.3.value), channel_id=1, source_target_pairs={{0,3},{1,2},{2,1},{3,0},{4,7},{5,6},{6,5},{7,4},{8,11},{9,10},{10,... | collective-permute-start | bytes 196616 | tf_op jit(solution)/shard_map/ppermute | solution.py:116
  70.3 2.8 %eliminate.3.inverse = f32[64,64]{1,0:T(8,128)S(1)} custom-call(f32[160,128]{1,0:T(8,128)S(1)} %collect.3.one, f32[160,128]{1,0:T(8,128)S(1)} %collective-permute-done.16.two), custom_call_target="tpu_custom_call" | custom-call | flops 100000000 | bytes 8388608 | tf_op jit(solution)/shard_map/eliminate/pallas_call | solution.py:42
  73.2 1.0 %widen.1 = (f32[64,512]{1,0:T(8,128)S(1)}, f32[64,512]{1,0:T(8,128)S(1)}, f32[32,128]{1,0:T(8,128)S(1)}) custom-call(f32[64,64]{1,0:T(8,128)S(1)} %eliminate.3.inverse, f32[256,128]{1,0:T(8,128)S(1)} %unfold.7.stacked.own, f32[256,128]{1,0:T(8,128)S(1)} %unfold.6.stacked.other), custom_call_target="tpu_custom_call" | custom-call | flops 100000000 | bytes 1048576 | tf_op jit(solution)/shard_map/widen/pallas_call | solution.py:42
  74.2 3.0 %final.2 = (f32[1024,1024]{1,0:T(8,128)}, f32[1024,1024]{1,0:T(8,128)}, f32[64,1024]{1,0:T(8,128)}) custom-call(f32[64,64]{1,0:T(8,128)S(1)} %eliminate.3.inverse, f32[64,512]{1,0:T(8,128)S(1)} %collective-permute-done.12.away, f32[64,512]{1,0:T(8,128)S(1)} %add.8.mine, f32[256,128]{1,0:T(8,128)S(1)} %unfold.7.stacked.own, ...), custom_call_target="tpu_custom_call" | custom-call | flops 201326592 | bytes 4194304 | tf_op jit(solution)/shard_map/final/pallas_call | solution.py:42
  77.3 1.6 %collective-permute-start.21 = (f32[32,128]{1,0:T(8,128)S(1)}, f32[32,128]{1,0:T(8,128)S(1)}, u32[]{:S(2)}, u32[]{:S(2)}) collective-permute-start(f32[32,128]{1,0:T(8,128)S(1)} %add.9.one), channel_id=1, source_target_pairs={{0,16},{8,24},{16,0},{24,8},{1,17},{9,25},{17,1},{25,9},{2,18},{10... | collective-permute-start | bytes 49160 | tf_op jit(solution)/shard_map/ppermute | solution.py:116
  78.8 2.8 %final.3 = (f32[1024,1024]{1,0:T(8,128)}, f32[1024,1024]{1,0:T(8,128)}) custom-call(f32[64,64]{1,0:T(8,128)S(1)} %eliminate.3.inverse, f32[64,512]{1,0:T(8,128)S(1)} %collective-permute-done.12.away, f32[64,512]{1,0:T(8,128)S(1)} %add.8.mine, f32[256,128]{1,0:T(8,128)S(1)} %unfold.6.stacked.other, ...), custom_call_target="tpu_custom_call", output_to_operand_aliasing={{0}: (5, {}), {1}: (6, {})} | custom-call | flops 201326592 | bytes 4194304 | tf_op jit(solution)/shard_map/final/pallas_call | solution.py:42
  81.6 3.8 %finish.1 = f32[64,1024]{1,0:T(8,128)} custom-call(f32[32,128]{1,0:T(8,128)S(1)} %add.9.one, f32[32,128]{1,0:T(8,128)S(1)} %collective-permute-done.21.two, f32[64,512]{1,0:T(8,128)S(1)} %get-tuple-element.70.own, f32[64,512]{1,0:T(8,128)S(1)} %get-tuple-element.71.other), custom_call_target="tpu_custom_call" | custom-call | flops 100000000 | bytes 8388608 | tf_op jit(solution)/shard_map/finish/pallas_call | solution.py:42
  (22 shorter events, 0.3 us)
Async XLA Ops:
  6.9 1.5 %collective-permute-start = (f32[64,512]{1,0:T(8,128)S(1)}, f32[64,512]{1,0:T(8,128)S(1)}, u32[]{:S(2)}, u32[]{:S(2)}) collective-permute-start(f32[64,512]{1,0:T(8,128)S(1)} %get-tuple-element.39), channel_id=1, source_target_pairs={{0,8},{8,0},{16,24},{24,16},{1,9},{9,1},{17,25},{25,17},{2,10},{10... | collective-permute-start | bytes 393224 | tf_op jit(solution)/shard_map/ppermute | solution.py:116
  8.4 6.8 %collective-permute-start.1 = (f32[64,512]{1,0:T(8,128)S(1)}, f32[64,512]{1,0:T(8,128)S(1)}, u32[]{:S(2)}, u32[]{:S(2)}) collective-permute-start(f32[64,512]{1,0:T(8,128)S(1)} %add.5.refs_0_), channel_id=1, source_target_pairs={{0,16},{8,24},{16,0},{24,8},{1,17},{9,25},{17,1},{25,9},{2,18},{10... | collective-permute-start | bytes 393224 | tf_op jit(solution)/shard_map/ppermute | solution.py:199
  15.2 1.4 %collective-permute-start.2 = (f32[64,512]{1,0:T(8,128)S(1)}, f32[64,512]{1,0:T(8,128)S(1)}, u32[]{:S(2)}, u32[]{:S(2)}) collective-permute-start(f32[64,512]{1,0:T(8,128)S(1)} %add.6.mine), channel_id=1, source_target_pairs={{0,8},{8,0},{16,24},{24,16},{1,9},{9,1},{17,25},{25,17},{2,10},{10... | collective-permute-start | bytes 393224 | tf_op jit(solution)/shard_map/ppermute | solution.py:116
  17.3 5.5 %collective-permute-start.3 = (f32[160,128]{1,0:T(8,128)S(1)}, f32[160,128]{1,0:T(8,128)S(1)}, u32[]{:S(2)}, u32[]{:S(2)}) collective-permute-start(f32[160,128]{1,0:T(8,128)S(1)} %get-tuple-element.44.sent), channel_id=1, source_target_pairs={{0,1},{1,0},{2,3},{3,2},{4,5},{5,4},{6,7},{7,6},{8,9},{9,8},{10,11... | collective-permute-start | bytes 245768 | tf_op jit(solution)/shard_map/ppermute | solution.py:116
  19.1 5.5 %collective-permute-start.4 = (f32[160,128]{1,0:T(8,128)S(1)}, f32[160,128]{1,0:T(8,128)S(1)}, u32[]{:S(2)}, u32[]{:S(2)}) collective-permute-start(f32[160,128]{1,0:T(8,128)S(1)} %get-tuple-element.46), channel_id=1, source_target_pairs={{0,3},{1,2},{2,1},{3,0},{4,7},{5,6},{6,5},{7,4},{8,11},{9,10},{10,... | collective-permute-start | bytes 245768 | tf_op jit(solution)/shard_map/ppermute | solution.py:116
  21.1 4.5 %collective-permute-start.5 = (f32[160,128]{1,0:T(8,128)S(1)}, f32[160,128]{1,0:T(8,128)S(1)}, u32[]{:S(2)}, u32[]{:S(2)}) collective-permute-start(f32[160,128]{1,0:T(8,128)S(1)} %get-tuple-element.47), channel_id=1, source_target_pairs={{0,2},{1,3},{2,0},{3,1},{4,6},{5,7},{6,4},{7,5},{8,10},{9,11},{10,... | collective-permute-start | bytes 245768 | tf_op jit(solution)/shard_map/ppermute | solution.py:116
  25.6 6.3 %collective-permute-start.6 = (f32[160,128]{1,0:T(8,128)S(1)}, f32[160,128]{1,0:T(8,128)S(1)}, u32[]{:S(2)}, u32[]{:S(2)}) collective-permute-start(f32[160,128]{1,0:T(8,128)S(1)} %collect.2.one), channel_id=1, source_target_pairs={{0,4},{1,5},{2,6},{3,7},{4,0},{5,1},{6,2},{7,3},{8,12},{9,13},{10,... | collective-permute-start | bytes 245768 | tf_op jit(solution)/shard_map/ppermute | solution.py:116
  31.9 6.3 %collective-permute-start.9 = (f32[128,128]{1,0:T(8,128)S(1)}, f32[128,128]{1,0:T(8,128)S(1)}, u32[]{:S(2)}, u32[]{:S(2)}) collective-permute-start(f32[128,128]{1,0:T(8,128)S(1)} %top.2.value), channel_id=1, source_target_pairs={{0,2},{1,3},{2,0},{3,1},{4,6},{5,7},{6,4},{7,5},{8,10},{9,11},{10,... | collective-permute-start | bytes 196616 | tf_op jit(solution)/shard_map/ppermute | solution.py:116
  32.2 6.0 %collective-permute-start.7 = (f32[128,128]{1,0:T(8,128)S(1)}, f32[128,128]{1,0:T(8,128)S(1)}, u32[]{:S(2)}, u32[]{:S(2)}) collective-permute-start(f32[128,128]{1,0:T(8,128)S(1)} %top.2.value), channel_id=1, source_target_pairs={{0,1},{1,0},{2,3},{3,2},{4,5},{5,4},{6,7},{7,6},{8,9},{9,8},{10,11... | collective-permute-start | bytes 196616 | tf_op jit(solution)/shard_map/ppermute | solution.py:116
  33.7 5.2 %collective-permute-start.8 = (f32[128,128]{1,0:T(8,128)S(1)}, f32[128,128]{1,0:T(8,128)S(1)}, u32[]{:S(2)}, u32[]{:S(2)}) collective-permute-start(f32[128,128]{1,0:T(8,128)S(1)} %top.2.value), channel_id=1, source_target_pairs={{0,3},{1,2},{2,1},{3,0},{4,7},{5,6},{6,5},{7,4},{8,11},{9,10},{10,... | collective-permute-start | bytes 196616 | tf_op jit(solution)/shard_map/ppermute | solution.py:116
  42.9 1.4 %collective-permute-start.10 = (f32[64,512]{1,0:T(8,128)S(1)}, f32[64,512]{1,0:T(8,128)S(1)}, u32[]{:S(2)}, u32[]{:S(2)}) collective-permute-start(f32[64,512]{1,0:T(8,128)S(1)} %get-tuple-element.53), channel_id=1, source_target_pairs={{0,8},{8,0},{16,24},{24,16},{1,9},{9,1},{17,25},{25,17},{2,10},{10... | collective-permute-start | bytes 393224 | tf_op jit(solution)/shard_map/ppermute | solution.py:116
  44.3 5.6 %collective-permute-start.11 = (f32[64,512]{1,0:T(8,128)S(1)}, f32[64,512]{1,0:T(8,128)S(1)}, u32[]{:S(2)}, u32[]{:S(2)}) collective-permute-start(f32[64,512]{1,0:T(8,128)S(1)} %add.7.refs_0_), channel_id=1, source_target_pairs={{0,16},{8,24},{16,0},{24,8},{1,17},{9,25},{17,1},{25,9},{2,18},{10... | collective-permute-start | bytes 393224 | tf_op jit(solution)/shard_map/ppermute | solution.py:199
  50.0 1.4 %collective-permute-start.12 = (f32[64,512]{1,0:T(8,128)S(1)}, f32[64,512]{1,0:T(8,128)S(1)}, u32[]{:S(2)}, u32[]{:S(2)}) collective-permute-start(f32[64,512]{1,0:T(8,128)S(1)} %add.8.mine), channel_id=1, source_target_pairs={{0,8},{8,0},{16,24},{24,16},{1,9},{9,1},{17,25},{25,17},{2,10},{10... | collective-permute-start | bytes 393224 | tf_op jit(solution)/shard_map/ppermute | solution.py:116
  52.1 4.5 %collective-permute-start.13 = (f32[160,128]{1,0:T(8,128)S(1)}, f32[160,128]{1,0:T(8,128)S(1)}, u32[]{:S(2)}, u32[]{:S(2)}) collective-permute-start(f32[160,128]{1,0:T(8,128)S(1)} %get-tuple-element.58.sent), channel_id=1, source_target_pairs={{0,1},{1,0},{2,3},{3,2},{4,5},{5,4},{6,7},{7,6},{8,9},{9,8},{10,11... | collective-permute-start | bytes 245768 | tf_op jit(solution)/shard_map/ppermute | solution.py:116
  53.2 5.9 %collective-permute-start.14 = (f32[160,128]{1,0:T(8,128)S(1)}, f32[160,128]{1,0:T(8,128)S(1)}, u32[]{:S(2)}, u32[]{:S(2)}) collective-permute-start(f32[160,128]{1,0:T(8,128)S(1)} %get-tuple-element.60), channel_id=1, source_target_pairs={{0,3},{1,2},{2,1},{3,0},{4,7},{5,6},{6,5},{7,4},{8,11},{9,10},{10,... | collective-permute-start | bytes 245768 | tf_op jit(solution)/shard_map/ppermute | solution.py:116
  56.0 4.5 %collective-permute-start.15 = (f32[160,128]{1,0:T(8,128)S(1)}, f32[160,128]{1,0:T(8,128)S(1)}, u32[]{:S(2)}, u32[]{:S(2)}) collective-permute-start(f32[160,128]{1,0:T(8,128)S(1)} %get-tuple-element.61), channel_id=1, source_target_pairs={{0,2},{1,3},{2,0},{3,1},{4,6},{5,7},{6,4},{7,5},{8,10},{9,11},{10,... | collective-permute-start | bytes 245768 | tf_op jit(solution)/shard_map/ppermute | solution.py:116
  60.5 6.3 %collective-permute-start.16 = (f32[160,128]{1,0:T(8,128)S(1)}, f32[160,128]{1,0:T(8,128)S(1)}, u32[]{:S(2)}, u32[]{:S(2)}) collective-permute-start(f32[160,128]{1,0:T(8,128)S(1)} %collect.3.one), channel_id=1, source_target_pairs={{0,4},{1,5},{2,6},{3,7},{4,0},{5,1},{6,2},{7,3},{8,12},{9,13},{10,... | collective-permute-start | bytes 245768 | tf_op jit(solution)/shard_map/ppermute | solution.py:116
  66.8 6.3 %collective-permute-start.19 = (f32[128,128]{1,0:T(8,128)S(1)}, f32[128,128]{1,0:T(8,128)S(1)}, u32[]{:S(2)}, u32[]{:S(2)}) collective-permute-start(f32[128,128]{1,0:T(8,128)S(1)} %top.3.value), channel_id=1, source_target_pairs={{0,2},{1,3},{2,0},{3,1},{4,6},{5,7},{6,4},{7,5},{8,10},{9,11},{10,... | collective-permute-start | bytes 196616 | tf_op jit(solution)/shard_map/ppermute | solution.py:116
  67.1 6.1 %collective-permute-start.17 = (f32[128,128]{1,0:T(8,128)S(1)}, f32[128,128]{1,0:T(8,128)S(1)}, u32[]{:S(2)}, u32[]{:S(2)}) collective-permute-start(f32[128,128]{1,0:T(8,128)S(1)} %top.3.value), channel_id=1, source_target_pairs={{0,1},{1,0},{2,3},{3,2},{4,5},{5,4},{6,7},{7,6},{8,9},{9,8},{10,11... | collective-permute-start | bytes 196616 | tf_op jit(solution)/shard_map/ppermute | solution.py:116
  67.7 5.5 %collective-permute-start.18 = (f32[128,128]{1,0:T(8,128)S(1)}, f32[128,128]{1,0:T(8,128)S(1)}, u32[]{:S(2)}, u32[]{:S(2)}) collective-permute-start(f32[128,128]{1,0:T(8,128)S(1)} %top.3.value), channel_id=1, source_target_pairs={{0,3},{1,2},{2,1},{3,0},{4,7},{5,6},{6,5},{7,4},{8,11},{9,10},{10,... | collective-permute-start | bytes 196616 | tf_op jit(solution)/shard_map/ppermute | solution.py:116
  74.2 3.0 %collective-permute-start.20 = (f32[32,128]{1,0:T(8,128)S(1)}, f32[32,128]{1,0:T(8,128)S(1)}, u32[]{:S(2)}, u32[]{:S(2)}) collective-permute-start(f32[32,128]{1,0:T(8,128)S(1)} %get-tuple-element.69.refs_0_), channel_id=1, source_target_pairs={{0,8},{8,0},{16,24},{24,16},{1,9},{9,1},{17,25},{25,17},{2,10},{10... | collective-permute-start | bytes 49160 | tf_op jit(solution)/shard_map/ppermute | solution.py:116
  77.3 4.4 %collective-permute-start.21 = (f32[32,128]{1,0:T(8,128)S(1)}, f32[32,128]{1,0:T(8,128)S(1)}, u32[]{:S(2)}, u32[]{:S(2)}) collective-permute-start(f32[32,128]{1,0:T(8,128)S(1)} %add.9.one), channel_id=1, source_target_pairs={{0,16},{8,24},{16,0},{24,8},{1,17},{9,25},{17,1},{25,9},{2,18},{10... | collective-permute-start | bytes 49160 | tf_op jit(solution)/shard_map/ppermute | solution.py:116

commit v9 on v8

--- a/solution.py
+++ b/solution.py
@@ -50,6 +50,13 @@
         compiler_params=pltpu.CompilerParams(vmem_limit_bytes=limit * MIB),
         cost_estimate=pl.CostEstimate(flops=cost[0], bytes_accessed=cost[1], transcendentals=0),
     )(*[pltpu.with_memory_space_constraint(a, pltpu.HBM) if m is pltpu.HBM else a for a, m in ins])
+
+
+def reciprocal(value):
+    guess = pl.reciprocal(value, approx=True)
+    for _ in range(2):
+        guess = guess * (2.0 - value * guess)
+    return guess
 
 
 def invert(packed, out):
@@ -78,7 +85,7 @@
             (j, p): jnp.broadcast_to(rows[j][:, k + p : k + p + 1], full) for j in after for p in range(wide)
         }
         for p in range(wide):
-            inverse = 1.0 / core[p, p]
+            inverse = reciprocal(core[p, p])
             factors = [core[p, q] * inverse for q in range(p + 1, wide)]
             for q, factor in zip(range(p + 1, wide), factors):
                 for t in range(q, wide):
@@ -157,7 +164,7 @@
             return call(body, "add", [(a, pltpu.VMEM) for a in arrays], [out], cost=(10**5, 10**6), limit=4)[0]
 
         def first(right):
-            def body(o_in, s_in, d_in, r_in, o, d, h0, l0, h1, l1, away, mine, sp, right, r_sem, sems):
+            def body(o_in, s_in, d_in, r_in, o, u, h0, l0, h1, l1, away, mine, sp, d, right, r_sem, sems):
                 s = place()
                 right_move = pltpu.make_async_copy(r_in, right, r_sem)
                 right_move.start()
@@ -176,7 +183,9 @@
                         moves[i, a].wait()
                     for p, (h, l) in enumerate(((h0, l0), (h1, l1))):
                         at = chunk(i), pl.ds(pix_at(p, s), half)
-                        pair = split(o[at] - sp[at] + d[at] * (1 / MU))
+                        pulled = o[at] + d[at] * (1 / MU)
+                        u[at] = pulled
+                        pair = split(pulled - sp[at])
                         h[chunk(i), :], l[chunk(i), :] = pair
                         term = dot_nt(rights[p], pair)
                         total = term if total is None else total + term
@@ -186,7 +195,7 @@
             ins = [(a, pltpu.HBM) for a in (observed, sparse_init, dual_init, right)]
             outs = [((n_rows, n_cols), F32, pltpu.VMEM)] * 2 + [((n_rows, half), BF16, pltpu.VMEM)] * 4
             outs += [((rank, n_rows // 2), F32, pltpu.VMEM)] * 2
-            scratch = [pltpu.VMEM((n_rows, n_cols), F32), pltpu.VMEM((rank, n_cols), F32)]
+            scratch = [pltpu.VMEM((n_rows, n_cols), F32)] * 2 + [pltpu.VMEM((rank, n_cols), F32)]
             scratch += [pltpu.SemaphoreType.DMA(()), pltpu.SemaphoreType.DMA((steps, 3))]
             cost = (6 * rank * n_rows * n_cols, 16 * n_rows * n_cols)
             got = call(body, "first", ins, outs, scratch, cost=cost)
@@ -313,25 +322,25 @@
             tops = jnp.concatenate([left_high, left_low, left_high], axis=0)
             return left, (wide_high, wide_low), tops, jnp.concatenate([wide_high, wide_high, wide_low], axis=0)
 
-        def middle(p, inverse, panel, stacked, o, d, before):
-            def body(inverse, away, mine, stacked, o, d, *rest):
+        def middle(p, inverse, panel, stacked, o, u, before):
+            def body(inverse, away, mine, stacked, o, u, *rest):
                 s = place()
                 base, high, low, *after = rest[2 * p :]
                 _, right, tops, wides = halves(inverse, (away, mine), stacked)
                 for i in range(steps):
                     lowrank = dot(tops[:, chunk(i)], wides, ((0,), (0,)))
                     at = chunk(i), pl.ds(pix_at(p, s), half)
-                    seen = o[at]
-                    value = seen + d[at] * (1 / MU) - lowrank
+                    value = u[at] - lowrank
                     scaled = jnp.clip(value, -TAU, TAU)
-                    base[chunk(i), :] = seen + scaled
-                    pair = split(seen + 2.0 * scaled - value)
+                    moved = o[at] + scaled
+                    base[chunk(i), :] = moved
+                    pair = split(moved + (scaled - value))
                     high[chunk(i), :], low[chunk(i), :] = pair
                     term = dot_nt(right, pair)
                     side, block = divmod(i, steps // 2)
                     after[side][:, chunk(block)] = rest[side][:, chunk(block)] + term if p else term
 
-            arrays = [inverse, *panel, stacked, o, d] + (list(before) if p else [])
+            arrays = [inverse, *panel, stacked, o, u] + (list(before) if p else [])
             outs = [((n_rows, half), F32, pltpu.VMEM)] + [((n_rows, half), BF16, pltpu.VMEM)] * 2
             outs += [((rank, n_rows // 2), F32, pltpu.VMEM)] * 2
             cost = (9 * rank * n_rows * n_cols, 4 * n_rows * n_cols)
@@ -339,42 +348,46 @@
             base, high, low, *part = call(body, "middle", ins, outs, cost=cost)
             return base, (high, low), part
 
-        def final(p, inverse, panel, stacked, base, before):
+        def put(sources, targets, p, s, sems):
+            moves = []
+            for i in range(steps):
+                for a, (source, target) in enumerate(zip(sources, targets)):
+                    block = target.at[pl.ds(gal_at(i, s), tall), pl.ds(pix_at(p, s), half)]
+                    move = pltpu.make_async_copy(source.at[chunk(i), :], block, sems.at[i, a])
+                    move.start(priority=(i + a) % 2)
+                    moves.append(move)
+            return moves
+
+        def final(p, inverse, panel, stacked, base, before=()):
             def body(inverse, away, mine, stacked, base, *rest):
                 s = place()
-                sparse, dual, *outs, sparse_part, dual_part, left_part, sems = rest[2 * p :]
+                sparse, dual, *outs = rest[len(before) :]
+                *outs, left_part, sems = outs
                 left, _, tops, wides = halves(inverse, (away, mine), stacked)
-                moves = []
-                if not p:
+                if p:
+                    moves = put(rest[:2], outs, 0, s, sems)
+                else:
                     for i in range(steps):
                         left_part[:, pl.ds(gal_at(i, s), tall)] = left[:, chunk(i)]
-                    moves.append(pltpu.make_async_copy(left_part, outs[0], sems.at[steps, 0]))
+                    moves = [pltpu.make_async_copy(left_part, outs[0], sems.at[0, 0])]
                     moves[0].start()
                 for i in range(steps):
                     value = base[chunk(i), :] - dot(tops[:, chunk(i)], wides, ((0,), (0,)))
                     scaled = jnp.clip(value, -TAU, TAU)
-                    sparse_part[chunk(i), :] = value - scaled
-                    dual_part[chunk(i), :] = MU * scaled
-                    for a, (source, target) in enumerate(((sparse_part, sparse), (dual_part, dual))):
-                        block = target.at[pl.ds(gal_at(i, s), tall), pl.ds(pix_at(p, s), half)]
-                        move = pltpu.make_async_copy(source.at[chunk(i), :], block, sems.at[i, a])
-                        move.start(priority=(i + a) % 2)
-                        moves.append(move)
+                    sparse[chunk(i), :] = value - scaled
+                    dual[chunk(i), :] = MU * scaled
                 for move in moves:
                     move.wait()
 
-            ins = [(a, pltpu.VMEM) for a in (inverse, *panel, stacked, base)]
-            outs = [((n_rows, n_cols), F32, pltpu.HBM)] * 2
-            aliases = {}
+            ins = [(a, pltpu.VMEM) for a in (inverse, *panel, stacked, base, *before)]
+            outs = [((n_rows, half), F32, pltpu.VMEM)] * 2
             if p:
-                ins += [(a, pltpu.HBM) for a in before[:2]]
-                aliases = {5: 0, 6: 1}
+                outs += [((n_rows, n_cols), F32, pltpu.HBM)] * 2
             else:
                 outs += [((rank, n_rows), F32, pltpu.HBM)]
-            scratch = [pltpu.VMEM((n_rows, half), F32)] * 2 + [pltpu.VMEM((rank, n_rows), F32)]
-            scratch += [pltpu.SemaphoreType.DMA((steps + 1, 2))]
+            scratch = [pltpu.VMEM((rank, n_rows), F32), pltpu.SemaphoreType.DMA((steps, 2))]
             cost = (3 * rank * n_rows * n_cols, 4 * n_rows * n_cols)
-            return call(body, "final", ins, outs, scratch, aliases, cost)
+            return call(body, "final", ins, outs, scratch, cost=cost)
 
         def widen(inverse, own, other):
             def body(inverse, own, other, wide_own, wide_other, out):
@@ -389,20 +402,25 @@
             outs = [((rank, half), F32, pltpu.VMEM)] * 2 + [((gram_rows, LANES), F32, pltpu.VMEM)]
             return call(body, "widen", ins, outs, cost=(10**8, MIB), limit=8)
 
-        def finish(one, two, wide):
-            def body(one, two, own, other, out, inverse, right, sem):
-                s = place()
+        def finish(one, two, wide, made, outs):
+            def body(one, two, own, other, sparse, dual, _, __, out, sparse_out, dual_out, inverse, right, sem, sems):
+                s = place()
+                moves = put((sparse, dual), (sparse_out, dual_out), 1, s, sems)
                 invert(one[...] + two[...], inverse)
                 for p, value in enumerate((own, other)):
-                    right[:, pl.ds(pix_at(p, s), half)] = dot(inverse[...], value[...], ((1,), (0,)), HIGH)
-                move = pltpu.make_async_copy(right, out, sem)
-                move.start()
-                move.wait()
-
-            ins = [(a, pltpu.VMEM) for a in (one, two, *wide)]
-            outs = [((rank, n_cols), F32, pltpu.HBM)]
-            scratch = [pltpu.VMEM((rank, rank), F32), pltpu.VMEM((rank, n_cols), F32), pltpu.SemaphoreType.DMA(())]
-            return call(body, "finish", ins, outs, scratch, cost=(10**8, 8 * MIB))[0]
+                    at = pl.ds(pix_at(p, s), half)
+                    right[:, at] = dot(inverse[...], value[...], ((1,), (0,)), HIGH)
+                    move = pltpu.make_async_copy(right.at[:, at], out.at[:, at], sem.at[p])
+                    move.start()
+                    moves.append(move)
+                for move in moves:
+                    move.wait()
+
+            ins = [(a, pltpu.VMEM) for a in (one, two, *wide, *made)] + [(a, pltpu.HBM) for a in outs]
+            results = [((rank, n_cols), F32, pltpu.HBM)] + [((n_rows, n_cols), F32, pltpu.HBM)] * 2
+            scratch = [pltpu.VMEM((rank, rank), F32), pltpu.VMEM((rank, n_cols), F32)]
+            scratch += [pltpu.SemaphoreType.DMA((2,)), pltpu.SemaphoreType.DMA((steps, 2))]
+            return call(body, "finish", ins, results, scratch, {6: 1, 7: 2}, cost=(10**8, 8 * MIB))
 
         seen, pulls, own, other, part = first(right_init)
         base = [None, None]
@@ -414,15 +432,14 @@
                 base[1], other, part = middle(1, inverse, panel, other_wide, seen, pulls, part)
             else:
                 *wide, gram = widen(inverse, own_wide, other_wide)
-                outs = final(0, inverse, panel, own_wide, base[0], None)
+                *made, left = final(0, inverse, panel, own_wide, base[0])
                 bit = 1
                 while 2 * bit < n_gal:
                     gram = add(gram, swap(gram, "gal", bit))
                     bit *= 2
                 got = swap(gram, "gal", bit)
-                sparse, dual = final(1, inverse, panel, other_wide, base[1], outs)
-                left = outs[2]
-                right = finish(gram, got, wide)
+                *made, sparse, dual = final(1, inverse, panel, other_wide, base[1], made)
+                right, sparse, dual = finish(gram, got, wide, made, (sparse, dual))
         return sparse, dual, left, right
 
     return jax.shard_map(

time: 85.8 us -> 87.4 us (1.019)
  waiting for transfers between devices: 29.3 us -> 30.4 us
    ppermute x20, waiting for transfers between devices: 21.5 us -> 22.6 us  [swap(): return lax.ppermute(value, axis, [(i, i ^ bit) for i in range(n)])]
  transfers between devices with their start and end apart: 22 -> 22, of which waited for: 15 -> 14; matrix products, arithmetic and copies ran while one was open for 0% -> 0% of each run, Pallas kernels for 14% -> 12%
where the time goes in v9:
time: 87.4 us; the launch traced here: 87.2 us
  waiting for transfers between devices  30.4 us (35%)
  Pallas kernels  29.3 us (34%)
  starting transfers between devices  26.5 us (30%)
  between operations  0.99 us (1%)
    pallas_call x26, Pallas kernels, call(): pl.pallas_call(body, name=name, in_specs=[pl.BlockSpec(memory_space=space...  29.3 us
    ppermute x20, waiting for transfers between devices, swap(): return lax.ppermute(value, axis, [(i, i ^ bit) for i in range(n)])  22.6 us
    ppermute x20, starting transfers between devices, swap(): return lax.ppermute(value, axis, [(i, i ^ bit) for i in range(n)])  21.9 us
    ppermute x2, waiting for transfers between devices, sum_gal(): lax.ppermute(mine, 'gal', [(i, (i + CORES * k) % n_gal) for i in range(n_...  7.84 us
    ppermute x2, starting transfers between devices, sum_gal(): lax.ppermute(mine, 'gal', [(i, (i + CORES * k) % n_gal) for i in range(n_...  4.53 us
  transfers between devices with their start and end apart: 22, of which 14 were waited for; matrix products, arithmetic and copies ran while one was open for 0% of the time, Pallas kernels for 12%

profile of v9, /device:TPU:0, one launch (start us, length us, event | category | flops | bytes accessed | tf_op | source)
XLA Modules:
  0.0 87.2 jit_solution(5441241768760680944)
XLA Ops:
  0.6 6.4 %first.1 = (f32[1024,1024]{1,0:T(8,128)S(1)}, f32[1024,1024]{1,0:T(8,128)S(1)}, bf16[1024,512]{1,0:T(8,128)(2,1)S(1)}, bf16[1024,512]{1,0:T(8,128)(2,1)S(1)}, bf...) custom-call(f32[1024,1024]{1,0:T(8,128)} %o_in.1, ...), custom_call_target="tpu_custom_call" | custom-call | flops 402653184 | bytes 16777216 | tf_op jit(solution)/shard_map/first/pallas_call | solution.py:42
  7.1 0.5 collective-permute-start
  7.6 1.0 %collective-permute-done.refs_1_ = f32[64,512]{1,0:T(8,128)S(1)} collective-permute-done((f32[64,512]{1,0:T(8,128)S(1)}, f32[64,512]{1,0:T(8,128)S(1)}, u32[]{:S(2)}, u32[]{:S(2)}) %collective-permute-start) | collective-permute-done | bytes 131104 | tf_op jit(solution)/shard_map/ppermute | solution.py:123
  8.6 2.9 %collective-permute-start.1 = (f32[64,512]{1,0:T(8,128)S(1)}, f32[64,512]{1,0:T(8,128)S(1)}, u32[]{:S(2)}, u32[]{:S(2)}) collective-permute-start(f32[64,512]{1,0:T(8,128)S(1)} %add.5.refs_0_), channel_id=1, source_target_pairs={{0,16},{8,24},{16,0},{24,8},{1,17},{9,25},{17,1},{25,9},{2,18},{10... | collective-permute-start | bytes 393224 | tf_op jit(solution)/shard_map/ppermute | solution.py:208
  11.5 3.8 %collective-permute-done.1.refs_1_ = f32[64,512]{1,0:T(8,128)S(1)} collective-permute-done((f32[64,512]{1,0:T(8,128)S(1)}, f32[64,512]{1,0:T(8,128)S(1)}, u32[]{:S(2)}, u32[]{:S(2)}) %collective-permute-start.1) | collective-permute-done | bytes 131104 | tf_op jit(solution)/shard_map/ppermute | solution.py:208
  15.4 0.1 collective-permute-start.2
  15.5 1.3 %collective-permute-done.2.away = f32[64,512]{1,0:T(8,128)S(1)} collective-permute-done((f32[64,512]{1,0:T(8,128)S(1)}, f32[64,512]{1,0:T(8,128)S(1)}, u32[]{:S(2)}, u32[]{:S(2)}) %collective-permute-start.2) | collective-permute-done | bytes 131104 | tf_op jit(solution)/shard_map/ppermute | solution.py:123
  16.8 0.7 multiply_other.2
  17.5 0.5 multiply_own.2
  18.0 1.9 %collective-permute-start.5 = (f32[160,128]{1,0:T(8,128)S(1)}, f32[160,128]{1,0:T(8,128)S(1)}, u32[]{:S(2)}, u32[]{:S(2)}) collective-permute-start(f32[160,128]{1,0:T(8,128)S(1)} %get-tuple-element.52), channel_id=1, source_target_pairs={{0,2},{1,3},{2,0},{3,1},{4,6},{5,7},{6,4},{7,5},{8,10},{9,11},{10,... | collective-permute-start | bytes 245768 | tf_op jit(solution)/shard_map/ppermute | solution.py:123
  19.8 1.4 %collective-permute-start.4 = (f32[160,128]{1,0:T(8,128)S(1)}, f32[160,128]{1,0:T(8,128)S(1)}, u32[]{:S(2)}, u32[]{:S(2)}) collective-permute-start(f32[160,128]{1,0:T(8,128)S(1)} %get-tuple-element.51), channel_id=1, source_target_pairs={{0,3},{1,2},{2,1},{3,0},{4,7},{5,6},{6,5},{7,4},{8,11},{9,10},{10,... | collective-permute-start | bytes 245768 | tf_op jit(solution)/shard_map/ppermute | solution.py:123
  21.2 0.3 collective-permute-start.3
  21.5 1.1 %collective-permute-done.5.refs_2_ = f32[160,128]{1,0:T(8,128)S(1)} collective-permute-done((f32[160,128]{1,0:T(8,128)S(1)}, f32[160,128]{1,0:T(8,128)S(1)}, u32[]{:S(2)}, u32[]{:S(2)}) %collective-permute-start.5) | collective-permute-done | bytes 81952 | tf_op jit(solution)/shard_map/ppermute | solution.py:123
  22.6 2.9 %collective-permute-done.4.refs_1_ = f32[160,128]{1,0:T(8,128)S(1)} collective-permute-done((f32[160,128]{1,0:T(8,128)S(1)}, f32[160,128]{1,0:T(8,128)S(1)}, u32[]{:S(2)}, u32[]{:S(2)}) %collective-permute-start.4) | collective-permute-done | bytes 81952 | tf_op jit(solution)/shard_map/ppermute | solution.py:123
  25.5 1.2 %collective-permute-done.3.refs_0_ = f32[160,128]{1,0:T(8,128)S(1)} collective-permute-done((f32[160,128]{1,0:T(8,128)S(1)}, f32[160,128]{1,0:T(8,128)S(1)}, u32[]{:S(2)}, u32[]{:S(2)}) %collective-permute-start.3) | collective-permute-done | bytes 81952 | tf_op jit(solution)/shard_map/ppermute | solution.py:123
  26.8 2.7 %collective-permute-start.6 = (f32[160,128]{1,0:T(8,128)S(1)}, f32[160,128]{1,0:T(8,128)S(1)}, u32[]{:S(2)}, u32[]{:S(2)}) collective-permute-start(f32[160,128]{1,0:T(8,128)S(1)} %collect.2.one), channel_id=1, source_target_pairs={{0,4},{1,5},{2,6},{3,7},{4,0},{5,1},{6,2},{7,3},{8,12},{9,13},{10,... | collective-permute-start | bytes 245768 | tf_op jit(solution)/shard_map/ppermute | solution.py:123
  29.4 4.0 %collective-permute-done.6.two = f32[160,128]{1,0:T(8,128)S(1)} collective-permute-done((f32[160,128]{1,0:T(8,128)S(1)}, f32[160,128]{1,0:T(8,128)S(1)}, u32[]{:S(2)}, u32[]{:S(2)}) %collective-permute-start.6) | collective-permute-done | bytes 81952 | tf_op jit(solution)/shard_map/ppermute | solution.py:123
  33.4 0.6 collective-permute-start.9
  34.0 1.6 %collective-permute-start.8 = (f32[128,128]{1,0:T(8,128)S(1)}, f32[128,128]{1,0:T(8,128)S(1)}, u32[]{:S(2)}, u32[]{:S(2)}) collective-permute-start(f32[128,128]{1,0:T(8,128)S(1)} %top.2.value), channel_id=1, source_target_pairs={{0,3},{1,2},{2,1},{3,0},{4,7},{5,6},{6,5},{7,4},{8,11},{9,10},{10,... | collective-permute-start | bytes 196616 | tf_op jit(solution)/shard_map/ppermute | solution.py:123
  35.6 1.4 %collective-permute-start.7 = (f32[128,128]{1,0:T(8,128)S(1)}, f32[128,128]{1,0:T(8,128)S(1)}, u32[]{:S(2)}, u32[]{:S(2)}) collective-permute-start(f32[128,128]{1,0:T(8,128)S(1)} %top.2.value), channel_id=1, source_target_pairs={{0,1},{1,0},{2,3},{3,2},{4,5},{5,4},{6,7},{7,6},{8,9},{9,8},{10,11... | collective-permute-start | bytes 196616 | tf_op jit(solution)/shard_map/ppermute | solution.py:123
  37.0 3.2 %eliminate.2.inverse = f32[64,64]{1,0:T(8,128)S(1)} custom-call(f32[160,128]{1,0:T(8,128)S(1)} %collect.2.one, f32[160,128]{1,0:T(8,128)S(1)} %collective-permute-done.6.two), custom_call_target="tpu_custom_call" | custom-call | flops 100000000 | bytes 8388608 | tf_op jit(solution)/shard_map/eliminate/pallas_call | solution.py:42
  40.3 1.8 %middle.2 = (f32[1024,512]{1,0:T(8,128)S(1)}, bf16[1024,512]{1,0:T(8,128)(2,1)S(1)}, bf16[1024,512]{1,0:T(8,128)(2,1)S(1)}, f32[64,512]{1,0:T(8,128)S(1)}, f32[64,512]{1,0:T(8,128)S(1)}) custom-call(f32[64,64]{1,0:T(8,128)S(1)} %eliminate.2.inverse, f32[64,512]{1,0:T(8,128)S(1)} %collective-permute-done.2.away, f32[64,512]{1,0:T(8,128)S(1)} %add.6.mine, ...), custom_call_target="tpu_custom_call" | custom-call | flops 603979776 | bytes 4194304 | tf_op jit(solution)/shard_map/middle/pallas_call | solution.py:42
  42.1 1.9 %middle.3 = (f32[1024,512]{1,0:T(8,128)S(1)}, bf16[1024,512]{1,0:T(8,128)(2,1)S(1)}, bf16[1024,512]{1,0:T(8,128)(2,1)S(1)}, f32[64,512]{1,0:T(8,128)S(1)}, f32[64,512]{1,0:T(8,128)S(1)}) custom-call(f32[64,64]{1,0:T(8,128)S(1)} %eliminate.2.inverse, f32[64,512]{1,0:T(8,128)S(1)} %collective-permute-done.2.away, f32[64,512]{1,0:T(8,128)S(1)} %add.6.mine, ...), custom_call_target="tpu_custom_call" | custom-call | flops 603979776 | bytes 4194304 | tf_op jit(solution)/shard_map/middle/pallas_call | solution.py:42
  44.0 0.1 collective-permute-start.10
  44.1 1.3 %collective-permute-done.10.refs_1_ = f32[64,512]{1,0:T(8,128)S(1)} collective-permute-done((f32[64,512]{1,0:T(8,128)S(1)}, f32[64,512]{1,0:T(8,128)S(1)}, u32[]{:S(2)}, u32[]{:S(2)}) %collective-permute-start.10) | collective-permute-done | bytes 131104 | tf_op jit(solution)/shard_map/ppermute | solution.py:123
  45.4 1.6 %collective-permute-start.11 = (f32[64,512]{1,0:T(8,128)S(1)}, f32[64,512]{1,0:T(8,128)S(1)}, u32[]{:S(2)}, u32[]{:S(2)}) collective-permute-start(f32[64,512]{1,0:T(8,128)S(1)} %add.7.refs_0_), channel_id=1, source_target_pairs={{0,16},{8,24},{16,0},{24,8},{1,17},{9,25},{17,1},{25,9},{2,18},{10... | collective-permute-start | bytes 393224 | tf_op jit(solution)/shard_map/ppermute | solution.py:208
  47.0 4.0 %collective-permute-done.11.refs_1_ = f32[64,512]{1,0:T(8,128)S(1)} collective-permute-done((f32[64,512]{1,0:T(8,128)S(1)}, f32[64,512]{1,0:T(8,128)S(1)}, u32[]{:S(2)}, u32[]{:S(2)}) %collective-permute-start.11) | collective-permute-done | bytes 131104 | tf_op jit(solution)/shard_map/ppermute | solution.py:208
  51.0 0.1 collective-permute-start.12
  51.1 1.3 %collective-permute-done.12.away = f32[64,512]{1,0:T(8,128)S(1)} collective-permute-done((f32[64,512]{1,0:T(8,128)S(1)}, f32[64,512]{1,0:T(8,128)S(1)}, u32[]{:S(2)}, u32[]{:S(2)}) %collective-permute-start.12) | collective-permute-done | bytes 131104 | tf_op jit(solution)/shard_map/ppermute | solution.py:123
  52.5 0.7 multiply_other.3
  53.2 0.5 multiply_own.3
  53.6 0.7 collective-permute-start.15
  54.3 1.8 %collective-permute-start.14 = (f32[160,128]{1,0:T(8,128)S(1)}, f32[160,128]{1,0:T(8,128)S(1)}, u32[]{:S(2)}, u32[]{:S(2)}) collective-permute-start(f32[160,128]{1,0:T(8,128)S(1)} %get-tuple-element.65), channel_id=1, source_target_pairs={{0,3},{1,2},{2,1},{3,0},{4,7},{5,6},{6,5},{7,4},{8,11},{9,10},{10,... | collective-permute-start | bytes 245768 | tf_op jit(solution)/shard_map/ppermute | solution.py:123
  56.1 1.1 %collective-permute-start.13 = (f32[160,128]{1,0:T(8,128)S(1)}, f32[160,128]{1,0:T(8,128)S(1)}, u32[]{:S(2)}, u32[]{:S(2)}) collective-permute-start(f32[160,128]{1,0:T(8,128)S(1)} %get-tuple-element.63.sent), channel_id=1, source_target_pairs={{0,1},{1,0},{2,3},{3,2},{4,5},{5,4},{6,7},{7,6},{8,9},{9,8},{10,11... | collective-permute-start | bytes 245768 | tf_op jit(solution)/shard_map/ppermute | solution.py:123
  57.2 1.8 %collective-permute-done.15.refs_2_ = f32[160,128]{1,0:T(8,128)S(1)} collective-permute-done((f32[160,128]{1,0:T(8,128)S(1)}, f32[160,128]{1,0:T(8,128)S(1)}, u32[]{:S(2)}, u32[]{:S(2)}) %collective-permute-start.15) | collective-permute-done | bytes 81952 | tf_op jit(solution)/shard_map/ppermute | solution.py:123
  59.0 1.5 %collective-permute-done.14.refs_1_ = f32[160,128]{1,0:T(8,128)S(1)} collective-permute-done((f32[160,128]{1,0:T(8,128)S(1)}, f32[160,128]{1,0:T(8,128)S(1)}, u32[]{:S(2)}, u32[]{:S(2)}) %collective-permute-start.14) | collective-permute-done | bytes 81952 | tf_op jit(solution)/shard_map/ppermute | solution.py:123
  60.5 1.1 %collective-permute-done.13.refs_0_ = f32[160,128]{1,0:T(8,128)S(1)} collective-permute-done((f32[160,128]{1,0:T(8,128)S(1)}, f32[160,128]{1,0:T(8,128)S(1)}, u32[]{:S(2)}, u32[]{:S(2)}) %collective-permute-start.13) | collective-permute-done | bytes 81952 | tf_op jit(solution)/shard_map/ppermute | solution.py:123
  61.6 2.8 %collective-permute-start.16 = (f32[160,128]{1,0:T(8,128)S(1)}, f32[160,128]{1,0:T(8,128)S(1)}, u32[]{:S(2)}, u32[]{:S(2)}) collective-permute-start(f32[160,128]{1,0:T(8,128)S(1)} %collect.3.one), channel_id=1, source_target_pairs={{0,4},{1,5},{2,6},{3,7},{4,0},{5,1},{6,2},{7,3},{8,12},{9,13},{10,... | collective-permute-start | bytes 245768 | tf_op jit(solution)/shard_map/ppermute | solution.py:123
  64.4 4.0 %collective-permute-done.16.two = f32[160,128]{1,0:T(8,128)S(1)} collective-permute-done((f32[160,128]{1,0:T(8,128)S(1)}, f32[160,128]{1,0:T(8,128)S(1)}, u32[]{:S(2)}, u32[]{:S(2)}) %collective-permute-start.16) | collective-permute-done | bytes 81952 | tf_op jit(solution)/shard_map/ppermute | solution.py:123
  68.3 0.4 collective-permute-start.17
  68.7 2.0 %collective-permute-start.19 = (f32[128,128]{1,0:T(8,128)S(1)}, f32[128,128]{1,0:T(8,128)S(1)}, u32[]{:S(2)}, u32[]{:S(2)}) collective-permute-start(f32[128,128]{1,0:T(8,128)S(1)} %top.3.value), channel_id=1, source_target_pairs={{0,3},{1,2},{2,1},{3,0},{4,7},{5,6},{6,5},{7,4},{8,11},{9,10},{10,... | collective-permute-start | bytes 196616 | tf_op jit(solution)/shard_map/ppermute | solution.py:123
  70.8 1.1 %collective-permute-start.18 = (f32[128,128]{1,0:T(8,128)S(1)}, f32[128,128]{1,0:T(8,128)S(1)}, u32[]{:S(2)}, u32[]{:S(2)}) collective-permute-start(f32[128,128]{1,0:T(8,128)S(1)} %top.3.value), channel_id=1, source_target_pairs={{0,1},{1,0},{2,3},{3,2},{4,5},{5,4},{6,7},{7,6},{8,9},{9,8},{10,11... | collective-permute-start | bytes 196616 | tf_op jit(solution)/shard_map/ppermute | solution.py:123
  71.9 3.2 %eliminate.3.inverse = f32[64,64]{1,0:T(8,128)S(1)} custom-call(f32[160,128]{1,0:T(8,128)S(1)} %collect.3.one, f32[160,128]{1,0:T(8,128)S(1)} %collective-permute-done.16.two), custom_call_target="tpu_custom_call" | custom-call | flops 100000000 | bytes 8388608 | tf_op jit(solution)/shard_map/eliminate/pallas_call | solution.py:42
  75.2 1.0 %widen.1 = (f32[64,512]{1,0:T(8,128)S(1)}, f32[64,512]{1,0:T(8,128)S(1)}, f32[32,128]{1,0:T(8,128)S(1)}) custom-call(f32[64,64]{1,0:T(8,128)S(1)} %eliminate.3.inverse, f32[256,128]{1,0:T(8,128)S(1)} %unfold.6.own.stacked, f32[256,128]{1,0:T(8,128)S(1)} %unfold.7.other.stacked), custom_call_target="tpu_custom_call" | custom-call | flops 100000000 | bytes 1048576 | tf_op jit(solution)/shard_map/widen/pallas_call | solution.py:42
  76.2 1.3 %final.2 = (f32[1024,512]{1,0:T(8,128)S(1)}, f32[1024,512]{1,0:T(8,128)S(1)}, f32[64,1024]{1,0:T(8,128)}) custom-call(f32[64,64]{1,0:T(8,128)S(1)} %eliminate.3.inverse, f32[64,512]{1,0:T(8,128)S(1)} %collective-permute-done.12.away, f32[64,512]{1,0:T(8,128)S(1)} %add.8.mine, f32[256,128]{1,0:T(8,128)S(1)} %unfold.6.own.stacked, ...), custom_call_target="tpu_custom_call" | custom-call | flops 201326592 | bytes 4194304 | tf_op jit(solution)/shard_map/final/pallas_call | solution.py:42
  77.6 1.6 %collective-permute-start.21 = (f32[32,128]{1,0:T(8,128)S(1)}, f32[32,128]{1,0:T(8,128)S(1)}, u32[]{:S(2)}, u32[]{:S(2)}) collective-permute-start(f32[32,128]{1,0:T(8,128)S(1)} %add.9.one), channel_id=1, source_target_pairs={{0,16},{8,24},{16,0},{24,8},{1,17},{9,25},{17,1},{25,9},{2,18},{10... | collective-permute-start | bytes 49160 | tf_op jit(solution)/shard_map/ppermute | solution.py:123
  79.2 2.2 %final.3 = (f32[1024,512]{1,0:T(8,128)S(1)}, f32[1024,512]{1,0:T(8,128)S(1)}, f32[1024,1024]{1,0:T(8,128)}, f32[1024,1024]{1,0:T(8,128)}) custom-call(f32[64,64]{1,0:T(8,128)S(1)} %eliminate.3.inverse, f32[64,512]{1,0:T(8,128)S(1)} %collective-permute-done.12.away, f32[64,512]{1,0:T(8,128)S(1)} %add.8.mine, f32[256,128]{1,0:T(8,128)S(1)} %unfold.7.other.stacked, ...), custom_call_target="tpu_custom_call" | custom-call | flops 201326592 | bytes 4194304 | tf_op jit(solution)/shard_map/final/pallas_call | solution.py:42
  81.4 5.6 %finish.1 = (f32[64,1024]{1,0:T(8,128)}, f32[1024,1024]{1,0:T(8,128)}, f32[1024,1024]{1,0:T(8,128)}) custom-call(f32[32,128]{1,0:T(8,128)S(1)} %add.9.one, f32[32,128]{1,0:T(8,128)S(1)} %collective-permute-done.21.two, f32[64,512]{1,0:T(8,128)S(1)} %get-tuple-element.68.own, ...), custom_call_target="tpu_custom_call", output_to_operand_aliasing={{1}: (6, {}), {2}: (7, {})} | custom-call | flops 100000000 | bytes 8388608 | tf_op jit(solution)/shard_map/finish/pallas_call | solution.py:42
  (22 shorter events, 0.3 us)
Async XLA Ops:
  7.1 1.5 %collective-permute-start = (f32[64,512]{1,0:T(8,128)S(1)}, f32[64,512]{1,0:T(8,128)S(1)}, u32[]{:S(2)}, u32[]{:S(2)}) collective-permute-start(f32[64,512]{1,0:T(8,128)S(1)} %get-tuple-element.44), channel_id=1, source_target_pairs={{0,8},{8,0},{16,24},{24,16},{1,9},{9,1},{17,25},{25,17},{2,10},{10... | collective-permute-start | bytes 393224 | tf_op jit(solution)/shard_map/ppermute | solution.py:123
  8.6 6.8 %collective-permute-start.1 = (f32[64,512]{1,0:T(8,128)S(1)}, f32[64,512]{1,0:T(8,128)S(1)}, u32[]{:S(2)}, u32[]{:S(2)}) collective-permute-start(f32[64,512]{1,0:T(8,128)S(1)} %add.5.refs_0_), channel_id=1, source_target_pairs={{0,16},{8,24},{16,0},{24,8},{1,17},{9,25},{17,1},{25,9},{2,18},{10... | collective-permute-start | bytes 393224 | tf_op jit(solution)/shard_map/ppermute | solution.py:208
  15.4 1.4 %collective-permute-start.2 = (f32[64,512]{1,0:T(8,128)S(1)}, f32[64,512]{1,0:T(8,128)S(1)}, u32[]{:S(2)}, u32[]{:S(2)}) collective-permute-start(f32[64,512]{1,0:T(8,128)S(1)} %add.6.mine), channel_id=1, source_target_pairs={{0,8},{8,0},{16,24},{24,16},{1,9},{9,1},{17,25},{25,17},{2,10},{10... | collective-permute-start | bytes 393224 | tf_op jit(solution)/shard_map/ppermute | solution.py:123
  18.0 4.6 %collective-permute-start.5 = (f32[160,128]{1,0:T(8,128)S(1)}, f32[160,128]{1,0:T(8,128)S(1)}, u32[]{:S(2)}, u32[]{:S(2)}) collective-permute-start(f32[160,128]{1,0:T(8,128)S(1)} %get-tuple-element.52), channel_id=1, source_target_pairs={{0,2},{1,3},{2,0},{3,1},{4,6},{5,7},{6,4},{7,5},{8,10},{9,11},{10,... | collective-permute-start | bytes 245768 | tf_op jit(solution)/shard_map/ppermute | solution.py:123
  19.8 5.7 %collective-permute-start.4 = (f32[160,128]{1,0:T(8,128)S(1)}, f32[160,128]{1,0:T(8,128)S(1)}, u32[]{:S(2)}, u32[]{:S(2)}) collective-permute-start(f32[160,128]{1,0:T(8,128)S(1)} %get-tuple-element.51), channel_id=1, source_target_pairs={{0,3},{1,2},{2,1},{3,0},{4,7},{5,6},{6,5},{7,4},{8,11},{9,10},{10,... | collective-permute-start | bytes 245768 | tf_op jit(solution)/shard_map/ppermute | solution.py:123
  21.2 5.6 %collective-permute-start.3 = (f32[160,128]{1,0:T(8,128)S(1)}, f32[160,128]{1,0:T(8,128)S(1)}, u32[]{:S(2)}, u32[]{:S(2)}) collective-permute-start(f32[160,128]{1,0:T(8,128)S(1)} %get-tuple-element.49.sent), channel_id=1, source_target_pairs={{0,1},{1,0},{2,3},{3,2},{4,5},{5,4},{6,7},{7,6},{8,9},{9,8},{10,11... | collective-permute-start | bytes 245768 | tf_op jit(solution)/shard_map/ppermute | solution.py:123
  26.8 6.6 %collective-permute-start.6 = (f32[160,128]{1,0:T(8,128)S(1)}, f32[160,128]{1,0:T(8,128)S(1)}, u32[]{:S(2)}, u32[]{:S(2)}) collective-permute-start(f32[160,128]{1,0:T(8,128)S(1)} %collect.2.one), channel_id=1, source_target_pairs={{0,4},{1,5},{2,6},{3,7},{4,0},{5,1},{6,2},{7,3},{8,12},{9,13},{10,... | collective-permute-start | bytes 245768 | tf_op jit(solution)/shard_map/ppermute | solution.py:123
  33.4 6.8 %collective-permute-start.9 = (f32[128,128]{1,0:T(8,128)S(1)}, f32[128,128]{1,0:T(8,128)S(1)}, u32[]{:S(2)}, u32[]{:S(2)}) collective-permute-start(f32[128,128]{1,0:T(8,128)S(1)} %top.2.value), channel_id=1, source_target_pairs={{0,2},{1,3},{2,0},{3,1},{4,6},{5,7},{6,4},{7,5},{8,10},{9,11},{10,... | collective-permute-start | bytes 196616 | tf_op jit(solution)/shard_map/ppermute | solution.py:123
  34.0 6.2 %collective-permute-start.8 = (f32[128,128]{1,0:T(8,128)S(1)}, f32[128,128]{1,0:T(8,128)S(1)}, u32[]{:S(2)}, u32[]{:S(2)}) collective-permute-start(f32[128,128]{1,0:T(8,128)S(1)} %top.2.value), channel_id=1, source_target_pairs={{0,3},{1,2},{2,1},{3,0},{4,7},{5,6},{6,5},{7,4},{8,11},{9,10},{10,... | collective-permute-start | bytes 196616 | tf_op jit(solution)/shard_map/ppermute | solution.py:123
  35.6 4.6 %collective-permute-start.7 = (f32[128,128]{1,0:T(8,128)S(1)}, f32[128,128]{1,0:T(8,128)S(1)}, u32[]{:S(2)}, u32[]{:S(2)}) collective-permute-start(f32[128,128]{1,0:T(8,128)S(1)} %top.2.value), channel_id=1, source_target_pairs={{0,1},{1,0},{2,3},{3,2},{4,5},{5,4},{6,7},{7,6},{8,9},{9,8},{10,11... | collective-permute-start | bytes 196616 | tf_op jit(solution)/shard_map/ppermute | solution.py:123
  44.0 1.4 %collective-permute-start.10 = (f32[64,512]{1,0:T(8,128)S(1)}, f32[64,512]{1,0:T(8,128)S(1)}, u32[]{:S(2)}, u32[]{:S(2)}) collective-permute-start(f32[64,512]{1,0:T(8,128)S(1)} %get-tuple-element.58), channel_id=1, source_target_pairs={{0,8},{8,0},{16,24},{24,16},{1,9},{9,1},{17,25},{25,17},{2,10},{10... | collective-permute-start | bytes 393224 | tf_op jit(solution)/shard_map/ppermute | solution.py:123
  45.4 5.6 %collective-permute-start.11 = (f32[64,512]{1,0:T(8,128)S(1)}, f32[64,512]{1,0:T(8,128)S(1)}, u32[]{:S(2)}, u32[]{:S(2)}) collective-permute-start(f32[64,512]{1,0:T(8,128)S(1)} %add.7.refs_0_), channel_id=1, source_target_pairs={{0,16},{8,24},{16,0},{24,8},{1,17},{9,25},{17,1},{25,9},{2,18},{10... | collective-permute-start | bytes 393224 | tf_op jit(solution)/shard_map/ppermute | solution.py:208
  51.0 1.4 %collective-permute-start.12 = (f32[64,512]{1,0:T(8,128)S(1)}, f32[64,512]{1,0:T(8,128)S(1)}, u32[]{:S(2)}, u32[]{:S(2)}) collective-permute-start(f32[64,512]{1,0:T(8,128)S(1)} %add.8.mine), channel_id=1, source_target_pairs={{0,8},{8,0},{16,24},{24,16},{1,9},{9,1},{17,25},{25,17},{2,10},{10... | collective-permute-start | bytes 393224 | tf_op jit(solution)/shard_map/ppermute | solution.py:123
  53.6 5.4 %collective-permute-start.15 = (f32[160,128]{1,0:T(8,128)S(1)}, f32[160,128]{1,0:T(8,128)S(1)}, u32[]{:S(2)}, u32[]{:S(2)}) collective-permute-start(f32[160,128]{1,0:T(8,128)S(1)} %get-tuple-element.66), channel_id=1, source_target_pairs={{0,2},{1,3},{2,0},{3,1},{4,6},{5,7},{6,4},{7,5},{8,10},{9,11},{10,... | collective-permute-start | bytes 245768 | tf_op jit(solution)/shard_map/ppermute | solution.py:123
  54.3 6.2 %collective-permute-start.14 = (f32[160,128]{1,0:T(8,128)S(1)}, f32[160,128]{1,0:T(8,128)S(1)}, u32[]{:S(2)}, u32[]{:S(2)}) collective-permute-start(f32[160,128]{1,0:T(8,128)S(1)} %get-tuple-element.65), channel_id=1, source_target_pairs={{0,3},{1,2},{2,1},{3,0},{4,7},{5,6},{6,5},{7,4},{8,11},{9,10},{10,... | collective-permute-start | bytes 245768 | tf_op jit(solution)/shard_map/ppermute | solution.py:123
  56.1 5.4 %collective-permute-start.13 = (f32[160,128]{1,0:T(8,128)S(1)}, f32[160,128]{1,0:T(8,128)S(1)}, u32[]{:S(2)}, u32[]{:S(2)}) collective-permute-start(f32[160,128]{1,0:T(8,128)S(1)} %get-tuple-element.63.sent), channel_id=1, source_target_pairs={{0,1},{1,0},{2,3},{3,2},{4,5},{5,4},{6,7},{7,6},{8,9},{9,8},{10,11... | collective-permute-start | bytes 245768 | tf_op jit(solution)/shard_map/ppermute | solution.py:123
  61.6 6.7 %collective-permute-start.16 = (f32[160,128]{1,0:T(8,128)S(1)}, f32[160,128]{1,0:T(8,128)S(1)}, u32[]{:S(2)}, u32[]{:S(2)}) collective-permute-start(f32[160,128]{1,0:T(8,128)S(1)} %collect.3.one), channel_id=1, source_target_pairs={{0,4},{1,5},{2,6},{3,7},{4,0},{5,1},{6,2},{7,3},{8,12},{9,13},{10,... | collective-permute-start | bytes 245768 | tf_op jit(solution)/shard_map/ppermute | solution.py:123
  68.3 6.8 %collective-permute-start.17 = (f32[128,128]{1,0:T(8,128)S(1)}, f32[128,128]{1,0:T(8,128)S(1)}, u32[]{:S(2)}, u32[]{:S(2)}) collective-permute-start(f32[128,128]{1,0:T(8,128)S(1)} %top.3.value), channel_id=1, source_target_pairs={{0,2},{1,3},{2,0},{3,1},{4,6},{5,7},{6,4},{7,5},{8,10},{9,11},{10,... | collective-permute-start | bytes 196616 | tf_op jit(solution)/shard_map/ppermute | solution.py:123
  68.7 6.4 %collective-permute-start.19 = (f32[128,128]{1,0:T(8,128)S(1)}, f32[128,128]{1,0:T(8,128)S(1)}, u32[]{:S(2)}, u32[]{:S(2)}) collective-permute-start(f32[128,128]{1,0:T(8,128)S(1)} %top.3.value), channel_id=1, source_target_pairs={{0,3},{1,2},{2,1},{3,0},{4,7},{5,6},{6,5},{7,4},{8,11},{9,10},{10,... | collective-permute-start | bytes 196616 | tf_op jit(solution)/shard_map/ppermute | solution.py:123
  70.8 4.4 %collective-permute-start.18 = (f32[128,128]{1,0:T(8,128)S(1)}, f32[128,128]{1,0:T(8,128)S(1)}, u32[]{:S(2)}, u32[]{:S(2)}) collective-permute-start(f32[128,128]{1,0:T(8,128)S(1)} %top.3.value), channel_id=1, source_target_pairs={{0,1},{1,0},{2,3},{3,2},{4,5},{5,4},{6,7},{7,6},{8,9},{9,8},{10,11... | collective-permute-start | bytes 196616 | tf_op jit(solution)/shard_map/ppermute | solution.py:123
  76.2 1.4 %collective-permute-start.20 = (f32[32,128]{1,0:T(8,128)S(1)}, f32[32,128]{1,0:T(8,128)S(1)}, u32[]{:S(2)}, u32[]{:S(2)}) collective-permute-start(f32[32,128]{1,0:T(8,128)S(1)} %get-tuple-element.67.refs_0_), channel_id=1, source_target_pairs={{0,8},{8,0},{16,24},{24,16},{1,9},{9,1},{17,25},{25,17},{2,10},{10... | collective-permute-start | bytes 49160 | tf_op jit(solution)/shard_map/ppermute | solution.py:123
  77.6 3.8 %collective-permute-start.21 = (f32[32,128]{1,0:T(8,128)S(1)}, f32[32,128]{1,0:T(8,128)S(1)}, u32[]{:S(2)}, u32[]{:S(2)}) collective-permute-start(f32[32,128]{1,0:T(8,128)S(1)} %add.9.one), channel_id=1, source_target_pairs={{0,16},{8,24},{16,0},{24,8},{1,17},{9,25},{17,1},{25,9},{2,18},{10... | collective-permute-start | bytes 49160 | tf_op jit(solution)/shard_map/ppermute | solution.py:123

commit v10 on v9

--- a/solution.py
+++ b/solution.py
@@ -50,13 +50,6 @@
         compiler_params=pltpu.CompilerParams(vmem_limit_bytes=limit * MIB),
         cost_estimate=pl.CostEstimate(flops=cost[0], bytes_accessed=cost[1], transcendentals=0),
     )(*[pltpu.with_memory_space_constraint(a, pltpu.HBM) if m is pltpu.HBM else a for a, m in ins])
-
-
-def reciprocal(value):
-    guess = pl.reciprocal(value, approx=True)
-    for _ in range(2):
-        guess = guess * (2.0 - value * guess)
-    return guess
 
 
 def invert(packed, out):
@@ -85,7 +78,7 @@
             (j, p): jnp.broadcast_to(rows[j][:, k + p : k + p + 1], full) for j in after for p in range(wide)
         }
         for p in range(wide):
-            inverse = reciprocal(core[p, p])
+            inverse = 1.0 / core[p, p]
             factors = [core[p, q] * inverse for q in range(p + 1, wide)]
             for q, factor in zip(range(p + 1, wide), factors):
                 for t in range(q, wide):
@@ -130,6 +123,7 @@
         steps = n_rows // tall
         quarter = rank * (half // LANES) // 2
         gram_rows = rank * rank // LANES
+        share = gram_rows // CORES
 
         def place():
             pix = lax.axis_index("pix")
@@ -212,19 +206,21 @@
             return swap(mine, "gal", 1), mine
 
         def multiply_other(panel, pair):
-            def body(away, mine, high, low, straight, across, stack):
+            def body(away, mine, high, low, straight, across, stack, gram):
                 s = place()
                 panel = join((away, mine))
                 put_stack(dot_nn(split(panel), (high[...], low[...])), stack)
-                gram = pack(dot(panel, panel, ((1,), (1,)), HIGH))
+                gram[...] = pack(dot(panel, panel, ((1,), (1,)), HIGH))
+                mine_rows = pl.ds(pl.multiple_of(s[0] * share, share), share)
                 for side, out in ((s[2], straight), (1 - s[2], across)):
                     out[:quarter, :] = stack[rows_at(side), :]
-                    out[quarter:, :] = gram
+                    out[quarter:, :] = gram[mine_rows, :]
 
             ins = [(a, pltpu.VMEM) for a in (*panel, *pair)]
-            outs = [((quarter + gram_rows, LANES), F32, pltpu.VMEM)] * 2
+            outs = [((quarter + share, LANES), F32, pltpu.VMEM)] * 2
             cost = (3 * rank * n_rows * n_cols, 2 * n_rows * n_cols)
-            return call(body, "multiply_other", ins, outs, [pltpu.VMEM((2 * quarter, LANES), F32)], cost=cost)
+            scratch = [pltpu.VMEM((rows, LANES), F32) for rows in (2 * quarter, gram_rows)]
+            return call(body, "multiply_other", ins, outs, scratch, cost=cost)
 
         def multiply_own(panel, pair, sent):
             def body(away, mine, high, low, sent, keep, out, stack):
@@ -235,7 +231,7 @@
                 out[quarter:, :] = sent[quarter:, :]
 
             ins = [(a, pltpu.VMEM) for a in (*panel, *pair, sent)]
-            outs = [((rows, LANES), F32, pltpu.VMEM) for rows in (quarter, quarter + gram_rows)]
+            outs = [((rows, LANES), F32, pltpu.VMEM) for rows in (quarter, quarter + share)]
             cost = (3 * rank * n_rows * n_cols, 2 * n_rows * n_cols)
             return call(body, "multiply_own", ins, outs, [pltpu.VMEM((2 * quarter, LANES), F32)], cost=cost)
 
@@ -246,11 +242,13 @@
         def rows_at(side):
             return pl.ds(pl.multiple_of(side * quarter, quarter), quarter)
 
-        def eliminate(one, two):
-            def body(one, two, out):
-                invert(one[-gram_rows:, :] + two[-gram_rows:, :], out)
-
-            ins = [(one, pltpu.VMEM), (two, pltpu.VMEM)]
+        def eliminate(mine, twin):
+            def body(mine, twin, out):
+                pair = jnp.concatenate([mine[...], twin[...]], axis=0)
+                turned = jnp.concatenate([twin[...], mine[...]], axis=0)
+                invert(jnp.where(place()[0] == 0, pair, turned), out)
+
+            ins = [(mine, pltpu.VMEM), (twin, pltpu.VMEM)]
             outs = [((rank, rank), F32, pltpu.VMEM)]
             return call(body, "eliminate", ins, outs, cost=(10**8, 8 * MIB), limit=4)[0]
 
@@ -266,10 +264,10 @@
                 out[rows:, :] = low
 
             ins = [(a, pltpu.VMEM) for a in (keep, sent, *gots)]
-            return small(body, "collect", ins, [rows + gram_rows])[0]
+            return small(body, "collect", ins, [rows + share])[0]
 
         def divide(level, total):
-            rows = (total.shape[0] - gram_rows) // 2
+            rows = (total.shape[0] - share) // 2
 
             def body(total, keep, out):
                 s = place()
@@ -277,7 +275,7 @@
                     ref[:rows, :] = total[pl.ds(pl.multiple_of(side * rows, rows), rows), :]
                 out[rows:, :] = total[2 * rows :, :]
 
-            return small(body, "divide", [(total, pltpu.VMEM)], [rows, rows + gram_rows])
+            return small(body, "divide", [(total, pltpu.VMEM)], [rows, rows + share])
 
         def unfold(level, value, got):
             rows = value.shape[0]
@@ -290,13 +288,22 @@
             ins = [(value, pltpu.VMEM), (got, pltpu.VMEM)]
             return small(body, "unfold", ins, [2 * rows])[0]
 
-        def top(one, two):
-            rows = one.shape[0] - gram_rows
+        def top(one, two, after):
+            rows = one.shape[0] - share
+
+            def body(one, two, _, out):
+                out[...] = one[:rows, :] + two[:rows, :]
+
+            ins = [(a, pltpu.VMEM) for a in (one, two, after)]
+            return call(body, "top", ins, [((rows, LANES), F32, pltpu.VMEM)], cost=(10**8, 8 * MIB), limit=4)[0]
+
+        def tail(one, two):
+            rows = one.shape[0] - share
 
             def body(one, two, out):
-                out[...] = one[:rows, :] + two[:rows, :]
-
-            return small(body, "top", [(one, pltpu.VMEM), (two, pltpu.VMEM)], [rows])[0]
+                out[...] = one[rows:, :] + two[rows:, :]
+
+            return small(body, "tail", [(one, pltpu.VMEM), (two, pltpu.VMEM)], [share])[0]
 
         def sum_pix(panel, own, other):
             straight, across = multiply_other(panel, other)
@@ -307,11 +314,15 @@
                 keep, sent = divide(level, total)
                 total = collect(keep, sent, [swap(sent, "pix", 1 << level)])
             got = swap(total, "pix", 1 << (levels - 1))
-            value = top(total, got)
-            inverse = eliminate(total, got)
+            gram = tail(total, got)
+            value = top(total, got, gram)
+            twin = swap(gram, "gal", 1)
+            inverse = eliminate(gram, twin)
             for level in range(levels - 2, 1, -1):
                 value = unfold(level, value, swap(value, "pix", 1 << level))
-            beside, straight, across = [swap(value, "pix", bit) for bit in (2, 1, 3)]
+            beside = swap(value, "pix", 2)
+            later, _ = lax.optimization_barrier((value, twin))
+            straight, across = swap(later, "pix", 1), swap(later, "pix", 3)
             return inverse, unfold(1, value, beside), unfold(1, straight, across)
 
         def halves(inverse, panel, stacked):
@@ -349,14 +360,19 @@
             return base, (high, low), part
 
         def put(sources, targets, p, s, sems):
-            moves = []
-            for i in range(steps):
+            def moves(i):
                 for a, (source, target) in enumerate(zip(sources, targets)):
                     block = target.at[pl.ds(gal_at(i, s), tall), pl.ds(pix_at(p, s), half)]
-                    move = pltpu.make_async_copy(source.at[chunk(i), :], block, sems.at[i, a])
-                    move.start(priority=(i + a) % 2)
-                    moves.append(move)
-            return moves
+                    rows = pl.ds(pl.multiple_of(i * tall, tall), tall)
+                    yield pltpu.make_async_copy(source.at[rows, :], block, sems.at[i, a])
+
+            def start(i, carry):
+                for a, move in enumerate(moves(i)):
+                    move.start(priority=a)
+                return carry
+
+            lax.fori_loop(0, steps, start, 0)
+            return [move for i in range(steps) for move in moves(i)]
 
         def final(p, inverse, panel, stacked, base, before=()):
             def body(inverse, away, mine, stacked, base, *rest):

time: 87.4 us -> 86 us (0.984)
  Pallas kernels: 29.3 us -> 26.9 us
  waiting for transfers between devices: 30.4 us -> 32.8 us
  starting transfers between devices: 26.5 us -> 25.2 us
    pallas_call x26 -> x28, Pallas kernels: 29.3 us -> 26.9 us  [call(): pl.pallas_call(body, name=name, in_specs=[pl.BlockSpec(memory_space=space...]
    ppermute x20 -> x22, waiting for transfers between devices: 22.6 us -> 25 us  [swap(): return lax.ppermute(value, axis, [(i, i ^ bit) for i in range(n)])]
    ppermute x20 -> x22, starting transfers between devices: 21.9 us -> 20.6 us  [swap(): return lax.ppermute(value, axis, [(i, i ^ bit) for i in range(n)])]
  transfers between devices with their start and end apart: 22 -> 24, of which waited for: 14 -> 18; matrix products, arithmetic and copies ran while one was open for 0% -> 0% of each run, Pallas kernels for 12% -> 13%
where the time goes in v10:
time: 86 us; the launch traced here: 85.8 us
  waiting for transfers between devices  32.8 us (38%)
  Pallas kernels  26.9 us (31%)
  starting transfers between devices  25.2 us (29%)
  between operations  0.96 us (1%)
    pallas_call x28, Pallas kernels, call(): pl.pallas_call(body, name=name, in_specs=[pl.BlockSpec(memory_space=space...  26.9 us
    ppermute x22, waiting for transfers between devices, swap(): return lax.ppermute(value, axis, [(i, i ^ bit) for i in range(n)])  25 us
    ppermute x22, starting transfers between devices, swap(): return lax.ppermute(value, axis, [(i, i ^ bit) for i in range(n)])  20.6 us
    ppermute x2, waiting for transfers between devices, sum_gal(): lax.ppermute(mine, 'gal', [(i, (i + CORES * k) % n_gal) for i in range(n_...  7.82 us
    ppermute x2, starting transfers between devices, sum_gal(): lax.ppermute(mine, 'gal', [(i, (i + CORES * k) % n_gal) for i in range(n_...  4.54 us
  transfers between devices with their start and end apart: 24, of which 18 were waited for; matrix products, arithmetic and copies ran while one was open for 0% of the time, Pallas kernels for 13%

profile of v10, /device:TPU:0, one launch (start us, length us, event | category | flops | bytes accessed | tf_op | source)
XLA Modules:
  0.0 85.8 jit_solution(12032446057431930133)
XLA Ops:
  0.6 6.4 %first.1 = (f32[1024,1024]{1,0:T(8,128)S(1)}, f32[1024,1024]{1,0:T(8,128)S(1)}, bf16[1024,512]{1,0:T(8,128)(2,1)S(1)}, bf16[1024,512]{1,0:T(8,128)(2,1)S(1)}, bf...) custom-call(f32[1024,1024]{1,0:T(8,128)} %o_in.1, ...), custom_call_target="tpu_custom_call" | custom-call | flops 402653184 | bytes 16777216 | tf_op jit(solution)/shard_map/first/pallas_call | solution.py:42
  7.1 0.5 collective-permute-start
  7.6 1.0 %collective-permute-done.refs_1_ = f32[64,512]{1,0:T(8,128)S(1)} collective-permute-done((f32[64,512]{1,0:T(8,128)S(1)}, f32[64,512]{1,0:T(8,128)S(1)}, u32[]{:S(2)}, u32[]{:S(2)}) %collective-permute-start) | collective-permute-done | bytes 131104 | tf_op jit(solution)/shard_map/ppermute | solution.py:116
  8.6 2.9 %collective-permute-start.1 = (f32[64,512]{1,0:T(8,128)S(1)}, f32[64,512]{1,0:T(8,128)S(1)}, u32[]{:S(2)}, u32[]{:S(2)}) collective-permute-start(f32[64,512]{1,0:T(8,128)S(1)} %add.5.refs_0_), channel_id=1, source_target_pairs={{0,16},{8,24},{16,0},{24,8},{1,17},{9,25},{17,1},{25,9},{2,18},{10... | collective-permute-start | bytes 393224 | tf_op jit(solution)/shard_map/ppermute | solution.py:202
  11.5 3.8 %collective-permute-done.1.refs_1_ = f32[64,512]{1,0:T(8,128)S(1)} collective-permute-done((f32[64,512]{1,0:T(8,128)S(1)}, f32[64,512]{1,0:T(8,128)S(1)}, u32[]{:S(2)}, u32[]{:S(2)}) %collective-permute-start.1) | collective-permute-done | bytes 131104 | tf_op jit(solution)/shard_map/ppermute | solution.py:202
  15.4 1.3 %collective-permute-done.2.away = f32[64,512]{1,0:T(8,128)S(1)} collective-permute-done((f32[64,512]{1,0:T(8,128)S(1)}, f32[64,512]{1,0:T(8,128)S(1)}, u32[]{:S(2)}, u32[]{:S(2)}) %collective-permute-start.2) | collective-permute-done | bytes 131104 | tf_op jit(solution)/shard_map/ppermute | solution.py:116
  16.8 0.7 multiply_other.2
  17.5 0.5 multiply_own.2
  18.0 1.9 %collective-permute-start.5 = (f32[144,128]{1,0:T(8,128)S(1)}, f32[144,128]{1,0:T(8,128)S(1)}, u32[]{:S(2)}, u32[]{:S(2)}) collective-permute-start(f32[144,128]{1,0:T(8,128)S(1)} %get-tuple-element.54), channel_id=1, source_target_pairs={{0,2},{1,3},{2,0},{3,1},{4,6},{5,7},{6,4},{7,5},{8,10},{9,11},{10,... | collective-permute-start | bytes 221192 | tf_op jit(solution)/shard_map/ppermute | solution.py:116
  19.8 1.4 %collective-permute-start.4 = (f32[144,128]{1,0:T(8,128)S(1)}, f32[144,128]{1,0:T(8,128)S(1)}, u32[]{:S(2)}, u32[]{:S(2)}) collective-permute-start(f32[144,128]{1,0:T(8,128)S(1)} %get-tuple-element.53), channel_id=1, source_target_pairs={{0,3},{1,2},{2,1},{3,0},{4,7},{5,6},{6,5},{7,4},{8,11},{9,10},{10,... | collective-permute-start | bytes 221192 | tf_op jit(solution)/shard_map/ppermute | solution.py:116
  21.2 0.3 collective-permute-start.3
  21.5 0.9 %collective-permute-done.5.refs_2_ = f32[144,128]{1,0:T(8,128)S(1)} collective-permute-done((f32[144,128]{1,0:T(8,128)S(1)}, f32[144,128]{1,0:T(8,128)S(1)}, u32[]{:S(2)}, u32[]{:S(2)}) %collective-permute-start.5) | collective-permute-done | bytes 73760 | tf_op jit(solution)/shard_map/ppermute | solution.py:116
  22.4 2.8 %collective-permute-done.4.refs_1_ = f32[144,128]{1,0:T(8,128)S(1)} collective-permute-done((f32[144,128]{1,0:T(8,128)S(1)}, f32[144,128]{1,0:T(8,128)S(1)}, u32[]{:S(2)}, u32[]{:S(2)}) %collective-permute-start.4) | collective-permute-done | bytes 73760 | tf_op jit(solution)/shard_map/ppermute | solution.py:116
  25.2 1.2 %collective-permute-done.3.refs_0_ = f32[144,128]{1,0:T(8,128)S(1)} collective-permute-done((f32[144,128]{1,0:T(8,128)S(1)}, f32[144,128]{1,0:T(8,128)S(1)}, u32[]{:S(2)}, u32[]{:S(2)}) %collective-permute-start.3) | collective-permute-done | bytes 73760 | tf_op jit(solution)/shard_map/ppermute | solution.py:116
  26.4 2.6 %collective-permute-start.6 = (f32[144,128]{1,0:T(8,128)S(1)}, f32[144,128]{1,0:T(8,128)S(1)}, u32[]{:S(2)}, u32[]{:S(2)}) collective-permute-start(f32[144,128]{1,0:T(8,128)S(1)} %collect.2.one), channel_id=1, source_target_pairs={{0,4},{1,5},{2,6},{3,7},{4,0},{5,1},{6,2},{7,3},{8,12},{9,13},{10,... | collective-permute-start | bytes 221192 | tf_op jit(solution)/shard_map/ppermute | solution.py:116
  29.1 3.7 %collective-permute-done.6.two = f32[144,128]{1,0:T(8,128)S(1)} collective-permute-done((f32[144,128]{1,0:T(8,128)S(1)}, f32[144,128]{1,0:T(8,128)S(1)}, u32[]{:S(2)}, u32[]{:S(2)}) %collective-permute-start.6) | collective-permute-done | bytes 73760 | tf_op jit(solution)/shard_map/ppermute | solution.py:116
  32.9 0.5 collective-permute-start.10
  33.3 1.2 %collective-permute-done.7.twin = f32[16,128]{1,0:T(8,128)S(1)} collective-permute-done((f32[16,128]{1,0:T(8,128)S(1)}, f32[16,128]{1,0:T(8,128)S(1)}, u32[]{:S(2)}, u32[]{:S(2)}) %collective-permute-start.7) | collective-permute-done | bytes 8224 | tf_op jit(solution)/shard_map/ppermute | solution.py:116
  34.5 1.8 %collective-permute-start.9 = (f32[128,128]{1,0:T(8,128)S(1)}, f32[128,128]{1,0:T(8,128)S(1)}, u32[]{:S(2)}, u32[]{:S(2)}) collective-permute-start(f32[128,128]{1,0:T(8,128)S(1)} %top.2.value), channel_id=1, source_target_pairs={{0,3},{1,2},{2,1},{3,0},{4,7},{5,6},{6,5},{7,4},{8,11},{9,10},{10,... | collective-permute-start | bytes 196616 | tf_op jit(solution)/shard_map/ppermute | solution.py:116
  36.3 1.3 %collective-permute-start.8 = (f32[128,128]{1,0:T(8,128)S(1)}, f32[128,128]{1,0:T(8,128)S(1)}, u32[]{:S(2)}, u32[]{:S(2)}) collective-permute-start(f32[128,128]{1,0:T(8,128)S(1)} %top.2.value), channel_id=1, source_target_pairs={{0,1},{1,0},{2,3},{3,2},{4,5},{5,4},{6,7},{7,6},{8,9},{9,8},{10,11... | collective-permute-start | bytes 196616 | tf_op jit(solution)/shard_map/ppermute | solution.py:116
  37.6 2.8 %eliminate.2.inverse = f32[64,64]{1,0:T(8,128)S(1)} custom-call(f32[16,128]{1,0:T(8,128)S(1)} %tail.2.mine._, f32[16,128]{1,0:T(8,128)S(1)} %collective-permute-done.7.twin), custom_call_target="tpu_custom_call" | custom-call | flops 100000000 | bytes 8388608 | tf_op jit(solution)/shard_map/eliminate/pallas_call | solution.py:42
  40.4 1.8 %middle.2 = (f32[1024,512]{1,0:T(8,128)S(1)}, bf16[1024,512]{1,0:T(8,128)(2,1)S(1)}, bf16[1024,512]{1,0:T(8,128)(2,1)S(1)}, f32[64,512]{1,0:T(8,128)S(1)}, f32[64,512]{1,0:T(8,128)S(1)}) custom-call(f32[64,64]{1,0:T(8,128)S(1)} %eliminate.2.inverse, f32[64,512]{1,0:T(8,128)S(1)} %collective-permute-done.2.away, f32[64,512]{1,0:T(8,128)S(1)} %add.6.mine, ...), custom_call_target="tpu_custom_call" | custom-call | flops 603979776 | bytes 4194304 | tf_op jit(solution)/shard_map/middle/pallas_call | solution.py:42
  42.3 1.8 %middle.3 = (f32[1024,512]{1,0:T(8,128)S(1)}, bf16[1024,512]{1,0:T(8,128)(2,1)S(1)}, bf16[1024,512]{1,0:T(8,128)(2,1)S(1)}, f32[64,512]{1,0:T(8,128)S(1)}, f32[64,512]{1,0:T(8,128)S(1)}) custom-call(f32[64,64]{1,0:T(8,128)S(1)} %eliminate.2.inverse, f32[64,512]{1,0:T(8,128)S(1)} %collective-permute-done.2.away, f32[64,512]{1,0:T(8,128)S(1)} %add.6.mine, ...), custom_call_target="tpu_custom_call" | custom-call | flops 603979776 | bytes 4194304 | tf_op jit(solution)/shard_map/middle/pallas_call | solution.py:42
  44.2 1.3 %collective-permute-done.11.refs_1_ = f32[64,512]{1,0:T(8,128)S(1)} collective-permute-done((f32[64,512]{1,0:T(8,128)S(1)}, f32[64,512]{1,0:T(8,128)S(1)}, u32[]{:S(2)}, u32[]{:S(2)}) %collective-permute-start.11) | collective-permute-done | bytes 131104 | tf_op jit(solution)/shard_map/ppermute | solution.py:116
  45.6 1.6 %collective-permute-start.12 = (f32[64,512]{1,0:T(8,128)S(1)}, f32[64,512]{1,0:T(8,128)S(1)}, u32[]{:S(2)}, u32[]{:S(2)}) collective-permute-start(f32[64,512]{1,0:T(8,128)S(1)} %add.7.refs_0_), channel_id=1, source_target_pairs={{0,16},{8,24},{16,0},{24,8},{1,17},{9,25},{17,1},{25,9},{2,18},{10... | collective-permute-start | bytes 393224 | tf_op jit(solution)/shard_map/ppermute | solution.py:202
  47.2 4.0 %collective-permute-done.12.refs_1_ = f32[64,512]{1,0:T(8,128)S(1)} collective-permute-done((f32[64,512]{1,0:T(8,128)S(1)}, f32[64,512]{1,0:T(8,128)S(1)}, u32[]{:S(2)}, u32[]{:S(2)}) %collective-permute-start.12) | collective-permute-done | bytes 131104 | tf_op jit(solution)/shard_map/ppermute | solution.py:202
  51.3 1.3 %collective-permute-done.13.away = f32[64,512]{1,0:T(8,128)S(1)} collective-permute-done((f32[64,512]{1,0:T(8,128)S(1)}, f32[64,512]{1,0:T(8,128)S(1)}, u32[]{:S(2)}, u32[]{:S(2)}) %collective-permute-start.13) | collective-permute-done | bytes 131104 | tf_op jit(solution)/shard_map/ppermute | solution.py:116
  52.6 0.7 multiply_other.3
  53.3 0.5 multiply_own.3
  53.8 0.5 collective-permute-start.16
  54.3 1.8 %collective-permute-start.15 = (f32[144,128]{1,0:T(8,128)S(1)}, f32[144,128]{1,0:T(8,128)S(1)}, u32[]{:S(2)}, u32[]{:S(2)}) collective-permute-start(f32[144,128]{1,0:T(8,128)S(1)} %get-tuple-element.68), channel_id=1, source_target_pairs={{0,3},{1,2},{2,1},{3,0},{4,7},{5,6},{6,5},{7,4},{8,11},{9,10},{10,... | collective-permute-start | bytes 221192 | tf_op jit(solution)/shard_map/ppermute | solution.py:116
  56.1 1.3 %collective-permute-start.14 = (f32[144,128]{1,0:T(8,128)S(1)}, f32[144,128]{1,0:T(8,128)S(1)}, u32[]{:S(2)}, u32[]{:S(2)}) collective-permute-start(f32[144,128]{1,0:T(8,128)S(1)} %get-tuple-element.66.sent), channel_id=1, source_target_pairs={{0,1},{1,0},{2,3},{3,2},{4,5},{5,4},{6,7},{7,6},{8,9},{9,8},{10,11... | collective-permute-start | bytes 221192 | tf_op jit(solution)/shard_map/ppermute | solution.py:116
  57.4 1.6 %collective-permute-done.16.refs_2_ = f32[144,128]{1,0:T(8,128)S(1)} collective-permute-done((f32[144,128]{1,0:T(8,128)S(1)}, f32[144,128]{1,0:T(8,128)S(1)}, u32[]{:S(2)}, u32[]{:S(2)}) %collective-permute-start.16) | collective-permute-done | bytes 73760 | tf_op jit(solution)/shard_map/ppermute | solution.py:116
  59.0 1.1 %collective-permute-done.15.refs_1_ = f32[144,128]{1,0:T(8,128)S(1)} collective-permute-done((f32[144,128]{1,0:T(8,128)S(1)}, f32[144,128]{1,0:T(8,128)S(1)}, u32[]{:S(2)}, u32[]{:S(2)}) %collective-permute-start.15) | collective-permute-done | bytes 73760 | tf_op jit(solution)/shard_map/ppermute | solution.py:116
  60.1 1.0 %collective-permute-done.14.refs_0_ = f32[144,128]{1,0:T(8,128)S(1)} collective-permute-done((f32[144,128]{1,0:T(8,128)S(1)}, f32[144,128]{1,0:T(8,128)S(1)}, u32[]{:S(2)}, u32[]{:S(2)}) %collective-permute-start.14) | collective-permute-done | bytes 73760 | tf_op jit(solution)/shard_map/ppermute | solution.py:116
  61.1 2.3 %collective-permute-start.17 = (f32[144,128]{1,0:T(8,128)S(1)}, f32[144,128]{1,0:T(8,128)S(1)}, u32[]{:S(2)}, u32[]{:S(2)}) collective-permute-start(f32[144,128]{1,0:T(8,128)S(1)} %collect.3.one), channel_id=1, source_target_pairs={{0,4},{1,5},{2,6},{3,7},{4,0},{5,1},{6,2},{7,3},{8,12},{9,13},{10,... | collective-permute-start | bytes 221192 | tf_op jit(solution)/shard_map/ppermute | solution.py:116
  63.5 3.9 %collective-permute-done.17.two = f32[144,128]{1,0:T(8,128)S(1)} collective-permute-done((f32[144,128]{1,0:T(8,128)S(1)}, f32[144,128]{1,0:T(8,128)S(1)}, u32[]{:S(2)}, u32[]{:S(2)}) %collective-permute-start.17) | collective-permute-done | bytes 73760 | tf_op jit(solution)/shard_map/ppermute | solution.py:116
  67.6 0.9 %collective-permute-done.18.twin = f32[16,128]{1,0:T(8,128)S(1)} collective-permute-done((f32[16,128]{1,0:T(8,128)S(1)}, f32[16,128]{1,0:T(8,128)S(1)}, u32[]{:S(2)}, u32[]{:S(2)}) %collective-permute-start.18) | collective-permute-done | bytes 8224 | tf_op jit(solution)/shard_map/ppermute | solution.py:116
  68.5 1.7 %collective-permute-start.21 = (f32[128,128]{1,0:T(8,128)S(1)}, f32[128,128]{1,0:T(8,128)S(1)}, u32[]{:S(2)}, u32[]{:S(2)}) collective-permute-start(f32[128,128]{1,0:T(8,128)S(1)} %top.3.value), channel_id=1, source_target_pairs={{0,3},{1,2},{2,1},{3,0},{4,7},{5,6},{6,5},{7,4},{8,11},{9,10},{10,... | collective-permute-start | bytes 196616 | tf_op jit(solution)/shard_map/ppermute | solution.py:116
  70.2 0.7 collective-permute-start.20
  70.9 2.8 %eliminate.3.inverse = f32[64,64]{1,0:T(8,128)S(1)} custom-call(f32[16,128]{1,0:T(8,128)S(1)} %tail.3.mine._, f32[16,128]{1,0:T(8,128)S(1)} %collective-permute-done.18.twin), custom_call_target="tpu_custom_call" | custom-call | flops 100000000 | bytes 8388608 | tf_op jit(solution)/shard_map/eliminate/pallas_call | solution.py:42
  73.7 0.5 collective-permute-done.21.got
  74.2 1.1 %collective-permute-done.20.value = f32[128,128]{1,0:T(8,128)S(1)} collective-permute-done((f32[128,128]{1,0:T(8,128)S(1)}, f32[128,128]{1,0:T(8,128)S(1)}, u32[]{:S(2)}, u32[]{:S(2)}) %collective-permute-start.20) | collective-permute-done | bytes 65568 | tf_op jit(solution)/shard_map/ppermute | solution.py:116
  75.4 1.0 %widen.1 = (f32[64,512]{1,0:T(8,128)S(1)}, f32[64,512]{1,0:T(8,128)S(1)}, f32[32,128]{1,0:T(8,128)S(1)}) custom-call(f32[64,64]{1,0:T(8,128)S(1)} %eliminate.3.inverse, f32[256,128]{1,0:T(8,128)S(1)} %unfold.6.own.stacked, f32[256,128]{1,0:T(8,128)S(1)} %unfold.7.other.stacked), custom_call_target="tpu_custom_call" | custom-call | flops 100000000 | bytes 1048576 | tf_op jit(solution)/shard_map/widen/pallas_call | solution.py:42
  76.4 1.1 %final.2 = (f32[1024,512]{1,0:T(8,128)S(1)}, f32[1024,512]{1,0:T(8,128)S(1)}, f32[64,1024]{1,0:T(8,128)}) custom-call(f32[64,64]{1,0:T(8,128)S(1)} %eliminate.3.inverse, f32[64,512]{1,0:T(8,128)S(1)} %collective-permute-done.13.away, f32[64,512]{1,0:T(8,128)S(1)} %add.8.mine, f32[256,128]{1,0:T(8,128)S(1)} %unfold.6.own.stacked, ...), custom_call_target="tpu_custom_call" | custom-call | flops 201326592 | bytes 4194304 | tf_op jit(solution)/shard_map/final/pallas_call | solution.py:42
  77.6 1.6 %collective-permute-start.23 = (f32[32,128]{1,0:T(8,128)S(1)}, f32[32,128]{1,0:T(8,128)S(1)}, u32[]{:S(2)}, u32[]{:S(2)}) collective-permute-start(f32[32,128]{1,0:T(8,128)S(1)} %add.9.one), channel_id=1, source_target_pairs={{0,16},{8,24},{16,0},{24,8},{1,17},{9,25},{17,1},{25,9},{2,18},{10... | collective-permute-start | bytes 49160 | tf_op jit(solution)/shard_map/ppermute | solution.py:116
  79.2 2.5 %final.3 = (f32[1024,512]{1,0:T(8,128)S(1)}, f32[1024,512]{1,0:T(8,128)S(1)}, f32[1024,1024]{1,0:T(8,128)}, f32[1024,1024]{1,0:T(8,128)}) custom-call(f32[64,64]{1,0:T(8,128)S(1)} %eliminate.3.inverse, f32[64,512]{1,0:T(8,128)S(1)} %collective-permute-done.13.away, f32[64,512]{1,0:T(8,128)S(1)} %add.8.mine, f32[256,128]{1,0:T(8,128)S(1)} %unfold.7.other.stacked, ...), custom_call_target="tpu_custom_call" | custom-call | flops 201326592 | bytes 4194304 | tf_op jit(solution)/shard_map/final/pallas_call | solution.py:42
  81.7 4.0 %finish.1 = (f32[64,1024]{1,0:T(8,128)}, f32[1024,1024]{1,0:T(8,128)}, f32[1024,1024]{1,0:T(8,128)}) custom-call(f32[32,128]{1,0:T(8,128)S(1)} %add.9.one, f32[32,128]{1,0:T(8,128)S(1)} %collective-permute-done.23.two, f32[64,512]{1,0:T(8,128)S(1)} %get-tuple-element.72.own, ...), custom_call_target="tpu_custom_call", output_to_operand_aliasing={{1}: (6, {}), {2}: (7, {})} | custom-call | flops 100000000 | bytes 8388608 | tf_op jit(solution)/shard_map/finish/pallas_call | solution.py:42
  (28 shorter events, 0.7 us)
Async XLA Ops:
  7.1 1.5 %collective-permute-start = (f32[64,512]{1,0:T(8,128)S(1)}, f32[64,512]{1,0:T(8,128)S(1)}, u32[]{:S(2)}, u32[]{:S(2)}) collective-permute-start(f32[64,512]{1,0:T(8,128)S(1)} %get-tuple-element.46), channel_id=1, source_target_pairs={{0,8},{8,0},{16,24},{24,16},{1,9},{9,1},{17,25},{25,17},{2,10},{10... | collective-permute-start | bytes 393224 | tf_op jit(solution)/shard_map/ppermute | solution.py:116
  8.6 6.8 %collective-permute-start.1 = (f32[64,512]{1,0:T(8,128)S(1)}, f32[64,512]{1,0:T(8,128)S(1)}, u32[]{:S(2)}, u32[]{:S(2)}) collective-permute-start(f32[64,512]{1,0:T(8,128)S(1)} %add.5.refs_0_), channel_id=1, source_target_pairs={{0,16},{8,24},{16,0},{24,8},{1,17},{9,25},{17,1},{25,9},{2,18},{10... | collective-permute-start | bytes 393224 | tf_op jit(solution)/shard_map/ppermute | solution.py:202
  15.4 1.4 %collective-permute-start.2 = (f32[64,512]{1,0:T(8,128)S(1)}, f32[64,512]{1,0:T(8,128)S(1)}, u32[]{:S(2)}, u32[]{:S(2)}) collective-permute-start(f32[64,512]{1,0:T(8,128)S(1)} %add.6.mine), channel_id=1, source_target_pairs={{0,8},{8,0},{16,24},{24,16},{1,9},{9,1},{17,25},{25,17},{2,10},{10... | collective-permute-start | bytes 393224 | tf_op jit(solution)/shard_map/ppermute | solution.py:116
  18.0 4.4 %collective-permute-start.5 = (f32[144,128]{1,0:T(8,128)S(1)}, f32[144,128]{1,0:T(8,128)S(1)}, u32[]{:S(2)}, u32[]{:S(2)}) collective-permute-start(f32[144,128]{1,0:T(8,128)S(1)} %get-tuple-element.54), channel_id=1, source_target_pairs={{0,2},{1,3},{2,0},{3,1},{4,6},{5,7},{6,4},{7,5},{8,10},{9,11},{10,... | collective-permute-start | bytes 221192 | tf_op jit(solution)/shard_map/ppermute | solution.py:116
  19.8 5.4 %collective-permute-start.4 = (f32[144,128]{1,0:T(8,128)S(1)}, f32[144,128]{1,0:T(8,128)S(1)}, u32[]{:S(2)}, u32[]{:S(2)}) collective-permute-start(f32[144,128]{1,0:T(8,128)S(1)} %get-tuple-element.53), channel_id=1, source_target_pairs={{0,3},{1,2},{2,1},{3,0},{4,7},{5,6},{6,5},{7,4},{8,11},{9,10},{10,... | collective-permute-start | bytes 221192 | tf_op jit(solution)/shard_map/ppermute | solution.py:116
  21.2 5.2 %collective-permute-start.3 = (f32[144,128]{1,0:T(8,128)S(1)}, f32[144,128]{1,0:T(8,128)S(1)}, u32[]{:S(2)}, u32[]{:S(2)}) collective-permute-start(f32[144,128]{1,0:T(8,128)S(1)} %get-tuple-element.51.sent), channel_id=1, source_target_pairs={{0,1},{1,0},{2,3},{3,2},{4,5},{5,4},{6,7},{7,6},{8,9},{9,8},{10,11... | collective-permute-start | bytes 221192 | tf_op jit(solution)/shard_map/ppermute | solution.py:116
  26.4 6.4 %collective-permute-start.6 = (f32[144,128]{1,0:T(8,128)S(1)}, f32[144,128]{1,0:T(8,128)S(1)}, u32[]{:S(2)}, u32[]{:S(2)}) collective-permute-start(f32[144,128]{1,0:T(8,128)S(1)} %collect.2.one), channel_id=1, source_target_pairs={{0,4},{1,5},{2,6},{3,7},{4,0},{5,1},{6,2},{7,3},{8,12},{9,13},{10,... | collective-permute-start | bytes 221192 | tf_op jit(solution)/shard_map/ppermute | solution.py:116
  32.9 7.5 %collective-permute-start.10 = (f32[128,128]{1,0:T(8,128)S(1)}, f32[128,128]{1,0:T(8,128)S(1)}, u32[]{:S(2)}, u32[]{:S(2)}) collective-permute-start(f32[128,128]{1,0:T(8,128)S(1)} %top.2.value), channel_id=1, source_target_pairs={{0,2},{1,3},{2,0},{3,1},{4,6},{5,7},{6,4},{7,5},{8,10},{9,11},{10,... | collective-permute-start | bytes 196616 | tf_op jit(solution)/shard_map/ppermute | solution.py:116
  33.3 1.2 %collective-permute-start.7 = (f32[16,128]{1,0:T(8,128)S(1)}, f32[16,128]{1,0:T(8,128)S(1)}, u32[]{:S(2)}, u32[]{:S(2)}) collective-permute-start(f32[16,128]{1,0:T(8,128)S(1)} %tail.2.mine._), channel_id=1, source_target_pairs={{0,8},{8,0},{16,24},{24,16},{1,9},{9,1},{17,25},{25,17},{2,10},{10... | collective-permute-start | bytes 24584 | tf_op jit(solution)/shard_map/ppermute | solution.py:116
  34.5 7.7 %collective-permute-start.9 = (f32[128,128]{1,0:T(8,128)S(1)}, f32[128,128]{1,0:T(8,128)S(1)}, u32[]{:S(2)}, u32[]{:S(2)}) collective-permute-start(f32[128,128]{1,0:T(8,128)S(1)} %top.2.value), channel_id=1, source_target_pairs={{0,3},{1,2},{2,1},{3,0},{4,7},{5,6},{6,5},{7,4},{8,11},{9,10},{10,... | collective-permute-start | bytes 196616 | tf_op jit(solution)/shard_map/ppermute | solution.py:116
  36.3 5.9 %collective-permute-start.8 = (f32[128,128]{1,0:T(8,128)S(1)}, f32[128,128]{1,0:T(8,128)S(1)}, u32[]{:S(2)}, u32[]{:S(2)}) collective-permute-start(f32[128,128]{1,0:T(8,128)S(1)} %top.2.value), channel_id=1, source_target_pairs={{0,1},{1,0},{2,3},{3,2},{4,5},{5,4},{6,7},{7,6},{8,9},{9,8},{10,11... | collective-permute-start | bytes 196616 | tf_op jit(solution)/shard_map/ppermute | solution.py:116
  44.1 1.4 %collective-permute-start.11 = (f32[64,512]{1,0:T(8,128)S(1)}, f32[64,512]{1,0:T(8,128)S(1)}, u32[]{:S(2)}, u32[]{:S(2)}) collective-permute-start(f32[64,512]{1,0:T(8,128)S(1)} %get-tuple-element.61), channel_id=1, source_target_pairs={{0,8},{8,0},{16,24},{24,16},{1,9},{9,1},{17,25},{25,17},{2,10},{10... | collective-permute-start | bytes 393224 | tf_op jit(solution)/shard_map/ppermute | solution.py:116
  45.6 5.6 %collective-permute-start.12 = (f32[64,512]{1,0:T(8,128)S(1)}, f32[64,512]{1,0:T(8,128)S(1)}, u32[]{:S(2)}, u32[]{:S(2)}) collective-permute-start(f32[64,512]{1,0:T(8,128)S(1)} %add.7.refs_0_), channel_id=1, source_target_pairs={{0,16},{8,24},{16,0},{24,8},{1,17},{9,25},{17,1},{25,9},{2,18},{10... | collective-permute-start | bytes 393224 | tf_op jit(solution)/shard_map/ppermute | solution.py:202
  51.2 1.4 %collective-permute-start.13 = (f32[64,512]{1,0:T(8,128)S(1)}, f32[64,512]{1,0:T(8,128)S(1)}, u32[]{:S(2)}, u32[]{:S(2)}) collective-permute-start(f32[64,512]{1,0:T(8,128)S(1)} %add.8.mine), channel_id=1, source_target_pairs={{0,8},{8,0},{16,24},{24,16},{1,9},{9,1},{17,25},{25,17},{2,10},{10... | collective-permute-start | bytes 393224 | tf_op jit(solution)/shard_map/ppermute | solution.py:116
  53.8 5.2 %collective-permute-start.16 = (f32[144,128]{1,0:T(8,128)S(1)}, f32[144,128]{1,0:T(8,128)S(1)}, u32[]{:S(2)}, u32[]{:S(2)}) collective-permute-start(f32[144,128]{1,0:T(8,128)S(1)} %get-tuple-element.69), channel_id=1, source_target_pairs={{0,2},{1,3},{2,0},{3,1},{4,6},{5,7},{6,4},{7,5},{8,10},{9,11},{10,... | collective-permute-start | bytes 221192 | tf_op jit(solution)/shard_map/ppermute | solution.py:116
  54.3 5.8 %collective-permute-start.15 = (f32[144,128]{1,0:T(8,128)S(1)}, f32[144,128]{1,0:T(8,128)S(1)}, u32[]{:S(2)}, u32[]{:S(2)}) collective-permute-start(f32[144,128]{1,0:T(8,128)S(1)} %get-tuple-element.68), channel_id=1, source_target_pairs={{0,3},{1,2},{2,1},{3,0},{4,7},{5,6},{6,5},{7,4},{8,11},{9,10},{10,... | collective-permute-start | bytes 221192 | tf_op jit(solution)/shard_map/ppermute | solution.py:116
  56.1 5.0 %collective-permute-start.14 = (f32[144,128]{1,0:T(8,128)S(1)}, f32[144,128]{1,0:T(8,128)S(1)}, u32[]{:S(2)}, u32[]{:S(2)}) collective-permute-start(f32[144,128]{1,0:T(8,128)S(1)} %get-tuple-element.66.sent), channel_id=1, source_target_pairs={{0,1},{1,0},{2,3},{3,2},{4,5},{5,4},{6,7},{7,6},{8,9},{9,8},{10,11... | collective-permute-start | bytes 221192 | tf_op jit(solution)/shard_map/ppermute | solution.py:116
  61.1 6.2 %collective-permute-start.17 = (f32[144,128]{1,0:T(8,128)S(1)}, f32[144,128]{1,0:T(8,128)S(1)}, u32[]{:S(2)}, u32[]{:S(2)}) collective-permute-start(f32[144,128]{1,0:T(8,128)S(1)} %collect.3.one), channel_id=1, source_target_pairs={{0,4},{1,5},{2,6},{3,7},{4,0},{5,1},{6,2},{7,3},{8,12},{9,13},{10,... | collective-permute-start | bytes 221192 | tf_op jit(solution)/shard_map/ppermute | solution.py:116
  67.3 1.2 %collective-permute-start.18 = (f32[16,128]{1,0:T(8,128)S(1)}, f32[16,128]{1,0:T(8,128)S(1)}, u32[]{:S(2)}, u32[]{:S(2)}) collective-permute-start(f32[16,128]{1,0:T(8,128)S(1)} %tail.3.mine._), channel_id=1, source_target_pairs={{0,8},{8,0},{16,24},{24,16},{1,9},{9,1},{17,25},{25,17},{2,10},{10... | collective-permute-start | bytes 24584 | tf_op jit(solution)/shard_map/ppermute | solution.py:116
  67.4 6.4 %collective-permute-start.19 = (f32[128,128]{1,0:T(8,128)S(1)}, f32[128,128]{1,0:T(8,128)S(1)}, u32[]{:S(2)}, u32[]{:S(2)}) collective-permute-start(f32[128,128]{1,0:T(8,128)S(1)} %top.3.value), channel_id=1, source_target_pairs={{0,2},{1,3},{2,0},{3,1},{4,6},{5,7},{6,4},{7,5},{8,10},{9,11},{10,... | collective-permute-start | bytes 196616 | tf_op jit(solution)/shard_map/ppermute | solution.py:116
  68.5 5.7 %collective-permute-start.21 = (f32[128,128]{1,0:T(8,128)S(1)}, f32[128,128]{1,0:T(8,128)S(1)}, u32[]{:S(2)}, u32[]{:S(2)}) collective-permute-start(f32[128,128]{1,0:T(8,128)S(1)} %top.3.value), channel_id=1, source_target_pairs={{0,3},{1,2},{2,1},{3,0},{4,7},{5,6},{6,5},{7,4},{8,11},{9,10},{10,... | collective-permute-start | bytes 196616 | tf_op jit(solution)/shard_map/ppermute | solution.py:116
  70.2 5.1 %collective-permute-start.20 = (f32[128,128]{1,0:T(8,128)S(1)}, f32[128,128]{1,0:T(8,128)S(1)}, u32[]{:S(2)}, u32[]{:S(2)}) collective-permute-start(f32[128,128]{1,0:T(8,128)S(1)} %top.3.value), channel_id=1, source_target_pairs={{0,1},{1,0},{2,3},{3,2},{4,5},{5,4},{6,7},{7,6},{8,9},{9,8},{10,11... | collective-permute-start | bytes 196616 | tf_op jit(solution)/shard_map/ppermute | solution.py:116
  76.4 1.2 %collective-permute-start.22 = (f32[32,128]{1,0:T(8,128)S(1)}, f32[32,128]{1,0:T(8,128)S(1)}, u32[]{:S(2)}, u32[]{:S(2)}) collective-permute-start(f32[32,128]{1,0:T(8,128)S(1)} %get-tuple-element.71.refs_0_), channel_id=1, source_target_pairs={{0,8},{8,0},{16,24},{24,16},{1,9},{9,1},{17,25},{25,17},{2,10},{10... | collective-permute-start | bytes 49160 | tf_op jit(solution)/shard_map/ppermute | solution.py:116
  77.6 4.1 %collective-permute-start.23 = (f32[32,128]{1,0:T(8,128)S(1)}, f32[32,128]{1,0:T(8,128)S(1)}, u32[]{:S(2)}, u32[]{:S(2)}) collective-permute-start(f32[32,128]{1,0:T(8,128)S(1)} %add.9.one), channel_id=1, source_target_pairs={{0,16},{8,24},{16,0},{24,8},{1,17},{9,25},{17,1},{25,9},{2,18},{10... | collective-permute-start | bytes 49160 | tf_op jit(solution)/shard_map/ppermute | solution.py:116

commit v11 on v9

--- a/solution.py
+++ b/solution.py
@@ -50,13 +50,6 @@
         compiler_params=pltpu.CompilerParams(vmem_limit_bytes=limit * MIB),
         cost_estimate=pl.CostEstimate(flops=cost[0], bytes_accessed=cost[1], transcendentals=0),
     )(*[pltpu.with_memory_space_constraint(a, pltpu.HBM) if m is pltpu.HBM else a for a, m in ins])
-
-
-def reciprocal(value):
-    guess = pl.reciprocal(value, approx=True)
-    for _ in range(2):
-        guess = guess * (2.0 - value * guess)
-    return guess
 
 
 def invert(packed, out):
@@ -85,7 +78,7 @@
             (j, p): jnp.broadcast_to(rows[j][:, k + p : k + p + 1], full) for j in after for p in range(wide)
         }
         for p in range(wide):
-            inverse = reciprocal(core[p, p])
+            inverse = 1.0 / core[p, p]
             factors = [core[p, q] * inverse for q in range(p + 1, wide)]
             for q, factor in zip(range(p + 1, wide), factors):
                 for t in range(q, wide):
@@ -211,32 +204,45 @@
             mine = add(mine, *got)
             return swap(mine, "gal", 1), mine
 
-        def multiply_other(panel, pair):
-            def body(away, mine, high, low, straight, across, stack):
-                s = place()
-                panel = join((away, mine))
-                put_stack(dot_nn(split(panel), (high[...], low[...])), stack)
-                gram = pack(dot(panel, panel, ((1,), (1,)), HIGH))
+        def multiply_mine(mine, pair, other_pair):
+            def body(mine, high, low, high_other, low_other, own, other, gram):
+                panel = split(mine[...])
+                for at, out in (((high, low), own), ((high_other, low_other), other)):
+                    put_stack(dot_nn(panel, [ref[n_rows // 2 :, :] for ref in at]), out)
+                gram[...] = pack(dot(mine[...], mine[...], ((1,), (1,)), HIGH))
+
+            ins = [(a, pltpu.VMEM) for a in (mine, *pair, *other_pair)]
+            outs = [((rows, LANES), F32, pltpu.VMEM) for rows in (2 * quarter, 2 * quarter, gram_rows)]
+            cost = (3 * rank * n_rows * n_cols, 2 * n_rows * n_cols)
+            return call(body, "multiply_mine", ins, outs, cost=cost)
+
+        def multiply_other(away, pair, before, gram):
+            def body(away, high, low, before, gram, straight, across, stack):
+                s = place()
+                pairs = [ref[: n_rows // 2, :] for ref in (high, low)]
+                put_stack(dot_nn(split(away[...]), pairs), stack)
+                total = gram[...] + pack(dot(away[...], away[...], ((1,), (1,)), HIGH))
                 for side, out in ((s[2], straight), (1 - s[2], across)):
-                    out[:quarter, :] = stack[rows_at(side), :]
-                    out[quarter:, :] = gram
-
-            ins = [(a, pltpu.VMEM) for a in (*panel, *pair)]
+                    out[:quarter, :] = stack[rows_at(side), :] + before[rows_at(side), :]
+                    out[quarter:, :] = total
+
+            ins = [(a, pltpu.VMEM) for a in (away, *pair, before, gram)]
             outs = [((quarter + gram_rows, LANES), F32, pltpu.VMEM)] * 2
-            cost = (3 * rank * n_rows * n_cols, 2 * n_rows * n_cols)
+            cost = (2 * rank * n_rows * n_cols, n_rows * n_cols)
             return call(body, "multiply_other", ins, outs, [pltpu.VMEM((2 * quarter, LANES), F32)], cost=cost)
 
-        def multiply_own(panel, pair, sent):
-            def body(away, mine, high, low, sent, keep, out, stack):
-                s = place()
-                put_stack(dot_nn(split(join((away, mine))), (high[...], low[...])), stack)
-                keep[...] = stack[rows_at(s[2]), :]
-                out[:quarter, :] = stack[rows_at(1 - s[2]), :]
+        def multiply_own(away, pair, before, sent):
+            def body(away, high, low, before, sent, keep, out, stack):
+                s = place()
+                pairs = [ref[: n_rows // 2, :] for ref in (high, low)]
+                put_stack(dot_nn(split(away[...]), pairs), stack)
+                for side, ref in ((s[2], keep), (1 - s[2], out)):
+                    ref[:quarter, :] = stack[rows_at(side), :] + before[rows_at(side), :]
                 out[quarter:, :] = sent[quarter:, :]
 
-            ins = [(a, pltpu.VMEM) for a in (*panel, *pair, sent)]
+            ins = [(a, pltpu.VMEM) for a in (away, *pair, before, sent)]
             outs = [((rows, LANES), F32, pltpu.VMEM) for rows in (quarter, quarter + gram_rows)]
-            cost = (3 * rank * n_rows * n_cols, 2 * n_rows * n_cols)
+            cost = (10**9, 8 * MIB)
             return call(body, "multiply_own", ins, outs, [pltpu.VMEM((2 * quarter, LANES), F32)], cost=cost)
 
         def put_stack(value, stack):
@@ -299,9 +305,11 @@
             return small(body, "top", [(one, pltpu.VMEM), (two, pltpu.VMEM)], [rows])[0]
 
         def sum_pix(panel, own, other):
-            straight, across = multiply_other(panel, other)
+            away, mine = panel
+            own_before, other_before, gram = multiply_mine(mine, own, other)
+            straight, across = multiply_other(away, other, other_before, gram)
             gots = [swap(straight, "pix", 1), swap(across, "pix", 3)]
-            keep, beside = multiply_own(panel, own, straight)
+            keep, beside = multiply_own(away, own, own_before, straight)
             total = collect(keep, straight, gots + [swap(beside, "pix", 2)])
             for level in range(2, levels - 1):
                 keep, sent = divide(level, total)
@@ -322,13 +330,17 @@
             tops = jnp.concatenate([left_high, left_low, left_high], axis=0)
             return left, (wide_high, wide_low), tops, jnp.concatenate([wide_high, wide_high, wide_low], axis=0)
 
-        def middle(p, inverse, panel, stacked, o, u, before):
-            def body(inverse, away, mine, stacked, o, u, *rest):
-                s = place()
-                base, high, low, *after = rest[2 * p :]
-                _, right, tops, wides = halves(inverse, (away, mine), stacked)
-                for i in range(steps):
-                    lowrank = dot(tops[:, chunk(i)], wides, ((0,), (0,)))
+        def middle(p, sides, inverse, panel, stacked, o, u, before, arrays=()):
+            n = len(sides)
+            blocks = [i for i in range(steps) if i // (steps // 2) in sides]
+
+            def body(inverse, *rest):
+                s = place()
+                panel, (stacked, o, u, *rest) = rest[:n], rest[n:]
+                base, high, low, *after = rest[n * p + len(arrays) :]
+                _, right, tops, wides = halves(inverse, panel, stacked)
+                for k, i in enumerate(blocks):
+                    lowrank = dot(tops[:, chunk(k)], wides, ((0,), (0,)))
                     at = chunk(i), pl.ds(pix_at(p, s), half)
                     value = u[at] - lowrank
                     scaled = jnp.clip(value, -TAU, TAU)
@@ -337,26 +349,33 @@
                     pair = split(moved + (scaled - value))
                     high[chunk(i), :], low[chunk(i), :] = pair
                     term = dot_nt(right, pair)
-                    side, block = divmod(i, steps // 2)
+                    side, block = divmod(k, steps // 2)
                     after[side][:, chunk(block)] = rest[side][:, chunk(block)] + term if p else term
 
-            arrays = [inverse, *panel, stacked, o, u] + (list(before) if p else [])
+            ins = [inverse, *[panel[side] for side in sides], stacked, o, u]
+            ins += [before[side] for side in sides] if p else []
+            aliases = {len(ins) + k: k for k in range(len(arrays))}
             outs = [((n_rows, half), F32, pltpu.VMEM)] + [((n_rows, half), BF16, pltpu.VMEM)] * 2
-            outs += [((rank, n_rows // 2), F32, pltpu.VMEM)] * 2
-            cost = (9 * rank * n_rows * n_cols, 4 * n_rows * n_cols)
-            ins = [(a, pltpu.VMEM) for a in arrays]
-            base, high, low, *part = call(body, "middle", ins, outs, cost=cost)
+            outs += [((rank, n_rows // 2), F32, pltpu.VMEM)] * n
+            cost = (9 * rank * n_rows * n_cols // (3 - n), 4 * n_rows * n_cols // (3 - n))
+            ins = [(a, pltpu.VMEM) for a in (*ins, *arrays)]
+            base, high, low, *part = call(body, "middle", ins, outs, aliases=aliases, cost=cost)
             return base, (high, low), part
 
         def put(sources, targets, p, s, sems):
-            moves = []
-            for i in range(steps):
+            def moves(i):
                 for a, (source, target) in enumerate(zip(sources, targets)):
                     block = target.at[pl.ds(gal_at(i, s), tall), pl.ds(pix_at(p, s), half)]
-                    move = pltpu.make_async_copy(source.at[chunk(i), :], block, sems.at[i, a])
-                    move.start(priority=(i + a) % 2)
-                    moves.append(move)
-            return moves
+                    rows = pl.ds(pl.multiple_of(i * tall, tall), tall)
+                    yield pltpu.make_async_copy(source.at[rows, :], block, sems.at[i, a])
+
+            def start(i, carry):
+                for a, move in enumerate(moves(i)):
+                    move.start(priority=a)
+                return carry
+
+            lax.fori_loop(0, steps, start, 0)
+            return [move for i in range(steps) for move in moves(i)]
 
         def final(p, inverse, panel, stacked, base, before=()):
             def body(inverse, away, mine, stacked, base, *rest):
@@ -428,8 +447,12 @@
             panel = sum_gal(part)
             inverse, own_wide, other_wide = sum_pix(panel, own, other)
             if step < ITERS - 1:
-                base[0], own, part = middle(0, inverse, panel, own_wide, seen, pulls, None)
-                base[1], other, part = middle(1, inverse, panel, other_wide, seen, pulls, part)
+                given = inverse, panel, own_wide, seen, pulls
+                base[0], own, part = middle(0, (0, 1), *given, None)
+                given = inverse, panel, other_wide, seen, pulls, part
+                base[1], other, away = middle(1, (0,), *given)
+                base[1], other, mine = middle(1, (1,), *given, (base[1], *other))
+                part = away + mine
             else:
                 *wide, gram = widen(inverse, own_wide, other_wide)
                 *made, left = final(0, inverse, panel, own_wide, base[0])

time: 87.4 us -> 84.4 us (0.966)
  Pallas kernels: 29.3 us -> 27.9 us
  waiting for transfers between devices: 30.4 us -> 29.1 us
    pallas_call x26 -> x29, Pallas kernels: 29.3 us -> 27.9 us  [call(): pl.pallas_call(body, name=name, in_specs=[pl.BlockSpec(memory_space=space...]
    ppermute x20, waiting for transfers between devices: 22.6 us -> 21.2 us  [swap(): return lax.ppermute(value, axis, [(i, i ^ bit) for i in range(n)])]
  transfers between devices with their start and end apart: 22 -> 22, of which waited for: 14 -> 16; matrix products, arithmetic and copies ran while one was open for 0% -> 0% of each run, Pallas kernels for 12% -> 14%
where the time goes in v11:
time: 84.4 us; the launch traced here: 84.3 us
  waiting for transfers between devices  29.1 us (34%)
  Pallas kernels  27.9 us (33%)
  starting transfers between devices  26.3 us (31%)
  between operations  0.97 us (1%)
    pallas_call x29, Pallas kernels, call(): pl.pallas_call(body, name=name, in_specs=[pl.BlockSpec(memory_space=space...  27.9 us
    ppermute x20, starting transfers between devices, swap(): return lax.ppermute(value, axis, [(i, i ^ bit) for i in range(n)])  21.8 us
    ppermute x20, waiting for transfers between devices, swap(): return lax.ppermute(value, axis, [(i, i ^ bit) for i in range(n)])  21.2 us
    ppermute x2, waiting for transfers between devices, sum_gal(): lax.ppermute(mine, 'gal', [(i, (i + CORES * k) % n_gal) for i in range(n_...  7.97 us
    ppermute x2, starting transfers between devices, sum_gal(): lax.ppermute(mine, 'gal', [(i, (i + CORES * k) % n_gal) for i in range(n_...  4.53 us
  transfers between devices with their start and end apart: 22, of which 16 were waited for; matrix products, arithmetic and copies ran while one was open for 0% of the time, Pallas kernels for 14%

profile of v11, /device:TPU:0, one launch (start us, length us, event | category | flops | bytes accessed | tf_op | source)
XLA Modules:
  0.0 84.3 jit_solution(8708472824998049471)
XLA Ops:
  0.6 6.4 %first.1 = (f32[1024,1024]{1,0:T(8,128)S(1)}, f32[1024,1024]{1,0:T(8,128)S(1)}, bf16[1024,512]{1,0:T(8,128)(2,1)S(1)}, bf16[1024,512]{1,0:T(8,128)(2,1)S(1)}, bf...) custom-call(f32[1024,1024]{1,0:T(8,128)} %o_in.1, ...), custom_call_target="tpu_custom_call" | custom-call | flops 402653184 | bytes 16777216 | tf_op jit(solution)/shard_map/first/pallas_call | solution.py:42
  7.1 0.5 collective-permute-start
  7.6 1.0 %collective-permute-done.refs_1_ = f32[64,512]{1,0:T(8,128)S(1)} collective-permute-done((f32[64,512]{1,0:T(8,128)S(1)}, f32[64,512]{1,0:T(8,128)S(1)}, u32[]{:S(2)}, u32[]{:S(2)}) %collective-permute-start) | collective-permute-done | bytes 131104 | tf_op jit(solution)/shard_map/ppermute | solution.py:116
  8.6 2.9 %collective-permute-start.1 = (f32[64,512]{1,0:T(8,128)S(1)}, f32[64,512]{1,0:T(8,128)S(1)}, u32[]{:S(2)}, u32[]{:S(2)}) collective-permute-start(f32[64,512]{1,0:T(8,128)S(1)} %add.5.refs_0_), channel_id=1, source_target_pairs={{0,16},{8,24},{16,0},{24,8},{1,17},{9,25},{17,1},{25,9},{2,18},{10... | collective-permute-start | bytes 393224 | tf_op jit(solution)/shard_map/ppermute | solution.py:201
  11.5 3.8 %collective-permute-done.1.refs_1_ = f32[64,512]{1,0:T(8,128)S(1)} collective-permute-done((f32[64,512]{1,0:T(8,128)S(1)}, f32[64,512]{1,0:T(8,128)S(1)}, u32[]{:S(2)}, u32[]{:S(2)}) %collective-permute-start.1) | collective-permute-done | bytes 131104 | tf_op jit(solution)/shard_map/ppermute | solution.py:201
  15.5 0.6 multiply_mine.2
  16.1 0.7 collective-permute-done.2.away.rest_0_
  16.8 0.5 multiply_other.2
  17.2 0.3 multiply_own.2
  17.6 1.9 %collective-permute-start.5 = (f32[160,128]{1,0:T(8,128)S(1)}, f32[160,128]{1,0:T(8,128)S(1)}, u32[]{:S(2)}, u32[]{:S(2)}) collective-permute-start(f32[160,128]{1,0:T(8,128)S(1)} %get-tuple-element.64), channel_id=1, source_target_pairs={{0,2},{1,3},{2,0},{3,1},{4,6},{5,7},{6,4},{7,5},{8,10},{9,11},{10,... | collective-permute-start | bytes 245768 | tf_op jit(solution)/shard_map/ppermute | solution.py:116
  19.4 1.4 %collective-permute-start.4 = (f32[160,128]{1,0:T(8,128)S(1)}, f32[160,128]{1,0:T(8,128)S(1)}, u32[]{:S(2)}, u32[]{:S(2)}) collective-permute-start(f32[160,128]{1,0:T(8,128)S(1)} %get-tuple-element.63), channel_id=1, source_target_pairs={{0,3},{1,2},{2,1},{3,0},{4,7},{5,6},{6,5},{7,4},{8,11},{9,10},{10,... | collective-permute-start | bytes 245768 | tf_op jit(solution)/shard_map/ppermute | solution.py:116
  20.8 0.3 collective-permute-start.3
  21.1 1.1 %collective-permute-done.5.refs_2_ = f32[160,128]{1,0:T(8,128)S(1)} collective-permute-done((f32[160,128]{1,0:T(8,128)S(1)}, f32[160,128]{1,0:T(8,128)S(1)}, u32[]{:S(2)}, u32[]{:S(2)}) %collective-permute-start.5) | collective-permute-done | bytes 81952 | tf_op jit(solution)/shard_map/ppermute | solution.py:116
  22.2 2.9 %collective-permute-done.4.refs_1_ = f32[160,128]{1,0:T(8,128)S(1)} collective-permute-done((f32[160,128]{1,0:T(8,128)S(1)}, f32[160,128]{1,0:T(8,128)S(1)}, u32[]{:S(2)}, u32[]{:S(2)}) %collective-permute-start.4) | collective-permute-done | bytes 81952 | tf_op jit(solution)/shard_map/ppermute | solution.py:116
  25.1 1.2 %collective-permute-done.3.refs_0_ = f32[160,128]{1,0:T(8,128)S(1)} collective-permute-done((f32[160,128]{1,0:T(8,128)S(1)}, f32[160,128]{1,0:T(8,128)S(1)}, u32[]{:S(2)}, u32[]{:S(2)}) %collective-permute-start.3) | collective-permute-done | bytes 81952 | tf_op jit(solution)/shard_map/ppermute | solution.py:116
  26.4 2.6 %collective-permute-start.6 = (f32[160,128]{1,0:T(8,128)S(1)}, f32[160,128]{1,0:T(8,128)S(1)}, u32[]{:S(2)}, u32[]{:S(2)}) collective-permute-start(f32[160,128]{1,0:T(8,128)S(1)} %collect.2.one), channel_id=1, source_target_pairs={{0,4},{1,5},{2,6},{3,7},{4,0},{5,1},{6,2},{7,3},{8,12},{9,13},{10,... | collective-permute-start | bytes 245768 | tf_op jit(solution)/shard_map/ppermute | solution.py:116
  29.0 4.0 %collective-permute-done.6.two = f32[160,128]{1,0:T(8,128)S(1)} collective-permute-done((f32[160,128]{1,0:T(8,128)S(1)}, f32[160,128]{1,0:T(8,128)S(1)}, u32[]{:S(2)}, u32[]{:S(2)}) %collective-permute-start.6) | collective-permute-done | bytes 81952 | tf_op jit(solution)/shard_map/ppermute | solution.py:116
  33.0 0.6 collective-permute-start.9
  33.6 1.6 %collective-permute-start.8 = (f32[128,128]{1,0:T(8,128)S(1)}, f32[128,128]{1,0:T(8,128)S(1)}, u32[]{:S(2)}, u32[]{:S(2)}) collective-permute-start(f32[128,128]{1,0:T(8,128)S(1)} %top.2.value), channel_id=1, source_target_pairs={{0,3},{1,2},{2,1},{3,0},{4,7},{5,6},{6,5},{7,4},{8,11},{9,10},{10,... | collective-permute-start | bytes 196616 | tf_op jit(solution)/shard_map/ppermute | solution.py:116
  35.2 1.4 %collective-permute-start.7 = (f32[128,128]{1,0:T(8,128)S(1)}, f32[128,128]{1,0:T(8,128)S(1)}, u32[]{:S(2)}, u32[]{:S(2)}) collective-permute-start(f32[128,128]{1,0:T(8,128)S(1)} %top.2.value), channel_id=1, source_target_pairs={{0,1},{1,0},{2,3},{3,2},{4,5},{5,4},{6,7},{7,6},{8,9},{9,8},{10,11... | collective-permute-start | bytes 196616 | tf_op jit(solution)/shard_map/ppermute | solution.py:116
  36.6 2.8 %eliminate.2.inverse = f32[64,64]{1,0:T(8,128)S(1)} custom-call(f32[160,128]{1,0:T(8,128)S(1)} %collect.2.one, f32[160,128]{1,0:T(8,128)S(1)} %collective-permute-done.6.two), custom_call_target="tpu_custom_call" | custom-call | flops 100000000 | bytes 8388608 | tf_op jit(solution)/shard_map/eliminate/pallas_call | solution.py:42
  39.5 1.8 %middle.3 = (f32[1024,512]{1,0:T(8,128)S(1)}, bf16[1024,512]{1,0:T(8,128)(2,1)S(1)}, bf16[1024,512]{1,0:T(8,128)(2,1)S(1)}, f32[64,512]{1,0:T(8,128)S(1)}, f32[64,512]{1,0:T(8,128)S(1)}) custom-call(f32[64,64]{1,0:T(8,128)S(1)} %eliminate.2.inverse, f32[64,512]{1,0:T(8,128)S(1)} %collective-permute-done.2.away.rest_0_, ...), custom_call_target="tpu_custom_call" | custom-call | flops 603979776 | bytes 4194304 | tf_op jit(solution)/shard_map/middle/pallas_call | solution.py:42
  41.3 1.1 %middle.4 = (f32[1024,512]{1,0:T(8,128)S(1)}, bf16[1024,512]{1,0:T(8,128)(2,1)S(1)}, bf16[1024,512]{1,0:T(8,128)(2,1)S(1)}, f32[64,512]{1,0:T(8,128)S(1)}) custom-call(f32[64,64]{1,0:T(8,128)S(1)} %eliminate.2.inverse, f32[64,512]{1,0:T(8,128)S(1)} %collective-permute-done.2.away.rest_0_, f32[256,128]{1,0:T(8,128)S(1)} %unfold.4.rest_1_, ...), custom_call_target="tpu_custom_call" | custom-call | flops 301989888 | bytes 2097152 | tf_op jit(solution)/shard_map/middle/pallas_call | solution.py:42
  42.5 1.1 %middle.5 = (f32[1024,512]{1,0:T(8,128)S(1)}, bf16[1024,512]{1,0:T(8,128)(2,1)S(1)}, bf16[1024,512]{1,0:T(8,128)(2,1)S(1)}, f32[64,512]{1,0:T(8,128)S(1)}) custom-call(f32[64,64]{1,0:T(8,128)S(1)} %eliminate.2.inverse, f32[64,512]{1,0:T(8,128)S(1)} %add.6.mine.rest_1_.rest_0_, ...), custom_call_target="tpu_custom_call", output_to_operand_aliasing={{0}: (6, {}), {1}: (7, {}), {2}: (8, {})} | custom-call | flops 301989888 | bytes 2097152 | tf_op jit(solution)/shard_map/middle/pallas_call | solution.py:42
  43.9 1.6 %collective-permute-start.11 = (f32[64,512]{1,0:T(8,128)S(1)}, f32[64,512]{1,0:T(8,128)S(1)}, u32[]{:S(2)}, u32[]{:S(2)}) collective-permute-start(f32[64,512]{1,0:T(8,128)S(1)} %add.7.refs_0_), channel_id=1, source_target_pairs={{0,16},{8,24},{16,0},{24,8},{1,17},{9,25},{17,1},{25,9},{2,18},{10... | collective-permute-start | bytes 393224 | tf_op jit(solution)/shard_map/ppermute | solution.py:201
  45.5 4.2 %collective-permute-done.11.refs_1_ = f32[64,512]{1,0:T(8,128)S(1)} collective-permute-done((f32[64,512]{1,0:T(8,128)S(1)}, f32[64,512]{1,0:T(8,128)S(1)}, u32[]{:S(2)}, u32[]{:S(2)}) %collective-permute-start.11) | collective-permute-done | bytes 131104 | tf_op jit(solution)/shard_map/ppermute | solution.py:201
  49.7 0.6 multiply_mine.3
  50.3 0.7 collective-permute-done.12.away
  51.1 0.5 multiply_other.3
  51.5 0.3 multiply_own.3
  51.8 1.0 %collective-permute-start.15 = (f32[160,128]{1,0:T(8,128)S(1)}, f32[160,128]{1,0:T(8,128)S(1)}, u32[]{:S(2)}, u32[]{:S(2)}) collective-permute-start(f32[160,128]{1,0:T(8,128)S(1)} %get-tuple-element.84), channel_id=1, source_target_pairs={{0,2},{1,3},{2,0},{3,1},{4,6},{5,7},{6,4},{7,5},{8,10},{9,11},{10,... | collective-permute-start | bytes 245768 | tf_op jit(solution)/shard_map/ppermute | solution.py:116
  52.9 1.8 %collective-permute-start.14 = (f32[160,128]{1,0:T(8,128)S(1)}, f32[160,128]{1,0:T(8,128)S(1)}, u32[]{:S(2)}, u32[]{:S(2)}) collective-permute-start(f32[160,128]{1,0:T(8,128)S(1)} %get-tuple-element.83), channel_id=1, source_target_pairs={{0,3},{1,2},{2,1},{3,0},{4,7},{5,6},{6,5},{7,4},{8,11},{9,10},{10,... | collective-permute-start | bytes 245768 | tf_op jit(solution)/shard_map/ppermute | solution.py:116
  54.7 0.7 collective-permute-start.13
  55.4 1.5 %collective-permute-done.15.refs_2_ = f32[160,128]{1,0:T(8,128)S(1)} collective-permute-done((f32[160,128]{1,0:T(8,128)S(1)}, f32[160,128]{1,0:T(8,128)S(1)}, u32[]{:S(2)}, u32[]{:S(2)}) %collective-permute-start.15) | collective-permute-done | bytes 81952 | tf_op jit(solution)/shard_map/ppermute | solution.py:116
  56.9 2.1 %collective-permute-done.14.refs_1_ = f32[160,128]{1,0:T(8,128)S(1)} collective-permute-done((f32[160,128]{1,0:T(8,128)S(1)}, f32[160,128]{1,0:T(8,128)S(1)}, u32[]{:S(2)}, u32[]{:S(2)}) %collective-permute-start.14) | collective-permute-done | bytes 81952 | tf_op jit(solution)/shard_map/ppermute | solution.py:116
  59.0 1.1 %collective-permute-done.13.refs_0_ = f32[160,128]{1,0:T(8,128)S(1)} collective-permute-done((f32[160,128]{1,0:T(8,128)S(1)}, f32[160,128]{1,0:T(8,128)S(1)}, u32[]{:S(2)}, u32[]{:S(2)}) %collective-permute-start.13) | collective-permute-done | bytes 81952 | tf_op jit(solution)/shard_map/ppermute | solution.py:116
  60.2 2.6 %collective-permute-start.16 = (f32[160,128]{1,0:T(8,128)S(1)}, f32[160,128]{1,0:T(8,128)S(1)}, u32[]{:S(2)}, u32[]{:S(2)}) collective-permute-start(f32[160,128]{1,0:T(8,128)S(1)} %collect.3.one), channel_id=1, source_target_pairs={{0,4},{1,5},{2,6},{3,7},{4,0},{5,1},{6,2},{7,3},{8,12},{9,13},{10,... | collective-permute-start | bytes 245768 | tf_op jit(solution)/shard_map/ppermute | solution.py:116
  62.8 3.9 %collective-permute-done.16.two = f32[160,128]{1,0:T(8,128)S(1)} collective-permute-done((f32[160,128]{1,0:T(8,128)S(1)}, f32[160,128]{1,0:T(8,128)S(1)}, u32[]{:S(2)}, u32[]{:S(2)}) %collective-permute-start.16) | collective-permute-done | bytes 81952 | tf_op jit(solution)/shard_map/ppermute | solution.py:116
  66.7 0.6 collective-permute-start.17
  67.3 2.1 %collective-permute-start.19 = (f32[128,128]{1,0:T(8,128)S(1)}, f32[128,128]{1,0:T(8,128)S(1)}, u32[]{:S(2)}, u32[]{:S(2)}) collective-permute-start(f32[128,128]{1,0:T(8,128)S(1)} %top.3.value), channel_id=1, source_target_pairs={{0,3},{1,2},{2,1},{3,0},{4,7},{5,6},{6,5},{7,4},{8,11},{9,10},{10,... | collective-permute-start | bytes 196616 | tf_op jit(solution)/shard_map/ppermute | solution.py:116
  69.3 0.9 %collective-permute-start.18 = (f32[128,128]{1,0:T(8,128)S(1)}, f32[128,128]{1,0:T(8,128)S(1)}, u32[]{:S(2)}, u32[]{:S(2)}) collective-permute-start(f32[128,128]{1,0:T(8,128)S(1)} %top.3.value), channel_id=1, source_target_pairs={{0,1},{1,0},{2,3},{3,2},{4,5},{5,4},{6,7},{7,6},{8,9},{9,8},{10,11... | collective-permute-start | bytes 196616 | tf_op jit(solution)/shard_map/ppermute | solution.py:116
  70.2 2.8 %eliminate.3.inverse = f32[64,64]{1,0:T(8,128)S(1)} custom-call(f32[160,128]{1,0:T(8,128)S(1)} %collect.3.one, f32[160,128]{1,0:T(8,128)S(1)} %collective-permute-done.16.two), custom_call_target="tpu_custom_call" | custom-call | flops 100000000 | bytes 8388608 | tf_op jit(solution)/shard_map/eliminate/pallas_call | solution.py:42
  73.1 0.5 collective-permute-done.18.value
  73.6 1.0 %widen.1 = (f32[64,512]{1,0:T(8,128)S(1)}, f32[64,512]{1,0:T(8,128)S(1)}, f32[32,128]{1,0:T(8,128)S(1)}) custom-call(f32[64,64]{1,0:T(8,128)S(1)} %eliminate.3.inverse, f32[256,128]{1,0:T(8,128)S(1)} %unfold.6.own.stacked, f32[256,128]{1,0:T(8,128)S(1)} %unfold.7.other.stacked), custom_call_target="tpu_custom_call" | custom-call | flops 100000000 | bytes 1048576 | tf_op jit(solution)/shard_map/widen/pallas_call | solution.py:42
  74.7 1.3 %final.2 = (f32[1024,512]{1,0:T(8,128)S(1)}, f32[1024,512]{1,0:T(8,128)S(1)}, f32[64,1024]{1,0:T(8,128)}) custom-call(f32[64,64]{1,0:T(8,128)S(1)} %eliminate.3.inverse, f32[64,512]{1,0:T(8,128)S(1)} %collective-permute-done.12.away, f32[64,512]{1,0:T(8,128)S(1)} %add.8.mine, f32[256,128]{1,0:T(8,128)S(1)} %unfold.6.own.stacked, ...), custom_call_target="tpu_custom_call" | custom-call | flops 201326592 | bytes 4194304 | tf_op jit(solution)/shard_map/final/pallas_call | solution.py:42
  76.0 1.6 %collective-permute-start.21 = (f32[32,128]{1,0:T(8,128)S(1)}, f32[32,128]{1,0:T(8,128)S(1)}, u32[]{:S(2)}, u32[]{:S(2)}) collective-permute-start(f32[32,128]{1,0:T(8,128)S(1)} %add.9.one), channel_id=1, source_target_pairs={{0,16},{8,24},{16,0},{24,8},{1,17},{9,25},{17,1},{25,9},{2,18},{10... | collective-permute-start | bytes 49160 | tf_op jit(solution)/shard_map/ppermute | solution.py:116
  77.6 2.5 %final.3 = (f32[1024,512]{1,0:T(8,128)S(1)}, f32[1024,512]{1,0:T(8,128)S(1)}, f32[1024,1024]{1,0:T(8,128)}, f32[1024,1024]{1,0:T(8,128)}) custom-call(f32[64,64]{1,0:T(8,128)S(1)} %eliminate.3.inverse, f32[64,512]{1,0:T(8,128)S(1)} %collective-permute-done.12.away, f32[64,512]{1,0:T(8,128)S(1)} %add.8.mine, f32[256,128]{1,0:T(8,128)S(1)} %unfold.7.other.stacked, ...), custom_call_target="tpu_custom_call" | custom-call | flops 201326592 | bytes 4194304 | tf_op jit(solution)/shard_map/final/pallas_call | solution.py:42
  80.2 4.0 %finish.1 = (f32[64,1024]{1,0:T(8,128)}, f32[1024,1024]{1,0:T(8,128)}, f32[1024,1024]{1,0:T(8,128)}) custom-call(f32[32,128]{1,0:T(8,128)S(1)} %add.9.one, f32[32,128]{1,0:T(8,128)S(1)} %collective-permute-done.21.two, f32[64,512]{1,0:T(8,128)S(1)} %get-tuple-element.86.own, ...), custom_call_target="tpu_custom_call", output_to_operand_aliasing={{1}: (6, {}), {2}: (7, {})} | custom-call | flops 100000000 | bytes 8388608 | tf_op jit(solution)/shard_map/finish/pallas_call | solution.py:42
  (25 shorter events, 0.7 us)
Async XLA Ops:
  7.1 1.5 %collective-permute-start = (f32[64,512]{1,0:T(8,128)S(1)}, f32[64,512]{1,0:T(8,128)S(1)}, u32[]{:S(2)}, u32[]{:S(2)}) collective-permute-start(f32[64,512]{1,0:T(8,128)S(1)} %get-tuple-element.53), channel_id=1, source_target_pairs={{0,8},{8,0},{16,24},{24,16},{1,9},{9,1},{17,25},{25,17},{2,10},{10... | collective-permute-start | bytes 393224 | tf_op jit(solution)/shard_map/ppermute | solution.py:116
  8.6 6.8 %collective-permute-start.1 = (f32[64,512]{1,0:T(8,128)S(1)}, f32[64,512]{1,0:T(8,128)S(1)}, u32[]{:S(2)}, u32[]{:S(2)}) collective-permute-start(f32[64,512]{1,0:T(8,128)S(1)} %add.5.refs_0_), channel_id=1, source_target_pairs={{0,16},{8,24},{16,0},{24,8},{1,17},{9,25},{17,1},{25,9},{2,18},{10... | collective-permute-start | bytes 393224 | tf_op jit(solution)/shard_map/ppermute | solution.py:201
  15.4 1.4 %collective-permute-start.2 = (f32[64,512]{1,0:T(8,128)S(1)}, f32[64,512]{1,0:T(8,128)S(1)}, u32[]{:S(2)}, u32[]{:S(2)}) collective-permute-start(f32[64,512]{1,0:T(8,128)S(1)} %add.6.mine.rest_1_.rest_0_), channel_id=1, source_target_pairs={{0,8},{8,0},{16,24},{24,16},{1,9},{9,1},{17,25},{25,17},{2,10},{10... | collective-permute-start | bytes 393224 | tf_op jit(solution)/shard_map/ppermute | solution.py:116
  17.6 4.6 %collective-permute-start.5 = (f32[160,128]{1,0:T(8,128)S(1)}, f32[160,128]{1,0:T(8,128)S(1)}, u32[]{:S(2)}, u32[]{:S(2)}) collective-permute-start(f32[160,128]{1,0:T(8,128)S(1)} %get-tuple-element.64), channel_id=1, source_target_pairs={{0,2},{1,3},{2,0},{3,1},{4,6},{5,7},{6,4},{7,5},{8,10},{9,11},{10,... | collective-permute-start | bytes 245768 | tf_op jit(solution)/shard_map/ppermute | solution.py:116
  19.4 5.7 %collective-permute-start.4 = (f32[160,128]{1,0:T(8,128)S(1)}, f32[160,128]{1,0:T(8,128)S(1)}, u32[]{:S(2)}, u32[]{:S(2)}) collective-permute-start(f32[160,128]{1,0:T(8,128)S(1)} %get-tuple-element.63), channel_id=1, source_target_pairs={{0,3},{1,2},{2,1},{3,0},{4,7},{5,6},{6,5},{7,4},{8,11},{9,10},{10,... | collective-permute-start | bytes 245768 | tf_op jit(solution)/shard_map/ppermute | solution.py:116
  20.8 5.6 %collective-permute-start.3 = (f32[160,128]{1,0:T(8,128)S(1)}, f32[160,128]{1,0:T(8,128)S(1)}, u32[]{:S(2)}, u32[]{:S(2)}) collective-permute-start(f32[160,128]{1,0:T(8,128)S(1)} %get-tuple-element.61.sent), channel_id=1, source_target_pairs={{0,1},{1,0},{2,3},{3,2},{4,5},{5,4},{6,7},{7,6},{8,9},{9,8},{10,11... | collective-permute-start | bytes 245768 | tf_op jit(solution)/shard_map/ppermute | solution.py:116
  26.4 6.6 %collective-permute-start.6 = (f32[160,128]{1,0:T(8,128)S(1)}, f32[160,128]{1,0:T(8,128)S(1)}, u32[]{:S(2)}, u32[]{:S(2)}) collective-permute-start(f32[160,128]{1,0:T(8,128)S(1)} %collect.2.one), channel_id=1, source_target_pairs={{0,4},{1,5},{2,6},{3,7},{4,0},{5,1},{6,2},{7,3},{8,12},{9,13},{10,... | collective-permute-start | bytes 245768 | tf_op jit(solution)/shard_map/ppermute | solution.py:116
  33.0 6.3 %collective-permute-start.9 = (f32[128,128]{1,0:T(8,128)S(1)}, f32[128,128]{1,0:T(8,128)S(1)}, u32[]{:S(2)}, u32[]{:S(2)}) collective-permute-start(f32[128,128]{1,0:T(8,128)S(1)} %top.2.value), channel_id=1, source_target_pairs={{0,2},{1,3},{2,0},{3,1},{4,6},{5,7},{6,4},{7,5},{8,10},{9,11},{10,... | collective-permute-start | bytes 196616 | tf_op jit(solution)/shard_map/ppermute | solution.py:116
  33.6 5.8 %collective-permute-start.8 = (f32[128,128]{1,0:T(8,128)S(1)}, f32[128,128]{1,0:T(8,128)S(1)}, u32[]{:S(2)}, u32[]{:S(2)}) collective-permute-start(f32[128,128]{1,0:T(8,128)S(1)} %top.2.value), channel_id=1, source_target_pairs={{0,3},{1,2},{2,1},{3,0},{4,7},{5,6},{6,5},{7,4},{8,11},{9,10},{10,... | collective-permute-start | bytes 196616 | tf_op jit(solution)/shard_map/ppermute | solution.py:116
  35.2 4.3 %collective-permute-start.7 = (f32[128,128]{1,0:T(8,128)S(1)}, f32[128,128]{1,0:T(8,128)S(1)}, u32[]{:S(2)}, u32[]{:S(2)}) collective-permute-start(f32[128,128]{1,0:T(8,128)S(1)} %top.2.value), channel_id=1, source_target_pairs={{0,1},{1,0},{2,3},{3,2},{4,5},{5,4},{6,7},{7,6},{8,9},{9,8},{10,11... | collective-permute-start | bytes 196616 | tf_op jit(solution)/shard_map/ppermute | solution.py:116
  42.5 1.4 %collective-permute-start.10 = (f32[64,512]{1,0:T(8,128)S(1)}, f32[64,512]{1,0:T(8,128)S(1)}, u32[]{:S(2)}, u32[]{:S(2)}) collective-permute-start(f32[64,512]{1,0:T(8,128)S(1)} %get-tuple-element.73), channel_id=1, source_target_pairs={{0,8},{8,0},{16,24},{24,16},{1,9},{9,1},{17,25},{25,17},{2,10},{10... | collective-permute-start | bytes 393224 | tf_op jit(solution)/shard_map/ppermute | solution.py:116
  43.9 5.7 %collective-permute-start.11 = (f32[64,512]{1,0:T(8,128)S(1)}, f32[64,512]{1,0:T(8,128)S(1)}, u32[]{:S(2)}, u32[]{:S(2)}) collective-permute-start(f32[64,512]{1,0:T(8,128)S(1)} %add.7.refs_0_), channel_id=1, source_target_pairs={{0,16},{8,24},{16,0},{24,8},{1,17},{9,25},{17,1},{25,9},{2,18},{10... | collective-permute-start | bytes 393224 | tf_op jit(solution)/shard_map/ppermute | solution.py:201
  49.6 1.4 %collective-permute-start.12 = (f32[64,512]{1,0:T(8,128)S(1)}, f32[64,512]{1,0:T(8,128)S(1)}, u32[]{:S(2)}, u32[]{:S(2)}) collective-permute-start(f32[64,512]{1,0:T(8,128)S(1)} %add.8.mine), channel_id=1, source_target_pairs={{0,8},{8,0},{16,24},{24,16},{1,9},{9,1},{17,25},{25,17},{2,10},{10... | collective-permute-start | bytes 393224 | tf_op jit(solution)/shard_map/ppermute | solution.py:116
  51.8 5.1 %collective-permute-start.15 = (f32[160,128]{1,0:T(8,128)S(1)}, f32[160,128]{1,0:T(8,128)S(1)}, u32[]{:S(2)}, u32[]{:S(2)}) collective-permute-start(f32[160,128]{1,0:T(8,128)S(1)} %get-tuple-element.84), channel_id=1, source_target_pairs={{0,2},{1,3},{2,0},{3,1},{4,6},{5,7},{6,4},{7,5},{8,10},{9,11},{10,... | collective-permute-start | bytes 245768 | tf_op jit(solution)/shard_map/ppermute | solution.py:116
  52.9 6.2 %collective-permute-start.14 = (f32[160,128]{1,0:T(8,128)S(1)}, f32[160,128]{1,0:T(8,128)S(1)}, u32[]{:S(2)}, u32[]{:S(2)}) collective-permute-start(f32[160,128]{1,0:T(8,128)S(1)} %get-tuple-element.83), channel_id=1, source_target_pairs={{0,3},{1,2},{2,1},{3,0},{4,7},{5,6},{6,5},{7,4},{8,11},{9,10},{10,... | collective-permute-start | bytes 245768 | tf_op jit(solution)/shard_map/ppermute | solution.py:116
  54.7 5.4 %collective-permute-start.13 = (f32[160,128]{1,0:T(8,128)S(1)}, f32[160,128]{1,0:T(8,128)S(1)}, u32[]{:S(2)}, u32[]{:S(2)}) collective-permute-start(f32[160,128]{1,0:T(8,128)S(1)} %get-tuple-element.81.sent), channel_id=1, source_target_pairs={{0,1},{1,0},{2,3},{3,2},{4,5},{5,4},{6,7},{7,6},{8,9},{9,8},{10,11... | collective-permute-start | bytes 245768 | tf_op jit(solution)/shard_map/ppermute | solution.py:116
  60.2 6.5 %collective-permute-start.16 = (f32[160,128]{1,0:T(8,128)S(1)}, f32[160,128]{1,0:T(8,128)S(1)}, u32[]{:S(2)}, u32[]{:S(2)}) collective-permute-start(f32[160,128]{1,0:T(8,128)S(1)} %collect.3.one), channel_id=1, source_target_pairs={{0,4},{1,5},{2,6},{3,7},{4,0},{5,1},{6,2},{7,3},{8,12},{9,13},{10,... | collective-permute-start | bytes 245768 | tf_op jit(solution)/shard_map/ppermute | solution.py:116
  66.7 6.3 %collective-permute-start.17 = (f32[128,128]{1,0:T(8,128)S(1)}, f32[128,128]{1,0:T(8,128)S(1)}, u32[]{:S(2)}, u32[]{:S(2)}) collective-permute-start(f32[128,128]{1,0:T(8,128)S(1)} %top.3.value), channel_id=1, source_target_pairs={{0,2},{1,3},{2,0},{3,1},{4,6},{5,7},{6,4},{7,5},{8,10},{9,11},{10,... | collective-permute-start | bytes 196616 | tf_op jit(solution)/shard_map/ppermute | solution.py:116
  67.3 5.8 %collective-permute-start.19 = (f32[128,128]{1,0:T(8,128)S(1)}, f32[128,128]{1,0:T(8,128)S(1)}, u32[]{:S(2)}, u32[]{:S(2)}) collective-permute-start(f32[128,128]{1,0:T(8,128)S(1)} %top.3.value), channel_id=1, source_target_pairs={{0,3},{1,2},{2,1},{3,0},{4,7},{5,6},{6,5},{7,4},{8,11},{9,10},{10,... | collective-permute-start | bytes 196616 | tf_op jit(solution)/shard_map/ppermute | solution.py:116
  69.3 4.3 %collective-permute-start.18 = (f32[128,128]{1,0:T(8,128)S(1)}, f32[128,128]{1,0:T(8,128)S(1)}, u32[]{:S(2)}, u32[]{:S(2)}) collective-permute-start(f32[128,128]{1,0:T(8,128)S(1)} %top.3.value), channel_id=1, source_target_pairs={{0,1},{1,0},{2,3},{3,2},{4,5},{5,4},{6,7},{7,6},{8,9},{9,8},{10,11... | collective-permute-start | bytes 196616 | tf_op jit(solution)/shard_map/ppermute | solution.py:116
  74.6 1.4 %collective-permute-start.20 = (f32[32,128]{1,0:T(8,128)S(1)}, f32[32,128]{1,0:T(8,128)S(1)}, u32[]{:S(2)}, u32[]{:S(2)}) collective-permute-start(f32[32,128]{1,0:T(8,128)S(1)} %get-tuple-element.85.refs_0_), channel_id=1, source_target_pairs={{0,8},{8,0},{16,24},{24,16},{1,9},{9,1},{17,25},{25,17},{2,10},{10... | collective-permute-start | bytes 49160 | tf_op jit(solution)/shard_map/ppermute | solution.py:116
  76.0 4.1 %collective-permute-start.21 = (f32[32,128]{1,0:T(8,128)S(1)}, f32[32,128]{1,0:T(8,128)S(1)}, u32[]{:S(2)}, u32[]{:S(2)}) collective-permute-start(f32[32,128]{1,0:T(8,128)S(1)} %add.9.one), channel_id=1, source_target_pairs={{0,16},{8,24},{16,0},{24,8},{1,17},{9,25},{17,1},{25,9},{2,18},{10... | collective-permute-start | bytes 49160 | tf_op jit(solution)/shard_map/ppermute | solution.py:116

commit v12 on v11

--- a/solution.py
+++ b/solution.py
@@ -64,7 +64,7 @@
         at = 8 * j % gram_rows
         eye = jnp.where(lane - rank == sub + 8 * j, 1.0, 0.0)
         rows.append(jnp.where(lane < rank, source[at : at + 8], eye))
-    wide = 4
+    wide = 8
     for k in range(0, rank, wide):
         r, at = divmod(k, 8)
         after = range(r if at + wide < 8 else r + 1, rank // 8)
@@ -322,25 +322,34 @@
             beside, straight, across = [swap(value, "pix", bit) for bit in (2, 1, 3)]
             return inverse, unfold(1, value, beside), unfold(1, straight, across)
 
-        def halves(inverse, panel, stacked):
+        def tops_of(inverse, panel):
             left = dot(inverse[...], join(panel), ((1,), (0,)), HIGH)
-            wide = dot(inverse[...], unstack(stacked), ((1,), (0,)), HIGH)
-            left_high, left_low = split(left)
-            wide_high, wide_low = split(wide)
-            tops = jnp.concatenate([left_high, left_low, left_high], axis=0)
-            return left, (wide_high, wide_low), tops, jnp.concatenate([wide_high, wide_high, wide_low], axis=0)
-
-        def middle(p, sides, inverse, panel, stacked, o, u, before, arrays=()):
+            high, low = split(left)
+            return left, jnp.concatenate([high, low, high], axis=0)
+
+        def wides_of(inverse, stacked):
+            high, low = split(dot(inverse[...], unstack(stacked), ((1,), (0,)), HIGH))
+            return (high, low), jnp.concatenate([high, high, low], axis=0)
+
+        tops_out = (3 * rank, n_rows), BF16, pltpu.VMEM
+
+        def middle(p, sides, inverse, left, stacked, o, u, before, arrays=()):
             n = len(sides)
             blocks = [i for i in range(steps) if i // (steps // 2) in sides]
+            lefts = [left] if p else list(left)
 
             def body(inverse, *rest):
                 s = place()
-                panel, (stacked, o, u, *rest) = rest[:n], rest[n:]
+                panel, (stacked, o, u, *rest) = rest[: len(lefts)], rest[len(lefts) :]
                 base, high, low, *after = rest[n * p + len(arrays) :]
-                _, right, tops, wides = halves(inverse, panel, stacked)
+                if p:
+                    tops = panel[0]
+                else:
+                    tops = after[n]
+                    tops[...] = tops_of(inverse, panel)[1]
+                right, wides = wides_of(inverse, stacked)
                 for k, i in enumerate(blocks):
-                    lowrank = dot(tops[:, chunk(k)], wides, ((0,), (0,)))
+                    lowrank = dot(tops[:, chunk(i)], wides, ((0,), (0,)))
                     at = chunk(i), pl.ds(pix_at(p, s), half)
                     value = u[at] - lowrank
                     scaled = jnp.clip(value, -TAU, TAU)
@@ -352,15 +361,15 @@
                     side, block = divmod(k, steps // 2)
                     after[side][:, chunk(block)] = rest[side][:, chunk(block)] + term if p else term
 
-            ins = [inverse, *[panel[side] for side in sides], stacked, o, u]
+            ins = [inverse, *lefts, stacked, o, u]
             ins += [before[side] for side in sides] if p else []
             aliases = {len(ins) + k: k for k in range(len(arrays))}
             outs = [((n_rows, half), F32, pltpu.VMEM)] + [((n_rows, half), BF16, pltpu.VMEM)] * 2
-            outs += [((rank, n_rows // 2), F32, pltpu.VMEM)] * n
+            outs += [((rank, n_rows // 2), F32, pltpu.VMEM)] * n + [tops_out] * (1 - p)
             cost = (9 * rank * n_rows * n_cols // (3 - n), 4 * n_rows * n_cols // (3 - n))
             ins = [(a, pltpu.VMEM) for a in (*ins, *arrays)]
-            base, high, low, *part = call(body, "middle", ins, outs, aliases=aliases, cost=cost)
-            return base, (high, low), part
+            base, high, low, *rest = call(body, "middle", ins, outs, aliases=aliases, cost=cost)
+            return base, (high, low), *((rest,) if p else (rest[:n], rest[n]))
 
         def put(sources, targets, p, s, sems):
             def moves(i):
@@ -377,19 +386,25 @@
             lax.fori_loop(0, steps, start, 0)
             return [move for i in range(steps) for move in moves(i)]
 
-        def final(p, inverse, panel, stacked, base, before=()):
-            def body(inverse, away, mine, stacked, base, *rest):
-                s = place()
-                sparse, dual, *outs = rest[len(before) :]
-                *outs, left_part, sems = outs
-                left, _, tops, wides = halves(inverse, (away, mine), stacked)
+        def final(p, inverse, left, stacked, base, before=()):
+            lefts = [left] if p else list(left)
+
+            def body(inverse, *rest):
+                s = place()
+                panel, (stacked, base, *rest) = rest[: len(lefts)], rest[len(lefts) :]
+                sparse, dual, *outs, left_part, sems = rest[len(before) :]
                 if p:
-                    moves = put(rest[:2], outs, 0, s, sems)
+                    moves = put(rest[:1], outs, 0, s, sems)
+                    tops = panel[0]
                 else:
+                    value, stack = tops_of(inverse, panel)
+                    tops = outs[1]
+                    tops[...] = stack
                     for i in range(steps):
-                        left_part[:, pl.ds(gal_at(i, s), tall)] = left[:, chunk(i)]
+                        left_part[:, pl.ds(gal_at(i, s), tall)] = value[:, chunk(i)]
                     moves = [pltpu.make_async_copy(left_part, outs[0], sems.at[0, 0])]
                     moves[0].start()
+                _, wides = wides_of(inverse, stacked)
                 for i in range(steps):
                     value = base[chunk(i), :] - dot(tops[:, chunk(i)], wides, ((0,), (0,)))
                     scaled = jnp.clip(value, -TAU, TAU)
@@ -398,13 +413,13 @@
                 for move in moves:
                     move.wait()
 
-            ins = [(a, pltpu.VMEM) for a in (inverse, *panel, stacked, base, *before)]
+            ins = [(a, pltpu.VMEM) for a in (inverse, *lefts, stacked, base, *before)]
             outs = [((n_rows, half), F32, pltpu.VMEM)] * 2
             if p:
-                outs += [((n_rows, n_cols), F32, pltpu.HBM)] * 2
+                outs += [((n_rows, n_cols), F32, pltpu.HBM)]
             else:
-                outs += [((rank, n_rows), F32, pltpu.HBM)]
-            scratch = [pltpu.VMEM((rank, n_rows), F32), pltpu.SemaphoreType.DMA((steps, 2))]
+                outs += [((rank, n_rows), F32, pltpu.HBM), tops_out]
+            scratch = [pltpu.VMEM((rank, n_rows), F32), pltpu.SemaphoreType.DMA((steps, 1))]
             cost = (3 * rank * n_rows * n_cols, 4 * n_rows * n_cols)
             return call(body, "final", ins, outs, scratch, cost=cost)
 
@@ -421,10 +436,13 @@
             outs = [((rank, half), F32, pltpu.VMEM)] * 2 + [((gram_rows, LANES), F32, pltpu.VMEM)]
             return call(body, "widen", ins, outs, cost=(10**8, MIB), limit=8)
 
-        def finish(one, two, wide, made, outs):
-            def body(one, two, own, other, sparse, dual, _, __, out, sparse_out, dual_out, inverse, right, sem, sems):
-                s = place()
-                moves = put((sparse, dual), (sparse_out, dual_out), 1, s, sems)
+        def finish(one, two, wide, made, first_dual, sparse):
+            def body(*refs):
+                one, two, own, other, sparse_1, dual_1, dual_0, _ = refs[:8]
+                out, sparse_out, dual_out, inverse, right, sem, sems, dual_sems = refs[8:]
+                s = place()
+                moves = put((sparse_1, dual_1), (sparse_out, dual_out), 1, s, sems)
+                moves += put((dual_0,), (dual_out,), 0, s, dual_sems)
                 invert(one[...] + two[...], inverse)
                 for p, value in enumerate((own, other)):
                     at = pl.ds(pix_at(p, s), half)
@@ -435,11 +453,11 @@
                 for move in moves:
                     move.wait()
 
-            ins = [(a, pltpu.VMEM) for a in (one, two, *wide, *made)] + [(a, pltpu.HBM) for a in outs]
+            ins = [(a, pltpu.VMEM) for a in (one, two, *wide, *made, first_dual)] + [(sparse, pltpu.HBM)]
             results = [((rank, n_cols), F32, pltpu.HBM)] + [((n_rows, n_cols), F32, pltpu.HBM)] * 2
             scratch = [pltpu.VMEM((rank, rank), F32), pltpu.VMEM((rank, n_cols), F32)]
-            scratch += [pltpu.SemaphoreType.DMA((2,)), pltpu.SemaphoreType.DMA((steps, 2))]
-            return call(body, "finish", ins, results, scratch, {6: 1, 7: 2}, cost=(10**8, 8 * MIB))
+            scratch += [pltpu.SemaphoreType.DMA(shape) for shape in ((2,), (steps, 2), (steps, 1))]
+            return call(body, "finish", ins, results, scratch, {7: 1}, cost=(10**8, 8 * MIB))
 
         seen, pulls, own, other, part = first(right_init)
         base = [None, None]
@@ -447,22 +465,22 @@
             panel = sum_gal(part)
             inverse, own_wide, other_wide = sum_pix(panel, own, other)
             if step < ITERS - 1:
-                given = inverse, panel, own_wide, seen, pulls
-                base[0], own, part = middle(0, (0, 1), *given, None)
-                given = inverse, panel, other_wide, seen, pulls, part
+                given = own_wide, seen, pulls
+                base[0], own, part, tops = middle(0, (0, 1), inverse, panel, *given, None)
+                given = inverse, tops, other_wide, seen, pulls, part
                 base[1], other, away = middle(1, (0,), *given)
                 base[1], other, mine = middle(1, (1,), *given, (base[1], *other))
                 part = away + mine
             else:
                 *wide, gram = widen(inverse, own_wide, other_wide)
-                *made, left = final(0, inverse, panel, own_wide, base[0])
+                *made, left, tops = final(0, inverse, panel, own_wide, base[0])
                 bit = 1
                 while 2 * bit < n_gal:
                     gram = add(gram, swap(gram, "gal", bit))
                     bit *= 2
                 got = swap(gram, "gal", bit)
-                *made, sparse, dual = final(1, inverse, panel, other_wide, base[1], made)
-                right, sparse, dual = finish(gram, got, wide, made, (sparse, dual))
+                *later, sparse = final(1, inverse, tops, other_wide, base[1], made[:1])
+                right, sparse, dual = finish(gram, got, wide, later, made[1], sparse)
         return sparse, dual, left, right
 
     return jax.shard_map(

time: 84.4 us -> 83 us (0.983)
  Pallas kernels: 27.9 us -> 23.8 us
  waiting for transfers between devices: 29.1 us -> 31.8 us
    pallas_call x29, Pallas kernels: 27.9 us -> 23.8 us  [call(): pl.pallas_call(body, name=name, in_specs=[pl.BlockSpec(memory_space=space...]
    ppermute x20, waiting for transfers between devices: 21.2 us -> 23.9 us  [swap(): return lax.ppermute(value, axis, [(i, i ^ bit) for i in range(n)])]
  transfers between devices with their start and end apart: 22 -> 22, of which waited for: 16 -> 19; matrix products, arithmetic and copies ran while one was open for 0% -> 0% of each run, Pallas kernels for 14% -> 11%
where the time goes in v12:
time: 83 us; the launch traced here: 82.8 us
  waiting for transfers between devices  31.8 us (38%)
  starting transfers between devices  26.3 us (32%)
  Pallas kernels  23.8 us (29%)
  between operations  0.95 us (1%)
    ppermute x20, waiting for transfers between devices, swap(): return lax.ppermute(value, axis, [(i, i ^ bit) for i in range(n)])  23.9 us
    pallas_call x29, Pallas kernels, call(): pl.pallas_call(body, name=name, in_specs=[pl.BlockSpec(memory_space=space...  23.8 us
    ppermute x20, starting transfers between devices, swap(): return lax.ppermute(value, axis, [(i, i ^ bit) for i in range(n)])  21.7 us
    ppermute x2, waiting for transfers between devices, sum_gal(): lax.ppermute(mine, 'gal', [(i, (i + CORES * k) % n_gal) for i in range(n_...  7.86 us
    ppermute x2, starting transfers between devices, sum_gal(): lax.ppermute(mine, 'gal', [(i, (i + CORES * k) % n_gal) for i in range(n_...  4.53 us
  transfers between devices with their start and end apart: 22, of which 19 were waited for; matrix products, arithmetic and copies ran while one was open for 0% of the time, Pallas kernels for 11%

profile of v12, /device:TPU:0, one launch (start us, length us, event | category | flops | bytes accessed | tf_op | source)
XLA Modules:
  0.0 82.8 jit_solution(8399029781786244255)
XLA Ops:
  0.6 6.4 %first.1 = (f32[1024,1024]{1,0:T(8,128)S(1)}, f32[1024,1024]{1,0:T(8,128)S(1)}, bf16[1024,512]{1,0:T(8,128)(2,1)S(1)}, bf16[1024,512]{1,0:T(8,128)(2,1)S(1)}, bf...) custom-call(f32[1024,1024]{1,0:T(8,128)} %o_in.1, ...), custom_call_target="tpu_custom_call" | custom-call | flops 402653184 | bytes 16777216 | tf_op jit(solution)/shard_map/first/pallas_call | solution.py:42
  7.1 0.5 collective-permute-start
  7.6 1.0 %collective-permute-done.refs_1_ = f32[64,512]{1,0:T(8,128)S(1)} collective-permute-done((f32[64,512]{1,0:T(8,128)S(1)}, f32[64,512]{1,0:T(8,128)S(1)}, u32[]{:S(2)}, u32[]{:S(2)}) %collective-permute-start) | collective-permute-done | bytes 131104 | tf_op jit(solution)/shard_map/ppermute | solution.py:116
  8.6 2.9 %collective-permute-start.1 = (f32[64,512]{1,0:T(8,128)S(1)}, f32[64,512]{1,0:T(8,128)S(1)}, u32[]{:S(2)}, u32[]{:S(2)}) collective-permute-start(f32[64,512]{1,0:T(8,128)S(1)} %add.5.refs_0_), channel_id=1, source_target_pairs={{0,16},{8,24},{16,0},{24,8},{1,17},{9,25},{17,1},{25,9},{2,18},{10... | collective-permute-start | bytes 393224 | tf_op jit(solution)/shard_map/ppermute | solution.py:201
  11.5 3.8 %collective-permute-done.1.refs_1_ = f32[64,512]{1,0:T(8,128)S(1)} collective-permute-done((f32[64,512]{1,0:T(8,128)S(1)}, f32[64,512]{1,0:T(8,128)S(1)}, u32[]{:S(2)}, u32[]{:S(2)}) %collective-permute-start.1) | collective-permute-done | bytes 131104 | tf_op jit(solution)/shard_map/ppermute | solution.py:201
  15.5 0.6 multiply_mine.2
  16.1 0.7 collective-permute-done.2.away.rest_0_
  16.8 0.5 multiply_other.2
  17.6 1.9 %collective-permute-start.5 = (f32[160,128]{1,0:T(8,128)S(1)}, f32[160,128]{1,0:T(8,128)S(1)}, u32[]{:S(2)}, u32[]{:S(2)}) collective-permute-start(f32[160,128]{1,0:T(8,128)S(1)} %get-tuple-element.65), channel_id=1, source_target_pairs={{0,2},{1,3},{2,0},{3,1},{4,6},{5,7},{6,4},{7,5},{8,10},{9,11},{10,... | collective-permute-start | bytes 245768 | tf_op jit(solution)/shard_map/ppermute | solution.py:116
  19.4 1.4 %collective-permute-start.4 = (f32[160,128]{1,0:T(8,128)S(1)}, f32[160,128]{1,0:T(8,128)S(1)}, u32[]{:S(2)}, u32[]{:S(2)}) collective-permute-start(f32[160,128]{1,0:T(8,128)S(1)} %get-tuple-element.64), channel_id=1, source_target_pairs={{0,3},{1,2},{2,1},{3,0},{4,7},{5,6},{6,5},{7,4},{8,11},{9,10},{10,... | collective-permute-start | bytes 245768 | tf_op jit(solution)/shard_map/ppermute | solution.py:116
  21.1 1.1 %collective-permute-done.5.refs_2_ = f32[160,128]{1,0:T(8,128)S(1)} collective-permute-done((f32[160,128]{1,0:T(8,128)S(1)}, f32[160,128]{1,0:T(8,128)S(1)}, u32[]{:S(2)}, u32[]{:S(2)}) %collective-permute-start.5) | collective-permute-done | bytes 81952 | tf_op jit(solution)/shard_map/ppermute | solution.py:116
  22.2 2.9 %collective-permute-done.4.refs_1_ = f32[160,128]{1,0:T(8,128)S(1)} collective-permute-done((f32[160,128]{1,0:T(8,128)S(1)}, f32[160,128]{1,0:T(8,128)S(1)}, u32[]{:S(2)}, u32[]{:S(2)}) %collective-permute-start.4) | collective-permute-done | bytes 81952 | tf_op jit(solution)/shard_map/ppermute | solution.py:116
  25.1 1.2 %collective-permute-done.3.refs_0_ = f32[160,128]{1,0:T(8,128)S(1)} collective-permute-done((f32[160,128]{1,0:T(8,128)S(1)}, f32[160,128]{1,0:T(8,128)S(1)}, u32[]{:S(2)}, u32[]{:S(2)}) %collective-permute-start.3) | collective-permute-done | bytes 81952 | tf_op jit(solution)/shard_map/ppermute | solution.py:116
  26.4 2.6 %collective-permute-start.6 = (f32[160,128]{1,0:T(8,128)S(1)}, f32[160,128]{1,0:T(8,128)S(1)}, u32[]{:S(2)}, u32[]{:S(2)}) collective-permute-start(f32[160,128]{1,0:T(8,128)S(1)} %collect.2.one), channel_id=1, source_target_pairs={{0,4},{1,5},{2,6},{3,7},{4,0},{5,1},{6,2},{7,3},{8,12},{9,13},{10,... | collective-permute-start | bytes 245768 | tf_op jit(solution)/shard_map/ppermute | solution.py:116
  29.0 4.0 %collective-permute-done.6.two = f32[160,128]{1,0:T(8,128)S(1)} collective-permute-done((f32[160,128]{1,0:T(8,128)S(1)}, f32[160,128]{1,0:T(8,128)S(1)}, u32[]{:S(2)}, u32[]{:S(2)}) %collective-permute-start.6) | collective-permute-done | bytes 81952 | tf_op jit(solution)/shard_map/ppermute | solution.py:116
  33.0 0.6 collective-permute-start.7
  33.6 1.6 %collective-permute-start.9 = (f32[128,128]{1,0:T(8,128)S(1)}, f32[128,128]{1,0:T(8,128)S(1)}, u32[]{:S(2)}, u32[]{:S(2)}) collective-permute-start(f32[128,128]{1,0:T(8,128)S(1)} %top.2.value), channel_id=1, source_target_pairs={{0,3},{1,2},{2,1},{3,0},{4,7},{5,6},{6,5},{7,4},{8,11},{9,10},{10,... | collective-permute-start | bytes 196616 | tf_op jit(solution)/shard_map/ppermute | solution.py:116
  35.2 1.4 %collective-permute-start.8 = (f32[128,128]{1,0:T(8,128)S(1)}, f32[128,128]{1,0:T(8,128)S(1)}, u32[]{:S(2)}, u32[]{:S(2)}) collective-permute-start(f32[128,128]{1,0:T(8,128)S(1)} %top.2.value), channel_id=1, source_target_pairs={{0,1},{1,0},{2,3},{3,2},{4,5},{5,4},{6,7},{7,6},{8,9},{9,8},{10,11... | collective-permute-start | bytes 196616 | tf_op jit(solution)/shard_map/ppermute | solution.py:116
  36.6 1.9 %eliminate.2.inverse = f32[64,64]{1,0:T(8,128)S(1)} custom-call(f32[160,128]{1,0:T(8,128)S(1)} %collect.2.one, f32[160,128]{1,0:T(8,128)S(1)} %collective-permute-done.6.two), custom_call_target="tpu_custom_call" | custom-call | flops 100000000 | bytes 8388608 | tf_op jit(solution)/shard_map/eliminate/pallas_call | solution.py:42
  38.8 0.7 collective-permute-done.8.value
  39.5 1.8 %middle.3 = (f32[1024,512]{1,0:T(8,128)S(1)}, bf16[1024,512]{1,0:T(8,128)(2,1)S(1)}, bf16[1024,512]{1,0:T(8,128)(2,1)S(1)}, f32[64,512]{1,0:T(8,128)S(1)}, f32[6...) custom-call(f32[64,64]{1,0:T(8,128)S(1)} %eliminate.2.inverse, f32[64,512]{1,0:T(8,128)S(1)} %collective-permute-done.2.away.rest_0_, ...), custom_call_target="tpu_custom_call" | custom-call | flops 603979776 | bytes 4194304 | tf_op jit(solution)/shard_map/middle/pallas_call | solution.py:42
  41.3 1.0 %middle.4 = (f32[1024,512]{1,0:T(8,128)S(1)}, bf16[1024,512]{1,0:T(8,128)(2,1)S(1)}, bf16[1024,512]{1,0:T(8,128)(2,1)S(1)}, f32[64,512]{1,0:T(8,128)S(1)}) custom-call(f32[64,64]{1,0:T(8,128)S(1)} %eliminate.2.inverse, bf16[192,1024]{1,0:T(8,128)(2,1)S(1)} %get-tuple-element.68.rest_0_, f32[256,128]{1,0:T(8,128)S(1)} %unfold.5.rest_1_, ...), custom_call_target="tpu_custom_call" | custom-call | flops 301989888 | bytes 2097152 | tf_op jit(solution)/shard_map/middle/pallas_call | solution.py:42
  42.4 1.0 %middle.5 = (f32[1024,512]{1,0:T(8,128)S(1)}, bf16[1024,512]{1,0:T(8,128)(2,1)S(1)}, bf16[1024,512]{1,0:T(8,128)(2,1)S(1)}, f32[64,512]{1,0:T(8,128)S(1)}) custom-call(f32[64,64]{1,0:T(8,128)S(1)} %eliminate.2.inverse, bf16[192,1024]{1,0:T(8,128)(2,1)S(1)} %get-tuple-element.68.rest_0_, ...), custom_call_target="tpu_custom_call", output_to_operand_aliasing={{0}: (6, {}), {1}: (7, {}), {2}: (8, {})} | custom-call | flops 301989888 | bytes 2097152 | tf_op jit(solution)/shard_map/middle/pallas_call | solution.py:42
  43.4 0.3 collective-permute-done.10.refs_1_
  43.8 1.6 %collective-permute-start.11 = (f32[64,512]{1,0:T(8,128)S(1)}, f32[64,512]{1,0:T(8,128)S(1)}, u32[]{:S(2)}, u32[]{:S(2)}) collective-permute-start(f32[64,512]{1,0:T(8,128)S(1)} %add.7.refs_0_), channel_id=1, source_target_pairs={{0,16},{8,24},{16,0},{24,8},{1,17},{9,25},{17,1},{25,9},{2,18},{10... | collective-permute-start | bytes 393224 | tf_op jit(solution)/shard_map/ppermute | solution.py:201
  45.4 4.1 %collective-permute-done.11.refs_1_ = f32[64,512]{1,0:T(8,128)S(1)} collective-permute-done((f32[64,512]{1,0:T(8,128)S(1)}, f32[64,512]{1,0:T(8,128)S(1)}, u32[]{:S(2)}, u32[]{:S(2)}) %collective-permute-start.11) | collective-permute-done | bytes 131104 | tf_op jit(solution)/shard_map/ppermute | solution.py:201
  49.5 0.6 multiply_mine.3
  50.1 0.7 collective-permute-done.12.away.rest_0_
  50.8 0.5 multiply_other.3
  51.6 1.0 %collective-permute-start.15 = (f32[160,128]{1,0:T(8,128)S(1)}, f32[160,128]{1,0:T(8,128)S(1)}, u32[]{:S(2)}, u32[]{:S(2)}) collective-permute-start(f32[160,128]{1,0:T(8,128)S(1)} %get-tuple-element.86), channel_id=1, source_target_pairs={{0,2},{1,3},{2,0},{3,1},{4,6},{5,7},{6,4},{7,5},{8,10},{9,11},{10,... | collective-permute-start | bytes 245768 | tf_op jit(solution)/shard_map/ppermute | solution.py:116
  52.7 1.8 %collective-permute-start.14 = (f32[160,128]{1,0:T(8,128)S(1)}, f32[160,128]{1,0:T(8,128)S(1)}, u32[]{:S(2)}, u32[]{:S(2)}) collective-permute-start(f32[160,128]{1,0:T(8,128)S(1)} %get-tuple-element.85), channel_id=1, source_target_pairs={{0,3},{1,2},{2,1},{3,0},{4,7},{5,6},{6,5},{7,4},{8,11},{9,10},{10,... | collective-permute-start | bytes 245768 | tf_op jit(solution)/shard_map/ppermute | solution.py:116
  54.5 0.7 collective-permute-start.13
  55.2 1.5 %collective-permute-done.15.refs_2_ = f32[160,128]{1,0:T(8,128)S(1)} collective-permute-done((f32[160,128]{1,0:T(8,128)S(1)}, f32[160,128]{1,0:T(8,128)S(1)}, u32[]{:S(2)}, u32[]{:S(2)}) %collective-permute-start.15) | collective-permute-done | bytes 81952 | tf_op jit(solution)/shard_map/ppermute | solution.py:116
  56.7 2.1 %collective-permute-done.14.refs_1_ = f32[160,128]{1,0:T(8,128)S(1)} collective-permute-done((f32[160,128]{1,0:T(8,128)S(1)}, f32[160,128]{1,0:T(8,128)S(1)}, u32[]{:S(2)}, u32[]{:S(2)}) %collective-permute-start.14) | collective-permute-done | bytes 81952 | tf_op jit(solution)/shard_map/ppermute | solution.py:116
  58.8 1.1 %collective-permute-done.13.refs_0_ = f32[160,128]{1,0:T(8,128)S(1)} collective-permute-done((f32[160,128]{1,0:T(8,128)S(1)}, f32[160,128]{1,0:T(8,128)S(1)}, u32[]{:S(2)}, u32[]{:S(2)}) %collective-permute-start.13) | collective-permute-done | bytes 81952 | tf_op jit(solution)/shard_map/ppermute | solution.py:116
  60.0 2.5 %collective-permute-start.16 = (f32[160,128]{1,0:T(8,128)S(1)}, f32[160,128]{1,0:T(8,128)S(1)}, u32[]{:S(2)}, u32[]{:S(2)}) collective-permute-start(f32[160,128]{1,0:T(8,128)S(1)} %collect.3.one), channel_id=1, source_target_pairs={{0,4},{1,5},{2,6},{3,7},{4,0},{5,1},{6,2},{7,3},{8,12},{9,13},{10,... | collective-permute-start | bytes 245768 | tf_op jit(solution)/shard_map/ppermute | solution.py:116
  62.5 4.0 %collective-permute-done.16.two = f32[160,128]{1,0:T(8,128)S(1)} collective-permute-done((f32[160,128]{1,0:T(8,128)S(1)}, f32[160,128]{1,0:T(8,128)S(1)}, u32[]{:S(2)}, u32[]{:S(2)}) %collective-permute-start.16) | collective-permute-done | bytes 81952 | tf_op jit(solution)/shard_map/ppermute | solution.py:116
  66.5 0.6 collective-permute-start.17
  67.1 2.1 %collective-permute-start.19 = (f32[128,128]{1,0:T(8,128)S(1)}, f32[128,128]{1,0:T(8,128)S(1)}, u32[]{:S(2)}, u32[]{:S(2)}) collective-permute-start(f32[128,128]{1,0:T(8,128)S(1)} %top.3.value), channel_id=1, source_target_pairs={{0,3},{1,2},{2,1},{3,0},{4,7},{5,6},{6,5},{7,4},{8,11},{9,10},{10,... | collective-permute-start | bytes 196616 | tf_op jit(solution)/shard_map/ppermute | solution.py:116
  69.1 0.9 %collective-permute-start.18 = (f32[128,128]{1,0:T(8,128)S(1)}, f32[128,128]{1,0:T(8,128)S(1)}, u32[]{:S(2)}, u32[]{:S(2)}) collective-permute-start(f32[128,128]{1,0:T(8,128)S(1)} %top.3.value), channel_id=1, source_target_pairs={{0,1},{1,0},{2,3},{3,2},{4,5},{5,4},{6,7},{7,6},{8,9},{9,8},{10,11... | collective-permute-start | bytes 196616 | tf_op jit(solution)/shard_map/ppermute | solution.py:116
  70.0 1.9 %eliminate.3.inverse = f32[64,64]{1,0:T(8,128)S(1)} custom-call(f32[160,128]{1,0:T(8,128)S(1)} %collect.3.one, f32[160,128]{1,0:T(8,128)S(1)} %collective-permute-done.16.two), custom_call_target="tpu_custom_call" | custom-call | flops 100000000 | bytes 8388608 | tf_op jit(solution)/shard_map/eliminate/pallas_call | solution.py:42
  72.2 1.2 %collective-permute-done.18.value = f32[128,128]{1,0:T(8,128)S(1)} collective-permute-done((f32[128,128]{1,0:T(8,128)S(1)}, f32[128,128]{1,0:T(8,128)S(1)}, u32[]{:S(2)}, u32[]{:S(2)}) %collective-permute-start.18) | collective-permute-done | bytes 65568 | tf_op jit(solution)/shard_map/ppermute | solution.py:116
  73.4 1.0 %widen.1 = (f32[64,512]{1,0:T(8,128)S(1)}, f32[64,512]{1,0:T(8,128)S(1)}, f32[32,128]{1,0:T(8,128)S(1)}) custom-call(f32[64,64]{1,0:T(8,128)S(1)} %eliminate.3.inverse, f32[256,128]{1,0:T(8,128)S(1)} %unfold.6.own.rest_2_, f32[256,128]{1,0:T(8,128)S(1)} %unfold.7.other.rest_1_), custom_call_target="tpu_custom_call" | custom-call | flops 100000000 | bytes 1048576 | tf_op jit(solution)/shard_map/widen/pallas_call | solution.py:42
  74.5 1.3 %final.2 = (f32[1024,512]{1,0:T(8,128)S(1)}, f32[1024,512]{1,0:T(8,128)S(1)}, f32[64,1024]{1,0:T(8,128)}, bf16[192,1024]{1,0:T(8,128)(2,1)S(1)}) custom-call(f32[64,64]{1,0:T(8,128)S(1)} %eliminate.3.inverse, f32[64,512]{1,0:T(8,128)S(1)} %collective-permute-done.12.away.rest_0_, f32[64,512]{1,0:T(8,128)S(1)} %add.8.mine.rest_1_, ...), custom_call_target="tpu_custom_call" | custom-call | flops 201326592 | bytes 4194304 | tf_op jit(solution)/shard_map/final/pallas_call | solution.py:42
  75.8 1.6 %collective-permute-start.21 = (f32[32,128]{1,0:T(8,128)S(1)}, f32[32,128]{1,0:T(8,128)S(1)}, u32[]{:S(2)}, u32[]{:S(2)}) collective-permute-start(f32[32,128]{1,0:T(8,128)S(1)} %add.9.refs_0_), channel_id=1, source_target_pairs={{0,16},{8,24},{16,0},{24,8},{1,17},{9,25},{17,1},{25,9},{2,18},{10... | collective-permute-start | bytes 49160 | tf_op jit(solution)/shard_map/ppermute | solution.py:116
  77.4 1.3 %final.3 = (f32[1024,512]{1,0:T(8,128)S(1)}, f32[1024,512]{1,0:T(8,128)S(1)}, f32[1024,1024]{1,0:T(8,128)}) custom-call(f32[64,64]{1,0:T(8,128)S(1)} %eliminate.3.inverse, bf16[192,1024]{1,0:T(8,128)(2,1)S(1)} %get-tuple-element.91.rest_0_, f32[256,128]{1,0:T(8,128)S(1)} %unfold.7.other.rest_1_, f32[1024,512]{1,0:T(8,128)S(1)} %get-tuple-element.92.rest_2_, ...), custom_call_target="tpu_custom_call" | custom-call | flops 201326592 | bytes 4194304 | tf_op jit(solution)/shard_map/final/pallas_call | solution.py:42
  78.7 0.9 %collective-permute-done.21.refs_1_ = f32[32,128]{1,0:T(8,128)S(1)} collective-permute-done((f32[32,128]{1,0:T(8,128)S(1)}, f32[32,128]{1,0:T(8,128)S(1)}, u32[]{:S(2)}, u32[]{:S(2)}) %collective-permute-start.21) | collective-permute-done | bytes 16416 | tf_op jit(solution)/shard_map/ppermute | solution.py:116
  79.6 3.1 %finish.1 = (f32[64,1024]{1,0:T(8,128)}, f32[1024,1024]{1,0:T(8,128)}, f32[1024,1024]{1,0:T(8,128)}) custom-call(f32[32,128]{1,0:T(8,128)S(1)} %add.9.refs_0_, f32[32,128]{1,0:T(8,128)S(1)} %collective-permute-done.21.refs_1_, f32[64,512]{1,0:T(8,128)S(1)} %get-tuple-element.88.refs_2_, ...), custom_call_target="tpu_custom_call", output_to_operand_aliasing={{1}: (7, {})} | custom-call | flops 100000000 | bytes 8388608 | tf_op jit(solution)/shard_map/finish/pallas_call | solution.py:42
  (25 shorter events, 1.9 us)
Async XLA Ops:
  7.1 1.5 %collective-permute-start = (f32[64,512]{1,0:T(8,128)S(1)}, f32[64,512]{1,0:T(8,128)S(1)}, u32[]{:S(2)}, u32[]{:S(2)}) collective-permute-start(f32[64,512]{1,0:T(8,128)S(1)} %get-tuple-element.54), channel_id=1, source_target_pairs={{0,8},{8,0},{16,24},{24,16},{1,9},{9,1},{17,25},{25,17},{2,10},{10... | collective-permute-start | bytes 393224 | tf_op jit(solution)/shard_map/ppermute | solution.py:116
  8.6 6.8 %collective-permute-start.1 = (f32[64,512]{1,0:T(8,128)S(1)}, f32[64,512]{1,0:T(8,128)S(1)}, u32[]{:S(2)}, u32[]{:S(2)}) collective-permute-start(f32[64,512]{1,0:T(8,128)S(1)} %add.5.refs_0_), channel_id=1, source_target_pairs={{0,16},{8,24},{16,0},{24,8},{1,17},{9,25},{17,1},{25,9},{2,18},{10... | collective-permute-start | bytes 393224 | tf_op jit(solution)/shard_map/ppermute | solution.py:201
  15.4 1.4 %collective-permute-start.2 = (f32[64,512]{1,0:T(8,128)S(1)}, f32[64,512]{1,0:T(8,128)S(1)}, u32[]{:S(2)}, u32[]{:S(2)}) collective-permute-start(f32[64,512]{1,0:T(8,128)S(1)} %add.6.mine.rest_1_), channel_id=1, source_target_pairs={{0,8},{8,0},{16,24},{24,16},{1,9},{9,1},{17,25},{25,17},{2,10},{10... | collective-permute-start | bytes 393224 | tf_op jit(solution)/shard_map/ppermute | solution.py:116
  17.6 4.6 %collective-permute-start.5 = (f32[160,128]{1,0:T(8,128)S(1)}, f32[160,128]{1,0:T(8,128)S(1)}, u32[]{:S(2)}, u32[]{:S(2)}) collective-permute-start(f32[160,128]{1,0:T(8,128)S(1)} %get-tuple-element.65), channel_id=1, source_target_pairs={{0,2},{1,3},{2,0},{3,1},{4,6},{5,7},{6,4},{7,5},{8,10},{9,11},{10,... | collective-permute-start | bytes 245768 | tf_op jit(solution)/shard_map/ppermute | solution.py:116
  19.4 5.7 %collective-permute-start.4 = (f32[160,128]{1,0:T(8,128)S(1)}, f32[160,128]{1,0:T(8,128)S(1)}, u32[]{:S(2)}, u32[]{:S(2)}) collective-permute-start(f32[160,128]{1,0:T(8,128)S(1)} %get-tuple-element.64), channel_id=1, source_target_pairs={{0,3},{1,2},{2,1},{3,0},{4,7},{5,6},{6,5},{7,4},{8,11},{9,10},{10,... | collective-permute-start | bytes 245768 | tf_op jit(solution)/shard_map/ppermute | solution.py:116
  20.8 5.6 %collective-permute-start.3 = (f32[160,128]{1,0:T(8,128)S(1)}, f32[160,128]{1,0:T(8,128)S(1)}, u32[]{:S(2)}, u32[]{:S(2)}) collective-permute-start(f32[160,128]{1,0:T(8,128)S(1)} %get-tuple-element.62.sent), channel_id=1, source_target_pairs={{0,1},{1,0},{2,3},{3,2},{4,5},{5,4},{6,7},{7,6},{8,9},{9,8},{10,11... | collective-permute-start | bytes 245768 | tf_op jit(solution)/shard_map/ppermute | solution.py:116
  26.4 6.6 %collective-permute-start.6 = (f32[160,128]{1,0:T(8,128)S(1)}, f32[160,128]{1,0:T(8,128)S(1)}, u32[]{:S(2)}, u32[]{:S(2)}) collective-permute-start(f32[160,128]{1,0:T(8,128)S(1)} %collect.2.one), channel_id=1, source_target_pairs={{0,4},{1,5},{2,6},{3,7},{4,0},{5,1},{6,2},{7,3},{8,12},{9,13},{10,... | collective-permute-start | bytes 245768 | tf_op jit(solution)/shard_map/ppermute | solution.py:116
  33.0 5.5 %collective-permute-start.7 = (f32[128,128]{1,0:T(8,128)S(1)}, f32[128,128]{1,0:T(8,128)S(1)}, u32[]{:S(2)}, u32[]{:S(2)}) collective-permute-start(f32[128,128]{1,0:T(8,128)S(1)} %top.2.value), channel_id=1, source_target_pairs={{0,2},{1,3},{2,0},{3,1},{4,6},{5,7},{6,4},{7,5},{8,10},{9,11},{10,... | collective-permute-start | bytes 196616 | tf_op jit(solution)/shard_map/ppermute | solution.py:116
  33.6 5.2 %collective-permute-start.9 = (f32[128,128]{1,0:T(8,128)S(1)}, f32[128,128]{1,0:T(8,128)S(1)}, u32[]{:S(2)}, u32[]{:S(2)}) collective-permute-start(f32[128,128]{1,0:T(8,128)S(1)} %top.2.value), channel_id=1, source_target_pairs={{0,3},{1,2},{2,1},{3,0},{4,7},{5,6},{6,5},{7,4},{8,11},{9,10},{10,... | collective-permute-start | bytes 196616 | tf_op jit(solution)/shard_map/ppermute | solution.py:116
  35.2 4.3 %collective-permute-start.8 = (f32[128,128]{1,0:T(8,128)S(1)}, f32[128,128]{1,0:T(8,128)S(1)}, u32[]{:S(2)}, u32[]{:S(2)}) collective-permute-start(f32[128,128]{1,0:T(8,128)S(1)} %top.2.value), channel_id=1, source_target_pairs={{0,1},{1,0},{2,3},{3,2},{4,5},{5,4},{6,7},{7,6},{8,9},{9,8},{10,11... | collective-permute-start | bytes 196616 | tf_op jit(solution)/shard_map/ppermute | solution.py:116
  42.3 1.4 %collective-permute-start.10 = (f32[64,512]{1,0:T(8,128)S(1)}, f32[64,512]{1,0:T(8,128)S(1)}, u32[]{:S(2)}, u32[]{:S(2)}) collective-permute-start(f32[64,512]{1,0:T(8,128)S(1)} %get-tuple-element.75), channel_id=1, source_target_pairs={{0,8},{8,0},{16,24},{24,16},{1,9},{9,1},{17,25},{25,17},{2,10},{10... | collective-permute-start | bytes 393224 | tf_op jit(solution)/shard_map/ppermute | solution.py:116
  43.8 5.6 %collective-permute-start.11 = (f32[64,512]{1,0:T(8,128)S(1)}, f32[64,512]{1,0:T(8,128)S(1)}, u32[]{:S(2)}, u32[]{:S(2)}) collective-permute-start(f32[64,512]{1,0:T(8,128)S(1)} %add.7.refs_0_), channel_id=1, source_target_pairs={{0,16},{8,24},{16,0},{24,8},{1,17},{9,25},{17,1},{25,9},{2,18},{10... | collective-permute-start | bytes 393224 | tf_op jit(solution)/shard_map/ppermute | solution.py:201
  49.4 1.4 %collective-permute-start.12 = (f32[64,512]{1,0:T(8,128)S(1)}, f32[64,512]{1,0:T(8,128)S(1)}, u32[]{:S(2)}, u32[]{:S(2)}) collective-permute-start(f32[64,512]{1,0:T(8,128)S(1)} %add.8.mine.rest_1_), channel_id=1, source_target_pairs={{0,8},{8,0},{16,24},{24,16},{1,9},{9,1},{17,25},{25,17},{2,10},{10... | collective-permute-start | bytes 393224 | tf_op jit(solution)/shard_map/ppermute | solution.py:116
  51.6 5.1 %collective-permute-start.15 = (f32[160,128]{1,0:T(8,128)S(1)}, f32[160,128]{1,0:T(8,128)S(1)}, u32[]{:S(2)}, u32[]{:S(2)}) collective-permute-start(f32[160,128]{1,0:T(8,128)S(1)} %get-tuple-element.86), channel_id=1, source_target_pairs={{0,2},{1,3},{2,0},{3,1},{4,6},{5,7},{6,4},{7,5},{8,10},{9,11},{10,... | collective-permute-start | bytes 245768 | tf_op jit(solution)/shard_map/ppermute | solution.py:116
  52.7 6.2 %collective-permute-start.14 = (f32[160,128]{1,0:T(8,128)S(1)}, f32[160,128]{1,0:T(8,128)S(1)}, u32[]{:S(2)}, u32[]{:S(2)}) collective-permute-start(f32[160,128]{1,0:T(8,128)S(1)} %get-tuple-element.85), channel_id=1, source_target_pairs={{0,3},{1,2},{2,1},{3,0},{4,7},{5,6},{6,5},{7,4},{8,11},{9,10},{10,... | collective-permute-start | bytes 245768 | tf_op jit(solution)/shard_map/ppermute | solution.py:116
  54.5 5.4 %collective-permute-start.13 = (f32[160,128]{1,0:T(8,128)S(1)}, f32[160,128]{1,0:T(8,128)S(1)}, u32[]{:S(2)}, u32[]{:S(2)}) collective-permute-start(f32[160,128]{1,0:T(8,128)S(1)} %get-tuple-element.83.sent), channel_id=1, source_target_pairs={{0,1},{1,0},{2,3},{3,2},{4,5},{5,4},{6,7},{7,6},{8,9},{9,8},{10,11... | collective-permute-start | bytes 245768 | tf_op jit(solution)/shard_map/ppermute | solution.py:116
  60.0 6.5 %collective-permute-start.16 = (f32[160,128]{1,0:T(8,128)S(1)}, f32[160,128]{1,0:T(8,128)S(1)}, u32[]{:S(2)}, u32[]{:S(2)}) collective-permute-start(f32[160,128]{1,0:T(8,128)S(1)} %collect.3.one), channel_id=1, source_target_pairs={{0,4},{1,5},{2,6},{3,7},{4,0},{5,1},{6,2},{7,3},{8,12},{9,13},{10,... | collective-permute-start | bytes 245768 | tf_op jit(solution)/shard_map/ppermute | solution.py:116
  66.5 5.5 %collective-permute-start.17 = (f32[128,128]{1,0:T(8,128)S(1)}, f32[128,128]{1,0:T(8,128)S(1)}, u32[]{:S(2)}, u32[]{:S(2)}) collective-permute-start(f32[128,128]{1,0:T(8,128)S(1)} %top.3.value), channel_id=1, source_target_pairs={{0,2},{1,3},{2,0},{3,1},{4,6},{5,7},{6,4},{7,5},{8,10},{9,11},{10,... | collective-permute-start | bytes 196616 | tf_op jit(solution)/shard_map/ppermute | solution.py:116
  67.1 5.2 %collective-permute-start.19 = (f32[128,128]{1,0:T(8,128)S(1)}, f32[128,128]{1,0:T(8,128)S(1)}, u32[]{:S(2)}, u32[]{:S(2)}) collective-permute-start(f32[128,128]{1,0:T(8,128)S(1)} %top.3.value), channel_id=1, source_target_pairs={{0,3},{1,2},{2,1},{3,0},{4,7},{5,6},{6,5},{7,4},{8,11},{9,10},{10,... | collective-permute-start | bytes 196616 | tf_op jit(solution)/shard_map/ppermute | solution.py:116
  69.1 4.3 %collective-permute-start.18 = (f32[128,128]{1,0:T(8,128)S(1)}, f32[128,128]{1,0:T(8,128)S(1)}, u32[]{:S(2)}, u32[]{:S(2)}) collective-permute-start(f32[128,128]{1,0:T(8,128)S(1)} %top.3.value), channel_id=1, source_target_pairs={{0,1},{1,0},{2,3},{3,2},{4,5},{5,4},{6,7},{7,6},{8,9},{9,8},{10,11... | collective-permute-start | bytes 196616 | tf_op jit(solution)/shard_map/ppermute | solution.py:116
  74.4 1.3 %collective-permute-start.20 = (f32[32,128]{1,0:T(8,128)S(1)}, f32[32,128]{1,0:T(8,128)S(1)}, u32[]{:S(2)}, u32[]{:S(2)}) collective-permute-start(f32[32,128]{1,0:T(8,128)S(1)} %get-tuple-element.87.refs_0_), channel_id=1, source_target_pairs={{0,8},{8,0},{16,24},{24,16},{1,9},{9,1},{17,25},{25,17},{2,10},{10... | collective-permute-start | bytes 49160 | tf_op jit(solution)/shard_map/ppermute | solution.py:116
  75.8 3.8 %collective-permute-start.21 = (f32[32,128]{1,0:T(8,128)S(1)}, f32[32,128]{1,0:T(8,128)S(1)}, u32[]{:S(2)}, u32[]{:S(2)}) collective-permute-start(f32[32,128]{1,0:T(8,128)S(1)} %add.9.refs_0_), channel_id=1, source_target_pairs={{0,16},{8,24},{16,0},{24,8},{1,17},{9,25},{17,1},{25,9},{2,18},{10... | collective-permute-start | bytes 49160 | tf_op jit(solution)/shard_map/ppermute | solution.py:116

commit v13 on v12

--- a/solution.py
+++ b/solution.py
@@ -320,7 +320,7 @@
             for level in range(levels - 2, 1, -1):
                 value = unfold(level, value, swap(value, "pix", 1 << level))
             beside, straight, across = [swap(value, "pix", bit) for bit in (2, 1, 3)]
-            return inverse, unfold(1, value, beside), unfold(1, straight, across)
+            return inverse, unfold(1, value, beside), (straight, across)
 
         def tops_of(inverse, panel):
             left = dot(inverse[...], join(panel), ((1,), (0,)), HIGH)
@@ -463,15 +463,17 @@
         base = [None, None]
         for step in range(ITERS):
             panel = sum_gal(part)
-            inverse, own_wide, other_wide = sum_pix(panel, own, other)
+            inverse, own_wide, quarters = sum_pix(panel, own, other)
             if step < ITERS - 1:
                 given = own_wide, seen, pulls
                 base[0], own, part, tops = middle(0, (0, 1), inverse, panel, *given, None)
-                given = inverse, tops, other_wide, seen, pulls, part
+                quarters, tops = lax.optimization_barrier((quarters, tops))
+                given = inverse, tops, unfold(1, *quarters), seen, pulls, part
                 base[1], other, away = middle(1, (0,), *given)
                 base[1], other, mine = middle(1, (1,), *given, (base[1], *other))
                 part = away + mine
             else:
+                other_wide = unfold(1, *quarters)
                 *wide, gram = widen(inverse, own_wide, other_wide)
                 *made, left, tops = final(0, inverse, panel, own_wide, base[0])
                 bit = 1

time: 83 us -> 81.6 us (0.983)
  waiting for transfers between devices: 31.8 us -> 30.5 us
    ppermute x20, waiting for transfers between devices: 23.9 us -> 22.6 us  [swap(): return lax.ppermute(value, axis, [(i, i ^ bit) for i in range(n)])]
  transfers between devices with their start and end apart: 22 -> 22, of which waited for: 19 -> 17; matrix products, arithmetic and copies ran while one was open for 0% -> 0% of each run, Pallas kernels for 11% -> 13%
where the time goes in v13:
time: 81.6 us; the launch traced here: 81.4 us
  waiting for transfers between devices  30.5 us (37%)
  starting transfers between devices  26.2 us (32%)
  Pallas kernels  23.8 us (29%)
  between operations  0.97 us (1%)
    pallas_call x29, Pallas kernels, call(): pl.pallas_call(body, name=name, in_specs=[pl.BlockSpec(memory_space=space...  23.8 us
    ppermute x20, waiting for transfers between devices, swap(): return lax.ppermute(value, axis, [(i, i ^ bit) for i in range(n)])  22.6 us
    ppermute x20, starting transfers between devices, swap(): return lax.ppermute(value, axis, [(i, i ^ bit) for i in range(n)])  21.7 us
    ppermute x2, waiting for transfers between devices, sum_gal(): lax.ppermute(mine, 'gal', [(i, (i + CORES * k) % n_gal) for i in range(n_...  7.86 us
    ppermute x2, starting transfers between devices, sum_gal(): lax.ppermute(mine, 'gal', [(i, (i + CORES * k) % n_gal) for i in range(n_...  4.53 us
  transfers between devices with their start and end apart: 22, of which 17 were waited for; matrix products, arithmetic and copies ran while one was open for 0% of the time, Pallas kernels for 13%

profile of v13, /device:TPU:0, one launch (start us, length us, event | category | flops | bytes accessed | tf_op | source)
XLA Modules:
  0.0 81.4 jit_solution(2349443229383298448)
XLA Ops:
  0.6 6.4 %first.1 = (f32[1024,1024]{1,0:T(8,128)S(1)}, f32[1024,1024]{1,0:T(8,128)S(1)}, bf16[1024,512]{1,0:T(8,128)(2,1)S(1)}, bf16[1024,512]{1,0:T(8,128)(2,1)S(1)}, bf...) custom-call(f32[1024,1024]{1,0:T(8,128)} %o_in.1, ...), custom_call_target="tpu_custom_call" | custom-call | flops 402653184 | bytes 16777216 | tf_op jit(solution)/shard_map/first/pallas_call | solution.py:42
  7.1 0.5 collective-permute-start
  7.6 1.0 %collective-permute-done.refs_1_ = f32[64,512]{1,0:T(8,128)S(1)} collective-permute-done((f32[64,512]{1,0:T(8,128)S(1)}, f32[64,512]{1,0:T(8,128)S(1)}, u32[]{:S(2)}, u32[]{:S(2)}) %collective-permute-start) | collective-permute-done | bytes 131104 | tf_op jit(solution)/shard_map/ppermute | solution.py:116
  8.6 2.9 %collective-permute-start.1 = (f32[64,512]{1,0:T(8,128)S(1)}, f32[64,512]{1,0:T(8,128)S(1)}, u32[]{:S(2)}, u32[]{:S(2)}) collective-permute-start(f32[64,512]{1,0:T(8,128)S(1)} %add.5.refs_0_), channel_id=1, source_target_pairs={{0,16},{8,24},{16,0},{24,8},{1,17},{9,25},{17,1},{25,9},{2,18},{10... | collective-permute-start | bytes 393224 | tf_op jit(solution)/shard_map/ppermute | solution.py:201
  11.5 3.8 %collective-permute-done.1.refs_1_ = f32[64,512]{1,0:T(8,128)S(1)} collective-permute-done((f32[64,512]{1,0:T(8,128)S(1)}, f32[64,512]{1,0:T(8,128)S(1)}, u32[]{:S(2)}, u32[]{:S(2)}) %collective-permute-start.1) | collective-permute-done | bytes 131104 | tf_op jit(solution)/shard_map/ppermute | solution.py:201
  15.5 0.6 multiply_mine.2
  16.1 0.7 collective-permute-done.2.away.rest_0_
  16.8 0.5 multiply_other.2
  17.2 0.3 multiply_own.2
  17.6 1.9 %collective-permute-start.5 = (f32[160,128]{1,0:T(8,128)S(1)}, f32[160,128]{1,0:T(8,128)S(1)}, u32[]{:S(2)}, u32[]{:S(2)}) collective-permute-start(f32[160,128]{1,0:T(8,128)S(1)} %get-tuple-element.68), channel_id=1, source_target_pairs={{0,2},{1,3},{2,0},{3,1},{4,6},{5,7},{6,4},{7,5},{8,10},{9,11},{10,... | collective-permute-start | bytes 245768 | tf_op jit(solution)/shard_map/ppermute | solution.py:116
  19.4 1.4 %collective-permute-start.4 = (f32[160,128]{1,0:T(8,128)S(1)}, f32[160,128]{1,0:T(8,128)S(1)}, u32[]{:S(2)}, u32[]{:S(2)}) collective-permute-start(f32[160,128]{1,0:T(8,128)S(1)} %get-tuple-element.67), channel_id=1, source_target_pairs={{0,3},{1,2},{2,1},{3,0},{4,7},{5,6},{6,5},{7,4},{8,11},{9,10},{10,... | collective-permute-start | bytes 245768 | tf_op jit(solution)/shard_map/ppermute | solution.py:116
  20.8 0.3 collective-permute-start.3
  21.1 1.1 %collective-permute-done.5.refs_2_ = f32[160,128]{1,0:T(8,128)S(1)} collective-permute-done((f32[160,128]{1,0:T(8,128)S(1)}, f32[160,128]{1,0:T(8,128)S(1)}, u32[]{:S(2)}, u32[]{:S(2)}) %collective-permute-start.5) | collective-permute-done | bytes 81952 | tf_op jit(solution)/shard_map/ppermute | solution.py:116
  22.2 2.9 %collective-permute-done.4.refs_1_ = f32[160,128]{1,0:T(8,128)S(1)} collective-permute-done((f32[160,128]{1,0:T(8,128)S(1)}, f32[160,128]{1,0:T(8,128)S(1)}, u32[]{:S(2)}, u32[]{:S(2)}) %collective-permute-start.4) | collective-permute-done | bytes 81952 | tf_op jit(solution)/shard_map/ppermute | solution.py:116
  25.1 1.2 %collective-permute-done.3.refs_0_ = f32[160,128]{1,0:T(8,128)S(1)} collective-permute-done((f32[160,128]{1,0:T(8,128)S(1)}, f32[160,128]{1,0:T(8,128)S(1)}, u32[]{:S(2)}, u32[]{:S(2)}) %collective-permute-start.3) | collective-permute-done | bytes 81952 | tf_op jit(solution)/shard_map/ppermute | solution.py:116
  26.4 2.6 %collective-permute-start.6 = (f32[160,128]{1,0:T(8,128)S(1)}, f32[160,128]{1,0:T(8,128)S(1)}, u32[]{:S(2)}, u32[]{:S(2)}) collective-permute-start(f32[160,128]{1,0:T(8,128)S(1)} %collect.2.one), channel_id=1, source_target_pairs={{0,4},{1,5},{2,6},{3,7},{4,0},{5,1},{6,2},{7,3},{8,12},{9,13},{10,... | collective-permute-start | bytes 245768 | tf_op jit(solution)/shard_map/ppermute | solution.py:116
  29.0 4.0 %collective-permute-done.6.two = f32[160,128]{1,0:T(8,128)S(1)} collective-permute-done((f32[160,128]{1,0:T(8,128)S(1)}, f32[160,128]{1,0:T(8,128)S(1)}, u32[]{:S(2)}, u32[]{:S(2)}) %collective-permute-start.6) | collective-permute-done | bytes 81952 | tf_op jit(solution)/shard_map/ppermute | solution.py:116
  33.0 0.6 collective-permute-start.9
  33.6 1.6 %collective-permute-start.8 = (f32[128,128]{1,0:T(8,128)S(1)}, f32[128,128]{1,0:T(8,128)S(1)}, u32[]{:S(2)}, u32[]{:S(2)}) collective-permute-start(f32[128,128]{1,0:T(8,128)S(1)} %top.2.value), channel_id=1, source_target_pairs={{0,3},{1,2},{2,1},{3,0},{4,7},{5,6},{6,5},{7,4},{8,11},{9,10},{10,... | collective-permute-start | bytes 196616 | tf_op jit(solution)/shard_map/ppermute | solution.py:116
  35.2 1.4 %collective-permute-start.7 = (f32[128,128]{1,0:T(8,128)S(1)}, f32[128,128]{1,0:T(8,128)S(1)}, u32[]{:S(2)}, u32[]{:S(2)}) collective-permute-start(f32[128,128]{1,0:T(8,128)S(1)} %top.2.value), channel_id=1, source_target_pairs={{0,1},{1,0},{2,3},{3,2},{4,5},{5,4},{6,7},{7,6},{8,9},{9,8},{10,11... | collective-permute-start | bytes 196616 | tf_op jit(solution)/shard_map/ppermute | solution.py:116
  36.6 1.9 %eliminate.2.inverse = f32[64,64]{1,0:T(8,128)S(1)} custom-call(f32[160,128]{1,0:T(8,128)S(1)} %collect.2.one, f32[160,128]{1,0:T(8,128)S(1)} %collective-permute-done.6.two), custom_call_target="tpu_custom_call" | custom-call | flops 100000000 | bytes 8388608 | tf_op jit(solution)/shard_map/eliminate/pallas_call | solution.py:42
  38.5 1.8 %middle.3 = (f32[1024,512]{1,0:T(8,128)S(1)}, bf16[1024,512]{1,0:T(8,128)(2,1)S(1)}, bf16[1024,512]{1,0:T(8,128)(2,1)S(1)}, f32[64,512]{1,0:T(8,128)S(1)}, f32[6...) custom-call(f32[64,64]{1,0:T(8,128)S(1)} %eliminate.2.inverse, f32[64,512]{1,0:T(8,128)S(1)} %collective-permute-done.2.away.rest_0_, ...), custom_call_target="tpu_custom_call" | custom-call | flops 603979776 | bytes 4194304 | tf_op jit(solution)/shard_map/middle/pallas_call | solution.py:42
  40.4 1.0 %middle.4 = (f32[1024,512]{1,0:T(8,128)S(1)}, bf16[1024,512]{1,0:T(8,128)(2,1)S(1)}, bf16[1024,512]{1,0:T(8,128)(2,1)S(1)}, f32[64,512]{1,0:T(8,128)S(1)}) custom-call(f32[64,64]{1,0:T(8,128)S(1)} %eliminate.2.inverse, bf16[192,1024]{1,0:T(8,128)(2,1)S(1)} %get-tuple-element.72.rest_0_, f32[256,128]{1,0:T(8,128)S(1)} %unfold.5.rest_1_, ...), custom_call_target="tpu_custom_call" | custom-call | flops 301989888 | bytes 2097152 | tf_op jit(solution)/shard_map/middle/pallas_call | solution.py:42
  41.5 1.0 %middle.5 = (f32[1024,512]{1,0:T(8,128)S(1)}, bf16[1024,512]{1,0:T(8,128)(2,1)S(1)}, bf16[1024,512]{1,0:T(8,128)(2,1)S(1)}, f32[64,512]{1,0:T(8,128)S(1)}) custom-call(f32[64,64]{1,0:T(8,128)S(1)} %eliminate.2.inverse, bf16[192,1024]{1,0:T(8,128)(2,1)S(1)} %get-tuple-element.72.rest_0_, ...), custom_call_target="tpu_custom_call", output_to_operand_aliasing={{0}: (6, {}), {1}: (7, {}), {2}: (8, {})} | custom-call | flops 301989888 | bytes 2097152 | tf_op jit(solution)/shard_map/middle/pallas_call | solution.py:42
  42.5 0.3 collective-permute-done.10.refs_1_
  42.8 1.6 %collective-permute-start.11 = (f32[64,512]{1,0:T(8,128)S(1)}, f32[64,512]{1,0:T(8,128)S(1)}, u32[]{:S(2)}, u32[]{:S(2)}) collective-permute-start(f32[64,512]{1,0:T(8,128)S(1)} %add.7.refs_0_), channel_id=1, source_target_pairs={{0,16},{8,24},{16,0},{24,8},{1,17},{9,25},{17,1},{25,9},{2,18},{10... | collective-permute-start | bytes 393224 | tf_op jit(solution)/shard_map/ppermute | solution.py:201
  44.4 4.0 %collective-permute-done.11.refs_1_ = f32[64,512]{1,0:T(8,128)S(1)} collective-permute-done((f32[64,512]{1,0:T(8,128)S(1)}, f32[64,512]{1,0:T(8,128)S(1)}, u32[]{:S(2)}, u32[]{:S(2)}) %collective-permute-start.11) | collective-permute-done | bytes 131104 | tf_op jit(solution)/shard_map/ppermute | solution.py:201
  48.6 0.6 multiply_mine.3
  49.2 0.7 collective-permute-done.12.away.rest_0_
  49.9 0.5 multiply_other.3
  50.7 0.6 collective-permute-start.15
  51.3 1.6 %collective-permute-start.14 = (f32[160,128]{1,0:T(8,128)S(1)}, f32[160,128]{1,0:T(8,128)S(1)}, u32[]{:S(2)}, u32[]{:S(2)}) collective-permute-start(f32[160,128]{1,0:T(8,128)S(1)} %get-tuple-element.91), channel_id=1, source_target_pairs={{0,3},{1,2},{2,1},{3,0},{4,7},{5,6},{6,5},{7,4},{8,11},{9,10},{10,... | collective-permute-start | bytes 245768 | tf_op jit(solution)/shard_map/ppermute | solution.py:116
  52.9 1.3 %collective-permute-start.13 = (f32[160,128]{1,0:T(8,128)S(1)}, f32[160,128]{1,0:T(8,128)S(1)}, u32[]{:S(2)}, u32[]{:S(2)}) collective-permute-start(f32[160,128]{1,0:T(8,128)S(1)} %get-tuple-element.89.sent), channel_id=1, source_target_pairs={{0,1},{1,0},{2,3},{3,2},{4,5},{5,4},{6,7},{7,6},{8,9},{9,8},{10,11... | collective-permute-start | bytes 245768 | tf_op jit(solution)/shard_map/ppermute | solution.py:116
  54.3 1.8 %collective-permute-done.15.refs_2_ = f32[160,128]{1,0:T(8,128)S(1)} collective-permute-done((f32[160,128]{1,0:T(8,128)S(1)}, f32[160,128]{1,0:T(8,128)S(1)}, u32[]{:S(2)}, u32[]{:S(2)}) %collective-permute-start.15) | collective-permute-done | bytes 81952 | tf_op jit(solution)/shard_map/ppermute | solution.py:116
  56.0 1.2 %collective-permute-done.14.refs_1_ = f32[160,128]{1,0:T(8,128)S(1)} collective-permute-done((f32[160,128]{1,0:T(8,128)S(1)}, f32[160,128]{1,0:T(8,128)S(1)}, u32[]{:S(2)}, u32[]{:S(2)}) %collective-permute-start.14) | collective-permute-done | bytes 81952 | tf_op jit(solution)/shard_map/ppermute | solution.py:116
  57.2 1.1 %collective-permute-done.13.refs_0_ = f32[160,128]{1,0:T(8,128)S(1)} collective-permute-done((f32[160,128]{1,0:T(8,128)S(1)}, f32[160,128]{1,0:T(8,128)S(1)}, u32[]{:S(2)}, u32[]{:S(2)}) %collective-permute-start.13) | collective-permute-done | bytes 81952 | tf_op jit(solution)/shard_map/ppermute | solution.py:116
  58.4 2.5 %collective-permute-start.16 = (f32[160,128]{1,0:T(8,128)S(1)}, f32[160,128]{1,0:T(8,128)S(1)}, u32[]{:S(2)}, u32[]{:S(2)}) collective-permute-start(f32[160,128]{1,0:T(8,128)S(1)} %collect.3.one), channel_id=1, source_target_pairs={{0,4},{1,5},{2,6},{3,7},{4,0},{5,1},{6,2},{7,3},{8,12},{9,13},{10,... | collective-permute-start | bytes 245768 | tf_op jit(solution)/shard_map/ppermute | solution.py:116
  60.9 4.1 %collective-permute-done.16.two = f32[160,128]{1,0:T(8,128)S(1)} collective-permute-done((f32[160,128]{1,0:T(8,128)S(1)}, f32[160,128]{1,0:T(8,128)S(1)}, u32[]{:S(2)}, u32[]{:S(2)}) %collective-permute-start.16) | collective-permute-done | bytes 81952 | tf_op jit(solution)/shard_map/ppermute | solution.py:116
  65.1 2.6 %collective-permute-start.19 = (f32[128,128]{1,0:T(8,128)S(1)}, f32[128,128]{1,0:T(8,128)S(1)}, u32[]{:S(2)}, u32[]{:S(2)}) collective-permute-start(f32[128,128]{1,0:T(8,128)S(1)} %top.3.value), channel_id=1, source_target_pairs={{0,3},{1,2},{2,1},{3,0},{4,7},{5,6},{6,5},{7,4},{8,11},{9,10},{10,... | collective-permute-start | bytes 196616 | tf_op jit(solution)/shard_map/ppermute | solution.py:116
  67.7 0.8 collective-permute-start.18
  68.5 1.9 %eliminate.3.inverse = f32[64,64]{1,0:T(8,128)S(1)} custom-call(f32[160,128]{1,0:T(8,128)S(1)} %collect.3.one, f32[160,128]{1,0:T(8,128)S(1)} %collective-permute-done.16.two), custom_call_target="tpu_custom_call" | custom-call | flops 100000000 | bytes 8388608 | tf_op jit(solution)/shard_map/eliminate/pallas_call | solution.py:42
  70.7 1.3 %collective-permute-done.18.value = f32[128,128]{1,0:T(8,128)S(1)} collective-permute-done((f32[128,128]{1,0:T(8,128)S(1)}, f32[128,128]{1,0:T(8,128)S(1)}, u32[]{:S(2)}, u32[]{:S(2)}) %collective-permute-start.18) | collective-permute-done | bytes 65568 | tf_op jit(solution)/shard_map/ppermute | solution.py:116
  72.0 1.0 %widen.1 = (f32[64,512]{1,0:T(8,128)S(1)}, f32[64,512]{1,0:T(8,128)S(1)}, f32[32,128]{1,0:T(8,128)S(1)}) custom-call(f32[64,64]{1,0:T(8,128)S(1)} %eliminate.3.inverse, f32[256,128]{1,0:T(8,128)S(1)} %unfold.6.own.rest_2_, f32[256,128]{1,0:T(8,128)S(1)} %unfold.7.other.rest_1_), custom_call_target="tpu_custom_call" | custom-call | flops 100000000 | bytes 1048576 | tf_op jit(solution)/shard_map/widen/pallas_call | solution.py:42
  73.1 1.3 %final.2 = (f32[1024,512]{1,0:T(8,128)S(1)}, f32[1024,512]{1,0:T(8,128)S(1)}, f32[64,1024]{1,0:T(8,128)}, bf16[192,1024]{1,0:T(8,128)(2,1)S(1)}) custom-call(f32[64,64]{1,0:T(8,128)S(1)} %eliminate.3.inverse, f32[64,512]{1,0:T(8,128)S(1)} %collective-permute-done.12.away.rest_0_, f32[64,512]{1,0:T(8,128)S(1)} %add.8.mine.rest_1_, ...), custom_call_target="tpu_custom_call" | custom-call | flops 201326592 | bytes 4194304 | tf_op jit(solution)/shard_map/final/pallas_call | solution.py:42
  74.4 1.6 %collective-permute-start.21 = (f32[32,128]{1,0:T(8,128)S(1)}, f32[32,128]{1,0:T(8,128)S(1)}, u32[]{:S(2)}, u32[]{:S(2)}) collective-permute-start(f32[32,128]{1,0:T(8,128)S(1)} %add.9.refs_0_), channel_id=1, source_target_pairs={{0,16},{8,24},{16,0},{24,8},{1,17},{9,25},{17,1},{25,9},{2,18},{10... | collective-permute-start | bytes 49160 | tf_op jit(solution)/shard_map/ppermute | solution.py:116
  76.0 1.3 %final.3 = (f32[1024,512]{1,0:T(8,128)S(1)}, f32[1024,512]{1,0:T(8,128)S(1)}, f32[1024,1024]{1,0:T(8,128)}) custom-call(f32[64,64]{1,0:T(8,128)S(1)} %eliminate.3.inverse, bf16[192,1024]{1,0:T(8,128)(2,1)S(1)} %get-tuple-element.97.rest_0_, f32[256,128]{1,0:T(8,128)S(1)} %unfold.7.other.rest_1_, f32[1024,512]{1,0:T(8,128)S(1)} %get-tuple-element.98.rest_2_, ...), custom_call_target="tpu_custom_call" | custom-call | flops 201326592 | bytes 4194304 | tf_op jit(solution)/shard_map/final/pallas_call | solution.py:42
  77.3 0.9 %collective-permute-done.21.refs_1_ = f32[32,128]{1,0:T(8,128)S(1)} collective-permute-done((f32[32,128]{1,0:T(8,128)S(1)}, f32[32,128]{1,0:T(8,128)S(1)}, u32[]{:S(2)}, u32[]{:S(2)}) %collective-permute-start.21) | collective-permute-done | bytes 16416 | tf_op jit(solution)/shard_map/ppermute | solution.py:116
  78.2 3.1 %finish.1 = (f32[64,1024]{1,0:T(8,128)}, f32[1024,1024]{1,0:T(8,128)}, f32[1024,1024]{1,0:T(8,128)}) custom-call(f32[32,128]{1,0:T(8,128)S(1)} %add.9.refs_0_, f32[32,128]{1,0:T(8,128)S(1)} %collective-permute-done.21.refs_1_, f32[64,512]{1,0:T(8,128)S(1)} %get-tuple-element.94.refs_2_, ...), custom_call_target="tpu_custom_call", output_to_operand_aliasing={{1}: (7, {})} | custom-call | flops 100000000 | bytes 8388608 | tf_op jit(solution)/shard_map/finish/pallas_call | solution.py:42
  (25 shorter events, 1.2 us)
Async XLA Ops:
  7.1 1.5 %collective-permute-start = (f32[64,512]{1,0:T(8,128)S(1)}, f32[64,512]{1,0:T(8,128)S(1)}, u32[]{:S(2)}, u32[]{:S(2)}) collective-permute-start(f32[64,512]{1,0:T(8,128)S(1)} %get-tuple-element.57), channel_id=1, source_target_pairs={{0,8},{8,0},{16,24},{24,16},{1,9},{9,1},{17,25},{25,17},{2,10},{10... | collective-permute-start | bytes 393224 | tf_op jit(solution)/shard_map/ppermute | solution.py:116
  8.6 6.8 %collective-permute-start.1 = (f32[64,512]{1,0:T(8,128)S(1)}, f32[64,512]{1,0:T(8,128)S(1)}, u32[]{:S(2)}, u32[]{:S(2)}) collective-permute-start(f32[64,512]{1,0:T(8,128)S(1)} %add.5.refs_0_), channel_id=1, source_target_pairs={{0,16},{8,24},{16,0},{24,8},{1,17},{9,25},{17,1},{25,9},{2,18},{10... | collective-permute-start | bytes 393224 | tf_op jit(solution)/shard_map/ppermute | solution.py:201
  15.4 1.4 %collective-permute-start.2 = (f32[64,512]{1,0:T(8,128)S(1)}, f32[64,512]{1,0:T(8,128)S(1)}, u32[]{:S(2)}, u32[]{:S(2)}) collective-permute-start(f32[64,512]{1,0:T(8,128)S(1)} %add.6.mine.rest_1_), channel_id=1, source_target_pairs={{0,8},{8,0},{16,24},{24,16},{1,9},{9,1},{17,25},{25,17},{2,10},{10... | collective-permute-start | bytes 393224 | tf_op jit(solution)/shard_map/ppermute | solution.py:116
  17.6 4.6 %collective-permute-start.5 = (f32[160,128]{1,0:T(8,128)S(1)}, f32[160,128]{1,0:T(8,128)S(1)}, u32[]{:S(2)}, u32[]{:S(2)}) collective-permute-start(f32[160,128]{1,0:T(8,128)S(1)} %get-tuple-element.68), channel_id=1, source_target_pairs={{0,2},{1,3},{2,0},{3,1},{4,6},{5,7},{6,4},{7,5},{8,10},{9,11},{10,... | collective-permute-start | bytes 245768 | tf_op jit(solution)/shard_map/ppermute | solution.py:116
  19.4 5.7 %collective-permute-start.4 = (f32[160,128]{1,0:T(8,128)S(1)}, f32[160,128]{1,0:T(8,128)S(1)}, u32[]{:S(2)}, u32[]{:S(2)}) collective-permute-start(f32[160,128]{1,0:T(8,128)S(1)} %get-tuple-element.67), channel_id=1, source_target_pairs={{0,3},{1,2},{2,1},{3,0},{4,7},{5,6},{6,5},{7,4},{8,11},{9,10},{10,... | collective-permute-start | bytes 245768 | tf_op jit(solution)/shard_map/ppermute | solution.py:116
  20.8 5.6 %collective-permute-start.3 = (f32[160,128]{1,0:T(8,128)S(1)}, f32[160,128]{1,0:T(8,128)S(1)}, u32[]{:S(2)}, u32[]{:S(2)}) collective-permute-start(f32[160,128]{1,0:T(8,128)S(1)} %get-tuple-element.65.sent), channel_id=1, source_target_pairs={{0,1},{1,0},{2,3},{3,2},{4,5},{5,4},{6,7},{7,6},{8,9},{9,8},{10,11... | collective-permute-start | bytes 245768 | tf_op jit(solution)/shard_map/ppermute | solution.py:116
  26.4 6.6 %collective-permute-start.6 = (f32[160,128]{1,0:T(8,128)S(1)}, f32[160,128]{1,0:T(8,128)S(1)}, u32[]{:S(2)}, u32[]{:S(2)}) collective-permute-start(f32[160,128]{1,0:T(8,128)S(1)} %collect.2.one), channel_id=1, source_target_pairs={{0,4},{1,5},{2,6},{3,7},{4,0},{5,1},{6,2},{7,3},{8,12},{9,13},{10,... | collective-permute-start | bytes 245768 | tf_op jit(solution)/shard_map/ppermute | solution.py:116
  33.0 5.5 %collective-permute-start.9 = (f32[128,128]{1,0:T(8,128)S(1)}, f32[128,128]{1,0:T(8,128)S(1)}, u32[]{:S(2)}, u32[]{:S(2)}) collective-permute-start(f32[128,128]{1,0:T(8,128)S(1)} %top.2.value), channel_id=1, source_target_pairs={{0,2},{1,3},{2,0},{3,1},{4,6},{5,7},{6,4},{7,5},{8,10},{9,11},{10,... | collective-permute-start | bytes 196616 | tf_op jit(solution)/shard_map/ppermute | solution.py:116
  33.6 6.7 %collective-permute-start.8 = (f32[128,128]{1,0:T(8,128)S(1)}, f32[128,128]{1,0:T(8,128)S(1)}, u32[]{:S(2)}, u32[]{:S(2)}) collective-permute-start(f32[128,128]{1,0:T(8,128)S(1)} %top.2.value), channel_id=1, source_target_pairs={{0,3},{1,2},{2,1},{3,0},{4,7},{5,6},{6,5},{7,4},{8,11},{9,10},{10,... | collective-permute-start | bytes 196616 | tf_op jit(solution)/shard_map/ppermute | solution.py:116
  35.2 5.2 %collective-permute-start.7 = (f32[128,128]{1,0:T(8,128)S(1)}, f32[128,128]{1,0:T(8,128)S(1)}, u32[]{:S(2)}, u32[]{:S(2)}) collective-permute-start(f32[128,128]{1,0:T(8,128)S(1)} %top.2.value), channel_id=1, source_target_pairs={{0,1},{1,0},{2,3},{3,2},{4,5},{5,4},{6,7},{7,6},{8,9},{9,8},{10,11... | collective-permute-start | bytes 196616 | tf_op jit(solution)/shard_map/ppermute | solution.py:116
  41.4 1.4 %collective-permute-start.10 = (f32[64,512]{1,0:T(8,128)S(1)}, f32[64,512]{1,0:T(8,128)S(1)}, u32[]{:S(2)}, u32[]{:S(2)}) collective-permute-start(f32[64,512]{1,0:T(8,128)S(1)} %get-tuple-element.81), channel_id=1, source_target_pairs={{0,8},{8,0},{16,24},{24,16},{1,9},{9,1},{17,25},{25,17},{2,10},{10... | collective-permute-start | bytes 393224 | tf_op jit(solution)/shard_map/ppermute | solution.py:116
  42.8 5.6 %collective-permute-start.11 = (f32[64,512]{1,0:T(8,128)S(1)}, f32[64,512]{1,0:T(8,128)S(1)}, u32[]{:S(2)}, u32[]{:S(2)}) collective-permute-start(f32[64,512]{1,0:T(8,128)S(1)} %add.7.refs_0_), channel_id=1, source_target_pairs={{0,16},{8,24},{16,0},{24,8},{1,17},{9,25},{17,1},{25,9},{2,18},{10... | collective-permute-start | bytes 393224 | tf_op jit(solution)/shard_map/ppermute | solution.py:201
  48.5 1.4 %collective-permute-start.12 = (f32[64,512]{1,0:T(8,128)S(1)}, f32[64,512]{1,0:T(8,128)S(1)}, u32[]{:S(2)}, u32[]{:S(2)}) collective-permute-start(f32[64,512]{1,0:T(8,128)S(1)} %add.8.mine.rest_1_), channel_id=1, source_target_pairs={{0,8},{8,0},{16,24},{24,16},{1,9},{9,1},{17,25},{25,17},{2,10},{10... | collective-permute-start | bytes 393224 | tf_op jit(solution)/shard_map/ppermute | solution.py:116
  50.7 5.4 %collective-permute-start.15 = (f32[160,128]{1,0:T(8,128)S(1)}, f32[160,128]{1,0:T(8,128)S(1)}, u32[]{:S(2)}, u32[]{:S(2)}) collective-permute-start(f32[160,128]{1,0:T(8,128)S(1)} %get-tuple-element.92), channel_id=1, source_target_pairs={{0,2},{1,3},{2,0},{3,1},{4,6},{5,7},{6,4},{7,5},{8,10},{9,11},{10,... | collective-permute-start | bytes 245768 | tf_op jit(solution)/shard_map/ppermute | solution.py:116
  51.3 5.9 %collective-permute-start.14 = (f32[160,128]{1,0:T(8,128)S(1)}, f32[160,128]{1,0:T(8,128)S(1)}, u32[]{:S(2)}, u32[]{:S(2)}) collective-permute-start(f32[160,128]{1,0:T(8,128)S(1)} %get-tuple-element.91), channel_id=1, source_target_pairs={{0,3},{1,2},{2,1},{3,0},{4,7},{5,6},{6,5},{7,4},{8,11},{9,10},{10,... | collective-permute-start | bytes 245768 | tf_op jit(solution)/shard_map/ppermute | solution.py:116
  52.9 5.5 %collective-permute-start.13 = (f32[160,128]{1,0:T(8,128)S(1)}, f32[160,128]{1,0:T(8,128)S(1)}, u32[]{:S(2)}, u32[]{:S(2)}) collective-permute-start(f32[160,128]{1,0:T(8,128)S(1)} %get-tuple-element.89.sent), channel_id=1, source_target_pairs={{0,1},{1,0},{2,3},{3,2},{4,5},{5,4},{6,7},{7,6},{8,9},{9,8},{10,11... | collective-permute-start | bytes 245768 | tf_op jit(solution)/shard_map/ppermute | solution.py:116
  58.4 6.5 %collective-permute-start.16 = (f32[160,128]{1,0:T(8,128)S(1)}, f32[160,128]{1,0:T(8,128)S(1)}, u32[]{:S(2)}, u32[]{:S(2)}) collective-permute-start(f32[160,128]{1,0:T(8,128)S(1)} %collect.3.one), channel_id=1, source_target_pairs={{0,4},{1,5},{2,6},{3,7},{4,0},{5,1},{6,2},{7,3},{8,12},{9,13},{10,... | collective-permute-start | bytes 245768 | tf_op jit(solution)/shard_map/ppermute | solution.py:116
  65.0 5.5 %collective-permute-start.17 = (f32[128,128]{1,0:T(8,128)S(1)}, f32[128,128]{1,0:T(8,128)S(1)}, u32[]{:S(2)}, u32[]{:S(2)}) collective-permute-start(f32[128,128]{1,0:T(8,128)S(1)} %top.3.value), channel_id=1, source_target_pairs={{0,2},{1,3},{2,0},{3,1},{4,6},{5,7},{6,4},{7,5},{8,10},{9,11},{10,... | collective-permute-start | bytes 196616 | tf_op jit(solution)/shard_map/ppermute | solution.py:116
  65.1 5.6 %collective-permute-start.19 = (f32[128,128]{1,0:T(8,128)S(1)}, f32[128,128]{1,0:T(8,128)S(1)}, u32[]{:S(2)}, u32[]{:S(2)}) collective-permute-start(f32[128,128]{1,0:T(8,128)S(1)} %top.3.value), channel_id=1, source_target_pairs={{0,3},{1,2},{2,1},{3,0},{4,7},{5,6},{6,5},{7,4},{8,11},{9,10},{10,... | collective-permute-start | bytes 196616 | tf_op jit(solution)/shard_map/ppermute | solution.py:116
  67.7 4.3 %collective-permute-start.18 = (f32[128,128]{1,0:T(8,128)S(1)}, f32[128,128]{1,0:T(8,128)S(1)}, u32[]{:S(2)}, u32[]{:S(2)}) collective-permute-start(f32[128,128]{1,0:T(8,128)S(1)} %top.3.value), channel_id=1, source_target_pairs={{0,1},{1,0},{2,3},{3,2},{4,5},{5,4},{6,7},{7,6},{8,9},{9,8},{10,11... | collective-permute-start | bytes 196616 | tf_op jit(solution)/shard_map/ppermute | solution.py:116
  73.0 1.3 %collective-permute-start.20 = (f32[32,128]{1,0:T(8,128)S(1)}, f32[32,128]{1,0:T(8,128)S(1)}, u32[]{:S(2)}, u32[]{:S(2)}) collective-permute-start(f32[32,128]{1,0:T(8,128)S(1)} %get-tuple-element.93.refs_0_), channel_id=1, source_target_pairs={{0,8},{8,0},{16,24},{24,16},{1,9},{9,1},{17,25},{25,17},{2,10},{10... | collective-permute-start | bytes 49160 | tf_op jit(solution)/shard_map/ppermute | solution.py:116
  74.4 3.8 %collective-permute-start.21 = (f32[32,128]{1,0:T(8,128)S(1)}, f32[32,128]{1,0:T(8,128)S(1)}, u32[]{:S(2)}, u32[]{:S(2)}) collective-permute-start(f32[32,128]{1,0:T(8,128)S(1)} %add.9.refs_0_), channel_id=1, source_target_pairs={{0,16},{8,24},{16,0},{24,8},{1,17},{9,25},{17,1},{25,9},{2,18},{10... | collective-permute-start | bytes 49160 | tf_op jit(solution)/shard_map/ppermute | solution.py:116

commit v14 on v13

--- a/solution.py
+++ b/solution.py
@@ -423,18 +423,17 @@
             cost = (3 * rank * n_rows * n_cols, 4 * n_rows * n_cols)
             return call(body, "final", ins, outs, scratch, cost=cost)
 
-        def widen(inverse, own, other):
-            def body(inverse, own, other, wide_own, wide_other, out):
-                grams = []
-                for stacked, wide in ((own, wide_own), (other, wide_other)):
-                    value = dot(inverse[...], unstack(stacked), ((1,), (0,)), HIGH)
-                    wide[...] = value
-                    grams.append(dot(value, value, ((1,), (1,)), HIGH))
-                out[...] = pack(grams[0] + grams[1])
-
-            ins = [(a, pltpu.VMEM) for a in (inverse, own, other)]
-            outs = [((rank, half), F32, pltpu.VMEM)] * 2 + [((gram_rows, LANES), F32, pltpu.VMEM)]
-            return call(body, "widen", ins, outs, cost=(10**8, MIB), limit=8)
+        def widen(inverse, stacked, gram=None):
+            def body(inverse, stacked, *rest):
+                *before, wide, out = rest
+                value = dot(inverse[...], unstack(stacked), ((1,), (0,)), HIGH)
+                wide[...] = value
+                term = pack(dot(value, value, ((1,), (1,)), HIGH))
+                out[...] = before[0][...] + term if before else term
+
+            arrays = (inverse, stacked) if gram is None else (inverse, stacked, gram)
+            outs = [((rank, half), F32, pltpu.VMEM), ((gram_rows, LANES), F32, pltpu.VMEM)]
+            return call(body, "widen", [(a, pltpu.VMEM) for a in arrays], outs, cost=(10**8, MIB), limit=8)
 
         def finish(one, two, wide, made, first_dual, sparse):
             def body(*refs):
@@ -473,8 +472,11 @@
                 base[1], other, mine = middle(1, (1,), *given, (base[1], *other))
                 part = away + mine
             else:
+                wide_own, gram = widen(inverse, own_wide)
+                quarters, gram = lax.optimization_barrier((quarters, gram))
                 other_wide = unfold(1, *quarters)
-                *wide, gram = widen(inverse, own_wide, other_wide)
+                wide_other, gram = widen(inverse, other_wide, gram)
+                wide = wide_own, wide_other
                 *made, left, tops = final(0, inverse, panel, own_wide, base[0])
                 bit = 1
                 while 2 * bit < n_gal:

time: 81.6 us -> 81.2 us (level)
    pallas_call x29 -> x30, Pallas kernels: 23.8 us -> 24 us  [call(): pl.pallas_call(body, name=name, in_specs=[pl.BlockSpec(memory_space=space...]
  transfers between devices with their start and end apart: 22 -> 22, of which waited for: 17 -> 16; matrix products, arithmetic and copies ran while one was open for 0% -> 0% of each run, Pallas kernels for 13% -> 14%
where the time goes in v14:
time: 81.2 us; the launch traced here: 81 us
  waiting for transfers between devices  29.8 us (37%)
  starting transfers between devices  26.2 us (32%)
  Pallas kernels  24 us (30%)
  between operations  0.97 us (1%)
    pallas_call x30, Pallas kernels, call(): pl.pallas_call(body, name=name, in_specs=[pl.BlockSpec(memory_space=space...  24 us
    ppermute x20, waiting for transfers between devices, swap(): return lax.ppermute(value, axis, [(i, i ^ bit) for i in range(n)])  22 us
    ppermute x20, starting transfers between devices, swap(): return lax.ppermute(value, axis, [(i, i ^ bit) for i in range(n)])  21.7 us
    ppermute x2, waiting for transfers between devices, sum_gal(): lax.ppermute(mine, 'gal', [(i, (i + CORES * k) % n_gal) for i in range(n_...  7.86 us
    ppermute x2, starting transfers between devices, sum_gal(): lax.ppermute(mine, 'gal', [(i, (i + CORES * k) % n_gal) for i in range(n_...  4.53 us
  transfers between devices with their start and end apart: 22, of which 16 were waited for; matrix products, arithmetic and copies ran while one was open for 0% of the time, Pallas kernels for 14%

profile of v14, /device:TPU:0, one launch (start us, length us, event | category | flops | bytes accessed | tf_op | source)
XLA Modules:
  0.0 81.0 jit_solution(8506940251338121198)
XLA Ops:
  0.6 6.4 %first.1 = (f32[1024,1024]{1,0:T(8,128)S(1)}, f32[1024,1024]{1,0:T(8,128)S(1)}, bf16[1024,512]{1,0:T(8,128)(2,1)S(1)}, bf16[1024,512]{1,0:T(8,128)(2,1)S(1)}, bf...) custom-call(f32[1024,1024]{1,0:T(8,128)} %o_in.1, ...), custom_call_target="tpu_custom_call" | custom-call | flops 402653184 | bytes 16777216 | tf_op jit(solution)/shard_map/first/pallas_call | solution.py:42
  7.1 0.5 collective-permute-start
  7.6 1.0 %collective-permute-done.refs_1_ = f32[64,512]{1,0:T(8,128)S(1)} collective-permute-done((f32[64,512]{1,0:T(8,128)S(1)}, f32[64,512]{1,0:T(8,128)S(1)}, u32[]{:S(2)}, u32[]{:S(2)}) %collective-permute-start) | collective-permute-done | bytes 131104 | tf_op jit(solution)/shard_map/ppermute | solution.py:116
  8.6 2.9 %collective-permute-start.1 = (f32[64,512]{1,0:T(8,128)S(1)}, f32[64,512]{1,0:T(8,128)S(1)}, u32[]{:S(2)}, u32[]{:S(2)}) collective-permute-start(f32[64,512]{1,0:T(8,128)S(1)} %add.5.refs_0_), channel_id=1, source_target_pairs={{0,16},{8,24},{16,0},{24,8},{1,17},{9,25},{17,1},{25,9},{2,18},{10... | collective-permute-start | bytes 393224 | tf_op jit(solution)/shard_map/ppermute | solution.py:201
  11.5 3.8 %collective-permute-done.1.refs_1_ = f32[64,512]{1,0:T(8,128)S(1)} collective-permute-done((f32[64,512]{1,0:T(8,128)S(1)}, f32[64,512]{1,0:T(8,128)S(1)}, u32[]{:S(2)}, u32[]{:S(2)}) %collective-permute-start.1) | collective-permute-done | bytes 131104 | tf_op jit(solution)/shard_map/ppermute | solution.py:201
  15.5 0.6 multiply_mine.2
  16.1 0.7 collective-permute-done.2.away.rest_0_
  16.8 0.5 multiply_other.2
  17.6 1.9 %collective-permute-start.5 = (f32[160,128]{1,0:T(8,128)S(1)}, f32[160,128]{1,0:T(8,128)S(1)}, u32[]{:S(2)}, u32[]{:S(2)}) collective-permute-start(f32[160,128]{1,0:T(8,128)S(1)} %get-tuple-element.72), channel_id=1, source_target_pairs={{0,2},{1,3},{2,0},{3,1},{4,6},{5,7},{6,4},{7,5},{8,10},{9,11},{10,... | collective-permute-start | bytes 245768 | tf_op jit(solution)/shard_map/ppermute | solution.py:116
  19.4 1.4 %collective-permute-start.4 = (f32[160,128]{1,0:T(8,128)S(1)}, f32[160,128]{1,0:T(8,128)S(1)}, u32[]{:S(2)}, u32[]{:S(2)}) collective-permute-start(f32[160,128]{1,0:T(8,128)S(1)} %get-tuple-element.71), channel_id=1, source_target_pairs={{0,3},{1,2},{2,1},{3,0},{4,7},{5,6},{6,5},{7,4},{8,11},{9,10},{10,... | collective-permute-start | bytes 245768 | tf_op jit(solution)/shard_map/ppermute | solution.py:116
  20.8 0.3 collective-permute-start.3
  21.1 1.1 %collective-permute-done.5.refs_2_ = f32[160,128]{1,0:T(8,128)S(1)} collective-permute-done((f32[160,128]{1,0:T(8,128)S(1)}, f32[160,128]{1,0:T(8,128)S(1)}, u32[]{:S(2)}, u32[]{:S(2)}) %collective-permute-start.5) | collective-permute-done | bytes 81952 | tf_op jit(solution)/shard_map/ppermute | solution.py:116
  22.2 2.9 %collective-permute-done.4.refs_1_ = f32[160,128]{1,0:T(8,128)S(1)} collective-permute-done((f32[160,128]{1,0:T(8,128)S(1)}, f32[160,128]{1,0:T(8,128)S(1)}, u32[]{:S(2)}, u32[]{:S(2)}) %collective-permute-start.4) | collective-permute-done | bytes 81952 | tf_op jit(solution)/shard_map/ppermute | solution.py:116
  25.1 1.2 %collective-permute-done.3.refs_0_ = f32[160,128]{1,0:T(8,128)S(1)} collective-permute-done((f32[160,128]{1,0:T(8,128)S(1)}, f32[160,128]{1,0:T(8,128)S(1)}, u32[]{:S(2)}, u32[]{:S(2)}) %collective-permute-start.3) | collective-permute-done | bytes 81952 | tf_op jit(solution)/shard_map/ppermute | solution.py:116
  26.4 2.6 %collective-permute-start.6 = (f32[160,128]{1,0:T(8,128)S(1)}, f32[160,128]{1,0:T(8,128)S(1)}, u32[]{:S(2)}, u32[]{:S(2)}) collective-permute-start(f32[160,128]{1,0:T(8,128)S(1)} %collect.2.one), channel_id=1, source_target_pairs={{0,4},{1,5},{2,6},{3,7},{4,0},{5,1},{6,2},{7,3},{8,12},{9,13},{10,... | collective-permute-start | bytes 245768 | tf_op jit(solution)/shard_map/ppermute | solution.py:116
  29.0 4.0 %collective-permute-done.6.two = f32[160,128]{1,0:T(8,128)S(1)} collective-permute-done((f32[160,128]{1,0:T(8,128)S(1)}, f32[160,128]{1,0:T(8,128)S(1)}, u32[]{:S(2)}, u32[]{:S(2)}) %collective-permute-start.6) | collective-permute-done | bytes 81952 | tf_op jit(solution)/shard_map/ppermute | solution.py:116
  33.0 0.6 collective-permute-start.9
  33.6 1.6 %collective-permute-start.8 = (f32[128,128]{1,0:T(8,128)S(1)}, f32[128,128]{1,0:T(8,128)S(1)}, u32[]{:S(2)}, u32[]{:S(2)}) collective-permute-start(f32[128,128]{1,0:T(8,128)S(1)} %top.2.value), channel_id=1, source_target_pairs={{0,3},{1,2},{2,1},{3,0},{4,7},{5,6},{6,5},{7,4},{8,11},{9,10},{10,... | collective-permute-start | bytes 196616 | tf_op jit(solution)/shard_map/ppermute | solution.py:116
  35.2 1.4 %collective-permute-start.7 = (f32[128,128]{1,0:T(8,128)S(1)}, f32[128,128]{1,0:T(8,128)S(1)}, u32[]{:S(2)}, u32[]{:S(2)}) collective-permute-start(f32[128,128]{1,0:T(8,128)S(1)} %top.2.value), channel_id=1, source_target_pairs={{0,1},{1,0},{2,3},{3,2},{4,5},{5,4},{6,7},{7,6},{8,9},{9,8},{10,11... | collective-permute-start | bytes 196616 | tf_op jit(solution)/shard_map/ppermute | solution.py:116
  36.6 1.9 %eliminate.2.inverse = f32[64,64]{1,0:T(8,128)S(1)} custom-call(f32[160,128]{1,0:T(8,128)S(1)} %collect.2.one, f32[160,128]{1,0:T(8,128)S(1)} %collective-permute-done.6.two), custom_call_target="tpu_custom_call" | custom-call | flops 100000000 | bytes 8388608 | tf_op jit(solution)/shard_map/eliminate/pallas_call | solution.py:42
  38.5 1.8 %middle.3 = (f32[1024,512]{1,0:T(8,128)S(1)}, bf16[1024,512]{1,0:T(8,128)(2,1)S(1)}, bf16[1024,512]{1,0:T(8,128)(2,1)S(1)}, f32[64,512]{1,0:T(8,128)S(1)}, f32[6...) custom-call(f32[64,64]{1,0:T(8,128)S(1)} %eliminate.2.inverse, f32[64,512]{1,0:T(8,128)S(1)} %collective-permute-done.2.away.rest_0_, ...), custom_call_target="tpu_custom_call" | custom-call | flops 603979776 | bytes 4194304 | tf_op jit(solution)/shard_map/middle/pallas_call | solution.py:42
  40.4 1.0 %middle.4 = (f32[1024,512]{1,0:T(8,128)S(1)}, bf16[1024,512]{1,0:T(8,128)(2,1)S(1)}, bf16[1024,512]{1,0:T(8,128)(2,1)S(1)}, f32[64,512]{1,0:T(8,128)S(1)}) custom-call(f32[64,64]{1,0:T(8,128)S(1)} %eliminate.2.inverse, bf16[192,1024]{1,0:T(8,128)(2,1)S(1)} %get-tuple-element.76.rest_0_, f32[256,128]{1,0:T(8,128)S(1)} %unfold.5.rest_1_, ...), custom_call_target="tpu_custom_call" | custom-call | flops 301989888 | bytes 2097152 | tf_op jit(solution)/shard_map/middle/pallas_call | solution.py:42
  41.5 1.0 %middle.5 = (f32[1024,512]{1,0:T(8,128)S(1)}, bf16[1024,512]{1,0:T(8,128)(2,1)S(1)}, bf16[1024,512]{1,0:T(8,128)(2,1)S(1)}, f32[64,512]{1,0:T(8,128)S(1)}) custom-call(f32[64,64]{1,0:T(8,128)S(1)} %eliminate.2.inverse, bf16[192,1024]{1,0:T(8,128)(2,1)S(1)} %get-tuple-element.76.rest_0_, ...), custom_call_target="tpu_custom_call", output_to_operand_aliasing={{0}: (6, {}), {1}: (7, {}), {2}: (8, {})} | custom-call | flops 301989888 | bytes 2097152 | tf_op jit(solution)/shard_map/middle/pallas_call | solution.py:42
  42.5 0.3 collective-permute-done.10.refs_1_
  42.8 1.6 %collective-permute-start.11 = (f32[64,512]{1,0:T(8,128)S(1)}, f32[64,512]{1,0:T(8,128)S(1)}, u32[]{:S(2)}, u32[]{:S(2)}) collective-permute-start(f32[64,512]{1,0:T(8,128)S(1)} %add.7.refs_0_), channel_id=1, source_target_pairs={{0,16},{8,24},{16,0},{24,8},{1,17},{9,25},{17,1},{25,9},{2,18},{10... | collective-permute-start | bytes 393224 | tf_op jit(solution)/shard_map/ppermute | solution.py:201
  44.4 4.0 %collective-permute-done.11.refs_1_ = f32[64,512]{1,0:T(8,128)S(1)} collective-permute-done((f32[64,512]{1,0:T(8,128)S(1)}, f32[64,512]{1,0:T(8,128)S(1)}, u32[]{:S(2)}, u32[]{:S(2)}) %collective-permute-start.11) | collective-permute-done | bytes 131104 | tf_op jit(solution)/shard_map/ppermute | solution.py:201
  48.6 0.6 multiply_mine.3
  49.2 0.7 collective-permute-done.12.away.rest_0_
  49.9 0.5 multiply_other.3
  50.7 0.6 collective-permute-start.15
  51.3 1.6 %collective-permute-start.14 = (f32[160,128]{1,0:T(8,128)S(1)}, f32[160,128]{1,0:T(8,128)S(1)}, u32[]{:S(2)}, u32[]{:S(2)}) collective-permute-start(f32[160,128]{1,0:T(8,128)S(1)} %get-tuple-element.95), channel_id=1, source_target_pairs={{0,3},{1,2},{2,1},{3,0},{4,7},{5,6},{6,5},{7,4},{8,11},{9,10},{10,... | collective-permute-start | bytes 245768 | tf_op jit(solution)/shard_map/ppermute | solution.py:116
  52.9 1.3 %collective-permute-start.13 = (f32[160,128]{1,0:T(8,128)S(1)}, f32[160,128]{1,0:T(8,128)S(1)}, u32[]{:S(2)}, u32[]{:S(2)}) collective-permute-start(f32[160,128]{1,0:T(8,128)S(1)} %get-tuple-element.93.sent), channel_id=1, source_target_pairs={{0,1},{1,0},{2,3},{3,2},{4,5},{5,4},{6,7},{7,6},{8,9},{9,8},{10,11... | collective-permute-start | bytes 245768 | tf_op jit(solution)/shard_map/ppermute | solution.py:116
  54.3 1.8 %collective-permute-done.15.refs_2_ = f32[160,128]{1,0:T(8,128)S(1)} collective-permute-done((f32[160,128]{1,0:T(8,128)S(1)}, f32[160,128]{1,0:T(8,128)S(1)}, u32[]{:S(2)}, u32[]{:S(2)}) %collective-permute-start.15) | collective-permute-done | bytes 81952 | tf_op jit(solution)/shard_map/ppermute | solution.py:116
  56.0 1.2 %collective-permute-done.14.refs_1_ = f32[160,128]{1,0:T(8,128)S(1)} collective-permute-done((f32[160,128]{1,0:T(8,128)S(1)}, f32[160,128]{1,0:T(8,128)S(1)}, u32[]{:S(2)}, u32[]{:S(2)}) %collective-permute-start.14) | collective-permute-done | bytes 81952 | tf_op jit(solution)/shard_map/ppermute | solution.py:116
  57.2 1.1 %collective-permute-done.13.refs_0_ = f32[160,128]{1,0:T(8,128)S(1)} collective-permute-done((f32[160,128]{1,0:T(8,128)S(1)}, f32[160,128]{1,0:T(8,128)S(1)}, u32[]{:S(2)}, u32[]{:S(2)}) %collective-permute-start.13) | collective-permute-done | bytes 81952 | tf_op jit(solution)/shard_map/ppermute | solution.py:116
  58.4 2.5 %collective-permute-start.16 = (f32[160,128]{1,0:T(8,128)S(1)}, f32[160,128]{1,0:T(8,128)S(1)}, u32[]{:S(2)}, u32[]{:S(2)}) collective-permute-start(f32[160,128]{1,0:T(8,128)S(1)} %collect.3.one), channel_id=1, source_target_pairs={{0,4},{1,5},{2,6},{3,7},{4,0},{5,1},{6,2},{7,3},{8,12},{9,13},{10,... | collective-permute-start | bytes 245768 | tf_op jit(solution)/shard_map/ppermute | solution.py:116
  60.9 4.1 %collective-permute-done.16.two = f32[160,128]{1,0:T(8,128)S(1)} collective-permute-done((f32[160,128]{1,0:T(8,128)S(1)}, f32[160,128]{1,0:T(8,128)S(1)}, u32[]{:S(2)}, u32[]{:S(2)}) %collective-permute-start.16) | collective-permute-done | bytes 81952 | tf_op jit(solution)/shard_map/ppermute | solution.py:116
  65.1 2.6 %collective-permute-start.18 = (f32[128,128]{1,0:T(8,128)S(1)}, f32[128,128]{1,0:T(8,128)S(1)}, u32[]{:S(2)}, u32[]{:S(2)}) collective-permute-start(f32[128,128]{1,0:T(8,128)S(1)} %top.3.value), channel_id=1, source_target_pairs={{0,3},{1,2},{2,1},{3,0},{4,7},{5,6},{6,5},{7,4},{8,11},{9,10},{10,... | collective-permute-start | bytes 196616 | tf_op jit(solution)/shard_map/ppermute | solution.py:116
  67.7 0.8 collective-permute-start.17
  68.5 1.9 %eliminate.3.inverse = f32[64,64]{1,0:T(8,128)S(1)} custom-call(f32[160,128]{1,0:T(8,128)S(1)} %collect.3.one, f32[160,128]{1,0:T(8,128)S(1)} %collective-permute-done.16.two), custom_call_target="tpu_custom_call" | custom-call | flops 100000000 | bytes 8388608 | tf_op jit(solution)/shard_map/eliminate/pallas_call | solution.py:42
  70.5 0.6 widen.2
  71.1 0.9 %collective-permute-done.17.value = f32[128,128]{1,0:T(8,128)S(1)} collective-permute-done((f32[128,128]{1,0:T(8,128)S(1)}, f32[128,128]{1,0:T(8,128)S(1)}, u32[]{:S(2)}, u32[]{:S(2)}) %collective-permute-start.17) | collective-permute-done | bytes 65568 | tf_op jit(solution)/shard_map/ppermute | solution.py:116
  72.0 0.6 widen.3
  72.7 1.3 %final.2 = (f32[1024,512]{1,0:T(8,128)S(1)}, f32[1024,512]{1,0:T(8,128)S(1)}, f32[64,1024]{1,0:T(8,128)}, bf16[192,1024]{1,0:T(8,128)(2,1)S(1)}) custom-call(f32[64,64]{1,0:T(8,128)S(1)} %eliminate.3.inverse, f32[64,512]{1,0:T(8,128)S(1)} %collective-permute-done.12.away.rest_0_, f32[64,512]{1,0:T(8,128)S(1)} %add.8.mine.rest_1_, ...), custom_call_target="tpu_custom_call" | custom-call | flops 201326592 | bytes 4194304 | tf_op jit(solution)/shard_map/final/pallas_call | solution.py:42
  74.0 1.6 %collective-permute-start.21 = (f32[32,128]{1,0:T(8,128)S(1)}, f32[32,128]{1,0:T(8,128)S(1)}, u32[]{:S(2)}, u32[]{:S(2)}) collective-permute-start(f32[32,128]{1,0:T(8,128)S(1)} %add.9.refs_0_), channel_id=1, source_target_pairs={{0,16},{8,24},{16,0},{24,8},{1,17},{9,25},{17,1},{25,9},{2,18},{10... | collective-permute-start | bytes 49160 | tf_op jit(solution)/shard_map/ppermute | solution.py:116
  75.6 1.3 %final.3 = (f32[1024,512]{1,0:T(8,128)S(1)}, f32[1024,512]{1,0:T(8,128)S(1)}, f32[1024,1024]{1,0:T(8,128)}) custom-call(f32[64,64]{1,0:T(8,128)S(1)} %eliminate.3.inverse, bf16[192,1024]{1,0:T(8,128)(2,1)S(1)} %get-tuple-element.105.rest_0_, f32[256,128]{1,0:T(8,128)S(1)} %unfold.7.stacked.rest_1_, f32[1024,512]{1,0:T(8,128)S(1)} %get-tuple-element.106.rest_2_, ...), custom_call_target="tpu_custom_call" | custom-call | flops 201326592 | bytes 4194304 | tf_op jit(solution)/shard_map/final/pallas_call | solution.py:42
  77.0 0.8 %collective-permute-done.21.refs_1_ = f32[32,128]{1,0:T(8,128)S(1)} collective-permute-done((f32[32,128]{1,0:T(8,128)S(1)}, f32[32,128]{1,0:T(8,128)S(1)}, u32[]{:S(2)}, u32[]{:S(2)}) %collective-permute-start.21) | collective-permute-done | bytes 16416 | tf_op jit(solution)/shard_map/ppermute | solution.py:116
  77.8 3.1 %finish.1 = (f32[64,1024]{1,0:T(8,128)}, f32[1024,1024]{1,0:T(8,128)}, f32[1024,1024]{1,0:T(8,128)}) custom-call(f32[32,128]{1,0:T(8,128)S(1)} %add.9.refs_0_, f32[32,128]{1,0:T(8,128)S(1)} %collective-permute-done.21.refs_1_, f32[64,512]{1,0:T(8,128)S(1)} %get-tuple-element.102.refs_2_, ...), custom_call_target="tpu_custom_call", output_to_operand_aliasing={{1}: (7, {})} | custom-call | flops 100000000 | bytes 8388608 | tf_op jit(solution)/shard_map/finish/pallas_call | solution.py:42
  (26 shorter events, 1.3 us)
Async XLA Ops:
  7.1 1.5 %collective-permute-start = (f32[64,512]{1,0:T(8,128)S(1)}, f32[64,512]{1,0:T(8,128)S(1)}, u32[]{:S(2)}, u32[]{:S(2)}) collective-permute-start(f32[64,512]{1,0:T(8,128)S(1)} %get-tuple-element.61), channel_id=1, source_target_pairs={{0,8},{8,0},{16,24},{24,16},{1,9},{9,1},{17,25},{25,17},{2,10},{10... | collective-permute-start | bytes 393224 | tf_op jit(solution)/shard_map/ppermute | solution.py:116
  8.6 6.8 %collective-permute-start.1 = (f32[64,512]{1,0:T(8,128)S(1)}, f32[64,512]{1,0:T(8,128)S(1)}, u32[]{:S(2)}, u32[]{:S(2)}) collective-permute-start(f32[64,512]{1,0:T(8,128)S(1)} %add.5.refs_0_), channel_id=1, source_target_pairs={{0,16},{8,24},{16,0},{24,8},{1,17},{9,25},{17,1},{25,9},{2,18},{10... | collective-permute-start | bytes 393224 | tf_op jit(solution)/shard_map/ppermute | solution.py:201
  15.4 1.4 %collective-permute-start.2 = (f32[64,512]{1,0:T(8,128)S(1)}, f32[64,512]{1,0:T(8,128)S(1)}, u32[]{:S(2)}, u32[]{:S(2)}) collective-permute-start(f32[64,512]{1,0:T(8,128)S(1)} %add.6.mine.rest_1_), channel_id=1, source_target_pairs={{0,8},{8,0},{16,24},{24,16},{1,9},{9,1},{17,25},{25,17},{2,10},{10... | collective-permute-start | bytes 393224 | tf_op jit(solution)/shard_map/ppermute | solution.py:116
  17.6 4.6 %collective-permute-start.5 = (f32[160,128]{1,0:T(8,128)S(1)}, f32[160,128]{1,0:T(8,128)S(1)}, u32[]{:S(2)}, u32[]{:S(2)}) collective-permute-start(f32[160,128]{1,0:T(8,128)S(1)} %get-tuple-element.72), channel_id=1, source_target_pairs={{0,2},{1,3},{2,0},{3,1},{4,6},{5,7},{6,4},{7,5},{8,10},{9,11},{10,... | collective-permute-start | bytes 245768 | tf_op jit(solution)/shard_map/ppermute | solution.py:116
  19.4 5.7 %collective-permute-start.4 = (f32[160,128]{1,0:T(8,128)S(1)}, f32[160,128]{1,0:T(8,128)S(1)}, u32[]{:S(2)}, u32[]{:S(2)}) collective-permute-start(f32[160,128]{1,0:T(8,128)S(1)} %get-tuple-element.71), channel_id=1, source_target_pairs={{0,3},{1,2},{2,1},{3,0},{4,7},{5,6},{6,5},{7,4},{8,11},{9,10},{10,... | collective-permute-start | bytes 245768 | tf_op jit(solution)/shard_map/ppermute | solution.py:116
  20.8 5.6 %collective-permute-start.3 = (f32[160,128]{1,0:T(8,128)S(1)}, f32[160,128]{1,0:T(8,128)S(1)}, u32[]{:S(2)}, u32[]{:S(2)}) collective-permute-start(f32[160,128]{1,0:T(8,128)S(1)} %get-tuple-element.69.sent), channel_id=1, source_target_pairs={{0,1},{1,0},{2,3},{3,2},{4,5},{5,4},{6,7},{7,6},{8,9},{9,8},{10,11... | collective-permute-start | bytes 245768 | tf_op jit(solution)/shard_map/ppermute | solution.py:116
  26.4 6.6 %collective-permute-start.6 = (f32[160,128]{1,0:T(8,128)S(1)}, f32[160,128]{1,0:T(8,128)S(1)}, u32[]{:S(2)}, u32[]{:S(2)}) collective-permute-start(f32[160,128]{1,0:T(8,128)S(1)} %collect.2.one), channel_id=1, source_target_pairs={{0,4},{1,5},{2,6},{3,7},{4,0},{5,1},{6,2},{7,3},{8,12},{9,13},{10,... | collective-permute-start | bytes 245768 | tf_op jit(solution)/shard_map/ppermute | solution.py:116
  33.0 5.5 %collective-permute-start.9 = (f32[128,128]{1,0:T(8,128)S(1)}, f32[128,128]{1,0:T(8,128)S(1)}, u32[]{:S(2)}, u32[]{:S(2)}) collective-permute-start(f32[128,128]{1,0:T(8,128)S(1)} %top.2.value), channel_id=1, source_target_pairs={{0,2},{1,3},{2,0},{3,1},{4,6},{5,7},{6,4},{7,5},{8,10},{9,11},{10,... | collective-permute-start | bytes 196616 | tf_op jit(solution)/shard_map/ppermute | solution.py:116
  33.6 6.7 %collective-permute-start.8 = (f32[128,128]{1,0:T(8,128)S(1)}, f32[128,128]{1,0:T(8,128)S(1)}, u32[]{:S(2)}, u32[]{:S(2)}) collective-permute-start(f32[128,128]{1,0:T(8,128)S(1)} %top.2.value), channel_id=1, source_target_pairs={{0,3},{1,2},{2,1},{3,0},{4,7},{5,6},{6,5},{7,4},{8,11},{9,10},{10,... | collective-permute-start | bytes 196616 | tf_op jit(solution)/shard_map/ppermute | solution.py:116
  35.2 5.2 %collective-permute-start.7 = (f32[128,128]{1,0:T(8,128)S(1)}, f32[128,128]{1,0:T(8,128)S(1)}, u32[]{:S(2)}, u32[]{:S(2)}) collective-permute-start(f32[128,128]{1,0:T(8,128)S(1)} %top.2.value), channel_id=1, source_target_pairs={{0,1},{1,0},{2,3},{3,2},{4,5},{5,4},{6,7},{7,6},{8,9},{9,8},{10,11... | collective-permute-start | bytes 196616 | tf_op jit(solution)/shard_map/ppermute | solution.py:116
  41.4 1.4 %collective-permute-start.10 = (f32[64,512]{1,0:T(8,128)S(1)}, f32[64,512]{1,0:T(8,128)S(1)}, u32[]{:S(2)}, u32[]{:S(2)}) collective-permute-start(f32[64,512]{1,0:T(8,128)S(1)} %get-tuple-element.85), channel_id=1, source_target_pairs={{0,8},{8,0},{16,24},{24,16},{1,9},{9,1},{17,25},{25,17},{2,10},{10... | collective-permute-start | bytes 393224 | tf_op jit(solution)/shard_map/ppermute | solution.py:116
  42.8 5.6 %collective-permute-start.11 = (f32[64,512]{1,0:T(8,128)S(1)}, f32[64,512]{1,0:T(8,128)S(1)}, u32[]{:S(2)}, u32[]{:S(2)}) collective-permute-start(f32[64,512]{1,0:T(8,128)S(1)} %add.7.refs_0_), channel_id=1, source_target_pairs={{0,16},{8,24},{16,0},{24,8},{1,17},{9,25},{17,1},{25,9},{2,18},{10... | collective-permute-start | bytes 393224 | tf_op jit(solution)/shard_map/ppermute | solution.py:201
  48.5 1.4 %collective-permute-start.12 = (f32[64,512]{1,0:T(8,128)S(1)}, f32[64,512]{1,0:T(8,128)S(1)}, u32[]{:S(2)}, u32[]{:S(2)}) collective-permute-start(f32[64,512]{1,0:T(8,128)S(1)} %add.8.mine.rest_1_), channel_id=1, source_target_pairs={{0,8},{8,0},{16,24},{24,16},{1,9},{9,1},{17,25},{25,17},{2,10},{10... | collective-permute-start | bytes 393224 | tf_op jit(solution)/shard_map/ppermute | solution.py:116
  50.7 5.4 %collective-permute-start.15 = (f32[160,128]{1,0:T(8,128)S(1)}, f32[160,128]{1,0:T(8,128)S(1)}, u32[]{:S(2)}, u32[]{:S(2)}) collective-permute-start(f32[160,128]{1,0:T(8,128)S(1)} %get-tuple-element.96), channel_id=1, source_target_pairs={{0,2},{1,3},{2,0},{3,1},{4,6},{5,7},{6,4},{7,5},{8,10},{9,11},{10,... | collective-permute-start | bytes 245768 | tf_op jit(solution)/shard_map/ppermute | solution.py:116
  51.3 5.9 %collective-permute-start.14 = (f32[160,128]{1,0:T(8,128)S(1)}, f32[160,128]{1,0:T(8,128)S(1)}, u32[]{:S(2)}, u32[]{:S(2)}) collective-permute-start(f32[160,128]{1,0:T(8,128)S(1)} %get-tuple-element.95), channel_id=1, source_target_pairs={{0,3},{1,2},{2,1},{3,0},{4,7},{5,6},{6,5},{7,4},{8,11},{9,10},{10,... | collective-permute-start | bytes 245768 | tf_op jit(solution)/shard_map/ppermute | solution.py:116
  52.9 5.5 %collective-permute-start.13 = (f32[160,128]{1,0:T(8,128)S(1)}, f32[160,128]{1,0:T(8,128)S(1)}, u32[]{:S(2)}, u32[]{:S(2)}) collective-permute-start(f32[160,128]{1,0:T(8,128)S(1)} %get-tuple-element.93.sent), channel_id=1, source_target_pairs={{0,1},{1,0},{2,3},{3,2},{4,5},{5,4},{6,7},{7,6},{8,9},{9,8},{10,11... | collective-permute-start | bytes 245768 | tf_op jit(solution)/shard_map/ppermute | solution.py:116
  58.4 6.5 %collective-permute-start.16 = (f32[160,128]{1,0:T(8,128)S(1)}, f32[160,128]{1,0:T(8,128)S(1)}, u32[]{:S(2)}, u32[]{:S(2)}) collective-permute-start(f32[160,128]{1,0:T(8,128)S(1)} %collect.3.one), channel_id=1, source_target_pairs={{0,4},{1,5},{2,6},{3,7},{4,0},{5,1},{6,2},{7,3},{8,12},{9,13},{10,... | collective-permute-start | bytes 245768 | tf_op jit(solution)/shard_map/ppermute | solution.py:116
  65.0 5.5 %collective-permute-start.19 = (f32[128,128]{1,0:T(8,128)S(1)}, f32[128,128]{1,0:T(8,128)S(1)}, u32[]{:S(2)}, u32[]{:S(2)}) collective-permute-start(f32[128,128]{1,0:T(8,128)S(1)} %top.3.value), channel_id=1, source_target_pairs={{0,2},{1,3},{2,0},{3,1},{4,6},{5,7},{6,4},{7,5},{8,10},{9,11},{10,... | collective-permute-start | bytes 196616 | tf_op jit(solution)/shard_map/ppermute | solution.py:116
  65.1 5.9 %collective-permute-start.18 = (f32[128,128]{1,0:T(8,128)S(1)}, f32[128,128]{1,0:T(8,128)S(1)}, u32[]{:S(2)}, u32[]{:S(2)}) collective-permute-start(f32[128,128]{1,0:T(8,128)S(1)} %top.3.value), channel_id=1, source_target_pairs={{0,3},{1,2},{2,1},{3,0},{4,7},{5,6},{6,5},{7,4},{8,11},{9,10},{10,... | collective-permute-start | bytes 196616 | tf_op jit(solution)/shard_map/ppermute | solution.py:116
  67.7 4.3 %collective-permute-start.17 = (f32[128,128]{1,0:T(8,128)S(1)}, f32[128,128]{1,0:T(8,128)S(1)}, u32[]{:S(2)}, u32[]{:S(2)}) collective-permute-start(f32[128,128]{1,0:T(8,128)S(1)} %top.3.value), channel_id=1, source_target_pairs={{0,1},{1,0},{2,3},{3,2},{4,5},{5,4},{6,7},{7,6},{8,9},{9,8},{10,11... | collective-permute-start | bytes 196616 | tf_op jit(solution)/shard_map/ppermute | solution.py:116
  72.6 1.3 %collective-permute-start.20 = (f32[32,128]{1,0:T(8,128)S(1)}, f32[32,128]{1,0:T(8,128)S(1)}, u32[]{:S(2)}, u32[]{:S(2)}) collective-permute-start(f32[32,128]{1,0:T(8,128)S(1)} %get-tuple-element.101.refs_0_), channel_id=1, source_target_pairs={{0,8},{8,0},{16,24},{24,16},{1,9},{9,1},{17,25},{25,17},{2,10},{10... | collective-permute-start | bytes 49160 | tf_op jit(solution)/shard_map/ppermute | solution.py:116
  74.0 3.8 %collective-permute-start.21 = (f32[32,128]{1,0:T(8,128)S(1)}, f32[32,128]{1,0:T(8,128)S(1)}, u32[]{:S(2)}, u32[]{:S(2)}) collective-permute-start(f32[32,128]{1,0:T(8,128)S(1)} %add.9.refs_0_), channel_id=1, source_target_pairs={{0,16},{8,24},{16,0},{24,8},{1,17},{9,25},{17,1},{25,9},{2,18},{10... | collective-permute-start | bytes 49160 | tf_op jit(solution)/shard_map/ppermute | solution.py:116

commit v15 on v14

--- a/solution.py
+++ b/solution.py
@@ -157,39 +157,45 @@
             return call(body, "add", [(a, pltpu.VMEM) for a in arrays], [out], cost=(10**5, 10**6), limit=4)[0]
 
         def first(right):
+            fine, blocks = tall // 2, 2 * steps
+
+            def rows(i):
+                return slice(fine * i, fine * (i + 1))
+
             def body(o_in, s_in, d_in, r_in, o, u, h0, l0, h1, l1, away, mine, sp, d, right, r_sem, sems):
                 s = place()
                 right_move = pltpu.make_async_copy(r_in, right, r_sem)
                 right_move.start()
                 moves = {}
-                for i in range(steps):
+                for i in range(blocks):
                     for a, (source, target) in enumerate(((o_in, o), (s_in, sp), (d_in, d))):
-                        block = source.at[pl.ds(gal_at(i, s), tall), :]
-                        move = pltpu.make_async_copy(block, target.at[chunk(i), :], sems.at[i, a])
+                        at = pl.multiple_of(gal_at(i // 2, s) + i % 2 * fine, fine)
+                        block = source.at[pl.ds(at, fine), :]
+                        move = pltpu.make_async_copy(block, target.at[rows(i), :], sems.at[i, a])
                         move.start(priority=(i + a) % 2)
                         moves[i, a] = move
                 right_move.wait()
                 rights = [split(right[:, pl.ds(pix_at(p, s), half)]) for p in (0, 1)]
-                for i in range(steps):
+                for i in range(blocks):
                     total = None
                     for a in range(3):
                         moves[i, a].wait()
                     for p, (h, l) in enumerate(((h0, l0), (h1, l1))):
-                        at = chunk(i), pl.ds(pix_at(p, s), half)
+                        at = rows(i), pl.ds(pix_at(p, s), half)
                         pulled = o[at] + d[at] * (1 / MU)
                         u[at] = pulled
                         pair = split(pulled - sp[at])
-                        h[chunk(i), :], l[chunk(i), :] = pair
+                        h[rows(i), :], l[rows(i), :] = pair
                         term = dot_nt(rights[p], pair)
                         total = term if total is None else total + term
-                    out = away if i < steps // 2 else mine
-                    out[:, chunk(i % (steps // 2))] = total
+                    out = away if i < steps else mine
+                    out[:, rows(i % steps)] = total
 
             ins = [(a, pltpu.HBM) for a in (observed, sparse_init, dual_init, right)]
             outs = [((n_rows, n_cols), F32, pltpu.VMEM)] * 2 + [((n_rows, half), BF16, pltpu.VMEM)] * 4
             outs += [((rank, n_rows // 2), F32, pltpu.VMEM)] * 2
             scratch = [pltpu.VMEM((n_rows, n_cols), F32)] * 2 + [pltpu.VMEM((rank, n_cols), F32)]
-            scratch += [pltpu.SemaphoreType.DMA(()), pltpu.SemaphoreType.DMA((steps, 3))]
+            scratch += [pltpu.SemaphoreType.DMA(()), pltpu.SemaphoreType.DMA((blocks, 3))]
             cost = (6 * rank * n_rows * n_cols, 16 * n_rows * n_cols)
             got = call(body, "first", ins, outs, scratch, cost=cost)
             return got[0], got[1], got[2:4], got[4:6], got[6:8]

time: 81.2 us -> 81.6 us (level)
  no operation moved by 1% of the time
where the time goes in v15:
time: 81.6 us; the launch traced here: 81.4 us
  waiting for transfers between devices  29.9 us (37%)
  starting transfers between devices  26.2 us (32%)
  Pallas kernels  24.4 us (30%)
  between operations  0.97 us (1%)
    pallas_call x30, Pallas kernels, call(): pl.pallas_call(body, name=name, in_specs=[pl.BlockSpec(memory_space=space...  24.4 us
    ppermute x20, waiting for transfers between devices, swap(): return lax.ppermute(value, axis, [(i, i ^ bit) for i in range(n)])  22 us
    ppermute x20, starting transfers between devices, swap(): return lax.ppermute(value, axis, [(i, i ^ bit) for i in range(n)])  21.7 us
    ppermute x2, waiting for transfers between devices, sum_gal(): lax.ppermute(mine, 'gal', [(i, (i + CORES * k) % n_gal) for i in range(n_...  7.88 us
    ppermute x2, starting transfers between devices, sum_gal(): lax.ppermute(mine, 'gal', [(i, (i + CORES * k) % n_gal) for i in range(n_...  4.51 us
  transfers between devices with their start and end apart: 22, of which 16 were waited for; matrix products, arithmetic and copies ran while one was open for 0% of the time, Pallas kernels for 14%

profile of v15, /device:TPU:0, one launch (start us, length us, event | category | flops | bytes accessed | tf_op | source)
XLA Modules:
  0.0 81.4 jit_solution(14352338091448988927)
XLA Ops:
  0.6 6.8 %first.1 = (f32[1024,1024]{1,0:T(8,128)S(1)}, f32[1024,1024]{1,0:T(8,128)S(1)}, bf16[1024,512]{1,0:T(8,128)(2,1)S(1)}, bf16[1024,512]{1,0:T(8,128)(2,1)S(1)}, bf...) custom-call(f32[1024,1024]{1,0:T(8,128)} %o_in.1, ...), custom_call_target="tpu_custom_call" | custom-call | flops 402653184 | bytes 16777216 | tf_op jit(solution)/shard_map/first/pallas_call | solution.py:42
  7.4 0.5 collective-permute-start
  8.0 1.0 %collective-permute-done.refs_1_ = f32[64,512]{1,0:T(8,128)S(1)} collective-permute-done((f32[64,512]{1,0:T(8,128)S(1)}, f32[64,512]{1,0:T(8,128)S(1)}, u32[]{:S(2)}, u32[]{:S(2)}) %collective-permute-start) | collective-permute-done | bytes 131104 | tf_op jit(solution)/shard_map/ppermute | solution.py:116
  9.0 2.9 %collective-permute-start.1 = (f32[64,512]{1,0:T(8,128)S(1)}, f32[64,512]{1,0:T(8,128)S(1)}, u32[]{:S(2)}, u32[]{:S(2)}) collective-permute-start(f32[64,512]{1,0:T(8,128)S(1)} %add.5.refs_0_), channel_id=1, source_target_pairs={{0,16},{8,24},{16,0},{24,8},{1,17},{9,25},{17,1},{25,9},{2,18},{10... | collective-permute-start | bytes 393224 | tf_op jit(solution)/shard_map/ppermute | solution.py:207
  11.9 3.8 %collective-permute-done.1.refs_1_ = f32[64,512]{1,0:T(8,128)S(1)} collective-permute-done((f32[64,512]{1,0:T(8,128)S(1)}, f32[64,512]{1,0:T(8,128)S(1)}, u32[]{:S(2)}, u32[]{:S(2)}) %collective-permute-start.1) | collective-permute-done | bytes 131104 | tf_op jit(solution)/shard_map/ppermute | solution.py:207
  15.8 0.6 multiply_mine.2
  16.4 0.7 collective-permute-done.2.away.rest_0_
  17.1 0.5 multiply_other.2
  17.9 1.9 %collective-permute-start.5 = (f32[160,128]{1,0:T(8,128)S(1)}, f32[160,128]{1,0:T(8,128)S(1)}, u32[]{:S(2)}, u32[]{:S(2)}) collective-permute-start(f32[160,128]{1,0:T(8,128)S(1)} %get-tuple-element.72), channel_id=1, source_target_pairs={{0,2},{1,3},{2,0},{3,1},{4,6},{5,7},{6,4},{7,5},{8,10},{9,11},{10,... | collective-permute-start | bytes 245768 | tf_op jit(solution)/shard_map/ppermute | solution.py:116
  19.8 1.4 %collective-permute-start.4 = (f32[160,128]{1,0:T(8,128)S(1)}, f32[160,128]{1,0:T(8,128)S(1)}, u32[]{:S(2)}, u32[]{:S(2)}) collective-permute-start(f32[160,128]{1,0:T(8,128)S(1)} %get-tuple-element.71), channel_id=1, source_target_pairs={{0,3},{1,2},{2,1},{3,0},{4,7},{5,6},{6,5},{7,4},{8,11},{9,10},{10,... | collective-permute-start | bytes 245768 | tf_op jit(solution)/shard_map/ppermute | solution.py:116
  21.2 0.3 collective-permute-start.3
  21.5 1.1 %collective-permute-done.5.refs_2_ = f32[160,128]{1,0:T(8,128)S(1)} collective-permute-done((f32[160,128]{1,0:T(8,128)S(1)}, f32[160,128]{1,0:T(8,128)S(1)}, u32[]{:S(2)}, u32[]{:S(2)}) %collective-permute-start.5) | collective-permute-done | bytes 81952 | tf_op jit(solution)/shard_map/ppermute | solution.py:116
  22.6 2.9 %collective-permute-done.4.refs_1_ = f32[160,128]{1,0:T(8,128)S(1)} collective-permute-done((f32[160,128]{1,0:T(8,128)S(1)}, f32[160,128]{1,0:T(8,128)S(1)}, u32[]{:S(2)}, u32[]{:S(2)}) %collective-permute-start.4) | collective-permute-done | bytes 81952 | tf_op jit(solution)/shard_map/ppermute | solution.py:116
  25.5 1.2 %collective-permute-done.3.refs_0_ = f32[160,128]{1,0:T(8,128)S(1)} collective-permute-done((f32[160,128]{1,0:T(8,128)S(1)}, f32[160,128]{1,0:T(8,128)S(1)}, u32[]{:S(2)}, u32[]{:S(2)}) %collective-permute-start.3) | collective-permute-done | bytes 81952 | tf_op jit(solution)/shard_map/ppermute | solution.py:116
  26.7 2.7 %collective-permute-start.6 = (f32[160,128]{1,0:T(8,128)S(1)}, f32[160,128]{1,0:T(8,128)S(1)}, u32[]{:S(2)}, u32[]{:S(2)}) collective-permute-start(f32[160,128]{1,0:T(8,128)S(1)} %collect.2.one), channel_id=1, source_target_pairs={{0,4},{1,5},{2,6},{3,7},{4,0},{5,1},{6,2},{7,3},{8,12},{9,13},{10,... | collective-permute-start | bytes 245768 | tf_op jit(solution)/shard_map/ppermute | solution.py:116
  29.4 4.0 %collective-permute-done.6.two = f32[160,128]{1,0:T(8,128)S(1)} collective-permute-done((f32[160,128]{1,0:T(8,128)S(1)}, f32[160,128]{1,0:T(8,128)S(1)}, u32[]{:S(2)}, u32[]{:S(2)}) %collective-permute-start.6) | collective-permute-done | bytes 81952 | tf_op jit(solution)/shard_map/ppermute | solution.py:116
  33.4 0.6 collective-permute-start.9
  34.0 1.6 %collective-permute-start.8 = (f32[128,128]{1,0:T(8,128)S(1)}, f32[128,128]{1,0:T(8,128)S(1)}, u32[]{:S(2)}, u32[]{:S(2)}) collective-permute-start(f32[128,128]{1,0:T(8,128)S(1)} %top.2.value), channel_id=1, source_target_pairs={{0,3},{1,2},{2,1},{3,0},{4,7},{5,6},{6,5},{7,4},{8,11},{9,10},{10,... | collective-permute-start | bytes 196616 | tf_op jit(solution)/shard_map/ppermute | solution.py:116
  35.6 1.4 %collective-permute-start.7 = (f32[128,128]{1,0:T(8,128)S(1)}, f32[128,128]{1,0:T(8,128)S(1)}, u32[]{:S(2)}, u32[]{:S(2)}) collective-permute-start(f32[128,128]{1,0:T(8,128)S(1)} %top.2.value), channel_id=1, source_target_pairs={{0,1},{1,0},{2,3},{3,2},{4,5},{5,4},{6,7},{7,6},{8,9},{9,8},{10,11... | collective-permute-start | bytes 196616 | tf_op jit(solution)/shard_map/ppermute | solution.py:116
  36.9 1.9 %eliminate.2.inverse = f32[64,64]{1,0:T(8,128)S(1)} custom-call(f32[160,128]{1,0:T(8,128)S(1)} %collect.2.one, f32[160,128]{1,0:T(8,128)S(1)} %collective-permute-done.6.two), custom_call_target="tpu_custom_call" | custom-call | flops 100000000 | bytes 8388608 | tf_op jit(solution)/shard_map/eliminate/pallas_call | solution.py:42
  38.9 1.8 %middle.3 = (f32[1024,512]{1,0:T(8,128)S(1)}, bf16[1024,512]{1,0:T(8,128)(2,1)S(1)}, bf16[1024,512]{1,0:T(8,128)(2,1)S(1)}, f32[64,512]{1,0:T(8,128)S(1)}, f32[6...) custom-call(f32[64,64]{1,0:T(8,128)S(1)} %eliminate.2.inverse, f32[64,512]{1,0:T(8,128)S(1)} %collective-permute-done.2.away.rest_0_, ...), custom_call_target="tpu_custom_call" | custom-call | flops 603979776 | bytes 4194304 | tf_op jit(solution)/shard_map/middle/pallas_call | solution.py:42
  40.8 1.0 %middle.4 = (f32[1024,512]{1,0:T(8,128)S(1)}, bf16[1024,512]{1,0:T(8,128)(2,1)S(1)}, bf16[1024,512]{1,0:T(8,128)(2,1)S(1)}, f32[64,512]{1,0:T(8,128)S(1)}) custom-call(f32[64,64]{1,0:T(8,128)S(1)} %eliminate.2.inverse, bf16[192,1024]{1,0:T(8,128)(2,1)S(1)} %get-tuple-element.76.rest_0_, f32[256,128]{1,0:T(8,128)S(1)} %unfold.5.rest_1_, ...), custom_call_target="tpu_custom_call" | custom-call | flops 301989888 | bytes 2097152 | tf_op jit(solution)/shard_map/middle/pallas_call | solution.py:42
  41.9 1.0 %middle.5 = (f32[1024,512]{1,0:T(8,128)S(1)}, bf16[1024,512]{1,0:T(8,128)(2,1)S(1)}, bf16[1024,512]{1,0:T(8,128)(2,1)S(1)}, f32[64,512]{1,0:T(8,128)S(1)}) custom-call(f32[64,64]{1,0:T(8,128)S(1)} %eliminate.2.inverse, bf16[192,1024]{1,0:T(8,128)(2,1)S(1)} %get-tuple-element.76.rest_0_, ...), custom_call_target="tpu_custom_call", output_to_operand_aliasing={{0}: (6, {}), {1}: (7, {}), {2}: (8, {})} | custom-call | flops 301989888 | bytes 2097152 | tf_op jit(solution)/shard_map/middle/pallas_call | solution.py:42
  42.9 0.3 collective-permute-done.10.refs_1_
  43.2 1.6 %collective-permute-start.11 = (f32[64,512]{1,0:T(8,128)S(1)}, f32[64,512]{1,0:T(8,128)S(1)}, u32[]{:S(2)}, u32[]{:S(2)}) collective-permute-start(f32[64,512]{1,0:T(8,128)S(1)} %add.7.refs_0_), channel_id=1, source_target_pairs={{0,16},{8,24},{16,0},{24,8},{1,17},{9,25},{17,1},{25,9},{2,18},{10... | collective-permute-start | bytes 393224 | tf_op jit(solution)/shard_map/ppermute | solution.py:207
  44.8 4.1 %collective-permute-done.11.refs_1_ = f32[64,512]{1,0:T(8,128)S(1)} collective-permute-done((f32[64,512]{1,0:T(8,128)S(1)}, f32[64,512]{1,0:T(8,128)S(1)}, u32[]{:S(2)}, u32[]{:S(2)}) %collective-permute-start.11) | collective-permute-done | bytes 131104 | tf_op jit(solution)/shard_map/ppermute | solution.py:207
  48.9 0.6 multiply_mine.3
  49.5 0.7 collective-permute-done.12.away.rest_0_
  50.3 0.5 multiply_other.3
  51.1 0.6 collective-permute-start.15
  51.7 1.6 %collective-permute-start.14 = (f32[160,128]{1,0:T(8,128)S(1)}, f32[160,128]{1,0:T(8,128)S(1)}, u32[]{:S(2)}, u32[]{:S(2)}) collective-permute-start(f32[160,128]{1,0:T(8,128)S(1)} %get-tuple-element.95), channel_id=1, source_target_pairs={{0,3},{1,2},{2,1},{3,0},{4,7},{5,6},{6,5},{7,4},{8,11},{9,10},{10,... | collective-permute-start | bytes 245768 | tf_op jit(solution)/shard_map/ppermute | solution.py:116
  53.3 1.4 %collective-permute-start.13 = (f32[160,128]{1,0:T(8,128)S(1)}, f32[160,128]{1,0:T(8,128)S(1)}, u32[]{:S(2)}, u32[]{:S(2)}) collective-permute-start(f32[160,128]{1,0:T(8,128)S(1)} %get-tuple-element.93.sent), channel_id=1, source_target_pairs={{0,1},{1,0},{2,3},{3,2},{4,5},{5,4},{6,7},{7,6},{8,9},{9,8},{10,11... | collective-permute-start | bytes 245768 | tf_op jit(solution)/shard_map/ppermute | solution.py:116
  54.6 1.8 %collective-permute-done.15.refs_2_ = f32[160,128]{1,0:T(8,128)S(1)} collective-permute-done((f32[160,128]{1,0:T(8,128)S(1)}, f32[160,128]{1,0:T(8,128)S(1)}, u32[]{:S(2)}, u32[]{:S(2)}) %collective-permute-start.15) | collective-permute-done | bytes 81952 | tf_op jit(solution)/shard_map/ppermute | solution.py:116
  56.4 1.2 %collective-permute-done.14.refs_1_ = f32[160,128]{1,0:T(8,128)S(1)} collective-permute-done((f32[160,128]{1,0:T(8,128)S(1)}, f32[160,128]{1,0:T(8,128)S(1)}, u32[]{:S(2)}, u32[]{:S(2)}) %collective-permute-start.14) | collective-permute-done | bytes 81952 | tf_op jit(solution)/shard_map/ppermute | solution.py:116
  57.6 1.2 %collective-permute-done.13.refs_0_ = f32[160,128]{1,0:T(8,128)S(1)} collective-permute-done((f32[160,128]{1,0:T(8,128)S(1)}, f32[160,128]{1,0:T(8,128)S(1)}, u32[]{:S(2)}, u32[]{:S(2)}) %collective-permute-start.13) | collective-permute-done | bytes 81952 | tf_op jit(solution)/shard_map/ppermute | solution.py:116
  58.8 2.5 %collective-permute-start.16 = (f32[160,128]{1,0:T(8,128)S(1)}, f32[160,128]{1,0:T(8,128)S(1)}, u32[]{:S(2)}, u32[]{:S(2)}) collective-permute-start(f32[160,128]{1,0:T(8,128)S(1)} %collect.3.one), channel_id=1, source_target_pairs={{0,4},{1,5},{2,6},{3,7},{4,0},{5,1},{6,2},{7,3},{8,12},{9,13},{10,... | collective-permute-start | bytes 245768 | tf_op jit(solution)/shard_map/ppermute | solution.py:116
  61.2 4.1 %collective-permute-done.16.two = f32[160,128]{1,0:T(8,128)S(1)} collective-permute-done((f32[160,128]{1,0:T(8,128)S(1)}, f32[160,128]{1,0:T(8,128)S(1)}, u32[]{:S(2)}, u32[]{:S(2)}) %collective-permute-start.16) | collective-permute-done | bytes 81952 | tf_op jit(solution)/shard_map/ppermute | solution.py:116
  65.5 2.7 %collective-permute-start.18 = (f32[128,128]{1,0:T(8,128)S(1)}, f32[128,128]{1,0:T(8,128)S(1)}, u32[]{:S(2)}, u32[]{:S(2)}) collective-permute-start(f32[128,128]{1,0:T(8,128)S(1)} %top.3.value), channel_id=1, source_target_pairs={{0,3},{1,2},{2,1},{3,0},{4,7},{5,6},{6,5},{7,4},{8,11},{9,10},{10,... | collective-permute-start | bytes 196616 | tf_op jit(solution)/shard_map/ppermute | solution.py:116
  68.1 0.8 collective-permute-start.17
  68.9 1.9 %eliminate.3.inverse = f32[64,64]{1,0:T(8,128)S(1)} custom-call(f32[160,128]{1,0:T(8,128)S(1)} %collect.3.one, f32[160,128]{1,0:T(8,128)S(1)} %collective-permute-done.16.two), custom_call_target="tpu_custom_call" | custom-call | flops 100000000 | bytes 8388608 | tf_op jit(solution)/shard_map/eliminate/pallas_call | solution.py:42
  70.8 0.6 widen.2
  71.5 0.9 %collective-permute-done.17.value = f32[128,128]{1,0:T(8,128)S(1)} collective-permute-done((f32[128,128]{1,0:T(8,128)S(1)}, f32[128,128]{1,0:T(8,128)S(1)}, u32[]{:S(2)}, u32[]{:S(2)}) %collective-permute-start.17) | collective-permute-done | bytes 65568 | tf_op jit(solution)/shard_map/ppermute | solution.py:116
  72.4 0.6 widen.3
  73.0 1.3 %final.2 = (f32[1024,512]{1,0:T(8,128)S(1)}, f32[1024,512]{1,0:T(8,128)S(1)}, f32[64,1024]{1,0:T(8,128)}, bf16[192,1024]{1,0:T(8,128)(2,1)S(1)}) custom-call(f32[64,64]{1,0:T(8,128)S(1)} %eliminate.3.inverse, f32[64,512]{1,0:T(8,128)S(1)} %collective-permute-done.12.away.rest_0_, f32[64,512]{1,0:T(8,128)S(1)} %add.8.mine.rest_1_, ...), custom_call_target="tpu_custom_call" | custom-call | flops 201326592 | bytes 4194304 | tf_op jit(solution)/shard_map/final/pallas_call | solution.py:42
  74.4 1.6 %collective-permute-start.21 = (f32[32,128]{1,0:T(8,128)S(1)}, f32[32,128]{1,0:T(8,128)S(1)}, u32[]{:S(2)}, u32[]{:S(2)}) collective-permute-start(f32[32,128]{1,0:T(8,128)S(1)} %add.9.refs_0_), channel_id=1, source_target_pairs={{0,16},{8,24},{16,0},{24,8},{1,17},{9,25},{17,1},{25,9},{2,18},{10... | collective-permute-start | bytes 49160 | tf_op jit(solution)/shard_map/ppermute | solution.py:116
  76.0 1.3 %final.3 = (f32[1024,512]{1,0:T(8,128)S(1)}, f32[1024,512]{1,0:T(8,128)S(1)}, f32[1024,1024]{1,0:T(8,128)}) custom-call(f32[64,64]{1,0:T(8,128)S(1)} %eliminate.3.inverse, bf16[192,1024]{1,0:T(8,128)(2,1)S(1)} %get-tuple-element.105.rest_0_, f32[256,128]{1,0:T(8,128)S(1)} %unfold.7.stacked.rest_1_, f32[1024,512]{1,0:T(8,128)S(1)} %get-tuple-element.106.rest_2_, ...), custom_call_target="tpu_custom_call" | custom-call | flops 201326592 | bytes 4194304 | tf_op jit(solution)/shard_map/final/pallas_call | solution.py:42
  77.3 0.9 %collective-permute-done.21.refs_1_ = f32[32,128]{1,0:T(8,128)S(1)} collective-permute-done((f32[32,128]{1,0:T(8,128)S(1)}, f32[32,128]{1,0:T(8,128)S(1)}, u32[]{:S(2)}, u32[]{:S(2)}) %collective-permute-start.21) | collective-permute-done | bytes 16416 | tf_op jit(solution)/shard_map/ppermute | solution.py:116
  78.2 3.1 %finish.1 = (f32[64,1024]{1,0:T(8,128)}, f32[1024,1024]{1,0:T(8,128)}, f32[1024,1024]{1,0:T(8,128)}) custom-call(f32[32,128]{1,0:T(8,128)S(1)} %add.9.refs_0_, f32[32,128]{1,0:T(8,128)S(1)} %collective-permute-done.21.refs_1_, f32[64,512]{1,0:T(8,128)S(1)} %get-tuple-element.102.refs_2_, ...), custom_call_target="tpu_custom_call", output_to_operand_aliasing={{1}: (7, {})} | custom-call | flops 100000000 | bytes 8388608 | tf_op jit(solution)/shard_map/finish/pallas_call | solution.py:42
  (26 shorter events, 1.2 us)
Async XLA Ops:
  7.4 1.5 %collective-permute-start = (f32[64,512]{1,0:T(8,128)S(1)}, f32[64,512]{1,0:T(8,128)S(1)}, u32[]{:S(2)}, u32[]{:S(2)}) collective-permute-start(f32[64,512]{1,0:T(8,128)S(1)} %get-tuple-element.61), channel_id=1, source_target_pairs={{0,8},{8,0},{16,24},{24,16},{1,9},{9,1},{17,25},{25,17},{2,10},{10... | collective-permute-start | bytes 393224 | tf_op jit(solution)/shard_map/ppermute | solution.py:116
  9.0 6.8 %collective-permute-start.1 = (f32[64,512]{1,0:T(8,128)S(1)}, f32[64,512]{1,0:T(8,128)S(1)}, u32[]{:S(2)}, u32[]{:S(2)}) collective-permute-start(f32[64,512]{1,0:T(8,128)S(1)} %add.5.refs_0_), channel_id=1, source_target_pairs={{0,16},{8,24},{16,0},{24,8},{1,17},{9,25},{17,1},{25,9},{2,18},{10... | collective-permute-start | bytes 393224 | tf_op jit(solution)/shard_map/ppermute | solution.py:207
  15.7 1.4 %collective-permute-start.2 = (f32[64,512]{1,0:T(8,128)S(1)}, f32[64,512]{1,0:T(8,128)S(1)}, u32[]{:S(2)}, u32[]{:S(2)}) collective-permute-start(f32[64,512]{1,0:T(8,128)S(1)} %add.6.mine.rest_1_), channel_id=1, source_target_pairs={{0,8},{8,0},{16,24},{24,16},{1,9},{9,1},{17,25},{25,17},{2,10},{10... | collective-permute-start | bytes 393224 | tf_op jit(solution)/shard_map/ppermute | solution.py:116
  17.9 4.6 %collective-permute-start.5 = (f32[160,128]{1,0:T(8,128)S(1)}, f32[160,128]{1,0:T(8,128)S(1)}, u32[]{:S(2)}, u32[]{:S(2)}) collective-permute-start(f32[160,128]{1,0:T(8,128)S(1)} %get-tuple-element.72), channel_id=1, source_target_pairs={{0,2},{1,3},{2,0},{3,1},{4,6},{5,7},{6,4},{7,5},{8,10},{9,11},{10,... | collective-permute-start | bytes 245768 | tf_op jit(solution)/shard_map/ppermute | solution.py:116
  19.8 5.7 %collective-permute-start.4 = (f32[160,128]{1,0:T(8,128)S(1)}, f32[160,128]{1,0:T(8,128)S(1)}, u32[]{:S(2)}, u32[]{:S(2)}) collective-permute-start(f32[160,128]{1,0:T(8,128)S(1)} %get-tuple-element.71), channel_id=1, source_target_pairs={{0,3},{1,2},{2,1},{3,0},{4,7},{5,6},{6,5},{7,4},{8,11},{9,10},{10,... | collective-permute-start | bytes 245768 | tf_op jit(solution)/shard_map/ppermute | solution.py:116
  21.2 5.6 %collective-permute-start.3 = (f32[160,128]{1,0:T(8,128)S(1)}, f32[160,128]{1,0:T(8,128)S(1)}, u32[]{:S(2)}, u32[]{:S(2)}) collective-permute-start(f32[160,128]{1,0:T(8,128)S(1)} %get-tuple-element.69.sent), channel_id=1, source_target_pairs={{0,1},{1,0},{2,3},{3,2},{4,5},{5,4},{6,7},{7,6},{8,9},{9,8},{10,11... | collective-permute-start | bytes 245768 | tf_op jit(solution)/shard_map/ppermute | solution.py:116
  26.7 6.6 %collective-permute-start.6 = (f32[160,128]{1,0:T(8,128)S(1)}, f32[160,128]{1,0:T(8,128)S(1)}, u32[]{:S(2)}, u32[]{:S(2)}) collective-permute-start(f32[160,128]{1,0:T(8,128)S(1)} %collect.2.one), channel_id=1, source_target_pairs={{0,4},{1,5},{2,6},{3,7},{4,0},{5,1},{6,2},{7,3},{8,12},{9,13},{10,... | collective-permute-start | bytes 245768 | tf_op jit(solution)/shard_map/ppermute | solution.py:116
  33.4 5.5 %collective-permute-start.9 = (f32[128,128]{1,0:T(8,128)S(1)}, f32[128,128]{1,0:T(8,128)S(1)}, u32[]{:S(2)}, u32[]{:S(2)}) collective-permute-start(f32[128,128]{1,0:T(8,128)S(1)} %top.2.value), channel_id=1, source_target_pairs={{0,2},{1,3},{2,0},{3,1},{4,6},{5,7},{6,4},{7,5},{8,10},{9,11},{10,... | collective-permute-start | bytes 196616 | tf_op jit(solution)/shard_map/ppermute | solution.py:116
  34.0 6.7 %collective-permute-start.8 = (f32[128,128]{1,0:T(8,128)S(1)}, f32[128,128]{1,0:T(8,128)S(1)}, u32[]{:S(2)}, u32[]{:S(2)}) collective-permute-start(f32[128,128]{1,0:T(8,128)S(1)} %top.2.value), channel_id=1, source_target_pairs={{0,3},{1,2},{2,1},{3,0},{4,7},{5,6},{6,5},{7,4},{8,11},{9,10},{10,... | collective-permute-start | bytes 196616 | tf_op jit(solution)/shard_map/ppermute | solution.py:116
  35.6 5.2 %collective-permute-start.7 = (f32[128,128]{1,0:T(8,128)S(1)}, f32[128,128]{1,0:T(8,128)S(1)}, u32[]{:S(2)}, u32[]{:S(2)}) collective-permute-start(f32[128,128]{1,0:T(8,128)S(1)} %top.2.value), channel_id=1, source_target_pairs={{0,1},{1,0},{2,3},{3,2},{4,5},{5,4},{6,7},{7,6},{8,9},{9,8},{10,11... | collective-permute-start | bytes 196616 | tf_op jit(solution)/shard_map/ppermute | solution.py:116
  41.8 1.4 %collective-permute-start.10 = (f32[64,512]{1,0:T(8,128)S(1)}, f32[64,512]{1,0:T(8,128)S(1)}, u32[]{:S(2)}, u32[]{:S(2)}) collective-permute-start(f32[64,512]{1,0:T(8,128)S(1)} %get-tuple-element.85), channel_id=1, source_target_pairs={{0,8},{8,0},{16,24},{24,16},{1,9},{9,1},{17,25},{25,17},{2,10},{10... | collective-permute-start | bytes 393224 | tf_op jit(solution)/shard_map/ppermute | solution.py:116
  43.2 5.6 %collective-permute-start.11 = (f32[64,512]{1,0:T(8,128)S(1)}, f32[64,512]{1,0:T(8,128)S(1)}, u32[]{:S(2)}, u32[]{:S(2)}) collective-permute-start(f32[64,512]{1,0:T(8,128)S(1)} %add.7.refs_0_), channel_id=1, source_target_pairs={{0,16},{8,24},{16,0},{24,8},{1,17},{9,25},{17,1},{25,9},{2,18},{10... | collective-permute-start | bytes 393224 | tf_op jit(solution)/shard_map/ppermute | solution.py:207
  48.9 1.4 %collective-permute-start.12 = (f32[64,512]{1,0:T(8,128)S(1)}, f32[64,512]{1,0:T(8,128)S(1)}, u32[]{:S(2)}, u32[]{:S(2)}) collective-permute-start(f32[64,512]{1,0:T(8,128)S(1)} %add.8.mine.rest_1_), channel_id=1, source_target_pairs={{0,8},{8,0},{16,24},{24,16},{1,9},{9,1},{17,25},{25,17},{2,10},{10... | collective-permute-start | bytes 393224 | tf_op jit(solution)/shard_map/ppermute | solution.py:116
  51.1 5.4 %collective-permute-start.15 = (f32[160,128]{1,0:T(8,128)S(1)}, f32[160,128]{1,0:T(8,128)S(1)}, u32[]{:S(2)}, u32[]{:S(2)}) collective-permute-start(f32[160,128]{1,0:T(8,128)S(1)} %get-tuple-element.96), channel_id=1, source_target_pairs={{0,2},{1,3},{2,0},{3,1},{4,6},{5,7},{6,4},{7,5},{8,10},{9,11},{10,... | collective-permute-start | bytes 245768 | tf_op jit(solution)/shard_map/ppermute | solution.py:116
  51.7 5.9 %collective-permute-start.14 = (f32[160,128]{1,0:T(8,128)S(1)}, f32[160,128]{1,0:T(8,128)S(1)}, u32[]{:S(2)}, u32[]{:S(2)}) collective-permute-start(f32[160,128]{1,0:T(8,128)S(1)} %get-tuple-element.95), channel_id=1, source_target_pairs={{0,3},{1,2},{2,1},{3,0},{4,7},{5,6},{6,5},{7,4},{8,11},{9,10},{10,... | collective-permute-start | bytes 245768 | tf_op jit(solution)/shard_map/ppermute | solution.py:116
  53.3 5.5 %collective-permute-start.13 = (f32[160,128]{1,0:T(8,128)S(1)}, f32[160,128]{1,0:T(8,128)S(1)}, u32[]{:S(2)}, u32[]{:S(2)}) collective-permute-start(f32[160,128]{1,0:T(8,128)S(1)} %get-tuple-element.93.sent), channel_id=1, source_target_pairs={{0,1},{1,0},{2,3},{3,2},{4,5},{5,4},{6,7},{7,6},{8,9},{9,8},{10,11... | collective-permute-start | bytes 245768 | tf_op jit(solution)/shard_map/ppermute | solution.py:116
  58.8 6.5 %collective-permute-start.16 = (f32[160,128]{1,0:T(8,128)S(1)}, f32[160,128]{1,0:T(8,128)S(1)}, u32[]{:S(2)}, u32[]{:S(2)}) collective-permute-start(f32[160,128]{1,0:T(8,128)S(1)} %collect.3.one), channel_id=1, source_target_pairs={{0,4},{1,5},{2,6},{3,7},{4,0},{5,1},{6,2},{7,3},{8,12},{9,13},{10,... | collective-permute-start | bytes 245768 | tf_op jit(solution)/shard_map/ppermute | solution.py:116
  65.3 5.5 %collective-permute-start.19 = (f32[128,128]{1,0:T(8,128)S(1)}, f32[128,128]{1,0:T(8,128)S(1)}, u32[]{:S(2)}, u32[]{:S(2)}) collective-permute-start(f32[128,128]{1,0:T(8,128)S(1)} %top.3.value), channel_id=1, source_target_pairs={{0,2},{1,3},{2,0},{3,1},{4,6},{5,7},{6,4},{7,5},{8,10},{9,11},{10,... | collective-permute-start | bytes 196616 | tf_op jit(solution)/shard_map/ppermute | solution.py:116
  65.5 6.0 %collective-permute-start.18 = (f32[128,128]{1,0:T(8,128)S(1)}, f32[128,128]{1,0:T(8,128)S(1)}, u32[]{:S(2)}, u32[]{:S(2)}) collective-permute-start(f32[128,128]{1,0:T(8,128)S(1)} %top.3.value), channel_id=1, source_target_pairs={{0,3},{1,2},{2,1},{3,0},{4,7},{5,6},{6,5},{7,4},{8,11},{9,10},{10,... | collective-permute-start | bytes 196616 | tf_op jit(solution)/shard_map/ppermute | solution.py:116
  68.1 4.3 %collective-permute-start.17 = (f32[128,128]{1,0:T(8,128)S(1)}, f32[128,128]{1,0:T(8,128)S(1)}, u32[]{:S(2)}, u32[]{:S(2)}) collective-permute-start(f32[128,128]{1,0:T(8,128)S(1)} %top.3.value), channel_id=1, source_target_pairs={{0,1},{1,0},{2,3},{3,2},{4,5},{5,4},{6,7},{7,6},{8,9},{9,8},{10,11... | collective-permute-start | bytes 196616 | tf_op jit(solution)/shard_map/ppermute | solution.py:116
  73.0 1.4 %collective-permute-start.20 = (f32[32,128]{1,0:T(8,128)S(1)}, f32[32,128]{1,0:T(8,128)S(1)}, u32[]{:S(2)}, u32[]{:S(2)}) collective-permute-start(f32[32,128]{1,0:T(8,128)S(1)} %get-tuple-element.101.refs_0_), channel_id=1, source_target_pairs={{0,8},{8,0},{16,24},{24,16},{1,9},{9,1},{17,25},{25,17},{2,10},{10... | collective-permute-start | bytes 49160 | tf_op jit(solution)/shard_map/ppermute | solution.py:116
  74.4 3.8 %collective-permute-start.21 = (f32[32,128]{1,0:T(8,128)S(1)}, f32[32,128]{1,0:T(8,128)S(1)}, u32[]{:S(2)}, u32[]{:S(2)}) collective-permute-start(f32[32,128]{1,0:T(8,128)S(1)} %add.9.refs_0_), channel_id=1, source_target_pairs={{0,16},{8,24},{16,0},{24,8},{1,17},{9,25},{17,1},{25,9},{2,18},{10... | collective-permute-start | bytes 49160 | tf_op jit(solution)/shard_map/ppermute | solution.py:116
